TPU v7x, 32 devices: a whole 2x2x4 slice. The times are simulated.
32 devices in a mesh: groups: 2 (over x), wide: 8 (over z, y), narrow: 2 (over core).
Axes of the slice: x: 2, y: 2, z: 4, core: 2. Of those that a mesh axis runs over, the one named last changes fastest.
Arguments:
- tokens: bfloat16 [4096, 4096], P(('groups', 'wide')), parts along dimension 0, may hold values from -6 to 6
- norm_gain: float32 [4096], replicated, may hold values from 0.1 to 1.9
- w_in: bfloat16 [4096, 1024], P('wide'), may hold values from -0.09375 to 0.09375
- w_out: bfloat16 [1024, 4096], P('wide', 'narrow'), may hold values from -0.1875 to 0.1875
- w_up: bfloat16 [8, 1024, 2688], P('wide', None, 'narrow'), may hold values from -0.1875 to 0.1875
- w_down: bfloat16 [8, 2688, 1024], P('wide', 'narrow'), may hold values from -0.15625 to 0.15625
- expert_ids: int32 [4096, 4], P(('groups', 'wide')), parts along dimension 0, may hold values from 0 to 7, all different within a row; in each aligned block of 256 rows (0 to 255, 256 to 511, ...) at most 192 rows name the same one
- gate_weights: float32 [4096, 4], P(('groups', 'wide')), parts along dimension 0, may hold values from 0.1 to 1
Outputs:
- result: bfloat16 [4096, 4096], P(('groups', 'wide'), 'narrow'), parts along dimension 0
There are 2 independent parts, one for each index of `groups`. A program takes and returns all parts, laid end to end along the dimension named above; an argument that names none is the same for every part. Nothing has to cross between parts.
Inputs may be any that keep to these rules, and one draw needn't show every extreme that they name: `expert_ids`: within the 256 rows of one index of wide, the entries of a row differ and no expert is named by more than 192 rows.
All inputs are finite; a program needn't handle non-finite values.
Results may differ from a plain program's by a relative error of at most 0.013.
Values may be sent and summed in bfloat16 or wider, within the bound.
No kernel may reach another device: no remote copies, remote signals or barrier semaphores. Data moves between devices by JAX's collectives and lax.ppermute only.
A program may use at most 128 MiB of HBM per device.

v0:
```python
import jax
import jax.numpy as jnp
from jax import lax
from jax.sharding import PartitionSpec as P


def local(tokens, norm_gain, w_in, w_out, w_up, w_down, expert_ids, gate_weights):
    experts = lax.axis_size("wide")
    tok_rows = tokens.shape[0]
    top_count = expert_ids.shape[1]
    capacity = 3 * tok_rows * top_count // (2 * experts)
    full_in, full_out = (
        lax.all_gather(w_in, "wide", axis=0, tiled=True),
        lax.all_gather(w_out, "wide", axis=0, tiled=True),
    )
    widened = tokens.astype(jnp.float32)
    scale = lax.rsqrt(jnp.mean(widened * widened, axis=-1, keepdims=True) + 1e-05)
    normed = (widened * scale * norm_gain).astype(jnp.bfloat16)
    latent = jnp.dot(normed, full_in, preferred_element_type=jnp.float32).astype(jnp.bfloat16)
    width = latent.shape[1]
    flat_ids = expert_ids.reshape(-1)
    onehot = (flat_ids[:, None] == jnp.arange(experts, dtype=jnp.int32)[None, :]).astype(jnp.int32)
    slot_index = jnp.sum((jnp.cumsum(onehot, axis=0) - 1) * onehot, axis=-1)
    target = flat_ids * capacity + slot_index
    repeated = jnp.repeat(latent, top_count, axis=0)
    buffer = jnp.zeros((experts * capacity, width), jnp.bfloat16).at[target].set(repeated)
    buffer = buffer.reshape(experts, capacity, width)
    up_weight = w_up[0]
    down_weight = w_down[0]
    received = lax.all_to_all(buffer, "wide", split_axis=0, concat_axis=0, tiled=True)
    sources = received.shape[0]
    items = received.shape[1]
    rows = received.reshape(sources * items, received.shape[2])
    hidden = jnp.dot(rows, up_weight, preferred_element_type=jnp.float32)
    hidden = jnp.square(jnp.maximum(hidden, 0.0)).astype(jnp.bfloat16)
    partial_value = jnp.dot(hidden, down_weight, preferred_element_type=jnp.float32)
    summed = lax.psum_scatter(
        partial_value.astype(jnp.bfloat16), "narrow", scatter_dimension=1, tiled=True
    ).astype(jnp.float32)
    outgoing = summed.astype(jnp.bfloat16).reshape(sources, items, summed.shape[1])
    returned = lax.all_to_all(outgoing, "wide", split_axis=0, concat_axis=0, tiled=True)
    columns = returned.shape[2]
    flat_back = returned.reshape(experts * capacity, columns)
    picked = flat_back[target].astype(jnp.float32).reshape(tok_rows, top_count, columns)
    mixture = jnp.sum(picked * gate_weights[:, :, None], axis=1).astype(jnp.bfloat16)
    mixture = lax.all_gather(mixture, "narrow", axis=1, tiled=True)
    branch = jnp.dot(mixture, full_out, preferred_element_type=jnp.float32)
    half_width = full_out.shape[1]
    own_half = lax.dynamic_slice_in_dim(
        widened, lax.axis_index("narrow") * half_width, half_width, 1
    )
    return (own_half + branch).astype(jnp.bfloat16)


def solution(mesh):
    in_specs = (
        P(("groups", "wide"), None),
        P(),
        P("wide", None),
        P("wide", "narrow"),
        P("wide", None, "narrow"),
        P("wide", "narrow", None),
        P(("groups", "wide"), None),
        P(("groups", "wide"), None),
    )
    out_specs = P(("groups", "wide"), "narrow")
    return jax.shard_map(local, mesh=mesh, in_specs=in_specs, out_specs=out_specs, check_vma=False)
```

profile of v0, /device:TPU:0, one launch (start us, length us, event | category | flops | bytes accessed | tf_op | source)
XLA Modules:
  0.0 364.9 jit_solution(6078926013426687952)
XLA Ops:
  6.5 0.0 copy-start
  6.5 0.0 copy-start.3
  6.5 0.0 all-gather.3.cloned.1.call-start
  6.5 0.7 all-gather.3.cloned.1.call-update
  7.3 0.0 reduce-scatter.2.cloned.1.call-start
  7.3 0.9 copy.11
  8.2 0.1 eq.29
  8.3 0.1 eq.25
  8.5 2.3 reduce-window.6
  10.7 0.3 slice_reduce_fusion
  11.0 0.2 reduce-window.9
  11.2 0.7 broadcast_multiply_fusion
  11.9 0.1 copy.10
  12.0 0.1 mul.52
  12.1 0.1 add_bitcast_fusion
  12.2 2.1 multiply_reduce_fusion
  14.4 122.8 %all-gather.3.cloned.1.call-done = bf16[4096,1024]{1,0:T(8,128)(2,1)} async-done(((bf16[512,1024]{1,0:T(8,128)(2,1)}), bf16[4096,1024]{1,0:T(8,128)(2,1)}) %all-gather.3.cloned.1.call-update) | async-done | bytes 8388624 | tf_op jit(solution)/shard_map/all_gather | solution.py:13
  137.2 0.0 copy-done.3
  137.2 6.4 %fusion.11 = bf16[256,1024]{1,0:T(8,128)(2,1)S(1)} fusion(bf16[4096,1024]{1,0:T(8,128)(2,1)} %all-gather.3.cloned.1.call-done, f32[4096]{0:T(1024)S(1)} %copy-done.3, f32[256]{0:T(256)S(1)} %add_rsqrt_fusion, bf16[256,4096]{1,0:T(8,128)(2,1)} %param.8), kind=kOutput, calls=%fused_computation.19 | convolution fusion | flops 2151940096 | bytes 11027456 | tf_op jit(solution)/shard_map/dot_general | solution.py:19
  143.6 2.0 broadcast_in_dim.5
  145.6 4.0 %reshape.96 = bf16[1024,1024]{1,0:T(8,128)(2,1)} reshape(bf16[256,4,1024]{2,1,0:T(4,128)(2,1)} %broadcast_in_dim.5) | data formatting | bytes 4194304 | tf_op jit(solution)/shard_map/reshape | solution.py:25
  149.5 8.1 %scatter_custom_fusion = bf16[1536,1024]{1,0:T(8,128)(2,1)} fusion(s32[1024]{0:T(1024)S(1)} %bitcast.36, bf16[1024,1024]{1,0:T(8,128)(2,1)} %reshape.96, bf16[]{:T(256)} %constant.6.clone.1), kind=kCustom, calls=%fused_computation.17 | custom fusion | bytes 3146240 | tf_op jit(solution)/shard_map/scatter | solution.py:26
  157.6 74.1 %all_to_all.10 = bf16[8,192,1024]{2,1,0:T(8,128)(2,1)S(1)} all-to-all(bf16[8,192,1024]{2,1,0:T(8,128)(2,1)} %bitcast.32), channel_id=1, replica_groups=mesh['groups'=2,'wide'=8,'narrow'=2] {'wide'}, dimensions={0} | all-to-all | bytes 6291456 | tf_op jit(solution)/shard_map/all_to_all | solution.py:30
  231.7 0.0 copy-done
  231.7 0.0 copy-start.2
  231.7 5.3 %fusion.1 = bf16[1536,1344]{1,0:T(8,128)(2,1)S(1)} fusion(bf16[1536,1024]{1,0:T(8,128)(2,1)S(1)} %bitcast.33, bf16[1,1024,1344]{1,2,0:T(8,128)(2,1)S(1)} %copy-done), kind=kOutput, calls=%fused_computation.4 | convolution fusion | flops 4234051584 | bytes 10027008 | tf_op jit(solution)/shard_map/dot_general | solution.py:34
  237.0 0.0 copy-done.2
  237.0 6.4 %convolution_convert_fusion = bf16[1536,1024]{1,0:T(8,128)(2,1)} fusion(bf16[1536,1344]{1,0:T(8,128)(2,1)S(1)} %fusion.1, bf16[1,1344,1024]{2,1,0:T(8,128)(2,1)S(1)} %copy-done.2), kind=kOutput, calls=%fused_computation.7 | convolution fusion | flops 4229431296 | bytes 10027008 | tf_op jit(solution)/shard_map/dot_general | solution.py:36
  243.5 0.0 reduce-scatter.2.cloned.1.call-update
  243.5 0.0 all-gather.5.cloned.1.call-start
  243.5 0.7 all-gather.5.cloned.1.call-update
  244.2 9.3 %reduce-scatter.2.cloned.1.call-done = bf16[1536,512]{1,0:T(8,128)(2,1)} async-done(((bf16[1536,1024]{1,0:T(8,128)(2,1)}), bf16[1536,512]{1,0:T(8,128)(2,1)}) %reduce-scatter.2.cloned.1.call-update) | async-done | bytes 1572880 | tf_op jit(solution)/shard_map/reduce_scatter | solution.py:37
  253.5 5.9 %all-to-all-start.1 = ((bf16[8,192,512]{2,1,0:T(8,128)(2,1)}), bf16[8,192,512]{2,1,0:T(8,128)(2,1)}, u32[]{:S(2)}, u32[]{:S(2)}) async-start(bf16[8,192,512]{2,1,0:T(8,128)(2,1)} %bitcast.34), calls=%async_computation.2 | async-start | bytes 3145728 | tf_op jit(solution)/shard_map/all_to_all | solution.py:41
  259.4 0.0 copy-start.1
  259.4 4.1 %convert_element_type.35 = f32[256,4096]{1,0:T(8,128)} convert(bf16[256,4096]{1,0:T(8,128)(2,1)} %param.8) | non-fusion elementwise | flops 1048576 | bytes 6291456 | tf_op jit(solution)/shard_map/convert_element_type | solution.py:16
  263.5 0.0 copy-done.1
  263.5 0.1 copy.13
  263.7 50.2 %all-to-all-done.1 = bf16[8,192,512]{2,1,0:T(8,128)(2,1)} async-done(((bf16[8,192,512]{2,1,0:T(8,128)(2,1)}), bf16[8,192,512]{2,1,0:T(8,128)(2,1)}, u32[]{:S(2)}, u32[]{:S(2)}) %all-to-all-start.1) | async-done | bytes 1572896 | tf_op jit(solution)/shard_map/all_to_all | solution.py:41
  313.9 6.8 %gather_fusion = bf16[1024,512]{1,0:T(8,128)(2,1)} fusion(bf16[1536,512]{1,0:T(8,128)(2,1)} %bitcast.8, s32[1024]{0:T(1024)S(1)} %broadcast_clamp_fusion), kind=kCustom, calls=%fused_computation | custom fusion | bytes 2101248 | tf_op jit(solution)/shard_map/gather | solution.py:44
  320.7 2.8 reshape.83
  323.5 3.0 multiply_reduce_fusion.1
  326.5 2.2 all_gather.10
  328.6 24.7 %all-gather.5.cloned.1.call-done = bf16[1024,2048]{1,0:T(8,128)(2,1)} async-done(((bf16[128,2048]{1,0:T(8,128)(2,1)}), bf16[1024,2048]{1,0:T(8,128)(2,1)}) %all-gather.5.cloned.1.call-update) | async-done | bytes 4194320 | tf_op jit(solution)/shard_map/all_gather | solution.py:14
  353.3 5.1 %fusion.4 = bf16[256,2048]{1,0:T(8,128)(2,1)} fusion(bf16[256,1024]{1,0:T(8,128)(2,1)S(1)} %all_gather.10, bf16[1024,2048]{1,0:T(8,128)(2,1)} %all-gather.5.cloned.1.call-done, f32[256,4096]{1,0:T(8,128)} %convert_element_type.35, s32[]{:T(128)S(6)} %select_n.14), kind=kOutput, calls=%fused_computation.11 | convolution fusion | flops 1074790400 | bytes 7864324 | tf_op jit(solution)/shard_map/dot_general | solution.py:47
  (5 shorter events, 0.0 us)
Async XLA Ops:
  6.5 225.2 %copy-start = (bf16[1,1024,1344]{1,2,0:T(8,128)(2,1)S(1)}, bf16[1,1024,1344]{1,2,0:T(8,128)(2,1)}, u32[]{:S(2)}) copy-start(bf16[1,1024,1344]{1,2,0:T(8,128)(2,1)} %param.12) | copy-start | bytes 8257540
  6.5 130.6 %copy-start.3 = (f32[4096]{0:T(1024)S(1)}, f32[4096]{0:T(1024)}, u32[]{:S(2)}) copy-start(f32[4096]{0:T(1024)} %param.9) | copy-start | bytes 49156
  6.5 130.6 %all-gather.3.cloned.1.call-start = ((), (), s32[]{:S(2)}) async-start(), calls=%async_computation.3 | async-start | bytes 9437184 | tf_op jit(solution)/shard_map/all_gather | solution.py:13
  7.3 246.3 %reduce-scatter.2.cloned.1.call-start = ((), (), s32[]{:S(2)}) async-start(), calls=%async_computation.4 | async-start | bytes 4718592 | tf_op jit(solution)/shard_map/reduce_scatter | solution.py:37
  231.7 5.3 %copy-start.2 = (bf16[1,1344,1024]{2,1,0:T(8,128)(2,1)S(1)}, bf16[1,1344,1024]{2,1,0:T(8,128)(2,1)}, u32[]{:S(2)}) copy-start(bf16[1,1344,1024]{2,1,0:T(8,128)(2,1)} %param.13) | copy-start | bytes 8257540
  243.5 109.8 %all-gather.5.cloned.1.call-start = ((), (), s32[]{:S(2)}) async-start(), calls=%async_computation.5 | async-start | bytes 4718592 | tf_op jit(solution)/shard_map/all_gather | solution.py:14
  253.5 60.4 %all-to-all-start.1 = ((bf16[8,192,512]{2,1,0:T(8,128)(2,1)}), bf16[8,192,512]{2,1,0:T(8,128)(2,1)}, u32[]{:S(2)}, u32[]{:S(2)}) async-start(bf16[8,192,512]{2,1,0:T(8,128)(2,1)} %bitcast.34), calls=%async_computation.2 | async-start | bytes 3145728 | tf_op jit(solution)/shard_map/all_to_all | solution.py:41
  259.4 4.1 %copy-start.1 = (f32[256,4]{0,1:T(4,128)S(1)}, f32[256,4]{0,1:T(4,128)}, u32[]{:S(2)}) copy-start(f32[256,4]{0,1:T(4,128)} %param.15) | copy-start | bytes 12292
Sparse Core Ops, SparseCore 0:
  9.5 127.6 all-gather.2
  243.6 9.8 reduce-scatter.1
  255.9 97.3 all-gather.4
where the time goes:
time: 365 us
  waiting for transfers between devices  208 us (57%)
  blocking collectives  76.3 us (21%)
  local copies, waits for them, and re-layouts  25.4 us (7%)
  matrix products  23.2 us (6%)
  between operations  13.2 us (4%)
  other arithmetic  12.4 us (3%)
  starting transfers between devices  6 us (2%)
    all_gather x1, waiting for transfers between devices, local(): lax.all_gather(w_in, 'wide', axis=0, tiled=True)  123 us
    all_to_all x1, blocking collectives, local(): lax.all_to_all(buffer, 'wide', split_axis=0, concat_axis=0, tiled=True)  74.1 us
    all_to_all x1, waiting for transfers between devices, local(): lax.all_to_all(outgoing, 'wide', split_axis=0, concat_axis=0, tiled=True)  50.2 us
    all_gather x1, waiting for transfers between devices, local(): lax.all_gather(w_out, 'wide', axis=0, tiled=True)  24.7 us
    reduce_scatter x1, waiting for transfers between devices, local(): lax.psum_scatter(partial_value.astype(jnp.bfloat16), 'narrow', scatter_di...  9.31 us
    scatter x1, local copies, waits for them, and re-layouts, local(): jnp.zeros((experts * capacity, width), jnp.bfloat16).at[target]  8.06 us
  transfers between devices with their start and end apart: 4, of which 4 were waited for; matrix products, arithmetic and copies ran while one was open for 7% of the time, Pallas kernels for 0%

commit v1 on v0

v1 whole, which is shorter than its diff:
```python
import jax
import jax.numpy as jnp
from jax import lax
from jax.sharding import PartitionSpec as P


def ring_order(mesh):
    wide = mesh.shape["wide"]
    line = mesh.devices.reshape(-1, wide, mesh.shape["narrow"])[0, :, 0]
    places = [tuple(getattr(d, "coords", (0,))) for d in line]
    spread = [len(set(c)) for c in zip(*places)]
    if sum(s > 1 for s in spread) == 2 and wide % 2 == 0:
        return list(range(0, wide, 2)) + list(range(wide - 1, 0, -2))
    return list(range(wide))


def make_local(order):
    wide = len(order)
    far = wide // 2
    up_perm = [(order[i], order[(i + 1) % wide]) for i in range(wide)]
    down_perm = [(order[(i + 1) % wide], order[i]) for i in range(wide)]
    place_of = [order.index(i) for i in range(wide)]

    def local(tokens, norm_gain, w_in, w_out, w_up, w_down, expert_ids, gate_weights):
        f32, bf16 = jnp.float32, jnp.bfloat16
        groups = lax.axis_size("groups")
        side = lax.axis_index("groups") % 2
        me = lax.axis_index("wide")
        core = lax.axis_index("narrow")
        rows, model = tokens.shape
        half_rows = rows // 2
        width = w_in.shape[1]
        half, quarter = width // 2, width // 4
        depth = w_in.shape[0]
        place = jnp.asarray(place_of)[me]

        def up(x):
            return lax.ppermute(x, "wide", up_perm)

        def down(x):
            return lax.ppermute(x, "wide", down_perm)

        def swap(x):
            return lax.ppermute(x, "narrow", [(0, 1), (1, 0)])

        def across(x):
            return lax.ppermute(x, "groups", [(i, i ^ 1) for i in range(groups)])

        def at(distance):
            return jnp.asarray(order)[(place + distance) % wide]

        def ordered(first, mine, other, axis):
            return jnp.concatenate(
                [jnp.where(first, mine, other), jnp.where(first, other, mine)], axis
            )

        named = expert_ids[:, :, None] == jnp.arange(wide, dtype=jnp.int32)
        dense = jnp.sum(jnp.where(named, gate_weights[:, :, None], 0.0), axis=1).T
        gates = lax.all_gather(dense, "wide", axis=0)
        gates = lax.dynamic_index_in_dim(gates, me, 1, keepdims=False)

        full_out = lax.all_gather(w_out, "wide", axis=0, tiled=True)

        own = lax.dynamic_slice_in_dim(w_in, (core * 2 + side) * quarter, quarter, 1)
        full_in = jnp.zeros((depth * wide, quarter), bf16)
        full_in = lax.dynamic_update_slice_in_dim(full_in, own, me * depth, 0)
        from_below = from_above = own
        for d in range(1, far + 1):
            if d == far:
                cut = depth // 2
                from_below = up(from_below[:cut])
                from_above = down(from_above[cut:])
                begin = at(far) * depth
                full_in = lax.dynamic_update_slice_in_dim(full_in, from_below, begin, 0)
                full_in = lax.dynamic_update_slice_in_dim(
                    full_in, from_above, begin + cut, 0
                )
            else:
                from_below, from_above = up(from_below), down(from_above)
                full_in = lax.dynamic_update_slice_in_dim(
                    full_in, from_below, at(-d) * depth, 0
                )
                full_in = lax.dynamic_update_slice_in_dim(
                    full_in, from_above, at(d) * depth, 0
                )

        widened = tokens.astype(f32)
        scale = lax.rsqrt(jnp.mean(widened * widened, axis=-1, keepdims=True) + 1e-05)
        normed = (widened * scale * norm_gain).astype(bf16)
        there = across(lax.dynamic_slice_in_dim(normed, core * half_rows, half_rows, 0))
        there = jnp.concatenate([there, swap(there)], axis=0)
        lat_there = jnp.dot(there, full_in, preferred_element_type=f32).astype(bf16)
        lat_other = across(lat_there)
        lat_mine = jnp.dot(normed, full_in, preferred_element_type=f32).astype(bf16)
        lat_other = ordered(core == 0, lat_other[:half_rows], lat_other[half_rows:], 0)
        latent = ordered(side == 0, lat_mine, lat_other, 1)

        up_weight = w_up[0]
        up_weight = jnp.concatenate(
            [
                lax.dynamic_slice_in_dim(up_weight, core * half, half, 0),
                lax.dynamic_slice_in_dim(up_weight, (1 - core) * half, half, 0),
            ],
            axis=0,
        )
        down_weight = w_down[0]
        down_weight = jnp.concatenate(
            [
                lax.dynamic_slice_in_dim(down_weight, core * half, half, 1),
                lax.dynamic_slice_in_dim(down_weight, (1 - core) * half, half, 1),
            ],
            axis=1,
        )

        def expert(x, gate):
            x = jnp.concatenate([x, swap(x)], axis=1)
            hidden = jnp.dot(x, up_weight, preferred_element_type=f32)
            hidden = jnp.square(jnp.maximum(hidden, 0.0)).astype(bf16)
            part = jnp.dot(hidden, down_weight, preferred_element_type=f32)
            part = (part * gate[:, None]).astype(bf16)
            return part[:, :half].astype(f32) + swap(part[:, half:]).astype(f32)

        def gate_of(distance):
            return lax.dynamic_index_in_dim(gates, at(distance), 0, keepdims=False)

        from_below = from_above = latent
        arrived = [(latent, gate_of(0))]
        for d in range(1, far + 1):
            if d == far:
                from_below = up(from_below[:half_rows])
                from_above = down(from_above[half_rows:])
                gate = gate_of(far)
            else:
                from_below, from_above = up(from_below), down(from_above)
                gate = jnp.concatenate([gate_of(-d), gate_of(d)])
            arrived.append((jnp.concatenate([from_below, from_above], axis=0), gate))
        parts = [expert(x, gate) for x, gate in arrived]

        to_above = up(parts[far][:half_rows].astype(bf16)).astype(f32)
        to_below = down(parts[far][half_rows:].astype(bf16)).astype(f32)
        for d in range(far - 1, 0, -1):
            below, above = parts[d][:rows], parts[d][rows:]
            if d == far - 1:
                above = jnp.concatenate(
                    [above[:half_rows] + to_above, above[half_rows:]], axis=0
                )
                below = jnp.concatenate(
                    [below[:half_rows], below[half_rows:] + to_below], axis=0
                )
            else:
                above, below = above + to_above, below + to_below
            to_above = up(above.astype(bf16)).astype(f32)
            to_below = down(below.astype(bf16)).astype(f32)
        mixture = (parts[0] + to_above + to_below).astype(bf16)
        mixture = ordered(core == 0, mixture, swap(mixture), 1)

        branch = jnp.dot(mixture, full_out, preferred_element_type=f32)
        columns = full_out.shape[1]
        kept = lax.dynamic_slice_in_dim(tokens, core * columns, columns, 1)
        return (kept.astype(f32) + branch).astype(bf16)

    return local


def solution(mesh):
    in_specs = (
        P(("groups", "wide"), None),
        P(),
        P("wide", None),
        P("wide", "narrow"),
        P("wide", None, "narrow"),
        P("wide", "narrow", None),
        P(("groups", "wide"), None),
        P(("groups", "wide"), None),
    )
    out_specs = P(("groups", "wide"), "narrow")
    local = make_local(ring_order(mesh))
    return jax.shard_map(
        local, mesh=mesh, in_specs=in_specs, out_specs=out_specs, check_vma=False
    )
```

time: 365 us -> 236 us (0.65)
  waiting for transfers between devices: 208 us -> 43.5 us
  blocking collectives: 76.3 us -> 31.2 us
  starting transfers between devices: 6 us -> 36.6 us
  between operations: 13.2 us -> 39.4 us
  matrix products: 23.2 us -> 39 us
  local copies, waits for them, and re-layouts: 25.4 us -> 35.1 us
    all_gather x2 -> x1, waiting for transfers between devices: 147 us -> 0.02 us  [local(): full_out = lax.all_gather(w_out, 'wide', axis=0, tiled=True)]
    all_to_all x1 -> x0, blocking collectives: 74.1 us -> none  [local(): lax.all_to_all(buffer, 'wide', split_axis=0, concat_axis=0, tiled=True)]
    all_to_all x1 -> x0, waiting for transfers between devices: 50.2 us -> none  [local(): lax.all_to_all(outgoing, 'wide', split_axis=0, concat_axis=0, tiled=True)]
    ppermute x0 -> x38, waiting for transfers between devices: none -> 43.5 us  [the longest x12 22.9 us: up(): return lax.ppermute(x, 'wide', up_perm)]
    ppermute x0 -> x38, starting transfers between devices: none -> 36.6 us  [the longest x12 18.9 us: down(): return lax.ppermute(x, 'wide', down_perm)]
    all_gather x1, blocking collectives: 2.18 us -> 31.2 us  [local(): gates = lax.all_gather(dense, 'wide', axis=0)]
    dot_general x4 -> x8, matrix products: 23.2 us -> 39 us  [the longest x5 28.4 us: expert(): part = jnp.dot(hidden, down_weight, preferred_element_type=f32)]
    dynamic_update_slice x0 -> x9, local copies, waits for them, and re-layouts: none -> 11.2 us  [the longest x3 4.06 us: local(): lax.dynamic_update_slice_in_dim(full_in, from_below, at(-d) * depth, 0)]
  transfers between devices with their start and end apart: 4 -> 39, of which waited for: 4 -> 18; matrix products, arithmetic and copies ran while one was open for 7% -> 31% of each run, Pallas kernels for 0% -> 0%
where the time goes in v1:
time: 236 us; the launch traced here: 234 us
  waiting for transfers between devices  43.5 us (18%)
  between operations  39.4 us (17%)
  matrix products  39 us (17%)
  starting transfers between devices  36.6 us (16%)
  local copies, waits for them, and re-layouts  35.1 us (15%)
  blocking collectives  31.2 us (13%)
  other arithmetic  9.48 us (4%)
    all_gather x1, blocking collectives, local(): gates = lax.all_gather(dense, 'wide', axis=0)  31.2 us
    dot_general x5, matrix products, expert(): part = jnp.dot(hidden, down_weight, preferred_element_type=f32)  28.4 us
    ppermute x12, waiting for transfers between devices, up(): return lax.ppermute(x, 'wide', up_perm)  22.9 us
    ppermute x12, starting transfers between devices, down(): return lax.ppermute(x, 'wide', down_perm)  18.9 us
    ppermute x12, waiting for transfers between devices, down(): return lax.ppermute(x, 'wide', down_perm)  13.8 us
    ppermute x12, starting transfers between devices, up(): return lax.ppermute(x, 'wide', up_perm)  12.8 us
    slice x5, local copies, waits for them, and re-layouts, expert(): return part[:, :half].astype(f32) + swap(part[:, half:]).astype(f32)  6.44 us
    ppermute x2, waiting for transfers between devices, across(): return lax.ppermute(x, 'groups', [(i, i ^ 1) for i in range(groups)])  5.25 us
  transfers between devices with their start and end apart: 39, of which 18 were waited for; matrix products, arithmetic and copies ran while one was open for 31% of the time, Pallas kernels for 0%

profile of v1, /device:TPU:0, one launch (start us, length us, event | category | flops | bytes accessed | tf_op | source)
XLA Modules:
  0.0 234.4 jit_solution(6561438901163420618)
XLA Ops:
  6.5 2.1 fusion
  8.7 2.2 fusion.2
  12.0 3.0 %collective-permute-start.8 = (bf16[128,4096]{1,0:T(8,128)(2,1)}, bf16[128,4096]{1,0:T(8,128)(2,1)}, u32[]{:S(2)}, u32[]{:S(2)}) collective-permute-start(bf16[128,4096]{1,0:T(8,128)(2,1)} %constant_dynamic-slice_fusion.8), channel_id=1, source_target_pairs={{0,16},{16,0},{1,17},{17,1},{2,18},{18,2},{3,19},{19,3},{4,20},{20... | collective-permute-start | bytes 3145736 | tf_op jit(solution)/shard_map/ppermute | solution.py:47
  15.0 1.5 broadcast_in_dim.14
  16.5 1.8 constant_dynamic-update-slice_fusion.16
  18.3 1.6 collective-permute-start
  42.9 31.2 %all-gather = f32[64,256]{1,0:T(8,128)S(1)} all-gather(f32[8,256]{1,0:T(8,128)S(1)} %bitcast.39), channel_id=2, replica_groups=mesh['groups'=2,'wide'=8,'narrow'=2] {'wide'}, dimensions={0}, use_global_device_ids=true | all-gather | bytes 73728 | tf_op jit(solution)/shard_map/all_gather | solution.py:59
  74.1 3.1 %dynamic-slice_bitcast_fusion.1 = (bf16[1344,512]{1,0:T(8,128)(2,1)S(1)}, bf16[1344,512]{1,0:T(8,128)(2,1)}) fusion(bf16[1,1344,1024]{2,1,0:T(8,128)(2,1)} %param.29, s32[]{:T(128)S(6)} %select_n.251, s32[]{:T(128)S(6)} %select_n.252), kind=kLoop, calls=%fused_computation.32 | loop fusion | bytes 5505032 | tf_op jit(solution)/shard_map/dynamic_slice | solution.py:109
  77.2 2.0 collective-permute-start.3
  83.7 1.7 constant_dynamic-update-slice_fusion.15
  85.6 5.5 %collective-permute-start.4 = (bf16[512,256]{1,0:T(8,128)(2,1)}, bf16[512,256]{1,0:T(8,128)(2,1)S(1)}, u32[]{:S(2)}, u32[]{:S(2)}) collective-permute-start(bf16[512,256]{1,0:T(8,128)(2,1)} %collective-permute-done.2), channel_id=1, source_target_pairs={{0,4},{4,8},{8,12},{12,14},{14,10},{10,6},{6,2},{2,0},{1,5},{5,9},... | collective-permute-start | bytes 786440 | tf_op jit(solution)/shard_map/ppermute | solution.py:38
  91.1 4.3 %collective-permute-done.3 = bf16[512,256]{1,0:T(8,128)(2,1)} collective-permute-done((bf16[512,256]{1,0:T(8,128)(2,1)}, bf16[512,256]{1,0:T(8,128)(2,1)}, u32[]{:S(2)}, u32[]{:S(2)}) %collective-permute-start.3) | collective-permute-done | bytes 262176 | tf_op jit(solution)/shard_map/ppermute | solution.py:41
  95.4 3.1 %collective-permute-start.5 = (bf16[512,256]{1,0:T(8,128)(2,1)}, bf16[512,256]{1,0:T(8,128)(2,1)S(1)}, u32[]{:S(2)}, u32[]{:S(2)}) collective-permute-start(bf16[512,256]{1,0:T(8,128)(2,1)} %collective-permute-done.3), channel_id=1, source_target_pairs={{4,0},{8,4},{12,8},{14,12},{10,14},{6,10},{2,6},{0,2},{5,1},{9,5},... | collective-permute-start | bytes 786440 | tf_op jit(solution)/shard_map/ppermute | solution.py:41
  98.5 1.7 constant_dynamic-update-slice_fusion.14
  100.1 1.7 constant_dynamic-update-slice_fusion.13
  101.8 1.7 constant_dynamic-update-slice_fusion.12
  104.5 2.1 collective-permute-start.7
  108.1 1.4 collective-permute-done.6
  110.8 3.5 %fusion.20 = bf16[256,256]{0,1:T(8,128)(2,1)} fusion(bf16[4096,256]{1,0:T(8,128)(2,1)} %constant_dynamic-update-slice_fusion.8, bf16[128,4096]{1,0:T(8,128)(2,1)S(1)} %collective-permute-done.9, bf16[128,4096]{1,0:T(8,128)(2,1)} %collective-permute-done.8), kind=kOutput, calls=%fused_computation.39 | convolution fusion | flops 541130752 | bytes 4325376 | tf_op jit(solution)/shard_map/dot_general | solution.py:92
  114.4 5.2 %collective-permute-done.10 = bf16[256,256]{0,1:T(8,128)(2,1)} collective-permute-done((bf16[256,256]{0,1:T(8,128)(2,1)}, bf16[256,256]{0,1:T(8,128)(2,1)}, u32[]{:S(2)}, u32[]{:S(2)}) %collective-permute-start.10) | collective-permute-done | bytes 131104 | tf_op jit(solution)/shard_map/ppermute | solution.py:47
  120.5 2.7 %broadcast_select_fusion.3 = (bf16[256,256]{0,1:T(8,128)(2,1)S(1)}, bf16[256,256]{0,1:T(8,128)(2,1)S(1)}) fusion(pred[]{:T(512)S(6)} %eq.38, bf16[128,256]{0,1:T(8,128)(2,1)S(1)} %get-tuple-element.28, bf16[128,256]{0,1:T(8,128)(2,1)S(1)} %get-tuple-element.27, bf16[256,4096]{1,0:T(8,128)(2,1)S(1)} %fusion.2, ...), kind=kOutput, calls=%fused_computation.87 | convolution fusion | flops 537329664 | bytes 4587521 | tf_op jit(solution)/shard_map/dot_general | solution.py:94
  123.4 2.1 collective-permute-start.14
  125.5 1.9 dynamic-slice_bitcast_fusion.3
  127.4 5.0 %collective-permute-done.13 = bf16[256,512]{0,1:T(8,128)(2,1)} collective-permute-done((bf16[256,512]{0,1:T(8,128)(2,1)S(1)}, bf16[256,512]{0,1:T(8,128)(2,1)}, u32[]{:S(2)}, u32[]{:S(2)}) %collective-permute-start.13) | collective-permute-done | bytes 262176 | tf_op jit(solution)/shard_map/ppermute | solution.py:38
  132.4 2.0 collective-permute-start.18
  135.2 4.8 %fusion.18 = bf16[256,1024]{1,0:T(8,128)(2,1)S(1)} fusion(bf16[256,512]{0,1:T(8,128)(2,1)} %copy-done.17, bf16[256,256]{0,1:T(8,128)(2,1)} %copy-done.10, bf16[256,256]{0,1:T(8,128)(2,1)} %copy-done.9, f32[256]{0:T(256)S(1)} %bitcast.47, bf16[1344,512]{1,0:T(8,128)(2,1)S(1)} %copy-done.2, bf16[1344,512]{1,0:T(8,128)(2,1)S(1)} %get-tuple-element.9, ...), kind=kOutput, calls=%fused_computation.37 | convolution fusion | flops 1423425536 | bytes 6554624 | tf_op jit(solution)/shard_map/dot_general | solution.py:119
  141.9 2.0 collective-permute-start.22
  144.9 1.8 constant_dynamic-update-slice_fusion.3
  146.8 1.7 constant_dynamic-update-slice_fusion.2
  148.9 1.9 collective-permute-done.21
  151.1 2.0 collective-permute-start.26
  154.6 1.4 collective-permute-done.25
  156.6 6.2 %multiply_convert_fusion.2 = bf16[512,1024]{1,0:T(8,128)(2,1)} fusion(f32[512]{0:T(512)S(1)} %pad_maximum_fusion.6, bf16[512,512]{0,1:T(8,128)(2,1)} %collective-permute-done.15, bf16[512,512]{0,1:T(8,128)(2,1)} %copy-done.11, bf16[1344,512]{1,0:T(8,128)(2,1)S(1)} %copy-done.2, bf16[1344,512]{1,0:T(8,128)(2,1)S(1)} %get-tuple-element.9, ...), kind=kOutput, calls=%fused_computation.30 | convolution fusion | flops 2834792448 | bytes 7604224 | tf_op jit(solution)/shard_map/dot_general | solution.py:119
  162.9 1.9 slice.121
  165.8 4.8 %fusion.19 = bf16[256,1024]{1,0:T(8,128)(2,1)S(1)} fusion(bf16[256,512]{0,1:T(8,128)(2,1)} %copy-done.18, bf16[256,512]{0,1:T(8,128)(2,1)} %copy-done.12, f32[256]{0:T(256)S(1)} %bitcast.46, bf16[1344,512]{1,0:T(8,128)(2,1)S(1)} %copy-done.2, bf16[1344,512]{1,0:T(8,128)(2,1)S(1)} %get-tuple-element.9, bf16[512,1344]{0,1:T(8,128)(2,1)} %get-tuple-element.8, ...), kind=kOutput, calls=%fused_computation.38 | convolution fusion | flops 1422901248 | bytes 6554624 | tf_op jit(solution)/shard_map/dot_general | solution.py:119
  171.5 6.2 %multiply_convert_fusion = bf16[512,1024]{1,0:T(8,128)(2,1)} fusion(f32[512]{0:T(512)S(1)} %pad_maximum_fusion.8, bf16[512,512]{0,1:T(8,128)(2,1)} %collective-permute-done.23, bf16[512,512]{0,1:T(8,128)(2,1)} %constant_dynamic-update-slice_fusion.4, bf16[1344,512]{1,0:T(8,128)(2,1)S(1)} %copy-done.2, bf16[1344,512]{1,0:T(8,128)(2,1)S(1)} %get-tuple-element.9, ...), kind=kOutput, calls=%fused_computation.28 | convolution fusion | flops 2834792448 | bytes 7604224 | tf_op jit(solution)/shard_map/dot_general | solution.py:119
  177.7 1.9 slice.127
  180.0 6.3 %multiply_convert_fusion.1 = bf16[512,1024]{1,0:T(8,128)(2,1)} fusion(f32[512]{0:T(512)S(1)} %pad_maximum_fusion.7, bf16[512,512]{0,1:T(8,128)(2,1)} %collective-permute-done.19, bf16[512,512]{0,1:T(8,128)(2,1)} %constant_dynamic-update-slice_fusion.2, bf16[1344,512]{1,0:T(8,128)(2,1)S(1)} %copy-done.2, bf16[1344,512]{1,0:T(8,128)(2,1)S(1)} %get-tuple-element.9, ...), kind=kOutput, calls=%fused_computation.29 | convolution fusion | flops 2834792448 | bytes 7604224 | tf_op jit(solution)/shard_map/dot_general | solution.py:119
  191.1 3.6 %collective-permute-done.29 = bf16[128,512]{1,0:T(8,128)(2,1)S(1)} collective-permute-done((bf16[128,512]{1,0:T(8,128)(2,1)S(1)}, bf16[128,512]{1,0:T(8,128)(2,1)S(1)}, u32[]{:S(2)}, u32[]{:S(2)}) %collective-permute-start.29) | collective-permute-done | bytes 131104 | tf_op jit(solution)/shard_map/ppermute | solution.py:38
  198.0 5.6 %collective-permute-done.34 = bf16[256,512]{1,0:T(8,128)(2,1)S(1)} collective-permute-done((bf16[256,512]{1,0:T(8,128)(2,1)S(1)}, bf16[256,512]{1,0:T(8,128)(2,1)S(1)}, u32[]{:S(2)}, u32[]{:S(2)}) %collective-permute-start.34) | collective-permute-done | bytes 262176 | tf_op jit(solution)/shard_map/ppermute | solution.py:41
  204.4 1.2 collective-permute-start.31
  206.5 1.2 convert_add_fusion.2
  207.7 3.4 %collective-permute-done.31 = bf16[256,512]{1,0:T(8,128)(2,1)S(1)} collective-permute-done((bf16[256,512]{1,0:T(8,128)(2,1)S(1)}, bf16[256,512]{1,0:T(8,128)(2,1)S(1)}, u32[]{:S(2)}, u32[]{:S(2)}) %collective-permute-start.31) | collective-permute-done | bytes 262176 | tf_op jit(solution)/shard_map/ppermute | solution.py:38
  212.2 1.7 collective-permute-start.32
  214.3 4.3 %collective-permute-done.32 = bf16[256,512]{1,0:T(8,128)(2,1)S(1)} collective-permute-done((bf16[256,512]{1,0:T(8,128)(2,1)S(1)}, bf16[256,512]{1,0:T(8,128)(2,1)S(1)}, u32[]{:S(2)}, u32[]{:S(2)}) %collective-permute-start.32) | collective-permute-done | bytes 262176 | tf_op jit(solution)/shard_map/ppermute | solution.py:38
  218.7 1.7 collective-permute-done.36
  221.5 1.5 collective-permute-done.37
  223.1 4.4 %fusion.11 = bf16[256,2048]{1,0:T(8,128)(2,1)} fusion(bf16[1024,2048]{1,0:T(8,128)(2,1)} %all-gather.3.cloned.1.call-done, bf16[256,4096]{1,0:T(8,128)(2,1)S(1)} %copy-done, s32[]{:T(128)S(6)} %select_n.216, bf16[256,512]{1,0:T(8,128)(2,1)S(1)} %get-tuple-element.20, bf16[256,512]{1,0:T(8,128)(2,1)S(1)} %get-tuple-element.19), kind=kOutput, calls=%fused_computation.21 | convolution fusion | flops 1076363264 | bytes 6815748 | tf_op jit(solution)/shard_map/dot_general | solution.py:157
  (135 shorter events, 29.3 us)
Async XLA Ops:
  6.5 216.6 %all-gather.3.cloned.1.call-start = ((), (), s32[]{:S(2)}) async-start(), calls=%async_computation | async-start | bytes 4718592 | tf_op jit(solution)/shard_map/all_gather | solution.py:62
  12.0 8.4 %copy-start.19 = (s32[8]{0:T(128)S(1)}, s32[8]{0:T(128)}, u32[]{:S(2)}) copy-start(s32[8]{0:T(128)} %constant.280.clone) | copy-start | bytes 100
  12.0 15.5 %copy-start.13 = (s32[8]{0:T(128)S(1)}, s32[8]{0:T(128)}, u32[]{:S(2)}) copy-start(s32[8]{0:T(128)} %constant.281.clone) | copy-start | bytes 100
  12.0 30.9 %copy-start.15 = (f32[256,4]{0,1:T(4,128)S(1)}, f32[256,4]{0,1:T(4,128)}, u32[]{:S(2)}) copy-start(f32[256,4]{0,1:T(4,128)} %param.31) | copy-start | bytes 12292
  12.0 30.9 %copy-start.16 = (s32[256,4]{0,1:T(4,128)S(1)}, s32[256,4]{0,1:T(4,128)}, u32[]{:S(2)}) copy-start(s32[256,4]{0,1:T(4,128)} %param.30) | copy-start | bytes 12292
  12.0 71.6 %collective-permute-start.8 = (bf16[128,4096]{1,0:T(8,128)(2,1)}, bf16[128,4096]{1,0:T(8,128)(2,1)}, u32[]{:S(2)}, u32[]{:S(2)}) collective-permute-start(bf16[128,4096]{1,0:T(8,128)(2,1)} %constant_dynamic-slice_fusion.8), channel_id=1, source_target_pairs={{0,16},{16,0},{1,17},{17,1},{2,18},{18,2},{3,19},{19,3},{4,20},{20... | collective-permute-start | bytes 3145736 | tf_op jit(solution)/shard_map/ppermute | solution.py:47
  18.3 58.9 %collective-permute-start = (bf16[512,256]{1,0:T(8,128)(2,1)}, bf16[512,256]{1,0:T(8,128)(2,1)}, u32[]{:S(2)}, u32[]{:S(2)}) collective-permute-start(bf16[512,256]{1,0:T(8,128)(2,1)} %get-tuple-element.6), channel_id=1, source_target_pairs={{0,4},{4,8},{8,12},{12,14},{14,10},{10,6},{6,2},{2,0},{1,5},{5,9},... | collective-permute-start | bytes 786440 | tf_op jit(solution)/shard_map/ppermute | solution.py:38
  19.9 57.3 %collective-permute-start.1 = (bf16[512,256]{1,0:T(8,128)(2,1)}, bf16[512,256]{1,0:T(8,128)(2,1)}, u32[]{:S(2)}, u32[]{:S(2)}) collective-permute-start(bf16[512,256]{1,0:T(8,128)(2,1)} %get-tuple-element.6), channel_id=1, source_target_pairs={{4,0},{8,4},{12,8},{14,12},{10,14},{6,10},{2,6},{0,2},{5,1},{9,5},... | collective-permute-start | bytes 786440 | tf_op jit(solution)/shard_map/ppermute | solution.py:41
  77.2 8.4 %collective-permute-start.2 = (bf16[512,256]{1,0:T(8,128)(2,1)}, bf16[512,256]{1,0:T(8,128)(2,1)}, u32[]{:S(2)}, u32[]{:S(2)}) collective-permute-start(bf16[512,256]{1,0:T(8,128)(2,1)} %collective-permute-done), channel_id=1, source_target_pairs={{0,4},{4,8},{8,12},{12,14},{14,10},{10,6},{6,2},{2,0},{1,5},{5,9},... | collective-permute-start | bytes 786440 | tf_op jit(solution)/shard_map/ppermute | solution.py:38
  77.2 18.2 %collective-permute-start.3 = (bf16[512,256]{1,0:T(8,128)(2,1)}, bf16[512,256]{1,0:T(8,128)(2,1)}, u32[]{:S(2)}, u32[]{:S(2)}) collective-permute-start(bf16[512,256]{1,0:T(8,128)(2,1)} %collective-permute-done.1), channel_id=1, source_target_pairs={{4,0},{8,4},{12,8},{14,12},{10,14},{6,10},{2,6},{0,2},{5,1},{9,5},... | collective-permute-start | bytes 786440 | tf_op jit(solution)/shard_map/ppermute | solution.py:41
  83.6 27.2 %collective-permute-start.9 = (bf16[128,4096]{1,0:T(8,128)(2,1)}, bf16[128,4096]{1,0:T(8,128)(2,1)S(1)}, u32[]{:S(2)}, u32[]{:S(2)}) collective-permute-start(bf16[128,4096]{1,0:T(8,128)(2,1)} %collective-permute-done.8), channel_id=1, source_target_pairs={{0,1},{1,0},{2,3},{3,2},{4,5},{5,4},{6,7},{7,6},{8,9},{9,8},{10,11... | collective-permute-start | bytes 3145736 | tf_op jit(solution)/shard_map/ppermute | solution.py:44
  85.6 18.9 %collective-permute-start.4 = (bf16[512,256]{1,0:T(8,128)(2,1)}, bf16[512,256]{1,0:T(8,128)(2,1)S(1)}, u32[]{:S(2)}, u32[]{:S(2)}) collective-permute-start(bf16[512,256]{1,0:T(8,128)(2,1)} %collective-permute-done.2), channel_id=1, source_target_pairs={{0,4},{4,8},{8,12},{12,14},{14,10},{10,6},{6,2},{2,0},{1,5},{5,9},... | collective-permute-start | bytes 786440 | tf_op jit(solution)/shard_map/ppermute | solution.py:38
  95.4 9.2 %collective-permute-start.5 = (bf16[512,256]{1,0:T(8,128)(2,1)}, bf16[512,256]{1,0:T(8,128)(2,1)S(1)}, u32[]{:S(2)}, u32[]{:S(2)}) collective-permute-start(bf16[512,256]{1,0:T(8,128)(2,1)} %collective-permute-done.3), channel_id=1, source_target_pairs={{4,0},{8,4},{12,8},{14,12},{10,14},{6,10},{2,6},{0,2},{5,1},{9,5},... | collective-permute-start | bytes 786440 | tf_op jit(solution)/shard_map/ppermute | solution.py:41
  104.5 5.0 %collective-permute-start.6 = (bf16[256,256]{1,0:T(8,128)(2,1)S(1)}, bf16[256,256]{1,0:T(8,128)(2,1)S(1)}, u32[]{:S(2)}, u32[]{:S(2)}) collective-permute-start(bf16[256,256]{1,0:T(8,128)(2,1)S(1)} %slice.114), channel_id=1, source_target_pairs={{0,4},{4,8},{8,12},{12,14},{14,10},{10,6},{6,2},{2,0},{1,5},{5,9},... | collective-permute-start | bytes 393224 | tf_op jit(solution)/shard_map/ppermute | solution.py:38
  104.5 5.6 %collective-permute-start.7 = (bf16[256,256]{1,0:T(8,128)(2,1)S(1)}, bf16[256,256]{1,0:T(8,128)(2,1)S(1)}, u32[]{:S(2)}, u32[]{:S(2)}) collective-permute-start(bf16[256,256]{1,0:T(8,128)(2,1)S(1)} %slice.115), channel_id=1, source_target_pairs={{4,0},{8,4},{12,8},{14,12},{10,14},{6,10},{2,6},{0,2},{5,1},{9,5},... | collective-permute-start | bytes 393224 | tf_op jit(solution)/shard_map/ppermute | solution.py:41
  114.3 5.3 %collective-permute-start.10 = (bf16[256,256]{0,1:T(8,128)(2,1)}, bf16[256,256]{0,1:T(8,128)(2,1)}, u32[]{:S(2)}, u32[]{:S(2)}) collective-permute-start(bf16[256,256]{0,1:T(8,128)(2,1)} %fusion.20), channel_id=1, source_target_pairs={{0,16},{16,0},{1,17},{17,1},{2,18},{18,2},{3,19},{19,3},{4,20},{20... | collective-permute-start | bytes 393224 | tf_op jit(solution)/shard_map/ppermute | solution.py:47
  123.2 11.9 %copy-start.2 = (bf16[1344,512]{1,0:T(8,128)(2,1)S(1)}, bf16[1344,512]{1,0:T(8,128)(2,1)}, u32[]{:S(2)}) copy-start(bf16[1344,512]{1,0:T(8,128)(2,1)} %get-tuple-element.10) | copy-start | bytes 4128772
  123.3 11.2 %collective-permute-start.11 = (bf16[256,512]{0,1:T(8,128)(2,1)S(1)}, bf16[256,512]{0,1:T(8,128)(2,1)S(1)}, u32[]{:S(2)}, u32[]{:S(2)}) collective-permute-start(bf16[256,512]{0,1:T(8,128)(2,1)S(1)} %pad_maximum_fusion.2), channel_id=1, source_target_pairs={{0,1},{1,0},{2,3},{3,2},{4,5},{5,4},{6,7},{7,6},{8,9},{9,8},{10,11... | collective-permute-start | bytes 786440 | tf_op jit(solution)/shard_map/ppermute | solution.py:44
  123.3 9.1 %collective-permute-start.13 = (bf16[256,512]{0,1:T(8,128)(2,1)S(1)}, bf16[256,512]{0,1:T(8,128)(2,1)}, u32[]{:S(2)}, u32[]{:S(2)}) collective-permute-start(bf16[256,512]{0,1:T(8,128)(2,1)S(1)} %pad_maximum_fusion.2), channel_id=1, source_target_pairs={{0,4},{4,8},{8,12},{12,14},{14,10},{10,6},{6,2},{2,0},{1,5},{5,9},... | collective-permute-start | bytes 786440 | tf_op jit(solution)/shard_map/ppermute | solution.py:38
  123.4 9.0 %collective-permute-start.14 = (bf16[256,512]{0,1:T(8,128)(2,1)S(1)}, bf16[256,512]{0,1:T(8,128)(2,1)}, u32[]{:S(2)}, u32[]{:S(2)}) collective-permute-start(bf16[256,512]{0,1:T(8,128)(2,1)S(1)} %pad_maximum_fusion.2), channel_id=1, source_target_pairs={{4,0},{8,4},{12,8},{14,12},{10,14},{6,10},{2,6},{0,2},{5,1},{9,5},... | collective-permute-start | bytes 786440 | tf_op jit(solution)/shard_map/ppermute | solution.py:41
  132.4 9.3 %collective-permute-start.17 = (bf16[256,512]{0,1:T(8,128)(2,1)}, bf16[256,512]{0,1:T(8,128)(2,1)}, u32[]{:S(2)}, u32[]{:S(2)}) collective-permute-start(bf16[256,512]{0,1:T(8,128)(2,1)} %collective-permute-done.13), channel_id=1, source_target_pairs={{0,4},{4,8},{8,12},{12,14},{14,10},{10,6},{6,2},{2,0},{1,5},{5,9},... | collective-permute-start | bytes 786440 | tf_op jit(solution)/shard_map/ppermute | solution.py:38
  132.4 9.4 %collective-permute-start.18 = (bf16[256,512]{0,1:T(8,128)(2,1)}, bf16[256,512]{0,1:T(8,128)(2,1)}, u32[]{:S(2)}, u32[]{:S(2)}) collective-permute-start(bf16[256,512]{0,1:T(8,128)(2,1)} %collective-permute-done.14), channel_id=1, source_target_pairs={{4,0},{8,4},{12,8},{14,12},{10,14},{6,10},{2,6},{0,2},{5,1},{9,5},... | collective-permute-start | bytes 786440 | tf_op jit(solution)/shard_map/ppermute | solution.py:41
  140.8 73.5 %collective-permute-start.12 = (bf16[256,512]{1,0:T(8,128)(2,1)}, bf16[256,512]{1,0:T(8,128)(2,1)}, u32[]{:S(2)}, u32[]{:S(2)}) collective-permute-start(bf16[256,512]{1,0:T(8,128)(2,1)} %slice.119), channel_id=1, source_target_pairs={{0,1},{1,0},{2,3},{3,2},{4,5},{5,4},{6,7},{7,6},{8,9},{9,8},{10,11... | collective-permute-start | bytes 786440 | tf_op jit(solution)/shard_map/ppermute | solution.py:44
  141.8 9.0 %collective-permute-start.21 = (bf16[256,512]{0,1:T(8,128)(2,1)}, bf16[256,512]{0,1:T(8,128)(2,1)S(1)}, u32[]{:S(2)}, u32[]{:S(2)}) collective-permute-start(bf16[256,512]{0,1:T(8,128)(2,1)} %collective-permute-done.17), channel_id=1, source_target_pairs={{0,4},{4,8},{8,12},{12,14},{14,10},{10,6},{6,2},{2,0},{1,5},{5,9},... | collective-permute-start | bytes 786440 | tf_op jit(solution)/shard_map/ppermute | solution.py:38
  141.9 9.3 %collective-permute-start.22 = (bf16[256,512]{0,1:T(8,128)(2,1)}, bf16[256,512]{0,1:T(8,128)(2,1)S(1)}, u32[]{:S(2)}, u32[]{:S(2)}) collective-permute-start(bf16[256,512]{0,1:T(8,128)(2,1)} %collective-permute-done.18), channel_id=1, source_target_pairs={{4,0},{8,4},{12,8},{14,12},{10,14},{6,10},{2,6},{0,2},{5,1},{9,5},... | collective-permute-start | bytes 786440 | tf_op jit(solution)/shard_map/ppermute | solution.py:41
  144.8 9.7 %copy-start.11 = (bf16[512,512]{0,1:T(8,128)(2,1)}, bf16[512,512]{0,1:T(8,128)(2,1)S(1)}, u32[]{:S(2)}) copy-start(bf16[512,512]{0,1:T(8,128)(2,1)S(1)} %constant_dynamic-update-slice_fusion) | copy-start | bytes 1572868
  144.8 11.8 %collective-permute-start.15 = (bf16[512,512]{0,1:T(8,128)(2,1)S(1)}, bf16[512,512]{0,1:T(8,128)(2,1)}, u32[]{:S(2)}, u32[]{:S(2)}) collective-permute-start(bf16[512,512]{0,1:T(8,128)(2,1)S(1)} %constant_dynamic-update-slice_fusion), channel_id=1, source_target_pairs={{0,1},{1,0},{2,3},{3,2},{4,5},{5,4},{6,7},{7,6},{8,9},{9,8},{10,11... | collective-permute-start | bytes 1572872 | tf_op jit(solution)/shard_map/ppermute | solution.py:44
  148.5 31.6 %collective-permute-start.19 = (bf16[512,512]{0,1:T(8,128)(2,1)}, bf16[512,512]{0,1:T(8,128)(2,1)}, u32[]{:S(2)}, u32[]{:S(2)}) collective-permute-start(bf16[512,512]{0,1:T(8,128)(2,1)} %constant_dynamic-update-slice_fusion.2), channel_id=1, source_target_pairs={{0,1},{1,0},{2,3},{3,2},{4,5},{5,4},{6,7},{7,6},{8,9},{9,8},{10,11... | collective-permute-start | bytes 1572872 | tf_op jit(solution)/shard_map/ppermute | solution.py:44
  150.8 5.2 %collective-permute-start.25 = (bf16[128,512]{0,1:T(8,128)(2,1)S(1)}, bf16[128,512]{0,1:T(8,128)(2,1)S(1)}, u32[]{:S(2)}, u32[]{:S(2)}) collective-permute-start(bf16[128,512]{0,1:T(8,128)(2,1)S(1)} %slice.129), channel_id=1, source_target_pairs={{0,4},{4,8},{8,12},{12,14},{14,10},{10,6},{6,2},{2,0},{1,5},{5,9},... | collective-permute-start | bytes 393224 | tf_op jit(solution)/shard_map/ppermute | solution.py:38
  151.1 5.3 %collective-permute-start.26 = (bf16[128,512]{0,1:T(8,128)(2,1)S(1)}, bf16[128,512]{0,1:T(8,128)(2,1)S(1)}, u32[]{:S(2)}, u32[]{:S(2)}) collective-permute-start(bf16[128,512]{0,1:T(8,128)(2,1)S(1)} %slice.130), channel_id=1, source_target_pairs={{4,0},{8,4},{12,8},{14,12},{10,14},{6,10},{2,6},{0,2},{5,1},{9,5},... | collective-permute-start | bytes 393224 | tf_op jit(solution)/shard_map/ppermute | solution.py:41
  156.0 15.5 %collective-permute-start.23 = (bf16[512,512]{0,1:T(8,128)(2,1)}, bf16[512,512]{0,1:T(8,128)(2,1)}, u32[]{:S(2)}, u32[]{:S(2)}) collective-permute-start(bf16[512,512]{0,1:T(8,128)(2,1)} %constant_dynamic-update-slice_fusion.4), channel_id=1, source_target_pairs={{0,1},{1,0},{2,3},{3,2},{4,5},{5,4},{6,7},{7,6},{8,9},{9,8},{10,11... | collective-permute-start | bytes 1572872 | tf_op jit(solution)/shard_map/ppermute | solution.py:44
  156.5 8.7 %collective-permute-start.27 = (bf16[256,512]{0,1:T(8,128)(2,1)S(1)}, bf16[256,512]{0,1:T(8,128)(2,1)S(1)}, u32[]{:S(2)}, u32[]{:S(2)}) collective-permute-start(bf16[256,512]{0,1:T(8,128)(2,1)S(1)} %constant_dynamic-update-slice_fusion.6), channel_id=1, source_target_pairs={{0,1},{1,0},{2,3},{3,2},{4,5},{5,4},{6,7},{7,6},{8,9},{9,8},{10,11... | collective-permute-start | bytes 786440 | tf_op jit(solution)/shard_map/ppermute | solution.py:44
  164.7 41.8 %collective-permute-start.16 = (bf16[512,512]{1,0:T(8,128)(2,1)}, bf16[512,512]{1,0:T(8,128)(2,1)}, u32[]{:S(2)}, u32[]{:S(2)}) collective-permute-start(bf16[512,512]{1,0:T(8,128)(2,1)} %slice.121), channel_id=1, source_target_pairs={{0,1},{1,0},{2,3},{3,2},{4,5},{5,4},{6,7},{7,6},{8,9},{9,8},{10,11... | collective-permute-start | bytes 1572872 | tf_op jit(solution)/shard_map/ppermute | solution.py:44
  171.4 16.3 %collective-permute-start.28 = (bf16[256,512]{1,0:T(8,128)(2,1)}, bf16[256,512]{1,0:T(8,128)(2,1)}, u32[]{:S(2)}, u32[]{:S(2)}) collective-permute-start(bf16[256,512]{1,0:T(8,128)(2,1)} %slice.132), channel_id=1, source_target_pairs={{0,1},{1,0},{2,3},{3,2},{4,5},{5,4},{6,7},{7,6},{8,9},{9,8},{10,11... | collective-permute-start | bytes 786440 | tf_op jit(solution)/shard_map/ppermute | solution.py:44
  179.6 10.2 %collective-permute-start.24 = (bf16[512,512]{1,0:T(8,128)(2,1)}, bf16[512,512]{1,0:T(8,128)(2,1)S(1)}, u32[]{:S(2)}, u32[]{:S(2)}) collective-permute-start(bf16[512,512]{1,0:T(8,128)(2,1)} %slice.127), channel_id=1, source_target_pairs={{0,1},{1,0},{2,3},{3,2},{4,5},{5,4},{6,7},{7,6},{8,9},{9,8},{10,11... | collective-permute-start | bytes 1572872 | tf_op jit(solution)/shard_map/ppermute | solution.py:44
  187.5 10.3 %collective-permute-start.20 = (bf16[512,512]{1,0:T(8,128)(2,1)S(1)}, bf16[512,512]{1,0:T(8,128)(2,1)S(1)}, u32[]{:S(2)}, u32[]{:S(2)}) collective-permute-start(bf16[512,512]{1,0:T(8,128)(2,1)S(1)} %slice.124), channel_id=1, source_target_pairs={{0,1},{1,0},{2,3},{3,2},{4,5},{5,4},{6,7},{7,6},{8,9},{9,8},{10,11... | collective-permute-start | bytes 1572872 | tf_op jit(solution)/shard_map/ppermute | solution.py:44
  188.8 5.9 %collective-permute-start.29 = (bf16[128,512]{1,0:T(8,128)(2,1)S(1)}, bf16[128,512]{1,0:T(8,128)(2,1)S(1)}, u32[]{:S(2)}, u32[]{:S(2)}) collective-permute-start(bf16[128,512]{1,0:T(8,128)(2,1)S(1)} %get-tuple-element.23), channel_id=1, source_target_pairs={{0,4},{4,8},{8,12},{12,14},{14,10},{10,6},{6,2},{2,0},{1,5},{5,9},... | collective-permute-start | bytes 393224 | tf_op jit(solution)/shard_map/ppermute | solution.py:38
  189.9 5.7 %collective-permute-start.33 = (bf16[128,512]{1,0:T(8,128)(2,1)S(1)}, bf16[128,512]{1,0:T(8,128)(2,1)S(1)}, u32[]{:S(2)}, u32[]{:S(2)}) collective-permute-start(bf16[128,512]{1,0:T(8,128)(2,1)S(1)} %get-tuple-element.24), channel_id=1, source_target_pairs={{4,0},{8,4},{12,8},{14,12},{10,14},{6,10},{2,6},{0,2},{5,1},{9,5},... | collective-permute-start | bytes 393224 | tf_op jit(solution)/shard_map/ppermute | solution.py:41
  195.7 7.9 %collective-permute-start.34 = (bf16[256,512]{1,0:T(8,128)(2,1)S(1)}, bf16[256,512]{1,0:T(8,128)(2,1)S(1)}, u32[]{:S(2)}, u32[]{:S(2)}) collective-permute-start(bf16[256,512]{1,0:T(8,128)(2,1)S(1)} %pad_maximum_fusion.4), channel_id=1, source_target_pairs={{4,0},{8,4},{12,8},{14,12},{10,14},{6,10},{2,6},{0,2},{5,1},{9,5},... | collective-permute-start | bytes 786440 | tf_op jit(solution)/shard_map/ppermute | solution.py:41
  196.6 9.9 %copy-start.4 = (bf16[512,1024]{1,0:T(8,128)(2,1)S(1)}, bf16[512,1024]{1,0:T(8,128)(2,1)}, u32[]{:S(2)}) copy-start(bf16[512,1024]{1,0:T(8,128)(2,1)} %multiply_convert_fusion.2) | copy-start | bytes 3145732
  196.6 7.6 %collective-permute-start.30 = (bf16[256,512]{1,0:T(8,128)(2,1)S(1)}, bf16[256,512]{1,0:T(8,128)(2,1)S(1)}, u32[]{:S(2)}, u32[]{:S(2)}) collective-permute-start(bf16[256,512]{1,0:T(8,128)(2,1)S(1)} %pad_maximum_fusion.3), channel_id=1, source_target_pairs={{0,4},{4,8},{8,12},{12,14},{14,10},{10,6},{6,2},{2,0},{1,5},{5,9},... | collective-permute-start | bytes 786440 | tf_op jit(solution)/shard_map/ppermute | solution.py:38
  204.4 6.7 %collective-permute-start.31 = (bf16[256,512]{1,0:T(8,128)(2,1)S(1)}, bf16[256,512]{1,0:T(8,128)(2,1)S(1)}, u32[]{:S(2)}, u32[]{:S(2)}) collective-permute-start(bf16[256,512]{1,0:T(8,128)(2,1)S(1)} %get-tuple-element.15), channel_id=1, source_target_pairs={{0,4},{4,8},{8,12},{12,14},{14,10},{10,6},{6,2},{2,0},{1,5},{5,9},... | collective-permute-start | bytes 786440 | tf_op jit(solution)/shard_map/ppermute | solution.py:38
  205.6 14.7 %copy-start.7 = (bf16[256,1024]{1,0:T(8,128)(2,1)S(1)}, bf16[256,1024]{1,0:T(8,128)(2,1)}, u32[]{:S(2)}) copy-start(bf16[256,1024]{1,0:T(8,128)(2,1)} %copy-done.6) | copy-start | bytes 1572868
  205.6 6.4 %collective-permute-start.35 = (bf16[256,512]{1,0:T(8,128)(2,1)S(1)}, bf16[256,512]{1,0:T(8,128)(2,1)S(1)}, u32[]{:S(2)}, u32[]{:S(2)}) collective-permute-start(bf16[256,512]{1,0:T(8,128)(2,1)S(1)} %get-tuple-element.16), channel_id=1, source_target_pairs={{4,0},{8,4},{12,8},{14,12},{10,14},{6,10},{2,6},{0,2},{5,1},{9,5},... | collective-permute-start | bytes 786440 | tf_op jit(solution)/shard_map/ppermute | solution.py:41
  207.7 15.4 %copy-start = (bf16[256,4096]{1,0:T(8,128)(2,1)S(1)}, bf16[256,4096]{1,0:T(8,128)(2,1)}, u32[]{:S(2)}) copy-start(bf16[256,4096]{1,0:T(8,128)(2,1)} %param.24) | copy-start | bytes 6291460
  212.2 6.4 %collective-permute-start.32 = (bf16[256,512]{1,0:T(8,128)(2,1)S(1)}, bf16[256,512]{1,0:T(8,128)(2,1)S(1)}, u32[]{:S(2)}, u32[]{:S(2)}) collective-permute-start(bf16[256,512]{1,0:T(8,128)(2,1)S(1)} %get-tuple-element.13), channel_id=1, source_target_pairs={{0,4},{4,8},{8,12},{12,14},{14,10},{10,6},{6,2},{2,0},{1,5},{5,9},... | collective-permute-start | bytes 786440 | tf_op jit(solution)/shard_map/ppermute | solution.py:38
  214.0 6.4 %collective-permute-start.36 = (bf16[256,512]{1,0:T(8,128)(2,1)S(1)}, bf16[256,512]{1,0:T(8,128)(2,1)S(1)}, u32[]{:S(2)}, u32[]{:S(2)}) collective-permute-start(bf16[256,512]{1,0:T(8,128)(2,1)S(1)} %get-tuple-element.14), channel_id=1, source_target_pairs={{4,0},{8,4},{12,8},{14,12},{10,14},{6,10},{2,6},{0,2},{5,1},{9,5},... | collective-permute-start | bytes 786440 | tf_op jit(solution)/shard_map/ppermute | solution.py:41
  221.4 1.6 collective-permute-start.37
  (11 other events, 44.6 us)
Sparse Core Ops, SparseCore 0:
  20.4 81.4 all-gather.2

commit v2 on v1

v2 whole, which is shorter than its diff:
```python
import functools

import jax
import jax.numpy as jnp
from jax import lax
from jax.experimental import pallas as pl
from jax.experimental.pallas import tpu as pltpu
from jax.sharding import PartitionSpec as P

F32, BF16 = jnp.float32, jnp.bfloat16
VMEM = pl.BlockSpec(memory_space=pltpu.VMEM)
SMEM = pl.BlockSpec(memory_space=pltpu.SMEM)
ANY = pl.BlockSpec(memory_space=pl.ANY)
LIMIT, BIG = 40 * 2**20, 60 * 2**20


def kernel_call(body, out, n_in, flops, nbytes, scratch=(), n_any=0, limit=LIMIT):
    return pl.pallas_call(
        body,
        out_shape=out,
        in_specs=[SMEM] + [VMEM] * (n_in - 1) + [ANY] * n_any,
        out_specs=jax.tree.map(lambda _: VMEM, out),
        scratch_shapes=list(scratch),
        compiler_params=pltpu.CompilerParams(vmem_limit_bytes=limit),
        cost_estimate=pl.CostEstimate(
            flops=flops, bytes_accessed=nbytes, transcendentals=0
        ),
    )


def norm_body(info, tokens, gain, out):
    rows, model = tokens.shape
    step = 16

    @pl.loop(0, rows // step)
    def _(i):
        at = pl.ds(pl.multiple_of(i * step, step), step)
        x = tokens[at, :].astype(F32)
        mean = jnp.sum(x * x, axis=1, keepdims=True) * (1.0 / model)
        x = tokens[at, :].astype(F32) * lax.rsqrt(mean + 1e-05) * gain[...]
        out[at, :] = x.astype(BF16)


def fetch(sources, places, done):
    copies = [
        pltpu.make_async_copy(a, b, done.at[i])
        for i, (a, b) in enumerate(zip(sources, places))
    ]
    for copy in copies:
        copy.start()

    def arrived(i):
        copies[i].wait()
        return places[i]

    return arrived


def places_for(arrays):
    return [pltpu.VMEM(a.shape, a.dtype) for a in arrays] + [
        pltpu.SemaphoreType.DMA((len(arrays),))
    ]


def project(info, left, count, depth, arrived):
    total = None
    for i in range(count - 1):
        if i < count - 2:
            block = arrived(i)[:depth, :]
        else:
            block = [arrived(j)[: depth // 2, :] for j in (i, i + 1)]
            block = jnp.concatenate(block, axis=0)
        begin = pl.multiple_of(info[2 + i] * depth, depth)
        term = jnp.dot(left(pl.ds(begin, depth)), block, preferred_element_type=F32)
        total = term if total is None else total + term
    return total


def there_body(depth, info, first, second, *rest):
    count = len(rest) // 2 - 1
    blocks, out, places, done = rest[:count], rest[count], rest[count + 1 : -1], rest[-1]
    half = first.shape[0]
    total = project(
        info,
        lambda at: jnp.concatenate([first[:, at], second[:, at]], axis=0),
        count,
        depth,
        fetch(blocks, places, done),
    ).astype(BF16)
    core = info[0]
    out[pl.ds(pl.multiple_of(core * half, half), half), :] = total[:half]
    out[pl.ds(pl.multiple_of((1 - core) * half, half), half), :] = total[half:]


def mine_body(depth, wide, info, normed, *rest):
    count = (len(rest) - 3) // 2
    blocks, out, gates = rest[:count], rest[count], rest[count + 1]
    places, done = rest[count + 2 : -1], rest[-1]
    total = project(
        info, lambda at: normed[:, at], count, depth, fetch(blocks, places, done)
    )
    out[...] = total.astype(BF16)
    blocks = places
    carried = [b[depth:, :] for b in blocks[:-2]] + [blocks[-1][depth // 2 :, :]]
    number = lax.broadcasted_iota(jnp.int32, carried[0].shape, 0)
    chosen = (number % wide == info[1]) & (number < 3 * wide)
    lines = [
        jnp.sum(jnp.where(chosen, c.astype(F32), 0.0), axis=0, keepdims=True)
        for c in carried
    ]
    gates[...] = jnp.concatenate(lines, axis=0).T


def expert_body(columns, info, *refs):
    n = len(columns)
    own, other = refs[:n], refs[n : 2 * n]
    gates, up, down, stay, give, x, total = refs[2 * n :]
    core = info[0]
    half = own[0].shape[1]
    here = pl.ds(pl.multiple_of(core * half, half), half)
    there = pl.ds(pl.multiple_of((1 - core) * half, half), half)
    begin = 0
    for a, b in zip(own, other):
        size = a.shape[0]
        x[begin : begin + size, here] = a[...]
        x[begin : begin + size, there] = b[...]
        begin += size
    hidden = up.shape[0]
    chunk = max(c for c in range(16, 513, 16) if hidden % c == 0)
    for i in range(hidden // chunk):
        at = slice(i * chunk, (i + 1) * chunk)
        h = lax.dot_general(
            x[...], up[at, :], (((1,), (1,)), ((), ())), preferred_element_type=F32
        )
        h = jnp.square(jnp.maximum(h, 0.0)).astype(BF16)
        part = jnp.dot(h, down[at, :], preferred_element_type=F32)
        if i == 0:
            total[...] = part
        else:
            total[...] += part
    begin = 0
    for j, (column, first) in enumerate(columns):
        size = own[j].shape[0]
        gate = gates[first : first + size, column : column + 1]
        rows = slice(begin, begin + size)
        stay[rows, :] = (total[rows, here] * gate).astype(BF16)
        give[rows, :] = (total[rows, there] * gate).astype(BF16)
        begin += size


def final_body(depth, info, kept, mine, back, *rest):
    *blocks, out, mixture, full, done = rest
    core, side, me = info[0], info[1], info[2]
    count = (len(blocks) - 1) // 2
    span = blocks[1].shape[1]
    places = [full.at[pl.ds(pl.multiple_of(me * depth, depth), depth), :]]
    for number in range(2):
        at = pl.ds(pl.multiple_of((side + number) % 2 * span, span), span)
        for i in range(count):
            size = blocks[1 + i].shape[0]
            begin = info[2 + min(1 + i, count - 1)] * depth
            if i == count - 1:
                begin = begin + size
            places.append(full.at[pl.ds(pl.multiple_of(begin, size), size), at])
    arrived = fetch(blocks, places, done)
    half = mine.shape[1]
    mixture[:, pl.ds(pl.multiple_of(core * half, half), half)] = mine[...]
    mixture[:, pl.ds(pl.multiple_of((1 - core) * half, half), half)] = back[...]
    for i in range(len(blocks)):
        arrived(i)
    step = 512
    for i in range(full.shape[1] // step):
        at = slice(i * step, (i + 1) * step)
        branch = jnp.dot(mixture[...], full[:, at], preferred_element_type=F32)
        out[:, at] = (kept[:, at].astype(F32) + branch).astype(BF16)


def after(x, *others):
    return lax.optimization_barrier((x, others))[0]


def both(*xs):
    return lax.optimization_barrier(xs)


def ring_order(mesh):
    wide = mesh.shape["wide"]
    line = mesh.devices.reshape(-1, wide, mesh.shape["narrow"])[0, :, 0]
    places = [tuple(getattr(d, "coords", (0,))) for d in line]
    spread = [len(set(c)) for c in zip(*places)]
    if sum(s > 1 for s in spread) == 2 and wide % 2 == 0:
        return list(range(0, wide, 2)) + list(range(wide - 1, 0, -2))
    return list(range(wide))


def make_local(order):
    wide = len(order)
    far = wide // 2
    up_perm = [(order[i], order[(i + 1) % wide]) for i in range(wide)]
    down_perm = [(order[(i + 1) % wide], order[i]) for i in range(wide)]
    offsets = [0] + [s * d for d in range(1, far) for s in (-1, 1)] + [far]
    sources = [[order[(order.index(i) + o) % wide] for o in offsets] for i in range(wide)]

    def local(tokens, norm_gain, w_in, w_out, w_up, w_down, expert_ids, gate_weights):
        groups = lax.axis_size("groups")
        side = lax.axis_index("groups") % 2
        me = lax.axis_index("wide")
        core = lax.axis_index("narrow")
        rows, model = tokens.shape
        half_rows = rows // 2
        depth, width = w_in.shape
        half, quarter = width // 2, width // 4
        info = jnp.concatenate(
            [jnp.stack([core, me]), jnp.asarray(sources, jnp.int32)[me]]
        ).astype(jnp.int32)

        def up(x):
            return lax.ppermute(x, "wide", up_perm)

        def down(x):
            return lax.ppermute(x, "wide", down_perm)

        def swap(x):
            return lax.ppermute(x, "narrow", [(0, 1), (1, 0)])

        def across(x):
            return lax.ppermute(x, "groups", [(i, i ^ 1) for i in range(groups)])

        def shape(*dims, kind=BF16):
            return jax.ShapeDtypeStruct(dims, kind)

        named = expert_ids[:, :, None] == jnp.arange(wide, dtype=jnp.int32)
        dense = jnp.sum(jnp.where(named, gate_weights[:, :, None], 0.0), axis=1).T
        high = dense.astype(BF16)
        rest = dense - high.astype(F32)
        middle = rest.astype(BF16)
        low = (rest - middle.astype(F32)).astype(BF16)
        empty = jnp.zeros((-3 * wide % 16, rows), BF16)

        block = lax.dynamic_slice_in_dim(w_in, (core * 2 + side) * quarter, quarter, 1)
        block = jnp.concatenate([block, high, middle, low, empty], axis=0)
        blocks = [block]
        below = above = block
        for _ in range(1, far):
            below, above = both(up(below), down(above))
            blocks += [below, above]
        blocks += both(up(below[: depth // 2]), down(above[depth // 2 :]))

        def norm(x):
            return kernel_call(
                norm_body,
                shape(*x.shape),
                3,
                8 * x.size,
                4 * x.size,
            )(info, x, norm_gain.reshape(1, model))

        normed = norm(after(tokens, block))
        raw = lax.dynamic_slice_in_dim(after(tokens, block), core * half_rows, half_rows, 0)
        first = norm(after(across(raw), blocks[-3], normed))
        second = swap(first)
        columns = w_out.shape[1]
        kept = lax.dynamic_slice_in_dim(tokens, core * columns, columns, 1)

        out_depth = w_out.shape[0]
        out_blocks = []
        out_below = out_above = lax.dynamic_slice_in_dim(
            w_out, side * (columns // 2), columns // 2, 1
        )

        def out_step(*others):
            nonlocal out_below, out_above
            out_below, out_above = after((out_below, out_above), *others)
            if len(out_blocks) == 2 * far - 2:
                cut = out_depth // 2
                out_below, out_above = out_below[:cut], out_above[cut:]
            out_below, out_above = both(up(out_below), down(out_above))
            out_blocks.extend([out_below, out_above])

        early = far // 2
        out_step(blocks[-3], blocks[-4])
        for _ in range(1, early):
            out_step()

        flops = 2 * rows * model * quarter
        nbytes = 2 * (rows * model + model * quarter)
        lat_there = kernel_call(
            functools.partial(there_body, depth),
            shape(rows, quarter),
            3,
            flops,
            nbytes,
            places_for(blocks),
            len(blocks),
            BIG,
        )(info, first, second, *blocks)
        lat_other = across(lat_there)
        lat_mine, gates = kernel_call(
            functools.partial(mine_body, depth, wide),
            (shape(rows, quarter), shape(rows, wide, kind=F32)),
            2,
            flops,
            nbytes,
            places_for(blocks),
            len(blocks),
            BIG,
        )(info, after(normed, lat_there), *blocks)
        latent = jnp.concatenate(
            [
                jnp.where(side == 0, lat_mine, lat_other),
                jnp.where(side == 0, lat_other, lat_mine),
            ],
            axis=1,
        )
        latent = after(latent, *out_blocks[:-2])

        up_weight, down_weight = w_up[0].T, w_down[0]
        hidden = up_weight.shape[0]

        def expert(xs, columns, *others):
            size = sum(x.shape[0] for x in xs)
            out = shape(size, half)
            ys = after([swap(x) for x in xs], *others)
            return kernel_call(
                functools.partial(expert_body, columns),
                (out, out),
                4 + 2 * len(xs),
                4 * size * width * hidden,
                4 * hidden * width + 4 * size * width,
                [pltpu.VMEM((size, width), BF16), pltpu.VMEM((size, width), F32)],
            )(info, *xs, *ys, gates, up_weight, down_weight)

        def total(stay, given, more=None):
            t = stay.astype(F32) + given.astype(F32)
            return t if more is None else t + more.astype(F32)

        def hand(first, number):
            handed.extend(both(*[across(b) for b in out_blocks[first : first + number]]))

        handed = []
        done = {0: expert([latent], [(0, 0)])}
        pairs = [(latent, latent)]
        for d in range(1, far + 1):
            below, above = pairs[-1]
            if d == 2:
                below, above = after((below, above), *done[0], *out_blocks)
            if d == 3:
                hand(0, 2)
                below, above = after((below, above), *handed)
            if d == far:
                below, above = after((below, above), *done[1])
                below, above = below[:half_rows], above[half_rows:]
            pairs.append(both(up(below), down(above)))
            if d == 2:
                done[1] = expert(pairs[1], [(1, 0), (2, 0)])
        hand(len(handed), 2)
        out_step(*pairs[far - 1])
        done[far] = expert(pairs[far], [(wide - 1, 0), (wide - 1, half_rows)])

        given = swap(done[far][1])
        back = total(done[far][0], given).astype(BF16)
        back, *_ = both(back, *out_blocks, *handed)
        to_above, to_below = both(up(back[:half_rows]), down(back[half_rows:]))
        for _ in range(early + 1, far):
            out_step()
        for d in range(far - 1, 0, -1):
            if d not in done:
                done[d] = expert(pairs[d], [(2 * d - 1, 0), (2 * d, 0)], given)
            given = swap(done[d][1])
            below = total(done[d][0][:rows], given[:rows])
            above = total(done[d][0][rows:], given[rows:])
            if d == far - 1:
                above = jnp.concatenate(
                    [above[:half_rows] + to_above.astype(F32), above[half_rows:]], axis=0
                )
                below = jnp.concatenate(
                    [below[:half_rows], below[half_rows:] + to_below.astype(F32)], axis=0
                )
            else:
                above, below = above + to_above.astype(F32), below + to_below.astype(F32)
            above, below = above.astype(BF16), below.astype(BF16)
            if d == far - 1:
                above, below = after((above, below), *out_blocks)
                hand(len(handed), 2)
            elif d == far - 2:
                above, below = after((above, below), *handed)
                hand(len(handed), len(out_blocks) - len(handed))
            else:
                above, below = after((above, below), *handed)
            to_above, to_below = both(up(above), down(below))
        mixture = total(done[0][0], swap(done[0][1]), to_above)
        mixture = (mixture + to_below.astype(F32)).astype(BF16)
        return kernel_call(
            functools.partial(final_body, out_depth),
            shape(rows, columns),
            4,
            2 * rows * width * columns,
            2 * width * columns + 4 * rows * columns,
            [
                pltpu.VMEM((rows, width), BF16),
                pltpu.VMEM((width, columns), BF16),
                pltpu.SemaphoreType.DMA((1 + 2 * len(out_blocks),)),
            ],
            1 + 2 * len(out_blocks),
            BIG,
        )(
            info.at[1].set(side.astype(jnp.int32)),
            kept,
            mixture,
            swap(mixture),
            w_out,
            *out_blocks,
            *handed,
        )

    return local


def solution(mesh):
    in_specs = (
        P(("groups", "wide"), None),
        P(),
        P("wide", None),
        P("wide", "narrow"),
        P("wide", None, "narrow"),
        P("wide", "narrow", None),
        P(("groups", "wide"), None),
        P(("groups", "wide"), None),
    )
    out_specs = P(("groups", "wide"), "narrow")
    local = make_local(ring_order(mesh))
    return jax.shard_map(
        local, mesh=mesh, in_specs=in_specs, out_specs=out_specs, check_vma=False
    )
```

time: 236 us -> 171 us (0.72)
  matrix products: 39 us -> 0 us
  between operations: 39.4 us -> 0.75 us
  Pallas kernels: 0 us -> 38.3 us
  blocking collectives: 31.2 us -> 0 us
  waiting for transfers between devices: 43.5 us -> 67 us
  local copies, waits for them, and re-layouts: 35.1 us -> 14.6 us
  starting transfers between devices: 36.6 us -> 47.1 us
  other arithmetic: 9.48 us -> 2.66 us
    dot_general x8 -> x0, matrix products: 39 us -> none  [the longest x5 28.4 us: expert(): part = jnp.dot(hidden, down_weight, preferred_element_type=f32)]
    pallas_call x0 -> x10, Pallas kernels: none -> 38.3 us  [the longest x5 18 us: expert(): kernel_call(functools.partial(expert_body, columns), (out, out), 4 + 2 *...]
    all_gather x1 -> x0, blocking collectives: 31.2 us -> none  [local(): gates = lax.all_gather(dense, 'wide', axis=0)]
    ppermute x12 -> x16, waiting for transfers between devices: 22.9 us -> 37.9 us  [up(): return lax.ppermute(x, 'wide', up_perm)]
    ppermute x2 -> x10, waiting for transfers between devices: 5.25 us -> 17.3 us  [across(): return lax.ppermute(x, 'groups', [(i, i ^ 1) for i in range(groups)])]
    dynamic_update_slice x9 -> x0, local copies, waits for them, and re-layouts: 11.2 us -> none  [the longest x3 4.06 us: local(): lax.dynamic_update_slice_in_dim(full_in, from_below, at(-d) * depth, 0)]
    ppermute x12 -> x16, starting transfers between devices: 12.8 us -> 23.5 us  [up(): return lax.ppermute(x, 'wide', up_perm)]
    ppermute x12 -> x16, starting transfers between devices: 18.9 us -> 9.9 us  [down(): return lax.ppermute(x, 'wide', down_perm)]
  transfers between devices with their start and end apart: 39 -> 58, of which waited for: 18 -> 27; matrix products, arithmetic and copies ran while one was open for 31% -> 4% of each run, Pallas kernels for 0% -> 18%
where the time goes in v2:
time: 171 us; the launch traced here: 170 us
  waiting for transfers between devices  67 us (39%)
  starting transfers between devices  47.1 us (28%)
  Pallas kernels  38.3 us (22%)
  local copies, waits for them, and re-layouts  14.6 us (9%)
  other arithmetic  2.66 us (2%)
    ppermute x16, waiting for transfers between devices, up(): return lax.ppermute(x, 'wide', up_perm)  37.9 us
    ppermute x16, starting transfers between devices, up(): return lax.ppermute(x, 'wide', up_perm)  23.5 us
    pallas_call x5, Pallas kernels, expert(): kernel_call(functools.partial(expert_body, columns), (out, out), 4 + 2 *...  18 us
    ppermute x10, waiting for transfers between devices, across(): return lax.ppermute(x, 'groups', [(i, i ^ 1) for i in range(groups)])  17.3 us
    ppermute x10, starting transfers between devices, across(): return lax.ppermute(x, 'groups', [(i, i ^ 1) for i in range(groups)])  11.7 us
    ppermute x16, waiting for transfers between devices, down(): return lax.ppermute(x, 'wide', down_perm)  11.3 us
    ppermute x16, starting transfers between devices, down(): return lax.ppermute(x, 'wide', down_perm)  9.9 us
    unnamed x73, local copies, waits for them, and re-layouts  7.65 us
  transfers between devices with their start and end apart: 58, of which 27 were waited for; matrix products, arithmetic and copies ran while one was open for 4% of the time, Pallas kernels for 18%

profile of v2, /device:TPU:0, one launch (start us, length us, event | category | flops | bytes accessed | tf_op | source)
XLA Modules:
  0.0 170.5 jit_solution(6366780574453832957)
XLA Ops:
  1.9 2.4 %constant_dynamic-slice_fusion.1 = bf16[128,4096]{1,0:T(8,128)(2,1)} fusion(bf16[256,4096]{1,0:T(8,128)(2,1)} %tokens, s32[]{:T(128)S(6)} %select_n.44), kind=kLoop, calls=%fused_computation.31 | loop fusion | bytes 2097156 | tf_op jit(solution)/shard_map/dynamic_slice | solution.py:259
  4.3 2.9 %collective-permute-start = (bf16[128,4096]{1,0:T(8,128)(2,1)}, bf16[128,4096]{1,0:T(8,128)(2,1)S(1)}, u32[]{:S(2)}, u32[]{:S(2)}) collective-permute-start(bf16[128,4096]{1,0:T(8,128)(2,1)} %constant_dynamic-slice_fusion.1), channel_id=1, source_target_pairs={{0,16},{16,0},{1,17},{17,1},{2,18},{18,2},{3,19},{19,3},{4,20},{20... | collective-permute-start | bytes 3145736 | tf_op jit(solution)/shard_map/ppermute | solution.py:227
  7.2 1.6 collective-permute-start.1
  9.3 6.1 %collective-permute-done.1.rest_1_ = bf16[544,256]{1,0:T(8,128)(2,1)S(1)} collective-permute-done((bf16[544,256]{1,0:T(8,128)(2,1)S(1)}, bf16[544,256]{1,0:T(8,128)(2,1)S(1)}, u32[]{:S(2)}, u32[]{:S(2)}) %collective-permute-start.1) | collective-permute-done | bytes 278560 | tf_op jit(solution)/shard_map/ppermute | solution.py:218
  16.6 1.6 collective-permute-start.3
  18.7 5.0 %collective-permute-done.3.rest_3_ = bf16[544,256]{1,0:T(8,128)(2,1)} collective-permute-done((bf16[544,256]{1,0:T(8,128)(2,1)S(1)}, bf16[544,256]{1,0:T(8,128)(2,1)}, u32[]{:S(2)}, u32[]{:S(2)}) %collective-permute-start.3) | collective-permute-done | bytes 278560 | tf_op jit(solution)/shard_map/ppermute | solution.py:218
  25.0 1.6 collective-permute-start.5
  27.8 2.9 %shard_map.91.normed = bf16[256,4096]{1,0:T(8,128)(2,1)S(1)} custom-call(s32[10]{0:T(128)S(1)} %pad_add_fusion.info, bf16[256,4096]{1,0:T(8,128)(2,1)S(1)} %copy-done.3, f32[1,4096]{1,0:T(1,128)S(1)} %bitcast.39), custom_call_target="tpu_custom_call" | custom-call | flops 8388608 | bytes 4194304 | tf_op jit(solution)/shard_map/pallas_call | solution.py:250
  33.4 1.7 %shard_map.92.first = bf16[128,4096]{1,0:T(8,128)(2,1)S(1)} custom-call(s32[10]{0:T(128)S(1)} %pad_add_fusion.info, bf16[128,4096]{1,0:T(8,128)(2,1)S(1)} %collective-permute-done.tokens, f32[1,4096]{1,0:T(1,128)S(1)} %bitcast.40), custom_call_target="tpu_custom_call" | custom-call | flops 4194304 | bytes 2097152 | tf_op jit(solution)/shard_map/pallas_call | solution.py:250
  37.6 1.6 collective-permute-start.11
  40.5 1.6 collective-permute-start.8
  42.1 6.7 %collective-permute-done.8.rest_7_ = bf16[256,256]{1,0:T(8,128)(2,1)S(1)} collective-permute-done((bf16[256,256]{1,0:T(8,128)(2,1)S(1)}, bf16[256,256]{1,0:T(8,128)(2,1)S(1)}, u32[]{:S(2)}, u32[]{:S(2)}) %collective-permute-start.8) | collective-permute-done | bytes 131104 | tf_op jit(solution)/shard_map/ppermute | solution.py:218
  50.5 4.9 %shard_map.93 = bf16[256,256]{1,0:T(8,128)(2,1)} custom-call(s32[10]{0:T(128)} %copy-done.9, bf16[128,4096]{1,0:T(8,128)(2,1)} %copy-done.6, bf16[128,4096]{1,0:T(8,128)(2,1)} %copy-done.16, bf16[544,256]{1,0:T(8,128)(2,1)} %copy-done.12, bf16[544,256]{1,0:T(8,128)(2,1)} %copy-done.14, bf16[544,256]{1,0:T(8,128)(2,1)} %copy-done.15, ...), custom_call_target="tpu_custom_call" | custom-call | flops 536870912 | bytes 4194304 | tf_op jit(solution)/shard_map/pallas_call | solution.py:287
  56.1 1.6 collective-permute-start.20
  58.1 4.9 %shard_map.94 = (bf16[256,256]{1,0:T(8,128)(2,1)}, f32[256,8]{1,0:T(8,128)}) custom-call(s32[10]{0:T(128)} %copy-done.9, bf16[256,4096]{1,0:T(8,128)(2,1)} %copy-done.5, bf16[544,256]{1,0:T(8,128)(2,1)} %copy-done.12, bf16[544,256]{1,0:T(8,128)(2,1)} %copy-done.14, bf16[544,256]{1,0:T(8,128)(2,1)} %copy-done.15, ...), custom_call_target="tpu_custom_call" | custom-call | flops 536870912 | bytes 4194304 | tf_op jit(solution)/shard_map/pallas_call | solution.py:298
  64.1 1.6 collective-permute-start.15
  66.2 1.6 collective-permute-start.26
  68.3 2.4 %collective-permute-done.15.refs_0_ = bf16[256,512]{1,0:T(8,128)(2,1)S(1)} collective-permute-done((bf16[256,512]{1,0:T(8,128)(2,1)S(1)}, bf16[256,512]{1,0:T(8,128)(2,1)S(1)}, u32[]{:S(2)}, u32[]{:S(2)}) %collective-permute-start.15) | collective-permute-done | bytes 262176 | tf_op jit(solution)/shard_map/ppermute | solution.py:218
  72.1 1.8 %copy-done.1 = bf16[1,1344,1024]{2,1,0:T(8,128)(2,1)S(1)} copy-done((bf16[1,1344,1024]{2,1,0:T(8,128)(2,1)S(1)}, bf16[1,1344,1024]{2,1,0:T(8,128)(2,1)}, u32[]{:S(2)}) %copy-start.1) | copy-done | bytes 2752536
  74.8 2.7 %shard_map.95 = (bf16[256,512]{1,0:T(8,128)(2,1)S(1)}, bf16[256,512]{1,0:T(8,128)(2,1)S(1)}) custom-call(s32[10]{0:T(128)S(1)} %copy-done.10, bf16[256,512]{1,0:T(8,128)(2,1)S(1)} %pad_maximum_fusion.refs_0_, bf16[256,512]{1,0:T(8,128)(2,1)S(1)} %collective-permute-done.13.refs_1_, f32[256,8]{1,0:T(8,128)S(1)} %copy-done.7, bf16[1344,1024]{1,0:T(8,128)(2,1)S(1)} %bitcast.29, ...), custom_call_target="tpu_custom_call" | custom-call | flops 1409286144 | bytes 6553600 | tf_op jit(solution)/shard_map/pallas_call | solution.py:324
  77.5 1.6 collective-permute-start.22
  80.5 3.3 %collective-permute-done.22.refs_0_ = bf16[256,512]{1,0:T(8,128)(2,1)S(1)} collective-permute-done((bf16[256,512]{1,0:T(8,128)(2,1)S(1)}, bf16[256,512]{1,0:T(8,128)(2,1)S(1)}, u32[]{:S(2)}, u32[]{:S(2)}) %collective-permute-start.22) | collective-permute-done | bytes 262176 | tf_op jit(solution)/shard_map/ppermute | solution.py:218
  83.9 1.8 %collective-permute-done.23.refs_1_ = bf16[256,512]{1,0:T(8,128)(2,1)S(1)} collective-permute-done((bf16[256,512]{1,0:T(8,128)(2,1)S(1)}, bf16[256,512]{1,0:T(8,128)(2,1)S(1)}, u32[]{:S(2)}, u32[]{:S(2)}) %collective-permute-start.23) | collective-permute-done | bytes 262176 | tf_op jit(solution)/shard_map/ppermute | solution.py:221
  85.7 1.9 %collective-permute-start.28 = (bf16[256,512]{1,0:T(8,128)(2,1)S(1)}, bf16[256,512]{1,0:T(8,128)(2,1)S(1)}, u32[]{:S(2)}, u32[]{:S(2)}) collective-permute-start(bf16[256,512]{1,0:T(8,128)(2,1)S(1)} %collective-permute-done.22.refs_0_), channel_id=1, source_target_pairs={{0,4},{4,8},{8,12},{12,14},{14,10},{10,6},{6,2},{2,0},{1,5},{5,9},... | collective-permute-start | bytes 786440 | tf_op jit(solution)/shard_map/ppermute | solution.py:218
  87.7 4.2 %shard_map.96 = (bf16[512,512]{1,0:T(8,128)(2,1)S(1)}, bf16[512,512]{1,0:T(8,128)(2,1)S(1)}) custom-call(s32[10]{0:T(128)S(1)} %copy-done.10, bf16[256,512]{1,0:T(8,128)(2,1)S(1)} %collective-permute-done.15.refs_0_, bf16[256,512]{1,0:T(8,128)(2,1)S(1)} %collective-permute-done.16.refs_1_, bf16[256,512]{1,0:T(8,128)(2,1)S(1)} %collective-permute-done.17.refs_2_, ...), custom_call_target="tpu_custom_call" | custom-call | flops 2818572288 | bytes 7602176 | tf_op jit(solution)/shard_map/pallas_call | solution.py:324
  93.3 2.0 %collective-permute-done.29.refs_1_ = bf16[256,512]{1,0:T(8,128)(2,1)S(1)} collective-permute-done((bf16[256,512]{1,0:T(8,128)(2,1)S(1)}, bf16[256,512]{1,0:T(8,128)(2,1)S(1)}, u32[]{:S(2)}, u32[]{:S(2)}) %collective-permute-start.29) | collective-permute-done | bytes 262176 | tf_op jit(solution)/shard_map/ppermute | solution.py:221
  95.5 2.1 %collective-permute-start.33 = (bf16[128,512]{1,0:T(8,128)(2,1)S(1)}, bf16[128,512]{1,0:T(8,128)(2,1)S(1)}, u32[]{:S(2)}, u32[]{:S(2)}) collective-permute-start(bf16[128,512]{1,0:T(8,128)(2,1)S(1)} %slice.89), channel_id=1, source_target_pairs={{4,0},{8,4},{12,8},{14,12},{10,14},{6,10},{2,6},{0,2},{5,1},{9,5},... | collective-permute-start | bytes 393224 | tf_op jit(solution)/shard_map/ppermute | solution.py:221
  97.5 2.9 %collective-permute-done.32.refs_0_ = bf16[128,512]{1,0:T(8,128)(2,1)S(1)} collective-permute-done((bf16[128,512]{1,0:T(8,128)(2,1)S(1)}, bf16[128,512]{1,0:T(8,128)(2,1)S(1)}, u32[]{:S(2)}, u32[]{:S(2)}) %collective-permute-start.32) | collective-permute-done | bytes 131104 | tf_op jit(solution)/shard_map/ppermute | solution.py:218
  101.0 1.5 collective-permute-start.41
  103.0 2.0 %collective-permute-start.39 = (bf16[128,1024]{1,0:T(8,128)(2,1)S(1)}, bf16[128,1024]{1,0:T(8,128)(2,1)S(1)}, u32[]{:S(2)}, u32[]{:S(2)}) collective-permute-start(bf16[128,1024]{1,0:T(8,128)(2,1)S(1)} %collective-permute-done.20.rest_3_), channel_id=1, source_target_pairs={{0,4},{4,8},{8,12},{12,14},{14,10},{10,6},{6,2},{2,0},{1,5},{5,9},... | collective-permute-start | bytes 786440 | tf_op jit(solution)/shard_map/ppermute | solution.py:218
  105.2 2.7 %shard_map.97 = (bf16[256,512]{1,0:T(8,128)(2,1)S(1)}, bf16[256,512]{1,0:T(8,128)(2,1)S(1)}) custom-call(s32[10]{0:T(128)S(1)} %copy-done.10, bf16[128,512]{1,0:T(8,128)(2,1)S(1)} %collective-permute-done.32.refs_0_, bf16[128,512]{1,0:T(8,128)(2,1)S(1)} %collective-permute-done.33.refs_1_, bf16[128,512]{1,0:T(8,128)(2,1)S(1)} %collective-permute-done.34.refs_2_, ...), custom_call_target="tpu_custom_call" | custom-call | flops 1409286144 | bytes 6553600 | tf_op jit(solution)/shard_map/pallas_call | solution.py:324
  107.9 2.3 %collective-permute-done.41.rest_11_ = bf16[128,1024]{1,0:T(8,128)(2,1)S(1)} collective-permute-done((bf16[128,1024]{1,0:T(8,128)(2,1)S(1)}, bf16[128,1024]{1,0:T(8,128)(2,1)S(1)}, u32[]{:S(2)}, u32[]{:S(2)}) %collective-permute-start.41) | collective-permute-done | bytes 262176 | tf_op jit(solution)/shard_map/ppermute | solution.py:227
  110.2 4.7 %collective-permute-done.42.rest_12_ = bf16[128,1024]{1,0:T(8,128)(2,1)S(1)} collective-permute-done((bf16[128,1024]{1,0:T(8,128)(2,1)}, bf16[128,1024]{1,0:T(8,128)(2,1)S(1)}, u32[]{:S(2)}, u32[]{:S(2)}) %collective-permute-start.42) | collective-permute-done | bytes 262176 | tf_op jit(solution)/shard_map/ppermute | solution.py:227
  115.5 2.2 %collective-permute-start.45 = (bf16[64,1024]{1,0:T(8,128)(2,1)S(1)}, bf16[64,1024]{1,0:T(8,128)(2,1)S(1)}, u32[]{:S(2)}, u32[]{:S(2)}) collective-permute-start(bf16[64,1024]{1,0:T(8,128)(2,1)S(1)} %slice.102), channel_id=1, source_target_pairs={{0,4},{4,8},{8,12},{12,14},{14,10},{10,6},{6,2},{2,0},{1,5},{5,9},... | collective-permute-start | bytes 393224 | tf_op jit(solution)/shard_map/ppermute | solution.py:218
  117.8 4.2 %shard_map.98 = (bf16[512,512]{1,0:T(8,128)(2,1)S(1)}, bf16[512,512]{1,0:T(8,128)(2,1)S(1)}) custom-call(s32[10]{0:T(128)S(1)} %copy-done.10, bf16[256,512]{1,0:T(8,128)(2,1)S(1)} %collective-permute-done.28.refs_0_, bf16[256,512]{1,0:T(8,128)(2,1)S(1)} %collective-permute-done.29.refs_1_, bf16[256,512]{1,0:T(8,128)(2,1)S(1)} %collective-permute-done.30.refs_2_, ...), custom_call_target="tpu_custom_call" | custom-call | flops 2818572288 | bytes 7602176 | tf_op jit(solution)/shard_map/pallas_call | solution.py:324
  122.4 1.8 %collective-permute-start.43 = (bf16[128,512]{1,0:T(8,128)(2,1)S(1)}, bf16[128,512]{1,0:T(8,128)(2,1)S(1)}, u32[]{:S(2)}, u32[]{:S(2)}) collective-permute-start(bf16[128,512]{1,0:T(8,128)(2,1)S(1)} %get-tuple-element.194), channel_id=1, source_target_pairs={{0,4},{4,8},{8,12},{12,14},{14,10},{10,6},{6,2},{2,0},{1,5},{5,9},... | collective-permute-start | bytes 393224 | tf_op jit(solution)/shard_map/ppermute | solution.py:218
  124.5 3.9 %collective-permute-done.43 = bf16[128,512]{1,0:T(8,128)(2,1)S(1)} collective-permute-done((bf16[128,512]{1,0:T(8,128)(2,1)S(1)}, bf16[128,512]{1,0:T(8,128)(2,1)S(1)}, u32[]{:S(2)}, u32[]{:S(2)}) %collective-permute-start.43) | collective-permute-done | bytes 131104 | tf_op jit(solution)/shard_map/ppermute | solution.py:218
  128.4 1.5 collective-permute-start.49
  130.4 4.2 %shard_map.99 = (bf16[512,512]{1,0:T(8,128)(2,1)S(1)}, bf16[512,512]{1,0:T(8,128)(2,1)S(1)}) custom-call(s32[10]{0:T(128)S(1)} %copy-done.10, bf16[256,512]{1,0:T(8,128)(2,1)S(1)} %collective-permute-done.22.refs_0_, bf16[256,512]{1,0:T(8,128)(2,1)S(1)} %collective-permute-done.23.refs_1_, bf16[256,512]{1,0:T(8,128)(2,1)S(1)} %collective-permute-done.24.refs_2_, ...), custom_call_target="tpu_custom_call" | custom-call | flops 2818572288 | bytes 7602176 | tf_op jit(solution)/shard_map/pallas_call | solution.py:324
  135.1 1.7 %collective-permute-start.47 = (bf16[256,512]{1,0:T(8,128)(2,1)S(1)}, bf16[256,512]{1,0:T(8,128)(2,1)S(1)}, u32[]{:S(2)}, u32[]{:S(2)}) collective-permute-start(bf16[256,512]{1,0:T(8,128)(2,1)S(1)} %pad_maximum_fusion.1), channel_id=1, source_target_pairs={{0,4},{4,8},{8,12},{12,14},{14,10},{10,6},{6,2},{2,0},{1,5},{5,9},... | collective-permute-start | bytes 786440 | tf_op jit(solution)/shard_map/ppermute | solution.py:218
  137.6 4.4 %collective-permute-done.50.rest_14_ = bf16[128,1024]{1,0:T(8,128)(2,1)S(1)} collective-permute-done((bf16[128,1024]{1,0:T(8,128)(2,1)S(1)}, bf16[128,1024]{1,0:T(8,128)(2,1)S(1)}, u32[]{:S(2)}, u32[]{:S(2)}) %collective-permute-start.50) | collective-permute-done | bytes 262176 | tf_op jit(solution)/shard_map/ppermute | solution.py:227
  142.0 1.8 %collective-permute-done.47 = bf16[256,512]{1,0:T(8,128)(2,1)S(1)} collective-permute-done((bf16[256,512]{1,0:T(8,128)(2,1)S(1)}, bf16[256,512]{1,0:T(8,128)(2,1)S(1)}, u32[]{:S(2)}, u32[]{:S(2)}) %collective-permute-start.47) | collective-permute-done | bytes 262176 | tf_op jit(solution)/shard_map/ppermute | solution.py:218
  145.9 1.7 collective-permute-start.52
  147.8 1.7 %collective-permute-start.54 = (bf16[64,1024]{1,0:T(8,128)(2,1)S(1)}, bf16[64,1024]{1,0:T(8,128)(2,1)S(1)}, u32[]{:S(2)}, u32[]{:S(2)}) collective-permute-start(bf16[64,1024]{1,0:T(8,128)(2,1)S(1)} %collective-permute-done.46.rest_8_), channel_id=1, source_target_pairs={{0,16},{16,0},{1,17},{17,1},{2,18},{18,2},{3,19},{19,3},{4,20},{20... | collective-permute-start | bytes 393224 | tf_op jit(solution)/shard_map/ppermute | solution.py:227
  149.6 3.6 %collective-permute-done.53.rest_15_ = bf16[64,1024]{1,0:T(8,128)(2,1)S(1)} collective-permute-done((bf16[64,1024]{1,0:T(8,128)(2,1)S(1)}, bf16[64,1024]{1,0:T(8,128)(2,1)S(1)}, u32[]{:S(2)}, u32[]{:S(2)}) %collective-permute-start.53) | collective-permute-done | bytes 131104 | tf_op jit(solution)/shard_map/ppermute | solution.py:227
  155.5 1.4 collective-permute-start.56
  156.9 4.3 %collective-permute-done.55 = bf16[256,512]{1,0:T(8,128)(2,1)S(1)} collective-permute-done((bf16[256,512]{1,0:T(8,128)(2,1)S(1)}, bf16[256,512]{1,0:T(8,128)(2,1)S(1)}, u32[]{:S(2)}, u32[]{:S(2)}) %collective-permute-start.55) | collective-permute-done | bytes 262176 | tf_op jit(solution)/shard_map/ppermute | solution.py:218
  164.4 5.9 %shard_map.100 = bf16[256,2048]{1,0:T(8,128)(2,1)} custom-call(s32[10]{0:T(128)} %copy-done.11, bf16[256,2048]{1,0:T(8,128)(2,1)} %constant_dynamic-slice_fusion.2.kept, bf16[256,512]{1,0:T(8,128)(2,1)} %copy-done.17, bf16[256,512]{1,0:T(8,128)(2,1)} %copy-done.31, bf16[128,2048]{1,0:T(8,128)(2,1)} %rest_0_.1, bf16[128,1024]{1,0:T(8,128)(2,1)} %copy-done.22, ...), custom_call_target="tpu_custom_call" | custom-call | flops 1073741824 | bytes 6291456 | tf_op jit(solution)/shard_map/pallas_call | solution.py:393
  (181 shorter events, 35.2 us)
Async XLA Ops:
  4.3 29.1 %collective-permute-start = (bf16[128,4096]{1,0:T(8,128)(2,1)}, bf16[128,4096]{1,0:T(8,128)(2,1)S(1)}, u32[]{:S(2)}, u32[]{:S(2)}) collective-permute-start(bf16[128,4096]{1,0:T(8,128)(2,1)} %constant_dynamic-slice_fusion.1), channel_id=1, source_target_pairs={{0,16},{16,0},{1,17},{17,1},{2,18},{18,2},{3,19},{19,3},{4,20},{20... | collective-permute-start | bytes 3145736 | tf_op jit(solution)/shard_map/ppermute | solution.py:227
  7.2 8.1 %collective-permute-start.1 = (bf16[544,256]{1,0:T(8,128)(2,1)S(1)}, bf16[544,256]{1,0:T(8,128)(2,1)S(1)}, u32[]{:S(2)}, u32[]{:S(2)}) collective-permute-start(bf16[544,256]{1,0:T(8,128)(2,1)S(1)} %constant_dynamic-update-slice_fusion.rest_0_), channel_id=1, source_target_pairs={{0,4},{4,8},{8,12},{12,14},{14,10},{10,6},{6,2},{2,0},{1,5},{5,9},... | collective-permute-start | bytes 835592 | tf_op jit(solution)/shard_map/ppermute | solution.py:218
  8.8 7.8 %collective-permute-start.2 = (bf16[544,256]{1,0:T(8,128)(2,1)S(1)}, bf16[544,256]{1,0:T(8,128)(2,1)S(1)}, u32[]{:S(2)}, u32[]{:S(2)}) collective-permute-start(bf16[544,256]{1,0:T(8,128)(2,1)S(1)} %constant_dynamic-update-slice_fusion.rest_0_), channel_id=1, source_target_pairs={{4,0},{8,4},{12,8},{14,12},{10,14},{6,10},{2,6},{0,2},{5,1},{9,5},... | collective-permute-start | bytes 835592 | tf_op jit(solution)/shard_map/ppermute | solution.py:221
  16.6 7.0 %collective-permute-start.3 = (bf16[544,256]{1,0:T(8,128)(2,1)S(1)}, bf16[544,256]{1,0:T(8,128)(2,1)}, u32[]{:S(2)}, u32[]{:S(2)}) collective-permute-start(bf16[544,256]{1,0:T(8,128)(2,1)S(1)} %collective-permute-done.1.rest_1_), channel_id=1, source_target_pairs={{0,4},{4,8},{8,12},{12,14},{14,10},{10,6},{6,2},{2,0},{1,5},{5,9},... | collective-permute-start | bytes 835592 | tf_op jit(solution)/shard_map/ppermute | solution.py:218
  18.2 6.7 %collective-permute-start.4 = (bf16[544,256]{1,0:T(8,128)(2,1)S(1)}, bf16[544,256]{1,0:T(8,128)(2,1)}, u32[]{:S(2)}, u32[]{:S(2)}) collective-permute-start(bf16[544,256]{1,0:T(8,128)(2,1)S(1)} %collective-permute-done.2.rest_2_), channel_id=1, source_target_pairs={{4,0},{8,4},{12,8},{14,12},{10,14},{6,10},{2,6},{0,2},{5,1},{9,5},... | collective-permute-start | bytes 835592 | tf_op jit(solution)/shard_map/ppermute | solution.py:221
  25.0 7.0 %collective-permute-start.5 = (bf16[544,256]{1,0:T(8,128)(2,1)}, bf16[544,256]{1,0:T(8,128)(2,1)}, u32[]{:S(2)}, u32[]{:S(2)}) collective-permute-start(bf16[544,256]{1,0:T(8,128)(2,1)} %collective-permute-done.3.rest_3_), channel_id=1, source_target_pairs={{0,4},{4,8},{8,12},{12,14},{14,10},{10,6},{6,2},{2,0},{1,5},{5,9},... | collective-permute-start | bytes 835592 | tf_op jit(solution)/shard_map/ppermute | solution.py:218
  26.5 6.9 %collective-permute-start.6 = (bf16[544,256]{1,0:T(8,128)(2,1)}, bf16[544,256]{1,0:T(8,128)(2,1)}, u32[]{:S(2)}, u32[]{:S(2)}) collective-permute-start(bf16[544,256]{1,0:T(8,128)(2,1)} %collective-permute-done.4.rest_4_), channel_id=1, source_target_pairs={{4,0},{8,4},{12,8},{14,12},{10,14},{6,10},{2,6},{0,2},{5,1},{9,5},... | collective-permute-start | bytes 835592 | tf_op jit(solution)/shard_map/ppermute | solution.py:221
  35.1 13.7 %collective-permute-start.7 = (bf16[128,4096]{1,0:T(8,128)(2,1)S(1)}, bf16[128,4096]{1,0:T(8,128)(2,1)S(1)}, u32[]{:S(2)}, u32[]{:S(2)}) collective-permute-start(bf16[128,4096]{1,0:T(8,128)(2,1)S(1)} %shard_map.92.first), channel_id=1, source_target_pairs={{0,1},{1,0},{2,3},{3,2},{4,5},{5,4},{6,7},{7,6},{8,9},{9,8},{10,11... | collective-permute-start | bytes 3145736 | tf_op jit(solution)/shard_map/ppermute | solution.py:224
  36.3 12.5 %collective-permute-start.9 = (bf16[288,256]{1,0:T(8,128)(2,1)S(1)}, bf16[288,256]{1,0:T(8,128)(2,1)S(1)}, u32[]{:S(2)}, u32[]{:S(2)}) collective-permute-start(bf16[288,256]{1,0:T(8,128)(2,1)S(1)} %slice.85), channel_id=1, source_target_pairs={{4,0},{8,4},{12,8},{14,12},{10,14},{6,10},{2,6},{0,2},{5,1},{9,5},... | collective-permute-start | bytes 442376 | tf_op jit(solution)/shard_map/ppermute | solution.py:221
  37.6 18.5 %collective-permute-start.11 = (bf16[128,1024]{1,0:T(8,128)(2,1)}, bf16[128,1024]{1,0:T(8,128)(2,1)S(1)}, u32[]{:S(2)}, u32[]{:S(2)}) collective-permute-start(bf16[128,1024]{1,0:T(8,128)(2,1)} %constant_dynamic-slice_fusion), channel_id=1, source_target_pairs={{0,4},{4,8},{8,12},{12,14},{14,10},{10,6},{6,2},{2,0},{1,5},{5,9},... | collective-permute-start | bytes 786440 | tf_op jit(solution)/shard_map/ppermute | solution.py:218
  39.1 16.9 %collective-permute-start.12 = (bf16[128,1024]{1,0:T(8,128)(2,1)}, bf16[128,1024]{1,0:T(8,128)(2,1)S(1)}, u32[]{:S(2)}, u32[]{:S(2)}) collective-permute-start(bf16[128,1024]{1,0:T(8,128)(2,1)} %constant_dynamic-slice_fusion), channel_id=1, source_target_pairs={{4,0},{8,4},{12,8},{14,12},{10,14},{6,10},{2,6},{0,2},{5,1},{9,5},... | collective-permute-start | bytes 786440 | tf_op jit(solution)/shard_map/ppermute | solution.py:221
  40.5 8.3 %collective-permute-start.8 = (bf16[256,256]{1,0:T(8,128)(2,1)S(1)}, bf16[256,256]{1,0:T(8,128)(2,1)S(1)}, u32[]{:S(2)}, u32[]{:S(2)}) collective-permute-start(bf16[256,256]{1,0:T(8,128)(2,1)S(1)} %slice.84), channel_id=1, source_target_pairs={{0,4},{4,8},{8,12},{12,14},{14,10},{10,6},{6,2},{2,0},{1,5},{5,9},... | collective-permute-start | bytes 393224 | tf_op jit(solution)/shard_map/ppermute | solution.py:218
  55.4 7.7 %collective-permute-start.10 = (bf16[256,256]{1,0:T(8,128)(2,1)}, bf16[256,256]{1,0:T(8,128)(2,1)S(1)}, u32[]{:S(2)}, u32[]{:S(2)}) collective-permute-start(bf16[256,256]{1,0:T(8,128)(2,1)} %shard_map.93), channel_id=1, source_target_pairs={{0,16},{16,0},{1,17},{17,1},{2,18},{18,2},{3,19},{19,3},{4,20},{20... | collective-permute-start | bytes 393224 | tf_op jit(solution)/shard_map/ppermute | solution.py:227
  56.1 10.1 %collective-permute-start.20 = (bf16[128,1024]{1,0:T(8,128)(2,1)S(1)}, bf16[128,1024]{1,0:T(8,128)(2,1)S(1)}, u32[]{:S(2)}, u32[]{:S(2)}) collective-permute-start(bf16[128,1024]{1,0:T(8,128)(2,1)S(1)} %collective-permute-done.11.rest_1_), channel_id=1, source_target_pairs={{0,4},{4,8},{8,12},{12,14},{14,10},{10,6},{6,2},{2,0},{1,5},{5,9},... | collective-permute-start | bytes 786440 | tf_op jit(solution)/shard_map/ppermute | solution.py:218
  57.7 10.0 %collective-permute-start.21 = (bf16[128,1024]{1,0:T(8,128)(2,1)S(1)}, bf16[128,1024]{1,0:T(8,128)(2,1)}, u32[]{:S(2)}, u32[]{:S(2)}) collective-permute-start(bf16[128,1024]{1,0:T(8,128)(2,1)S(1)} %collective-permute-done.12.rest_2_), channel_id=1, source_target_pairs={{4,0},{8,4},{12,8},{14,12},{10,14},{6,10},{2,6},{0,2},{5,1},{9,5},... | collective-permute-start | bytes 786440 | tf_op jit(solution)/shard_map/ppermute | solution.py:221
  64.1 6.6 %collective-permute-start.15 = (bf16[256,512]{1,0:T(8,128)(2,1)S(1)}, bf16[256,512]{1,0:T(8,128)(2,1)S(1)}, u32[]{:S(2)}, u32[]{:S(2)}) collective-permute-start(bf16[256,512]{1,0:T(8,128)(2,1)S(1)} %pad_maximum_fusion.refs_0_), channel_id=1, source_target_pairs={{0,4},{4,8},{8,12},{12,14},{14,10},{10,6},{6,2},{2,0},{1,5},{5,9},... | collective-permute-start | bytes 786440 | tf_op jit(solution)/shard_map/ppermute | solution.py:218
  65.7 6.4 %collective-permute-start.16 = (bf16[256,512]{1,0:T(8,128)(2,1)S(1)}, bf16[256,512]{1,0:T(8,128)(2,1)S(1)}, u32[]{:S(2)}, u32[]{:S(2)}) collective-permute-start(bf16[256,512]{1,0:T(8,128)(2,1)S(1)} %pad_maximum_fusion.refs_0_), channel_id=1, source_target_pairs={{4,0},{8,4},{12,8},{14,12},{10,14},{6,10},{2,6},{0,2},{5,1},{9,5},... | collective-permute-start | bytes 786440 | tf_op jit(solution)/shard_map/ppermute | solution.py:221
  66.2 13.4 %collective-permute-start.26 = (bf16[128,1024]{1,0:T(8,128)(2,1)S(1)}, bf16[128,1024]{1,0:T(8,128)(2,1)S(1)}, u32[]{:S(2)}, u32[]{:S(2)}) collective-permute-start(bf16[128,1024]{1,0:T(8,128)(2,1)S(1)} %collective-permute-done.11.rest_1_), channel_id=1, source_target_pairs={{0,16},{16,0},{1,17},{17,1},{2,18},{18,2},{3,19},{19,3},{4,20},{20... | collective-permute-start | bytes 786440 | tf_op jit(solution)/shard_map/ppermute | solution.py:227
  67.7 12.8 %collective-permute-start.27 = (bf16[128,1024]{1,0:T(8,128)(2,1)S(1)}, bf16[128,1024]{1,0:T(8,128)(2,1)S(1)}, u32[]{:S(2)}, u32[]{:S(2)}) collective-permute-start(bf16[128,1024]{1,0:T(8,128)(2,1)S(1)} %collective-permute-done.12.rest_2_), channel_id=1, source_target_pairs={{0,16},{16,0},{1,17},{17,1},{2,18},{18,2},{3,19},{19,3},{4,20},{20... | collective-permute-start | bytes 786440 | tf_op jit(solution)/shard_map/ppermute | solution.py:227
  77.5 6.4 %collective-permute-start.22 = (bf16[256,512]{1,0:T(8,128)(2,1)S(1)}, bf16[256,512]{1,0:T(8,128)(2,1)S(1)}, u32[]{:S(2)}, u32[]{:S(2)}) collective-permute-start(bf16[256,512]{1,0:T(8,128)(2,1)S(1)} %collective-permute-done.15.refs_0_), channel_id=1, source_target_pairs={{0,4},{4,8},{8,12},{12,14},{14,10},{10,6},{6,2},{2,0},{1,5},{5,9},... | collective-permute-start | bytes 786440 | tf_op jit(solution)/shard_map/ppermute | solution.py:218
  79.0 6.6 %collective-permute-start.23 = (bf16[256,512]{1,0:T(8,128)(2,1)S(1)}, bf16[256,512]{1,0:T(8,128)(2,1)S(1)}, u32[]{:S(2)}, u32[]{:S(2)}) collective-permute-start(bf16[256,512]{1,0:T(8,128)(2,1)S(1)} %collective-permute-done.16.refs_1_), channel_id=1, source_target_pairs={{4,0},{8,4},{12,8},{14,12},{10,14},{6,10},{2,6},{0,2},{5,1},{9,5},... | collective-permute-start | bytes 786440 | tf_op jit(solution)/shard_map/ppermute | solution.py:221
  79.5 8.2 %collective-permute-start.17 = (bf16[256,512]{1,0:T(8,128)(2,1)S(1)}, bf16[256,512]{1,0:T(8,128)(2,1)S(1)}, u32[]{:S(2)}, u32[]{:S(2)}) collective-permute-start(bf16[256,512]{1,0:T(8,128)(2,1)S(1)} %collective-permute-done.15.refs_0_), channel_id=1, source_target_pairs={{0,1},{1,0},{2,3},{3,2},{4,5},{5,4},{6,7},{7,6},{8,9},{9,8},{10,11... | collective-permute-start | bytes 786440 | tf_op jit(solution)/shard_map/ppermute | solution.py:224
  79.5 8.1 %collective-permute-start.18 = (bf16[256,512]{1,0:T(8,128)(2,1)S(1)}, bf16[256,512]{1,0:T(8,128)(2,1)S(1)}, u32[]{:S(2)}, u32[]{:S(2)}) collective-permute-start(bf16[256,512]{1,0:T(8,128)(2,1)S(1)} %collective-permute-done.16.refs_1_), channel_id=1, source_target_pairs={{0,1},{1,0},{2,3},{3,2},{4,5},{5,4},{6,7},{7,6},{8,9},{9,8},{10,11... | collective-permute-start | bytes 786440 | tf_op jit(solution)/shard_map/ppermute | solution.py:224
  85.7 7.7 %collective-permute-start.28 = (bf16[256,512]{1,0:T(8,128)(2,1)S(1)}, bf16[256,512]{1,0:T(8,128)(2,1)S(1)}, u32[]{:S(2)}, u32[]{:S(2)}) collective-permute-start(bf16[256,512]{1,0:T(8,128)(2,1)S(1)} %collective-permute-done.22.refs_0_), channel_id=1, source_target_pairs={{0,4},{4,8},{8,12},{12,14},{14,10},{10,6},{6,2},{2,0},{1,5},{5,9},... | collective-permute-start | bytes 786440 | tf_op jit(solution)/shard_map/ppermute | solution.py:218
  87.6 7.8 %collective-permute-start.29 = (bf16[256,512]{1,0:T(8,128)(2,1)S(1)}, bf16[256,512]{1,0:T(8,128)(2,1)S(1)}, u32[]{:S(2)}, u32[]{:S(2)}) collective-permute-start(bf16[256,512]{1,0:T(8,128)(2,1)S(1)} %collective-permute-done.23.refs_1_), channel_id=1, source_target_pairs={{4,0},{8,4},{12,8},{14,12},{10,14},{6,10},{2,6},{0,2},{5,1},{9,5},... | collective-permute-start | bytes 786440 | tf_op jit(solution)/shard_map/ppermute | solution.py:221
  101.0 9.2 %collective-permute-start.41 = (bf16[128,1024]{1,0:T(8,128)(2,1)S(1)}, bf16[128,1024]{1,0:T(8,128)(2,1)S(1)}, u32[]{:S(2)}, u32[]{:S(2)}) collective-permute-start(bf16[128,1024]{1,0:T(8,128)(2,1)S(1)} %collective-permute-done.20.rest_3_), channel_id=1, source_target_pairs={{0,16},{16,0},{1,17},{17,1},{2,18},{18,2},{3,19},{19,3},{4,20},{20... | collective-permute-start | bytes 786440 | tf_op jit(solution)/shard_map/ppermute | solution.py:227
  102.5 12.3 %collective-permute-start.42 = (bf16[128,1024]{1,0:T(8,128)(2,1)}, bf16[128,1024]{1,0:T(8,128)(2,1)S(1)}, u32[]{:S(2)}, u32[]{:S(2)}) collective-permute-start(bf16[128,1024]{1,0:T(8,128)(2,1)} %collective-permute-done.21.rest_4_), channel_id=1, source_target_pairs={{0,16},{16,0},{1,17},{17,1},{2,18},{18,2},{3,19},{19,3},{4,20},{20... | collective-permute-start | bytes 786440 | tf_op jit(solution)/shard_map/ppermute | solution.py:227
  103.0 12.5 %collective-permute-start.30 = (bf16[256,512]{1,0:T(8,128)(2,1)S(1)}, bf16[256,512]{1,0:T(8,128)(2,1)S(1)}, u32[]{:S(2)}, u32[]{:S(2)}) collective-permute-start(bf16[256,512]{1,0:T(8,128)(2,1)S(1)} %collective-permute-done.28.refs_0_), channel_id=1, source_target_pairs={{0,1},{1,0},{2,3},{3,2},{4,5},{5,4},{6,7},{7,6},{8,9},{9,8},{10,11... | collective-permute-start | bytes 786440 | tf_op jit(solution)/shard_map/ppermute | solution.py:224
  103.0 11.8 %collective-permute-start.39 = (bf16[128,1024]{1,0:T(8,128)(2,1)S(1)}, bf16[128,1024]{1,0:T(8,128)(2,1)S(1)}, u32[]{:S(2)}, u32[]{:S(2)}) collective-permute-start(bf16[128,1024]{1,0:T(8,128)(2,1)S(1)} %collective-permute-done.20.rest_3_), channel_id=1, source_target_pairs={{0,4},{4,8},{8,12},{12,14},{14,10},{10,6},{6,2},{2,0},{1,5},{5,9},... | collective-permute-start | bytes 786440 | tf_op jit(solution)/shard_map/ppermute | solution.py:218
  105.0 10.3 %collective-permute-start.40 = (bf16[128,1024]{1,0:T(8,128)(2,1)}, bf16[128,1024]{1,0:T(8,128)(2,1)S(1)}, u32[]{:S(2)}, u32[]{:S(2)}) collective-permute-start(bf16[128,1024]{1,0:T(8,128)(2,1)} %collective-permute-done.21.rest_4_), channel_id=1, source_target_pairs={{4,0},{8,4},{12,8},{14,12},{10,14},{6,10},{2,6},{0,2},{5,1},{9,5},... | collective-permute-start | bytes 786440 | tf_op jit(solution)/shard_map/ppermute | solution.py:221
  110.2 7.5 %collective-permute-start.31 = (bf16[256,512]{1,0:T(8,128)(2,1)S(1)}, bf16[256,512]{1,0:T(8,128)(2,1)S(1)}, u32[]{:S(2)}, u32[]{:S(2)}) collective-permute-start(bf16[256,512]{1,0:T(8,128)(2,1)S(1)} %collective-permute-done.29.refs_1_), channel_id=1, source_target_pairs={{0,1},{1,0},{2,3},{3,2},{4,5},{5,4},{6,7},{7,6},{8,9},{9,8},{10,11... | collective-permute-start | bytes 786440 | tf_op jit(solution)/shard_map/ppermute | solution.py:224
  114.8 15.6 %collective-permute-start.24 = (bf16[256,512]{1,0:T(8,128)(2,1)S(1)}, bf16[256,512]{1,0:T(8,128)(2,1)S(1)}, u32[]{:S(2)}, u32[]{:S(2)}) collective-permute-start(bf16[256,512]{1,0:T(8,128)(2,1)S(1)} %collective-permute-done.22.refs_0_), channel_id=1, source_target_pairs={{0,1},{1,0},{2,3},{3,2},{4,5},{5,4},{6,7},{7,6},{8,9},{9,8},{10,11... | collective-permute-start | bytes 786440 | tf_op jit(solution)/shard_map/ppermute | solution.py:224
  115.3 15.1 %collective-permute-start.25 = (bf16[256,512]{1,0:T(8,128)(2,1)S(1)}, bf16[256,512]{1,0:T(8,128)(2,1)S(1)}, u32[]{:S(2)}, u32[]{:S(2)}) collective-permute-start(bf16[256,512]{1,0:T(8,128)(2,1)S(1)} %collective-permute-done.23.refs_1_), channel_id=1, source_target_pairs={{0,1},{1,0},{2,3},{3,2},{4,5},{5,4},{6,7},{7,6},{8,9},{9,8},{10,11... | collective-permute-start | bytes 786440 | tf_op jit(solution)/shard_map/ppermute | solution.py:224
  115.5 6.9 %collective-permute-start.45 = (bf16[64,1024]{1,0:T(8,128)(2,1)S(1)}, bf16[64,1024]{1,0:T(8,128)(2,1)S(1)}, u32[]{:S(2)}, u32[]{:S(2)}) collective-permute-start(bf16[64,1024]{1,0:T(8,128)(2,1)S(1)} %slice.102), channel_id=1, source_target_pairs={{0,4},{4,8},{8,12},{12,14},{14,10},{10,6},{6,2},{2,0},{1,5},{5,9},... | collective-permute-start | bytes 393224 | tf_op jit(solution)/shard_map/ppermute | solution.py:218
  117.7 6.5 %collective-permute-start.46 = (bf16[64,1024]{1,0:T(8,128)(2,1)S(1)}, bf16[64,1024]{1,0:T(8,128)(2,1)S(1)}, u32[]{:S(2)}, u32[]{:S(2)}) collective-permute-start(bf16[64,1024]{1,0:T(8,128)(2,1)S(1)} %slice.103), channel_id=1, source_target_pairs={{4,0},{8,4},{12,8},{14,12},{10,14},{6,10},{2,6},{0,2},{5,1},{9,5},... | collective-permute-start | bytes 393224 | tf_op jit(solution)/shard_map/ppermute | solution.py:221
  122.0 8.4 %collective-permute-start.37 = (bf16[512,512]{1,0:T(8,128)(2,1)S(1)}, bf16[512,512]{1,0:T(8,128)(2,1)S(1)}, u32[]{:S(2)}, u32[]{:S(2)}) collective-permute-start(bf16[512,512]{1,0:T(8,128)(2,1)S(1)} %get-tuple-element.151), channel_id=1, source_target_pairs={{0,1},{1,0},{2,3},{3,2},{4,5},{5,4},{6,7},{7,6},{8,9},{9,8},{10,11... | collective-permute-start | bytes 1572872 | tf_op jit(solution)/shard_map/ppermute | solution.py:224
  122.4 6.0 %collective-permute-start.43 = (bf16[128,512]{1,0:T(8,128)(2,1)S(1)}, bf16[128,512]{1,0:T(8,128)(2,1)S(1)}, u32[]{:S(2)}, u32[]{:S(2)}) collective-permute-start(bf16[128,512]{1,0:T(8,128)(2,1)S(1)} %get-tuple-element.194), channel_id=1, source_target_pairs={{0,4},{4,8},{8,12},{12,14},{14,10},{10,6},{6,2},{2,0},{1,5},{5,9},... | collective-permute-start | bytes 393224 | tf_op jit(solution)/shard_map/ppermute | solution.py:218
  128.4 9.2 %collective-permute-start.49 = (bf16[128,1024]{1,0:T(8,128)(2,1)S(1)}, bf16[128,1024]{1,0:T(8,128)(2,1)S(1)}, u32[]{:S(2)}, u32[]{:S(2)}) collective-permute-start(bf16[128,1024]{1,0:T(8,128)(2,1)S(1)} %collective-permute-done.39.rest_5_), channel_id=1, source_target_pairs={{0,16},{16,0},{1,17},{17,1},{2,18},{18,2},{3,19},{19,3},{4,20},{20... | collective-permute-start | bytes 786440 | tf_op jit(solution)/shard_map/ppermute | solution.py:227
  129.9 12.1 %collective-permute-start.50 = (bf16[128,1024]{1,0:T(8,128)(2,1)S(1)}, bf16[128,1024]{1,0:T(8,128)(2,1)S(1)}, u32[]{:S(2)}, u32[]{:S(2)}) collective-permute-start(bf16[128,1024]{1,0:T(8,128)(2,1)S(1)} %collective-permute-done.40.rest_6_), channel_id=1, source_target_pairs={{0,16},{16,0},{1,17},{17,1},{2,18},{18,2},{3,19},{19,3},{4,20},{20... | collective-permute-start | bytes 786440 | tf_op jit(solution)/shard_map/ppermute | solution.py:227
  134.7 10.6 %collective-permute-start.38 = (bf16[512,512]{1,0:T(8,128)(2,1)S(1)}, bf16[512,512]{1,0:T(8,128)(2,1)S(1)}, u32[]{:S(2)}, u32[]{:S(2)}) collective-permute-start(bf16[512,512]{1,0:T(8,128)(2,1)S(1)} %get-tuple-element.155), channel_id=1, source_target_pairs={{0,1},{1,0},{2,3},{3,2},{4,5},{5,4},{6,7},{7,6},{8,9},{9,8},{10,11... | collective-permute-start | bytes 1572872 | tf_op jit(solution)/shard_map/ppermute | solution.py:224
  135.1 8.8 %collective-permute-start.47 = (bf16[256,512]{1,0:T(8,128)(2,1)S(1)}, bf16[256,512]{1,0:T(8,128)(2,1)S(1)}, u32[]{:S(2)}, u32[]{:S(2)}) collective-permute-start(bf16[256,512]{1,0:T(8,128)(2,1)S(1)} %pad_maximum_fusion.1), channel_id=1, source_target_pairs={{0,4},{4,8},{8,12},{12,14},{14,10},{10,6},{6,2},{2,0},{1,5},{5,9},... | collective-permute-start | bytes 786440 | tf_op jit(solution)/shard_map/ppermute | solution.py:218
  136.8 8.4 %collective-permute-start.48 = (bf16[256,512]{1,0:T(8,128)(2,1)S(1)}, bf16[256,512]{1,0:T(8,128)(2,1)S(1)}, u32[]{:S(2)}, u32[]{:S(2)}) collective-permute-start(bf16[256,512]{1,0:T(8,128)(2,1)S(1)} %pad_maximum_fusion.2), channel_id=1, source_target_pairs={{4,0},{8,4},{12,8},{14,12},{10,14},{6,10},{2,6},{0,2},{5,1},{9,5},... | collective-permute-start | bytes 786440 | tf_op jit(solution)/shard_map/ppermute | solution.py:221
  137.6 17.0 %collective-permute-start.19 = (bf16[512,512]{1,0:T(8,128)(2,1)S(1)}, bf16[512,512]{1,0:T(8,128)(2,1)S(1)}, u32[]{:S(2)}, u32[]{:S(2)}) collective-permute-start(bf16[512,512]{1,0:T(8,128)(2,1)S(1)} %get-tuple-element.127), channel_id=1, source_target_pairs={{0,1},{1,0},{2,3},{3,2},{4,5},{5,4},{6,7},{7,6},{8,9},{9,8},{10,11... | collective-permute-start | bytes 1572872 | tf_op jit(solution)/shard_map/ppermute | solution.py:224
  145.5 9.1 %collective-permute-start.51 = (bf16[256,512]{1,0:T(8,128)(2,1)S(1)}, bf16[256,512]{1,0:T(8,128)(2,1)S(1)}, u32[]{:S(2)}, u32[]{:S(2)}) collective-permute-start(bf16[256,512]{1,0:T(8,128)(2,1)S(1)} %get-tuple-element.177), channel_id=1, source_target_pairs={{0,4},{4,8},{8,12},{12,14},{14,10},{10,6},{6,2},{2,0},{1,5},{5,9},... | collective-permute-start | bytes 786440 | tf_op jit(solution)/shard_map/ppermute | solution.py:218
  145.9 8.7 %collective-permute-start.52 = (bf16[256,512]{1,0:T(8,128)(2,1)S(1)}, bf16[256,512]{1,0:T(8,128)(2,1)S(1)}, u32[]{:S(2)}, u32[]{:S(2)}) collective-permute-start(bf16[256,512]{1,0:T(8,128)(2,1)S(1)} %get-tuple-element.178), channel_id=1, source_target_pairs={{4,0},{8,4},{12,8},{14,12},{10,14},{6,10},{2,6},{0,2},{5,1},{9,5},... | collective-permute-start | bytes 786440 | tf_op jit(solution)/shard_map/ppermute | solution.py:221
  147.8 6.8 %collective-permute-start.54 = (bf16[64,1024]{1,0:T(8,128)(2,1)S(1)}, bf16[64,1024]{1,0:T(8,128)(2,1)S(1)}, u32[]{:S(2)}, u32[]{:S(2)}) collective-permute-start(bf16[64,1024]{1,0:T(8,128)(2,1)S(1)} %collective-permute-done.46.rest_8_), channel_id=1, source_target_pairs={{0,16},{16,0},{1,17},{17,1},{2,18},{18,2},{3,19},{19,3},{4,20},{20... | collective-permute-start | bytes 393224 | tf_op jit(solution)/shard_map/ppermute | solution.py:227
  154.9 6.4 %collective-permute-start.55 = (bf16[256,512]{1,0:T(8,128)(2,1)S(1)}, bf16[256,512]{1,0:T(8,128)(2,1)S(1)}, u32[]{:S(2)}, u32[]{:S(2)}) collective-permute-start(bf16[256,512]{1,0:T(8,128)(2,1)S(1)} %get-tuple-element.183), channel_id=1, source_target_pairs={{0,4},{4,8},{8,12},{12,14},{14,10},{10,6},{6,2},{2,0},{1,5},{5,9},... | collective-permute-start | bytes 786440 | tf_op jit(solution)/shard_map/ppermute | solution.py:218
  155.5 6.4 %collective-permute-start.56 = (bf16[256,512]{1,0:T(8,128)(2,1)S(1)}, bf16[256,512]{1,0:T(8,128)(2,1)S(1)}, u32[]{:S(2)}, u32[]{:S(2)}) collective-permute-start(bf16[256,512]{1,0:T(8,128)(2,1)S(1)} %get-tuple-element.184), channel_id=1, source_target_pairs={{4,0},{8,4},{12,8},{14,12},{10,14},{6,10},{2,6},{0,2},{5,1},{9,5},... | collective-permute-start | bytes 786440 | tf_op jit(solution)/shard_map/ppermute | solution.py:221
  (46 other events, 474.0 us)

commit v3 on v2

v3 whole, which is shorter than its diff:
```python
import functools

import jax
import jax.numpy as jnp
from jax import lax
from jax.experimental import pallas as pl
from jax.experimental.pallas import tpu as pltpu
from jax.sharding import PartitionSpec as P

F32, BF16 = jnp.float32, jnp.bfloat16
VMEM = pl.BlockSpec(memory_space=pltpu.VMEM)
SMEM = pl.BlockSpec(memory_space=pltpu.SMEM)
ANY = pl.BlockSpec(memory_space=pl.ANY)
LIMIT, BIG = 20 * 2**20, 20 * 2**20


def kernel_call(body, out, n_in, flops, nbytes, scratch=(), n_any=0, limit=LIMIT):
    return pl.pallas_call(
        body,
        out_shape=out,
        in_specs=[SMEM] + [VMEM] * (n_in - 1) + [ANY] * n_any,
        out_specs=jax.tree.map(lambda _: VMEM, out),
        scratch_shapes=list(scratch),
        compiler_params=pltpu.CompilerParams(vmem_limit_bytes=limit),
        cost_estimate=pl.CostEstimate(
            flops=flops, bytes_accessed=nbytes, transcendentals=0
        ),
    )


def norm_body(info, tokens, gain, out):
    rows, model = tokens.shape
    step = 16

    @pl.loop(0, rows // step)
    def _(i):
        at = pl.ds(pl.multiple_of(i * step, step), step)
        x = tokens[at, :].astype(F32)
        mean = jnp.sum(x * x, axis=1, keepdims=True) * (1.0 / model)
        x = tokens[at, :].astype(F32) * lax.rsqrt(mean + 1e-05) * gain[...]
        out[at, :] = x.astype(BF16)


def fetch(sources, places, done):
    copies = [
        pltpu.make_async_copy(a, b, done.at[i])
        for i, (a, b) in enumerate(zip(sources, places))
    ]
    for copy in copies:
        copy.start()

    def arrived(i):
        copies[i].wait()
        return places[i]

    return arrived


def places_for(arrays):
    return [pltpu.VMEM(a.shape, a.dtype) for a in arrays] + [
        pltpu.SemaphoreType.DMA((len(arrays),))
    ]


def start_body(wide, info, ids, weights, tokens, w_in, raw, block, done):
    rows, depth, quarter = raw.shape[0], w_in.shape[0], block.shape[1]
    columns = pl.ds(pl.multiple_of(info[1] * quarter, quarter), quarter)
    parts = done.shape[0] // 2
    copies = []
    for i in range(parts):
        size = rows // parts
        at = pl.ds(pl.multiple_of(info[0] * rows + i * size, size), size)
        to = raw.at[pl.ds(i * size, size), :]
        copies.append(pltpu.make_async_copy(tokens.at[at, :], to, done.at[i]))
        at = pl.ds(i * (depth // parts), depth // parts)
        copies.append(
            pltpu.make_async_copy(w_in.at[at, columns], block.at[at, :], done.at[parts + i])
        )
    for copy in copies:
        copy.start()
    number = lax.broadcasted_iota(jnp.int32, (wide, ids.shape[1]), 0)
    dense = jnp.zeros(number.shape, F32)
    for k in range(ids.shape[0]):
        dense += jnp.where(ids[k : k + 1, :] == number, weights[k : k + 1, :], 0.0)
    terms = []
    for _ in range(3):
        terms.append(dense.astype(BF16).astype(F32))
        dense = dense - terms[-1]
    empty = block.shape[0] - depth - 3 * wide
    if empty:
        terms.append(jnp.zeros((empty, ids.shape[1]), F32))
    block[depth:, :] = jnp.concatenate(terms, axis=0).astype(BF16)
    for copy in copies:
        copy.wait()


def pack_body(info, first, second, out, done):
    size = first.shape[0]
    places = [out.at[pl.ds(0, size), :], out.at[pl.ds(size, second.shape[0]), :]]
    arrived = fetch([first, second], places, done)
    arrived(0), arrived(1)


def near_body(depth, n, info, *refs):
    lefts, rest = refs[:n], refs[n:]
    count = (len(rest) - 3) // 2
    blocks, out, columns = rest[:count], rest[count], rest[count + 1]
    places, done = rest[count + 2 : -1], rest[-1]
    arrived = fetch(blocks, places, done)
    total = None
    for i in range(count):
        at = pl.ds(pl.multiple_of(info[2 + i] * depth, depth), depth)
        left = jnp.concatenate([a[:, at] for a in lefts], axis=0)
        term = jnp.dot(left, arrived(i)[:depth, :], preferred_element_type=F32)
        total = term if total is None else total + term
    out[...] = total
    at = pl.ds(pl.multiple_of(info[2 + count] * depth, depth), depth)
    columns[...] = jnp.concatenate([a[:, at] for a in lefts], axis=0)


def far_body(depth, info, partial, left, low, high, out):
    right = jnp.concatenate([low[: depth // 2, :], high[: depth // 2, :]], axis=0)
    total = jnp.dot(left[...], right, preferred_element_type=F32) + partial[...]
    total = total.astype(BF16)
    core, half = info[0], total.shape[0] // 2
    out[pl.ds(pl.multiple_of(core * half, half), half), :] = total[:half]
    out[pl.ds(pl.multiple_of((1 - core) * half, half), half), :] = total[half:]


def mine_body(depth, wide, first, info, normed, *refs):
    refs, (out, gates) = list(refs[:-2]), refs[-2:]
    total = lines = None
    if first:
        total, lines = refs.pop()[...], refs.pop()[...]
    other = refs.pop() if first == wide - 1 else None
    extra = -(-3 * wide // 16) * 16
    number = lax.broadcasted_iota(jnp.int32, (extra, refs[0].shape[1]), 0)
    chosen = (number % wide == info[1]) & (number < 3 * wide)
    i = first
    while refs:
        block = refs.pop(0)
        if i < wide - 1:
            right, carried = block[:depth, :], block[depth:, :]
        else:
            high = refs.pop(0)
            right = [block[...], high[: depth // 2, :]]
            right, carried = jnp.concatenate(right, axis=0), high[depth // 2 :, :]
        at = pl.ds(pl.multiple_of(info[2 + i] * depth, depth), depth)
        term = jnp.dot(normed[:, at], right, preferred_element_type=F32)
        total = term if total is None else total + term
        line = jnp.where(chosen, carried.astype(F32), 0.0)
        line = jnp.sum(line, axis=0, keepdims=True)
        lines = line if lines is None else jnp.concatenate([lines, line], axis=0)
        i += 1
    if other is None:
        out[...] = total
        gates[...] = lines
        return
    size = total.shape[1]
    side = info[2 + wide]
    out[:, pl.ds(pl.multiple_of(side * size, size), size)] = total.astype(BF16)
    out[:, pl.ds(pl.multiple_of((1 - side) * size, size), size)] = other[...]
    gates[...] = lines.T


def expert_body(columns, info, *refs):
    n = len(columns)
    own, other = refs[:n], refs[n : 2 * n]
    gates, up, down, stay, give, x, total = refs[2 * n :]
    core = info[0]
    half = own[0].shape[1]
    here = pl.ds(pl.multiple_of(core * half, half), half)
    there = pl.ds(pl.multiple_of((1 - core) * half, half), half)
    begin = 0
    for a, b in zip(own, other):
        size = a.shape[0]
        x[begin : begin + size, here] = a[...]
        x[begin : begin + size, there] = b[...]
        begin += size
    hidden = up.shape[0]
    chunk = max(c for c in range(16, 513, 16) if hidden % c == 0)
    for i in range(hidden // chunk):
        at = slice(i * chunk, (i + 1) * chunk)
        h = lax.dot_general(
            x[...], up[at, :], (((1,), (1,)), ((), ())), preferred_element_type=F32
        )
        h = jnp.square(jnp.maximum(h, 0.0)).astype(BF16)
        part = jnp.dot(h, down[at, :], preferred_element_type=F32)
        if i == 0:
            total[...] = part
        else:
            total[...] += part
    begin = 0
    for j, (column, first) in enumerate(columns):
        size = own[j].shape[0]
        gate = gates[first : first + size, column : column + 1]
        rows = slice(begin, begin + size)
        stay[rows, :] = (total[rows, here] * gate).astype(BF16)
        give[rows, :] = (total[rows, there] * gate).astype(BF16)
        begin += size


def final_body(depth, info, kept, mine, back, *rest):
    *blocks, out, mixture, full, done = rest
    core, side, me = info[0], info[1], info[2]
    count = (len(blocks) - 1) * 2 // 3
    pairs = [(b, b.shape[0] // 2) for b in blocks[1 + count :]]
    blocks = blocks[: 1 + count] + [
        b.at[pl.ds(i * size, size), :] for b, size in pairs for i in range(2)
    ]
    span = blocks[1].shape[1]
    places = [full.at[pl.ds(pl.multiple_of(me * depth, depth), depth), :]]
    for number in range(2):
        at = pl.ds(pl.multiple_of((side + number) % 2 * span, span), span)
        for i in range(count):
            size = blocks[1 + i].shape[0]
            begin = info[2 + min(1 + i, count - 1)] * depth
            if i == count - 1:
                begin = begin + size
            places.append(full.at[pl.ds(pl.multiple_of(begin, size), size), at])
    arrived = fetch(blocks, places, done)
    half = mine.shape[1]
    mixture[:, pl.ds(pl.multiple_of(core * half, half), half)] = mine[...]
    mixture[:, pl.ds(pl.multiple_of((1 - core) * half, half), half)] = back[...]
    for i in range(len(blocks)):
        arrived(i)
    step = 512
    for i in range(full.shape[1] // step):
        at = slice(i * step, (i + 1) * step)
        branch = jnp.dot(mixture[...], full[:, at], preferred_element_type=F32)
        out[:, at] = (kept[:, at].astype(F32) + branch).astype(BF16)


def after(x, *others):
    return lax.optimization_barrier((x, others))[0]


def both(*xs):
    return lax.optimization_barrier(xs)


def ring_order(mesh):
    wide = mesh.shape["wide"]
    line = mesh.devices.reshape(-1, wide, mesh.shape["narrow"])[0, :, 0]
    places = [tuple(getattr(d, "coords", (0,))) for d in line]
    spread = [len(set(c)) for c in zip(*places)]
    if sum(s > 1 for s in spread) == 2 and wide % 2 == 0:
        return list(range(0, wide, 2)) + list(range(wide - 1, 0, -2))
    return list(range(wide))


def make_local(order):
    wide = len(order)
    far = wide // 2
    up_perm = [(order[i], order[(i + 1) % wide]) for i in range(wide)]
    down_perm = [(order[(i + 1) % wide], order[i]) for i in range(wide)]
    offsets = [0] + [s * d for d in range(1, far) for s in (-1, 1)] + [far]
    sources = [[order[(order.index(i) + o) % wide] for o in offsets] for i in range(wide)]

    def local(tokens, norm_gain, w_in, w_out, w_up, w_down, expert_ids, gate_weights):
        groups = lax.axis_size("groups")
        side = lax.axis_index("groups") % 2
        me = lax.axis_index("wide")
        core = lax.axis_index("narrow")
        rows, model = tokens.shape
        half_rows = rows // 2
        depth, width = w_in.shape
        half, quarter = width // 2, width // 4
        info = jnp.concatenate(
            [
                jnp.stack([core, me]),
                jnp.asarray(sources, jnp.int32)[me],
                side.reshape(1),
            ]
        ).astype(jnp.int32)

        def up(x):
            return lax.ppermute(x, "wide", up_perm)

        def down(x):
            return lax.ppermute(x, "wide", down_perm)

        def swap(x):
            return lax.ppermute(x, "narrow", [(0, 1), (1, 0)])

        def across(x):
            return lax.ppermute(x, "groups", [(i, i ^ 1) for i in range(groups)])

        def shape(*dims, kind=BF16):
            return jax.ShapeDtypeStruct(dims, kind)

        columns = w_out.shape[1]
        out_half = lax.dynamic_slice_in_dim(
            w_out, side * (columns // 2), columns // 2, 1
        )
        out_depth = w_out.shape[0]
        out_blocks = []
        out_below = out_above = out_half

        def out_step(*others, beside=()):
            nonlocal out_below, out_above
            out_below, out_above = after((out_below, out_above), *others)
            if len(out_blocks) == 2 * far - 2:
                cut = out_depth // 2
                out_below, out_above = out_below[:cut], out_above[cut:]
            moved = both(up(out_below), down(out_above), *beside)
            out_below, out_above = moved[:2]
            out_blocks.extend([out_below, out_above])

        handed = []

        packs = []

        def pack(*others):
            pair = out_blocks[2 * len(packs) :][:2]
            out = shape(2 * pair[0].shape[0], pair[0].shape[1])
            one = kernel_call(
                pack_body,
                out,
                1,
                out.size,
                4 * out.size,
                [pltpu.SemaphoreType.DMA((2,))],
                2,
            )(after(info, *others), *pair)
            packs.append(one)
            return [one]

        def hand(*others):
            handed.append(across(after(packs[len(handed)], *others)))

        out_step()

        extra = -(-3 * wide // 16) * 16
        raw, block = pl.pallas_call(
            functools.partial(start_body, wide),
            out_shape=(shape(half_rows, model), shape(depth + extra, quarter)),
            in_specs=[SMEM, VMEM, VMEM, ANY, ANY],
            out_specs=(VMEM, VMEM),
            scratch_shapes=[pltpu.SemaphoreType.DMA((8,))],
        )(
            jnp.stack([core, core * 2 + side]).astype(jnp.int32),
            expert_ids.T,
            gate_weights.T,
            tokens,
            w_in,
        )
        block = after(block, *out_blocks)

        def norm(x, *others):
            return kernel_call(
                norm_body,
                shape(*x.shape),
                3,
                8 * x.size,
                4 * x.size,
            )(after(info, *others), x, norm_gain.reshape(1, model))

        def step(below, above, *beside):
            return both(up(below), down(above), *beside)[:2]

        first = across(raw)
        flops = 2 * rows * model * quarter
        nbytes = 2 * (rows * model + model * quarter)

        def near(*lefts):
            return kernel_call(
                functools.partial(near_body, depth, len(lefts)),
                (shape(rows, quarter, kind=F32), shape(rows, depth)),
                1 + len(lefts),
                flops,
                nbytes,
                places_for(blocks),
                len(blocks),
                BIG,
            )(info, *lefts, *blocks)

        def mine(first, part, *before, others=()):
            last = first + len(part) > wide
            outs = shape(rows, half) if last else shape(rows, quarter, kind=F32)
            number = min(first + len(part), wide)
            lines = shape(rows, wide, kind=F32) if last else shape(number, rows, kind=F32)
            return kernel_call(
                functools.partial(mine_body, depth, wide, first),
                (outs, lines),
                2 + len(part) + len(before),
                flops * len(part) // wide,
                nbytes * len(part) // wide,
            )(after(info, *others), normed, *part, *before)

        blocks = [block]
        below = above = block
        lat_mine = []
        for d in range(1, far):
            beside = []
            if d == 1:
                normed = norm(tokens, block)
                beside = [normed]
            else:
                begin = 0 if d == 2 else 2 * d - 3
                lat_mine = mine(begin, blocks[begin:], *lat_mine[::-1])
                beside = [*lat_mine]
            if d == 2:
                kept = lax.dynamic_slice_in_dim(
                    after(tokens, below), core * columns, columns, 1
                )
                beside += [kept, *pack(below)]
            elif d == 3:
                first = norm(first, below)
                beside += [first]
            below, above = step(below, above, *beside)
            blocks += [below, above]
        second = swap(after(first, below))
        near_there = near(first, second)
        begin = len(blocks) - 2
        lat_mine = mine(begin, blocks[begin:], *lat_mine[::-1])
        ends = step(below[: depth // 2], above[depth // 2 :], *near_there, *lat_mine)

        lat_there = kernel_call(
            functools.partial(far_body, depth),
            shape(rows, quarter),
            5,
            flops // wide,
            nbytes // wide,
        )(info, *near_there, *ends)
        lat_other = across(lat_there)
        out_step(lat_there)
        latent, gates = mine(len(blocks), ends, lat_other, *lat_mine[::-1])
        up_weight, down_weight = w_up[0].T, w_down[0]
        hidden = up_weight.shape[0]

        def expert(xs, columns, *others, swapped=None):
            size = sum(x.shape[0] for x in xs)
            out = shape(size, half)
            ys = swapped or [swap(x) for x in xs]
            return kernel_call(
                functools.partial(expert_body, columns),
                (out, out),
                4 + 2 * len(xs),
                4 * size * width * hidden,
                4 * hidden * width + 4 * size * width,
                [pltpu.VMEM((size, width), BF16), pltpu.VMEM((size, width), F32)],
            )(after(info, *others), *xs, *ys, gates, up_weight, down_weight)

        def total(stay, given, more=None):
            t = stay.astype(F32) + given.astype(F32)
            return t if more is None else t + more.astype(F32)

        done = {}
        pairs = [(latent, latent)]
        for d in range(1, far + 1):
            below, above = pairs[-1]
            beside = []
            if d == 1:
                swapped = swap(latent)
                beside = [*out_blocks, swapped]
                hand(latent)
            elif d == 2:
                beside = [*pack(below), *handed]
                hand()
            elif d == 3:
                done[1] = expert(pairs[1], [(1, 0), (2, 0)], below)
                beside = [*done[1], *handed]
            if d == far:
                done[d - 1] = expert(pairs[d - 1], [(2 * d - 3, 0), (2 * d - 2, 0)])
                beside = [*done[d - 1]]
                below, above = below[:half_rows], above[half_rows:]
            pairs.append(step(below, above, *beside))
        below, above = pairs[far]
        done[far] = expert([below, above], [(wide - 1, 0), (wide - 1, half_rows)])

        given = swap(done[far][1])
        back = total(done[far][0], given).astype(BF16)
        out_step(*pairs[far])
        back = after(back, *out_blocks)
        done[far - 2] = expert(
            pairs[far - 2], [(2 * far - 5, 0), (2 * far - 4, 0)], back
        )
        beside = [*done[far - 2], *pack(back)]
        out_step(back)
        to_above, to_below = step(
            back[:half_rows], back[half_rows:], *beside, *out_blocks
        )
        for d in range(far - 1, 0, -1):
            given = swap(done[d][1])
            below = total(done[d][0][:rows], given[:rows])
            above = total(done[d][0][rows:], given[rows:])
            if d == far - 1:
                above = jnp.concatenate(
                    [above[:half_rows] + to_above.astype(F32), above[half_rows:]], axis=0
                )
                below = jnp.concatenate(
                    [below[:half_rows], below[half_rows:] + to_below.astype(F32)], axis=0
                )
            else:
                above, below = above + to_above.astype(F32), below + to_below.astype(F32)
            above, below = above.astype(BF16), below.astype(BF16)
            beside = []
            if d > 1 and d - 1 not in done:
                done[d - 1] = expert(
                    pairs[d - 1], [(2 * d - 3, 0), (2 * d - 2, 0)], to_above, to_below
                )
                beside += done[d - 1]
            if d == 2:
                done[0] = expert(
                    [latent], [(0, 0)], to_above, to_below, swapped=[swapped]
                )
                beside += done[0]
            if d == 1:
                given0 = swap(done[0][1])
                beside += [given0]
            if len(out_blocks) < 2 * far:
                out_step(to_above, to_below)
                beside += out_blocks
            if len(packs) < far:
                beside += pack(to_above)
            beside += handed[2:]
            if len(handed) < far:
                hand(to_above)
            to_above, to_below = step(above, below, *beside)
        mixture = total(done[0][0], given0, to_above)
        mixture = (mixture + to_below.astype(F32)).astype(BF16)
        return kernel_call(
            functools.partial(final_body, out_depth),
            shape(rows, columns),
            4,
            2 * rows * width * columns,
            2 * width * columns + 4 * rows * columns,
            [
                pltpu.VMEM((rows, width), BF16),
                pltpu.VMEM((width, columns), BF16),
                pltpu.SemaphoreType.DMA((1 + 2 * len(out_blocks),)),
            ],
            1 + len(out_blocks) + len(handed),
            BIG,
        )(
            info.at[1].set(side.astype(jnp.int32)),
            kept,
            mixture,
            swap(mixture),
            w_out,
            *out_blocks,
            *handed,
        )

    return local


def solution(mesh):
    in_specs = (
        P(("groups", "wide"), None),
        P(),
        P("wide", None),
        P("wide", "narrow"),
        P("wide", None, "narrow"),
        P("wide", "narrow", None),
        P(("groups", "wide"), None),
        P(("groups", "wide"), None),
    )
    out_specs = P(("groups", "wide"), "narrow")
    local = make_local(ring_order(mesh))
    return jax.shard_map(
        local, mesh=mesh, in_specs=in_specs, out_specs=out_specs, check_vma=False
    )
```

time: 171 us -> 138 us (0.81)
  waiting for transfers between devices: 67 us -> 46.2 us
  local copies, waits for them, and re-layouts: 14.6 us -> 6.88 us
  starting transfers between devices: 47.1 us -> 43.6 us
    ppermute x16, waiting for transfers between devices: 37.9 us -> 20.6 us  [up(): return lax.ppermute(x, 'wide', up_perm)]
    ppermute x10 -> x6, waiting for transfers between devices: 17.3 us -> 12 us  [across(): return lax.ppermute(x, 'groups', [(i, i ^ 1) for i in range(groups)])]
    ppermute x10 -> x6, starting transfers between devices: 11.7 us -> 7.16 us  [across(): return lax.ppermute(x, 'groups', [(i, i ^ 1) for i in range(groups)])]
    dynamic_slice x2 -> x1, local copies, waits for them, and re-layouts: 3.45 us -> 0.07 us  [local(): lax.dynamic_slice_in_dim(after(tokens, below), core * columns, columns, 1)]
    unnamed x73 -> x26, local copies, waits for them, and re-layouts: 7.65 us -> 5 us
    pallas_call x2 -> x11, Pallas kernels: 9.82 us -> 12.3 us  [the longest x4 3.39 us: mine(): kernel_call(functools.partial(mine_body, depth, wide, first), (outs, line...]
    pallas_call x1, Pallas kernels: 5.86 us -> 3.41 us  [local(): kernel_call(functools.partial(final_body, out_depth), shape(rows, columns...]
    slice x3, local copies, waits for them, and re-layouts: 2.03 us -> 0.04 us  [the longest x2 0.02 us: local(): ends = step(below[:depth // 2], above[depth // 2:], *near_there, *lat_mine)]
  transfers between devices with their start and end apart: 58 -> 54, of which waited for: 27 -> 30; matrix products, arithmetic and copies ran while one was open for 4% -> 2% of each run, Pallas kernels for 18% -> 25%
where the time goes in v3:
time: 138 us
  waiting for transfers between devices  46.2 us (33%)
  starting transfers between devices  43.6 us (32%)
  Pallas kernels  39 us (28%)
  local copies, waits for them, and re-layouts  6.88 us (5%)
  other arithmetic  1.6 us (1%)
    ppermute x16, starting transfers between devices, up(): return lax.ppermute(x, 'wide', up_perm)  22.6 us
    ppermute x16, waiting for transfers between devices, up(): return lax.ppermute(x, 'wide', up_perm)  20.6 us
    pallas_call x5, Pallas kernels, expert(): kernel_call(functools.partial(expert_body, columns), (out, out), 4 + 2 *...  18 us
    ppermute x16, waiting for transfers between devices, down(): return lax.ppermute(x, 'wide', down_perm)  12.1 us
    ppermute x6, waiting for transfers between devices, across(): return lax.ppermute(x, 'groups', [(i, i ^ 1) for i in range(groups)])  12 us
    ppermute x16, starting transfers between devices, down(): return lax.ppermute(x, 'wide', down_perm)  11.4 us
    ppermute x6, starting transfers between devices, across(): return lax.ppermute(x, 'groups', [(i, i ^ 1) for i in range(groups)])  7.16 us
    pallas_call x2, Pallas kernels, norm(): kernel_call(norm_body, shape(*x.shape), 3, 8 * x.size, 4 * x.size)  5.32 us
  transfers between devices with their start and end apart: 54, of which 30 were waited for; matrix products, arithmetic and copies ran while one was open for 2% of the time, Pallas kernels for 25%

profile of v3, /device:TPU:0, one launch (start us, length us, event | category | flops | bytes accessed | tf_op | source)
XLA Modules:
  0.0 138.0 jit_solution(4847907080992967084)
XLA Ops:
  1.0 3.1 %collective-permute-start = (bf16[128,1024]{1,0:T(8,128)(2,1)S(1)}, bf16[128,1024]{1,0:T(8,128)(2,1)S(1)}, u32[]{:S(2)}, u32[]{:S(2)}) collective-permute-start(bf16[128,1024]{1,0:T(8,128)(2,1)S(1)} %constant_dynamic-slice_fusion.1), channel_id=1, source_target_pairs={{0,4},{4,8},{8,12},{12,14},{14,10},{10,6},{6,2},{2,0},{1,5},{5,9},... | collective-permute-start | bytes 786440 | tf_op jit(solution)/shard_map/ppermute | solution.py:278
  4.7 3.1 %shard_map.91 = (bf16[128,4096]{1,0:T(8,128)(2,1)}, bf16[544,256]{1,0:T(8,128)(2,1)}) custom-call(s32[2]{0:T(128)} %pad_add_fusion.1.info, s32[4,256]{1,0:T(4,128)} %bitcast.25, f32[4,256]{1,0:T(4,128)} %bitcast.26, bf16[256,4096]{1,0:T(8,128)(2,1)} %tokens.3, bf16[512,1024]{1,0:T(8,128)(2,1)} %w_in.1), custom_call_target="tpu_custom_call" | custom-call | tf_op jit(solution)/shard_map/pallas_call | solution.py:335
  7.8 2.0 %collective-permute-start.8 = (bf16[128,4096]{1,0:T(8,128)(2,1)}, bf16[128,4096]{1,0:T(8,128)(2,1)}, u32[]{:S(2)}, u32[]{:S(2)}) collective-permute-start(bf16[128,4096]{1,0:T(8,128)(2,1)} %get-tuple-element.112), channel_id=1, source_target_pairs={{0,16},{16,0},{1,17},{17,1},{2,18},{18,2},{3,19},{19,3},{4,20},{20... | collective-permute-start | bytes 3145736 | tf_op jit(solution)/shard_map/ppermute | solution.py:287
  12.6 1.6 %collective-permute-start.2 = (bf16[544,256]{1,0:T(8,128)(2,1)}, bf16[544,256]{1,0:T(8,128)(2,1)S(1)}, u32[]{:S(2)}, u32[]{:S(2)}) collective-permute-start(bf16[544,256]{1,0:T(8,128)(2,1)} %get-tuple-element.99.refs_0_.refs_2_), channel_id=1, source_target_pairs={{0,4},{4,8},{8,12},{12,14},{14,10},{10,6},{6,2},{2,0},{1,5},{5,9},... | collective-permute-start | bytes 835592 | tf_op jit(solution)/shard_map/ppermute | solution.py:278
  15.4 1.6 %copy-done = bf16[256,4096]{1,0:T(8,128)(2,1)S(1)} copy-done((bf16[256,4096]{1,0:T(8,128)(2,1)S(1)}, bf16[256,4096]{1,0:T(8,128)(2,1)}, u32[]{:S(2)}) %copy-start) | copy-done | bytes 2097176
  16.9 2.9 %shard_map.92.normed = bf16[256,4096]{1,0:T(8,128)(2,1)S(1)} custom-call(s32[11]{0:T(128)S(1)} %pad_add_fusion.info, bf16[256,4096]{1,0:T(8,128)(2,1)S(1)} %copy-done, f32[1,4096]{1,0:T(1,128)S(1)} %bitcast.23), custom_call_target="tpu_custom_call" | custom-call | flops 8388608 | bytes 4194304 | tf_op jit(solution)/shard_map/pallas_call | solution.py:351
  20.0 1.3 collective-permute-done.3.refs_2_.refs_4_
  21.3 1.6 %collective-permute-start.4 = (bf16[544,256]{1,0:T(8,128)(2,1)S(1)}, bf16[544,256]{1,0:T(8,128)(2,1)S(1)}, u32[]{:S(2)}, u32[]{:S(2)}) collective-permute-start(bf16[544,256]{1,0:T(8,128)(2,1)S(1)} %collective-permute-done.2.refs_1_.refs_3_), channel_id=1, source_target_pairs={{0,4},{4,8},{8,12},{12,14},{14,10},{10,6},{6,2},{2,0},{1,5},{5,9},... | collective-permute-start | bytes 835592 | tf_op jit(solution)/shard_map/ppermute | solution.py:278
  27.8 1.6 %collective-permute-done.5.refs_1_.refs_6_ = bf16[544,256]{1,0:T(8,128)(2,1)S(1)} collective-permute-done((bf16[544,256]{1,0:T(8,128)(2,1)S(1)}, bf16[544,256]{1,0:T(8,128)(2,1)S(1)}, u32[]{:S(2)}, u32[]{:S(2)}) %collective-permute-start.5) | collective-permute-done | bytes 278560 | tf_op jit(solution)/shard_map/ppermute | solution.py:281
  29.4 1.5 %collective-permute-start.6 = (bf16[544,256]{1,0:T(8,128)(2,1)S(1)}, bf16[544,256]{1,0:T(8,128)(2,1)S(1)}, u32[]{:S(2)}, u32[]{:S(2)}) collective-permute-start(bf16[544,256]{1,0:T(8,128)(2,1)S(1)} %collective-permute-done.4.refs_0_.refs_5_), channel_id=1, source_target_pairs={{0,4},{4,8},{8,12},{12,14},{14,10},{10,6},{6,2},{2,0},{1,5},{5,9},... | collective-permute-start | bytes 835592 | tf_op jit(solution)/shard_map/ppermute | solution.py:278
  32.8 2.4 %shard_map.96.refs_0_ = bf16[128,4096]{1,0:T(8,128)(2,1)S(1)} custom-call(s32[11]{0:T(128)S(1)} %pad_add_fusion.info, bf16[128,4096]{1,0:T(8,128)(2,1)} %collective-permute-done.8.tokens, f32[1,4096]{1,0:T(1,128)S(1)} %bitcast.24), custom_call_target="tpu_custom_call" | custom-call | flops 4194304 | bytes 2097152 | tf_op jit(solution)/shard_map/pallas_call | solution.py:351
  35.9 1.5 %collective-permute-done.7.refs_8_.refs_1_ = bf16[544,256]{1,0:T(8,128)(2,1)S(1)} collective-permute-done((bf16[544,256]{1,0:T(8,128)(2,1)S(1)}, bf16[544,256]{1,0:T(8,128)(2,1)S(1)}, u32[]{:S(2)}, u32[]{:S(2)}) %collective-permute-start.7) | collective-permute-done | bytes 278560 | tf_op jit(solution)/shard_map/ppermute | solution.py:281
  38.1 1.6 %collective-permute-start.9 = (bf16[256,256]{1,0:T(8,128)(2,1)S(1)}, bf16[256,256]{1,0:T(8,128)(2,1)S(1)}, u32[]{:S(2)}, u32[]{:S(2)}) collective-permute-start(bf16[256,256]{1,0:T(8,128)(2,1)S(1)} %slice.84), channel_id=1, source_target_pairs={{0,4},{4,8},{8,12},{12,14},{14,10},{10,6},{6,2},{2,0},{1,5},{5,9},... | collective-permute-start | bytes 393224 | tf_op jit(solution)/shard_map/ppermute | solution.py:278
  40.5 2.4 %shard_map.97 = (f32[256,256]{1,0:T(8,128)S(1)}, bf16[256,512]{1,0:T(8,128)(2,1)S(1)}) custom-call(s32[11]{0:T(128)S(1)} %pad_add_fusion.info, bf16[128,4096]{1,0:T(8,128)(2,1)S(1)} %shard_map.96.refs_0_, bf16[128,4096]{1,0:T(8,128)(2,1)S(1)} %collective-permute-done.11.refs_1_, bf16[544,256]{1,0:T(8,128)(2,1)S(1)} %copy-done.5, ...), custom_call_target="tpu_custom_call" | custom-call | flops 536870912 | bytes 4194304 | tf_op jit(solution)/shard_map/pallas_call | solution.py:367
  44.6 1.6 %collective-permute-start.12 = (bf16[256,256]{1,0:T(8,128)(2,1)S(1)}, bf16[256,256]{1,0:T(8,128)(2,1)S(1)}, u32[]{:S(2)}, u32[]{:S(2)}) collective-permute-start(bf16[256,256]{1,0:T(8,128)(2,1)S(1)} %shard_map.99), channel_id=1, source_target_pairs={{0,16},{16,0},{1,17},{17,1},{2,18},{18,2},{3,19},{19,3},{4,20},{20... | collective-permute-start | bytes 393224 | tf_op jit(solution)/shard_map/ppermute | solution.py:287
  46.1 1.5 %collective-permute-start.15 = (bf16[128,1024]{1,0:T(8,128)(2,1)S(1)}, bf16[128,1024]{1,0:T(8,128)(2,1)S(1)}, u32[]{:S(2)}, u32[]{:S(2)}) collective-permute-start(bf16[128,1024]{1,0:T(8,128)(2,1)S(1)} %copy-done.8), channel_id=1, source_target_pairs={{0,4},{4,8},{8,12},{12,14},{14,10},{10,6},{6,2},{2,0},{1,5},{5,9},... | collective-permute-start | bytes 786440 | tf_op jit(solution)/shard_map/ppermute | solution.py:278
  48.2 1.6 %collective-permute-done.12.refs_2_ = bf16[256,256]{1,0:T(8,128)(2,1)S(1)} collective-permute-done((bf16[256,256]{1,0:T(8,128)(2,1)S(1)}, bf16[256,256]{1,0:T(8,128)(2,1)S(1)}, u32[]{:S(2)}, u32[]{:S(2)}) %collective-permute-start.12) | collective-permute-done | bytes 131104 | tf_op jit(solution)/shard_map/ppermute | solution.py:287
  50.5 1.6 %collective-permute-start.13 = (bf16[256,512]{1,0:T(8,128)(2,1)S(1)}, bf16[256,512]{1,0:T(8,128)(2,1)S(1)}, u32[]{:S(2)}, u32[]{:S(2)}) collective-permute-start(bf16[256,512]{1,0:T(8,128)(2,1)S(1)} %get-tuple-element.122.refs_0_), channel_id=1, source_target_pairs={{0,4},{4,8},{8,12},{12,14},{14,10},{10,6},{6,2},{2,0},{1,5},{5,9},... | collective-permute-start | bytes 786440 | tf_op jit(solution)/shard_map/ppermute | solution.py:278
  52.6 2.8 %collective-permute-done.15.first.rest_3_ = bf16[128,1024]{1,0:T(8,128)(2,1)S(1)} collective-permute-done((bf16[128,1024]{1,0:T(8,128)(2,1)S(1)}, bf16[128,1024]{1,0:T(8,128)(2,1)S(1)}, u32[]{:S(2)}, u32[]{:S(2)}) %collective-permute-start.15) | collective-permute-done | bytes 262176 | tf_op jit(solution)/shard_map/ppermute | solution.py:278
  55.4 1.3 collective-permute-done.16.second.rest_4_
  56.7 2.7 %collective-permute-done.13.refs_0_ = bf16[256,512]{1,0:T(8,128)(2,1)S(1)} collective-permute-done((bf16[256,512]{1,0:T(8,128)(2,1)S(1)}, bf16[256,512]{1,0:T(8,128)(2,1)S(1)}, u32[]{:S(2)}, u32[]{:S(2)}) %collective-permute-start.13) | collective-permute-done | bytes 262176 | tf_op jit(solution)/shard_map/ppermute | solution.py:278
  59.4 1.2 collective-permute-done.14.refs_1_
  60.7 1.2 collective-permute-start.18
  63.8 3.5 %collective-permute-done.18.refs_0_ = bf16[256,512]{1,0:T(8,128)(2,1)S(1)} collective-permute-done((bf16[256,512]{1,0:T(8,128)(2,1)S(1)}, bf16[256,512]{1,0:T(8,128)(2,1)S(1)}, u32[]{:S(2)}, u32[]{:S(2)}) %collective-permute-start.18) | collective-permute-done | bytes 262176 | tf_op jit(solution)/shard_map/ppermute | solution.py:278
  69.0 1.2 collective-permute-start.22
  70.2 4.2 %shard_map.102 = (bf16[512,512]{1,0:T(8,128)(2,1)S(1)}, bf16[512,512]{1,0:T(8,128)(2,1)S(1)}) custom-call(s32[11]{0:T(128)S(1)} %pad_add_fusion.info, bf16[256,512]{1,0:T(8,128)(2,1)S(1)} %collective-permute-done.13.refs_0_, bf16[256,512]{1,0:T(8,128)(2,1)S(1)} %collective-permute-done.14.refs_1_, bf16[256,512]{1,0:T(8,128)(2,1)S(1)} %collective-permute-done.23.refs_2_, ...), custom_call_target="tpu_custom_call" | custom-call | flops 2818572288 | bytes 7602176 | tf_op jit(solution)/shard_map/pallas_call | solution.py:436
  75.5 3.1 %collective-permute-done.25.rest_10_ = bf16[256,1024]{1,0:T(8,128)(2,1)S(1)} collective-permute-done((bf16[256,1024]{1,0:T(8,128)(2,1)S(1)}, bf16[256,1024]{1,0:T(8,128)(2,1)S(1)}, u32[]{:S(2)}, u32[]{:S(2)}) %collective-permute-start.25) | collective-permute-done | bytes 524320 | tf_op jit(solution)/shard_map/ppermute | solution.py:287
  79.2 1.2 collective-permute-start.29
  81.3 4.2 %shard_map.103 = (bf16[512,512]{1,0:T(8,128)(2,1)S(1)}, bf16[512,512]{1,0:T(8,128)(2,1)S(1)}) custom-call(s32[11]{0:T(128)S(1)} %pad_add_fusion.info, bf16[256,512]{1,0:T(8,128)(2,1)S(1)} %collective-permute-done.21.refs_0_, bf16[256,512]{1,0:T(8,128)(2,1)S(1)} %collective-permute-done.22.refs_1_, bf16[256,512]{1,0:T(8,128)(2,1)S(1)} %collective-permute-done.26.refs_2_, ...), custom_call_target="tpu_custom_call" | custom-call | flops 2818572288 | bytes 7602176 | tf_op jit(solution)/shard_map/pallas_call | solution.py:436
  86.1 1.2 collective-permute-start.34
  88.1 2.7 %shard_map.104 = (bf16[256,512]{1,0:T(8,128)(2,1)S(1)}, bf16[256,512]{1,0:T(8,128)(2,1)S(1)}) custom-call(s32[11]{0:T(128)S(1)} %pad_add_fusion.info, bf16[128,512]{1,0:T(8,128)(2,1)S(1)} %collective-permute-done.29.refs_0_, bf16[128,512]{1,0:T(8,128)(2,1)S(1)} %collective-permute-done.30.refs_1_, bf16[128,512]{1,0:T(8,128)(2,1)S(1)} %collective-permute-done.31.refs_2_, ...), custom_call_target="tpu_custom_call" | custom-call | flops 1409286144 | bytes 6553600 | tf_op jit(solution)/shard_map/pallas_call | solution.py:436
  91.5 2.9 %collective-permute-done.34.first.rest_5_ = bf16[128,1024]{1,0:T(8,128)(2,1)S(1)} collective-permute-done((bf16[128,1024]{1,0:T(8,128)(2,1)S(1)}, bf16[128,1024]{1,0:T(8,128)(2,1)S(1)}, u32[]{:S(2)}, u32[]{:S(2)}) %collective-permute-start.34) | collective-permute-done | bytes 262176 | tf_op jit(solution)/shard_map/ppermute | solution.py:278
  95.3 1.3 collective-permute-start.36
  98.0 1.3 collective-permute-start.40
  100.1 4.2 %shard_map.105 = (bf16[512,512]{1,0:T(8,128)(2,1)S(1)}, bf16[512,512]{1,0:T(8,128)(2,1)S(1)}) custom-call(s32[11]{0:T(128)S(1)} %pad_add_fusion.info, bf16[256,512]{1,0:T(8,128)(2,1)S(1)} %collective-permute-done.18.refs_0_, bf16[256,512]{1,0:T(8,128)(2,1)S(1)} %collective-permute-done.19.refs_1_, bf16[256,512]{1,0:T(8,128)(2,1)S(1)} %collective-permute-done.38.refs_2_, ...), custom_call_target="tpu_custom_call" | custom-call | flops 2818572288 | bytes 7602176 | tf_op jit(solution)/shard_map/pallas_call | solution.py:436
  104.7 1.3 collective-permute-start.42
  107.8 1.6 %collective-permute-start.49 = (bf16[256,1024]{1,0:T(8,128)(2,1)S(1)}, bf16[256,1024]{1,0:T(8,128)(2,1)S(1)}, u32[]{:S(2)}, u32[]{:S(2)}) collective-permute-start(bf16[256,1024]{1,0:T(8,128)(2,1)S(1)} %shard_map.106), channel_id=1, source_target_pairs={{0,16},{16,0},{1,17},{17,1},{2,18},{18,2},{3,19},{19,3},{4,20},{20... | collective-permute-start | bytes 1572872 | tf_op jit(solution)/shard_map/ppermute | solution.py:287
  109.4 4.1 %collective-permute-done.42 = bf16[256,512]{1,0:T(8,128)(2,1)S(1)} collective-permute-done((bf16[256,512]{1,0:T(8,128)(2,1)S(1)}, bf16[256,512]{1,0:T(8,128)(2,1)S(1)}, u32[]{:S(2)}, u32[]{:S(2)}) %collective-permute-start.42) | collective-permute-done | bytes 262176 | tf_op jit(solution)/shard_map/ppermute | solution.py:278
  113.5 1.1 collective-permute-done.43
  115.3 1.6 %collective-permute-start.48 = (bf16[256,512]{1,0:T(8,128)(2,1)S(1)}, bf16[256,512]{1,0:T(8,128)(2,1)S(1)}, u32[]{:S(2)}, u32[]{:S(2)}) collective-permute-start(bf16[256,512]{1,0:T(8,128)(2,1)S(1)} %get-tuple-element.173), channel_id=1, source_target_pairs={{4,0},{8,4},{12,8},{14,12},{10,14},{6,10},{2,6},{0,2},{5,1},{9,5},... | collective-permute-start | bytes 786440 | tf_op jit(solution)/shard_map/ppermute | solution.py:281
  116.9 2.7 %shard_map.108 = (bf16[256,512]{1,0:T(8,128)(2,1)S(1)}, bf16[256,512]{1,0:T(8,128)(2,1)S(1)}) custom-call(s32[11]{0:T(128)S(1)} %pad_add_fusion.info, bf16[256,512]{1,0:T(8,128)(2,1)S(1)} %get-tuple-element.122.refs_0_, bf16[256,512]{1,0:T(8,128)(2,1)S(1)} %collective-permute-done.17.refs_1_, f32[256,8]{1,0:T(8,128)S(1)} %get-tuple-element.134.refs_4_.refs_2_, ...), custom_call_target="tpu_custom_call" | custom-call | flops 1409286144 | bytes 6553600 | tf_op jit(solution)/shard_map/pallas_call | solution.py:436
  119.7 2.5 %collective-permute-done.49.rest_11_ = bf16[256,1024]{1,0:T(8,128)(2,1)S(1)} collective-permute-done((bf16[256,1024]{1,0:T(8,128)(2,1)S(1)}, bf16[256,1024]{1,0:T(8,128)(2,1)S(1)}, u32[]{:S(2)}, u32[]{:S(2)}) %collective-permute-start.49) | collective-permute-done | bytes 524320 | tf_op jit(solution)/shard_map/ppermute | solution.py:287
  122.2 1.5 %collective-permute-start.52 = (bf16[128,1024]{1,0:T(8,128)(2,1)S(1)}, bf16[128,1024]{1,0:T(8,128)(2,1)S(1)}, u32[]{:S(2)}, u32[]{:S(2)}) collective-permute-start(bf16[128,1024]{1,0:T(8,128)(2,1)S(1)} %shard_map.107), channel_id=1, source_target_pairs={{0,16},{16,0},{1,17},{17,1},{2,18},{18,2},{3,19},{19,3},{4,20},{20... | collective-permute-start | bytes 786440 | tf_op jit(solution)/shard_map/ppermute | solution.py:287
  124.0 1.3 collective-permute-start.50
  126.0 4.1 %collective-permute-done.52.rest_12_ = bf16[128,1024]{1,0:T(8,128)(2,1)S(1)} collective-permute-done((bf16[128,1024]{1,0:T(8,128)(2,1)S(1)}, bf16[128,1024]{1,0:T(8,128)(2,1)S(1)}, u32[]{:S(2)}, u32[]{:S(2)}) %collective-permute-start.52) | collective-permute-done | bytes 262176 | tf_op jit(solution)/shard_map/ppermute | solution.py:287
  130.2 1.5 %collective-permute-done.50 = bf16[256,512]{1,0:T(8,128)(2,1)S(1)} collective-permute-done((bf16[256,512]{1,0:T(8,128)(2,1)S(1)}, bf16[256,512]{1,0:T(8,128)(2,1)S(1)}, u32[]{:S(2)}, u32[]{:S(2)}) %collective-permute-start.50) | collective-permute-done | bytes 262176 | tf_op jit(solution)/shard_map/ppermute | solution.py:278
  132.9 1.5 %collective-permute-done.53.back = bf16[256,512]{1,0:T(8,128)(2,1)S(1)} collective-permute-done((bf16[256,512]{1,0:T(8,128)(2,1)S(1)}, bf16[256,512]{1,0:T(8,128)(2,1)S(1)}, u32[]{:S(2)}, u32[]{:S(2)}) %collective-permute-start.53) | collective-permute-done | bytes 262176 | tf_op jit(solution)/shard_map/ppermute | solution.py:284
  134.4 3.4 %shard_map.109 = bf16[256,2048]{1,0:T(8,128)(2,1)} custom-call(s32[11]{0:T(128)S(1)} %constant_dynamic-update-slice_fusion.info, bf16[256,2048]{1,0:T(8,128)(2,1)S(1)} %constant_dynamic-slice_fusion.kept, bf16[256,512]{1,0:T(8,128)(2,1)S(1)} %add_convert_fusion.mine, bf16[256,512]{1,0:T(8,128)(2,1)S(1)} %collective-permute-done.53.back, ...), custom_call_target="tpu_custom_call" | custom-call | flops 1073741824 | bytes 6291456 | tf_op jit(solution)/shard_map/pallas_call | solution.py:523
  (129 shorter events, 34.5 us)
Async XLA Ops:
  1.0 9.3 %collective-permute-start = (bf16[128,1024]{1,0:T(8,128)(2,1)S(1)}, bf16[128,1024]{1,0:T(8,128)(2,1)S(1)}, u32[]{:S(2)}, u32[]{:S(2)}) collective-permute-start(bf16[128,1024]{1,0:T(8,128)(2,1)S(1)} %constant_dynamic-slice_fusion.1), channel_id=1, source_target_pairs={{0,4},{4,8},{8,12},{12,14},{14,10},{10,6},{6,2},{2,0},{1,5},{5,9},... | collective-permute-start | bytes 786440 | tf_op jit(solution)/shard_map/ppermute | solution.py:278
  4.1 7.8 %collective-permute-start.1 = (bf16[128,1024]{1,0:T(8,128)(2,1)S(1)}, bf16[128,1024]{1,0:T(8,128)(2,1)S(1)}, u32[]{:S(2)}, u32[]{:S(2)}) collective-permute-start(bf16[128,1024]{1,0:T(8,128)(2,1)S(1)} %constant_dynamic-slice_fusion.1), channel_id=1, source_target_pairs={{4,0},{8,4},{12,8},{14,12},{10,14},{6,10},{2,6},{0,2},{5,1},{9,5},... | collective-permute-start | bytes 786440 | tf_op jit(solution)/shard_map/ppermute | solution.py:281
  7.8 25.0 %collective-permute-start.8 = (bf16[128,4096]{1,0:T(8,128)(2,1)}, bf16[128,4096]{1,0:T(8,128)(2,1)}, u32[]{:S(2)}, u32[]{:S(2)}) collective-permute-start(bf16[128,4096]{1,0:T(8,128)(2,1)} %get-tuple-element.112), channel_id=1, source_target_pairs={{0,16},{16,0},{1,17},{17,1},{2,18},{18,2},{3,19},{19,3},{4,20},{20... | collective-permute-start | bytes 3145736 | tf_op jit(solution)/shard_map/ppermute | solution.py:287
  12.6 7.4 %collective-permute-start.2 = (bf16[544,256]{1,0:T(8,128)(2,1)}, bf16[544,256]{1,0:T(8,128)(2,1)S(1)}, u32[]{:S(2)}, u32[]{:S(2)}) collective-permute-start(bf16[544,256]{1,0:T(8,128)(2,1)} %get-tuple-element.99.refs_0_.refs_2_), channel_id=1, source_target_pairs={{0,4},{4,8},{8,12},{12,14},{14,10},{10,6},{6,2},{2,0},{1,5},{5,9},... | collective-permute-start | bytes 835592 | tf_op jit(solution)/shard_map/ppermute | solution.py:278
  14.1 7.1 %collective-permute-start.3 = (bf16[544,256]{1,0:T(8,128)(2,1)}, bf16[544,256]{1,0:T(8,128)(2,1)S(1)}, u32[]{:S(2)}, u32[]{:S(2)}) collective-permute-start(bf16[544,256]{1,0:T(8,128)(2,1)} %get-tuple-element.99.refs_0_.refs_2_), channel_id=1, source_target_pairs={{4,0},{8,4},{12,8},{14,12},{10,14},{6,10},{2,6},{0,2},{5,1},{9,5},... | collective-permute-start | bytes 835592 | tf_op jit(solution)/shard_map/ppermute | solution.py:281
  21.3 6.5 %collective-permute-start.4 = (bf16[544,256]{1,0:T(8,128)(2,1)S(1)}, bf16[544,256]{1,0:T(8,128)(2,1)S(1)}, u32[]{:S(2)}, u32[]{:S(2)}) collective-permute-start(bf16[544,256]{1,0:T(8,128)(2,1)S(1)} %collective-permute-done.2.refs_1_.refs_3_), channel_id=1, source_target_pairs={{0,4},{4,8},{8,12},{12,14},{14,10},{10,6},{6,2},{2,0},{1,5},{5,9},... | collective-permute-start | bytes 835592 | tf_op jit(solution)/shard_map/ppermute | solution.py:278
  22.8 6.5 %collective-permute-start.5 = (bf16[544,256]{1,0:T(8,128)(2,1)S(1)}, bf16[544,256]{1,0:T(8,128)(2,1)S(1)}, u32[]{:S(2)}, u32[]{:S(2)}) collective-permute-start(bf16[544,256]{1,0:T(8,128)(2,1)S(1)} %collective-permute-done.3.refs_2_.refs_4_), channel_id=1, source_target_pairs={{4,0},{8,4},{12,8},{14,12},{10,14},{6,10},{2,6},{0,2},{5,1},{9,5},... | collective-permute-start | bytes 835592 | tf_op jit(solution)/shard_map/ppermute | solution.py:281
  29.4 6.5 %collective-permute-start.6 = (bf16[544,256]{1,0:T(8,128)(2,1)S(1)}, bf16[544,256]{1,0:T(8,128)(2,1)S(1)}, u32[]{:S(2)}, u32[]{:S(2)}) collective-permute-start(bf16[544,256]{1,0:T(8,128)(2,1)S(1)} %collective-permute-done.4.refs_0_.refs_5_), channel_id=1, source_target_pairs={{0,4},{4,8},{8,12},{12,14},{14,10},{10,6},{6,2},{2,0},{1,5},{5,9},... | collective-permute-start | bytes 835592 | tf_op jit(solution)/shard_map/ppermute | solution.py:278
  30.9 6.5 %collective-permute-start.7 = (bf16[544,256]{1,0:T(8,128)(2,1)S(1)}, bf16[544,256]{1,0:T(8,128)(2,1)S(1)}, u32[]{:S(2)}, u32[]{:S(2)}) collective-permute-start(bf16[544,256]{1,0:T(8,128)(2,1)S(1)} %collective-permute-done.5.refs_1_.refs_6_), channel_id=1, source_target_pairs={{4,0},{8,4},{12,8},{14,12},{10,14},{6,10},{2,6},{0,2},{5,1},{9,5},... | collective-permute-start | bytes 835592 | tf_op jit(solution)/shard_map/ppermute | solution.py:281
  37.5 6.3 %collective-permute-start.10 = (bf16[288,256]{1,0:T(8,128)(2,1)S(1)}, bf16[288,256]{1,0:T(8,128)(2,1)S(1)}, u32[]{:S(2)}, u32[]{:S(2)}) collective-permute-start(bf16[288,256]{1,0:T(8,128)(2,1)S(1)} %slice.85), channel_id=1, source_target_pairs={{4,0},{8,4},{12,8},{14,12},{10,14},{6,10},{2,6},{0,2},{5,1},{9,5},... | collective-permute-start | bytes 442376 | tf_op jit(solution)/shard_map/ppermute | solution.py:281
  38.1 5.7 %collective-permute-start.9 = (bf16[256,256]{1,0:T(8,128)(2,1)S(1)}, bf16[256,256]{1,0:T(8,128)(2,1)S(1)}, u32[]{:S(2)}, u32[]{:S(2)}) collective-permute-start(bf16[256,256]{1,0:T(8,128)(2,1)S(1)} %slice.84), channel_id=1, source_target_pairs={{0,4},{4,8},{8,12},{12,14},{14,10},{10,6},{6,2},{2,0},{1,5},{5,9},... | collective-permute-start | bytes 393224 | tf_op jit(solution)/shard_map/ppermute | solution.py:278
  44.6 5.2 %collective-permute-start.12 = (bf16[256,256]{1,0:T(8,128)(2,1)S(1)}, bf16[256,256]{1,0:T(8,128)(2,1)S(1)}, u32[]{:S(2)}, u32[]{:S(2)}) collective-permute-start(bf16[256,256]{1,0:T(8,128)(2,1)S(1)} %shard_map.99), channel_id=1, source_target_pairs={{0,16},{16,0},{1,17},{17,1},{2,18},{18,2},{3,19},{19,3},{4,20},{20... | collective-permute-start | bytes 393224 | tf_op jit(solution)/shard_map/ppermute | solution.py:287
  46.1 9.2 %collective-permute-start.15 = (bf16[128,1024]{1,0:T(8,128)(2,1)S(1)}, bf16[128,1024]{1,0:T(8,128)(2,1)S(1)}, u32[]{:S(2)}, u32[]{:S(2)}) collective-permute-start(bf16[128,1024]{1,0:T(8,128)(2,1)S(1)} %copy-done.8), channel_id=1, source_target_pairs={{0,4},{4,8},{8,12},{12,14},{14,10},{10,6},{6,2},{2,0},{1,5},{5,9},... | collective-permute-start | bytes 786440 | tf_op jit(solution)/shard_map/ppermute | solution.py:278
  47.7 9.1 %collective-permute-start.16 = (bf16[128,1024]{1,0:T(8,128)(2,1)S(1)}, bf16[128,1024]{1,0:T(8,128)(2,1)S(1)}, u32[]{:S(2)}, u32[]{:S(2)}) collective-permute-start(bf16[128,1024]{1,0:T(8,128)(2,1)S(1)} %copy-done.11), channel_id=1, source_target_pairs={{4,0},{8,4},{12,8},{14,12},{10,14},{6,10},{2,6},{0,2},{5,1},{9,5},... | collective-permute-start | bytes 786440 | tf_op jit(solution)/shard_map/ppermute | solution.py:281
  50.5 8.9 %collective-permute-start.13 = (bf16[256,512]{1,0:T(8,128)(2,1)S(1)}, bf16[256,512]{1,0:T(8,128)(2,1)S(1)}, u32[]{:S(2)}, u32[]{:S(2)}) collective-permute-start(bf16[256,512]{1,0:T(8,128)(2,1)S(1)} %get-tuple-element.122.refs_0_), channel_id=1, source_target_pairs={{0,4},{4,8},{8,12},{12,14},{14,10},{10,6},{6,2},{2,0},{1,5},{5,9},... | collective-permute-start | bytes 786440 | tf_op jit(solution)/shard_map/ppermute | solution.py:278
  52.1 8.5 %collective-permute-start.14 = (bf16[256,512]{1,0:T(8,128)(2,1)S(1)}, bf16[256,512]{1,0:T(8,128)(2,1)S(1)}, u32[]{:S(2)}, u32[]{:S(2)}) collective-permute-start(bf16[256,512]{1,0:T(8,128)(2,1)S(1)} %get-tuple-element.122.refs_0_), channel_id=1, source_target_pairs={{4,0},{8,4},{12,8},{14,12},{10,14},{6,10},{2,6},{0,2},{5,1},{9,5},... | collective-permute-start | bytes 786440 | tf_op jit(solution)/shard_map/ppermute | solution.py:281
  52.6 8.0 %collective-permute-start.17 = (bf16[256,512]{1,0:T(8,128)(2,1)S(1)}, bf16[256,512]{1,0:T(8,128)(2,1)S(1)}, u32[]{:S(2)}, u32[]{:S(2)}) collective-permute-start(bf16[256,512]{1,0:T(8,128)(2,1)S(1)} %get-tuple-element.122.refs_0_), channel_id=1, source_target_pairs={{0,1},{1,0},{2,3},{3,2},{4,5},{5,4},{6,7},{7,6},{8,9},{9,8},{10,11... | collective-permute-start | bytes 786440 | tf_op jit(solution)/shard_map/ppermute | solution.py:284
  55.4 12.8 %collective-permute-start.20 = (bf16[256,1024]{1,0:T(8,128)(2,1)S(1)}, bf16[256,1024]{1,0:T(8,128)(2,1)S(1)}, u32[]{:S(2)}, u32[]{:S(2)}) collective-permute-start(bf16[256,1024]{1,0:T(8,128)(2,1)S(1)} %shard_map.94), channel_id=1, source_target_pairs={{0,16},{16,0},{1,17},{17,1},{2,18},{18,2},{3,19},{19,3},{4,20},{20... | collective-permute-start | bytes 1572872 | tf_op jit(solution)/shard_map/ppermute | solution.py:287
  60.7 6.6 %collective-permute-start.18 = (bf16[256,512]{1,0:T(8,128)(2,1)S(1)}, bf16[256,512]{1,0:T(8,128)(2,1)S(1)}, u32[]{:S(2)}, u32[]{:S(2)}) collective-permute-start(bf16[256,512]{1,0:T(8,128)(2,1)S(1)} %collective-permute-done.13.refs_0_), channel_id=1, source_target_pairs={{0,4},{4,8},{8,12},{12,14},{14,10},{10,6},{6,2},{2,0},{1,5},{5,9},... | collective-permute-start | bytes 786440 | tf_op jit(solution)/shard_map/ppermute | solution.py:278
  61.8 6.4 %collective-permute-start.19 = (bf16[256,512]{1,0:T(8,128)(2,1)S(1)}, bf16[256,512]{1,0:T(8,128)(2,1)S(1)}, u32[]{:S(2)}, u32[]{:S(2)}) collective-permute-start(bf16[256,512]{1,0:T(8,128)(2,1)S(1)} %collective-permute-done.14.refs_1_), channel_id=1, source_target_pairs={{4,0},{8,4},{12,8},{14,12},{10,14},{6,10},{2,6},{0,2},{5,1},{9,5},... | collective-permute-start | bytes 786440 | tf_op jit(solution)/shard_map/ppermute | solution.py:281
  62.7 7.5 %collective-permute-start.23 = (bf16[256,512]{1,0:T(8,128)(2,1)S(1)}, bf16[256,512]{1,0:T(8,128)(2,1)S(1)}, u32[]{:S(2)}, u32[]{:S(2)}) collective-permute-start(bf16[256,512]{1,0:T(8,128)(2,1)S(1)} %collective-permute-done.13.refs_0_), channel_id=1, source_target_pairs={{0,1},{1,0},{2,3},{3,2},{4,5},{5,4},{6,7},{7,6},{8,9},{9,8},{10,11... | collective-permute-start | bytes 786440 | tf_op jit(solution)/shard_map/ppermute | solution.py:284
  62.7 7.5 %collective-permute-start.24 = (bf16[256,512]{1,0:T(8,128)(2,1)S(1)}, bf16[256,512]{1,0:T(8,128)(2,1)S(1)}, u32[]{:S(2)}, u32[]{:S(2)}) collective-permute-start(bf16[256,512]{1,0:T(8,128)(2,1)S(1)} %collective-permute-done.14.refs_1_), channel_id=1, source_target_pairs={{0,1},{1,0},{2,3},{3,2},{4,5},{5,4},{6,7},{7,6},{8,9},{9,8},{10,11... | collective-permute-start | bytes 786440 | tf_op jit(solution)/shard_map/ppermute | solution.py:284
  67.3 11.3 %collective-permute-start.25 = (bf16[256,1024]{1,0:T(8,128)(2,1)S(1)}, bf16[256,1024]{1,0:T(8,128)(2,1)S(1)}, u32[]{:S(2)}, u32[]{:S(2)}) collective-permute-start(bf16[256,1024]{1,0:T(8,128)(2,1)S(1)} %shard_map.101), channel_id=1, source_target_pairs={{0,16},{16,0},{1,17},{17,1},{2,18},{18,2},{3,19},{19,3},{4,20},{20... | collective-permute-start | bytes 1572872 | tf_op jit(solution)/shard_map/ppermute | solution.py:287
  68.2 6.4 %collective-permute-start.21 = (bf16[256,512]{1,0:T(8,128)(2,1)S(1)}, bf16[256,512]{1,0:T(8,128)(2,1)S(1)}, u32[]{:S(2)}, u32[]{:S(2)}) collective-permute-start(bf16[256,512]{1,0:T(8,128)(2,1)S(1)} %collective-permute-done.18.refs_0_), channel_id=1, source_target_pairs={{0,4},{4,8},{8,12},{12,14},{14,10},{10,6},{6,2},{2,0},{1,5},{5,9},... | collective-permute-start | bytes 786440 | tf_op jit(solution)/shard_map/ppermute | solution.py:278
  69.0 6.5 %collective-permute-start.22 = (bf16[256,512]{1,0:T(8,128)(2,1)S(1)}, bf16[256,512]{1,0:T(8,128)(2,1)S(1)}, u32[]{:S(2)}, u32[]{:S(2)}) collective-permute-start(bf16[256,512]{1,0:T(8,128)(2,1)S(1)} %collective-permute-done.19.refs_1_), channel_id=1, source_target_pairs={{4,0},{8,4},{12,8},{14,12},{10,14},{6,10},{2,6},{0,2},{5,1},{9,5},... | collective-permute-start | bytes 786440 | tf_op jit(solution)/shard_map/ppermute | solution.py:281
  79.2 6.3 %collective-permute-start.29 = (bf16[128,512]{1,0:T(8,128)(2,1)S(1)}, bf16[128,512]{1,0:T(8,128)(2,1)S(1)}, u32[]{:S(2)}, u32[]{:S(2)}) collective-permute-start(bf16[128,512]{1,0:T(8,128)(2,1)S(1)} %slice.89), channel_id=1, source_target_pairs={{0,4},{4,8},{8,12},{12,14},{14,10},{10,6},{6,2},{2,0},{1,5},{5,9},... | collective-permute-start | bytes 393224 | tf_op jit(solution)/shard_map/ppermute | solution.py:278
  80.3 5.1 %collective-permute-start.30 = (bf16[128,512]{1,0:T(8,128)(2,1)S(1)}, bf16[128,512]{1,0:T(8,128)(2,1)S(1)}, u32[]{:S(2)}, u32[]{:S(2)}) collective-permute-start(bf16[128,512]{1,0:T(8,128)(2,1)S(1)} %slice.90), channel_id=1, source_target_pairs={{4,0},{8,4},{12,8},{14,12},{10,14},{6,10},{2,6},{0,2},{5,1},{9,5},... | collective-permute-start | bytes 393224 | tf_op jit(solution)/shard_map/ppermute | solution.py:281
  86.1 8.3 %collective-permute-start.34 = (bf16[128,1024]{1,0:T(8,128)(2,1)S(1)}, bf16[128,1024]{1,0:T(8,128)(2,1)S(1)}, u32[]{:S(2)}, u32[]{:S(2)}) collective-permute-start(bf16[128,1024]{1,0:T(8,128)(2,1)S(1)} %collective-permute-done.15.first.rest_3_), channel_id=1, source_target_pairs={{0,4},{4,8},{8,12},{12,14},{14,10},{10,6},{6,2},{2,0},{1,5},{5,9},... | collective-permute-start | bytes 786440 | tf_op jit(solution)/shard_map/ppermute | solution.py:278
  87.3 7.9 %collective-permute-start.35 = (bf16[128,1024]{1,0:T(8,128)(2,1)S(1)}, bf16[128,1024]{1,0:T(8,128)(2,1)S(1)}, u32[]{:S(2)}, u32[]{:S(2)}) collective-permute-start(bf16[128,1024]{1,0:T(8,128)(2,1)S(1)} %collective-permute-done.16.second.rest_4_), channel_id=1, source_target_pairs={{4,0},{8,4},{12,8},{14,12},{10,14},{6,10},{2,6},{0,2},{5,1},{9,5},... | collective-permute-start | bytes 786440 | tf_op jit(solution)/shard_map/ppermute | solution.py:281
  90.8 4.4 %collective-permute-start.33 = (bf16[256,512]{1,0:T(8,128)(2,1)S(1)}, bf16[256,512]{1,0:T(8,128)(2,1)S(1)}, u32[]{:S(2)}, u32[]{:S(2)}) collective-permute-start(bf16[256,512]{1,0:T(8,128)(2,1)S(1)} %get-tuple-element.144), channel_id=1, source_target_pairs={{0,1},{1,0},{2,3},{3,2},{4,5},{5,4},{6,7},{7,6},{8,9},{9,8},{10,11... | collective-permute-start | bytes 786440 | tf_op jit(solution)/shard_map/ppermute | solution.py:284
  90.9 7.2 %collective-permute-start.38 = (bf16[256,512]{1,0:T(8,128)(2,1)S(1)}, bf16[256,512]{1,0:T(8,128)(2,1)S(1)}, u32[]{:S(2)}, u32[]{:S(2)}) collective-permute-start(bf16[256,512]{1,0:T(8,128)(2,1)S(1)} %collective-permute-done.18.refs_0_), channel_id=1, source_target_pairs={{0,1},{1,0},{2,3},{3,2},{4,5},{5,4},{6,7},{7,6},{8,9},{9,8},{10,11... | collective-permute-start | bytes 786440 | tf_op jit(solution)/shard_map/ppermute | solution.py:284
  91.4 8.0 %collective-permute-start.39 = (bf16[256,512]{1,0:T(8,128)(2,1)S(1)}, bf16[256,512]{1,0:T(8,128)(2,1)S(1)}, u32[]{:S(2)}, u32[]{:S(2)}) collective-permute-start(bf16[256,512]{1,0:T(8,128)(2,1)S(1)} %collective-permute-done.19.refs_1_), channel_id=1, source_target_pairs={{0,1},{1,0},{2,3},{3,2},{4,5},{5,4},{6,7},{7,6},{8,9},{9,8},{10,11... | collective-permute-start | bytes 786440 | tf_op jit(solution)/shard_map/ppermute | solution.py:284
  94.4 10.0 %collective-permute-start.28 = (bf16[512,512]{1,0:T(8,128)(2,1)S(1)}, bf16[512,512]{1,0:T(8,128)(2,1)S(1)}, u32[]{:S(2)}, u32[]{:S(2)}) collective-permute-start(bf16[512,512]{1,0:T(8,128)(2,1)S(1)} %get-tuple-element.140), channel_id=1, source_target_pairs={{0,1},{1,0},{2,3},{3,2},{4,5},{5,4},{6,7},{7,6},{8,9},{9,8},{10,11... | collective-permute-start | bytes 1572872 | tf_op jit(solution)/shard_map/ppermute | solution.py:284
  95.3 9.3 %collective-permute-start.36 = (bf16[128,512]{1,0:T(8,128)(2,1)S(1)}, bf16[128,512]{1,0:T(8,128)(2,1)S(1)}, u32[]{:S(2)}, u32[]{:S(2)}) collective-permute-start(bf16[128,512]{1,0:T(8,128)(2,1)S(1)} %get-tuple-element.178), channel_id=1, source_target_pairs={{0,4},{4,8},{8,12},{12,14},{14,10},{10,6},{6,2},{2,0},{1,5},{5,9},... | collective-permute-start | bytes 393224 | tf_op jit(solution)/shard_map/ppermute | solution.py:278
  96.6 8.0 %collective-permute-start.37 = (bf16[128,512]{1,0:T(8,128)(2,1)S(1)}, bf16[128,512]{1,0:T(8,128)(2,1)S(1)}, u32[]{:S(2)}, u32[]{:S(2)}) collective-permute-start(bf16[128,512]{1,0:T(8,128)(2,1)S(1)} %get-tuple-element.177), channel_id=1, source_target_pairs={{4,0},{8,4},{12,8},{14,12},{10,14},{6,10},{2,6},{0,2},{5,1},{9,5},... | collective-permute-start | bytes 393224 | tf_op jit(solution)/shard_map/ppermute | solution.py:281
  98.0 6.6 %collective-permute-start.40 = (bf16[64,1024]{1,0:T(8,128)(2,1)S(1)}, bf16[64,1024]{1,0:T(8,128)(2,1)S(1)}, u32[]{:S(2)}, u32[]{:S(2)}) collective-permute-start(bf16[64,1024]{1,0:T(8,128)(2,1)S(1)} %slice.93), channel_id=1, source_target_pairs={{0,4},{4,8},{8,12},{12,14},{14,10},{10,6},{6,2},{2,0},{1,5},{5,9},... | collective-permute-start | bytes 393224 | tf_op jit(solution)/shard_map/ppermute | solution.py:278
  99.4 5.3 %collective-permute-start.41 = (bf16[64,1024]{1,0:T(8,128)(2,1)S(1)}, bf16[64,1024]{1,0:T(8,128)(2,1)S(1)}, u32[]{:S(2)}, u32[]{:S(2)}) collective-permute-start(bf16[64,1024]{1,0:T(8,128)(2,1)S(1)} %slice.94), channel_id=1, source_target_pairs={{4,0},{8,4},{12,8},{14,12},{10,14},{6,10},{2,6},{0,2},{5,1},{9,5},... | collective-permute-start | bytes 393224 | tf_op jit(solution)/shard_map/ppermute | solution.py:281
  104.3 10.3 %collective-permute-start.46 = (bf16[512,512]{1,0:T(8,128)(2,1)S(1)}, bf16[512,512]{1,0:T(8,128)(2,1)S(1)}, u32[]{:S(2)}, u32[]{:S(2)}) collective-permute-start(bf16[512,512]{1,0:T(8,128)(2,1)S(1)} %get-tuple-element.152), channel_id=1, source_target_pairs={{0,1},{1,0},{2,3},{3,2},{4,5},{5,4},{6,7},{7,6},{8,9},{9,8},{10,11... | collective-permute-start | bytes 1572872 | tf_op jit(solution)/shard_map/ppermute | solution.py:284
  104.7 8.8 %collective-permute-start.42 = (bf16[256,512]{1,0:T(8,128)(2,1)S(1)}, bf16[256,512]{1,0:T(8,128)(2,1)S(1)}, u32[]{:S(2)}, u32[]{:S(2)}) collective-permute-start(bf16[256,512]{1,0:T(8,128)(2,1)S(1)} %pad_maximum_fusion), channel_id=1, source_target_pairs={{0,4},{4,8},{8,12},{12,14},{14,10},{10,6},{6,2},{2,0},{1,5},{5,9},... | collective-permute-start | bytes 786440 | tf_op jit(solution)/shard_map/ppermute | solution.py:278
  106.1 8.5 %collective-permute-start.43 = (bf16[256,512]{1,0:T(8,128)(2,1)S(1)}, bf16[256,512]{1,0:T(8,128)(2,1)S(1)}, u32[]{:S(2)}, u32[]{:S(2)}) collective-permute-start(bf16[256,512]{1,0:T(8,128)(2,1)S(1)} %pad_maximum_fusion.1), channel_id=1, source_target_pairs={{4,0},{8,4},{12,8},{14,12},{10,14},{6,10},{2,6},{0,2},{5,1},{9,5},... | collective-permute-start | bytes 786440 | tf_op jit(solution)/shard_map/ppermute | solution.py:281
  106.9 16.8 %collective-permute-start.45 = (bf16[512,512]{1,0:T(8,128)(2,1)S(1)}, bf16[512,512]{1,0:T(8,128)(2,1)S(1)}, u32[]{:S(2)}, u32[]{:S(2)}) collective-permute-start(bf16[512,512]{1,0:T(8,128)(2,1)S(1)} %get-tuple-element.136), channel_id=1, source_target_pairs={{0,1},{1,0},{2,3},{3,2},{4,5},{5,4},{6,7},{7,6},{8,9},{9,8},{10,11... | collective-permute-start | bytes 1572872 | tf_op jit(solution)/shard_map/ppermute | solution.py:284
  107.8 14.4 %collective-permute-start.49 = (bf16[256,1024]{1,0:T(8,128)(2,1)S(1)}, bf16[256,1024]{1,0:T(8,128)(2,1)S(1)}, u32[]{:S(2)}, u32[]{:S(2)}) collective-permute-start(bf16[256,1024]{1,0:T(8,128)(2,1)S(1)} %shard_map.106), channel_id=1, source_target_pairs={{0,16},{16,0},{1,17},{17,1},{2,18},{18,2},{3,19},{19,3},{4,20},{20... | collective-permute-start | bytes 1572872 | tf_op jit(solution)/shard_map/ppermute | solution.py:287
  114.8 8.9 %collective-permute-start.47 = (bf16[256,512]{1,0:T(8,128)(2,1)S(1)}, bf16[256,512]{1,0:T(8,128)(2,1)S(1)}, u32[]{:S(2)}, u32[]{:S(2)}) collective-permute-start(bf16[256,512]{1,0:T(8,128)(2,1)S(1)} %get-tuple-element.174), channel_id=1, source_target_pairs={{0,4},{4,8},{8,12},{12,14},{14,10},{10,6},{6,2},{2,0},{1,5},{5,9},... | collective-permute-start | bytes 786440 | tf_op jit(solution)/shard_map/ppermute | solution.py:278
  115.3 8.4 %collective-permute-start.48 = (bf16[256,512]{1,0:T(8,128)(2,1)S(1)}, bf16[256,512]{1,0:T(8,128)(2,1)S(1)}, u32[]{:S(2)}, u32[]{:S(2)}) collective-permute-start(bf16[256,512]{1,0:T(8,128)(2,1)S(1)} %get-tuple-element.173), channel_id=1, source_target_pairs={{4,0},{8,4},{12,8},{14,12},{10,14},{6,10},{2,6},{0,2},{5,1},{9,5},... | collective-permute-start | bytes 786440 | tf_op jit(solution)/shard_map/ppermute | solution.py:281
  119.6 6.4 %collective-permute-start.44 = (bf16[256,512]{1,0:T(8,128)(2,1)S(1)}, bf16[256,512]{1,0:T(8,128)(2,1)S(1)}, u32[]{:S(2)}, u32[]{:S(2)}) collective-permute-start(bf16[256,512]{1,0:T(8,128)(2,1)S(1)} %get-tuple-element.164), channel_id=1, source_target_pairs={{0,1},{1,0},{2,3},{3,2},{4,5},{5,4},{6,7},{7,6},{8,9},{9,8},{10,11... | collective-permute-start | bytes 786440 | tf_op jit(solution)/shard_map/ppermute | solution.py:284
  122.2 7.9 %collective-permute-start.52 = (bf16[128,1024]{1,0:T(8,128)(2,1)S(1)}, bf16[128,1024]{1,0:T(8,128)(2,1)S(1)}, u32[]{:S(2)}, u32[]{:S(2)}) collective-permute-start(bf16[128,1024]{1,0:T(8,128)(2,1)S(1)} %shard_map.107), channel_id=1, source_target_pairs={{0,16},{16,0},{1,17},{17,1},{2,18},{18,2},{3,19},{19,3},{4,20},{20... | collective-permute-start | bytes 786440 | tf_op jit(solution)/shard_map/ppermute | solution.py:287
  124.0 7.7 %collective-permute-start.50 = (bf16[256,512]{1,0:T(8,128)(2,1)S(1)}, bf16[256,512]{1,0:T(8,128)(2,1)S(1)}, u32[]{:S(2)}, u32[]{:S(2)}) collective-permute-start(bf16[256,512]{1,0:T(8,128)(2,1)S(1)} %get-tuple-element.172), channel_id=1, source_target_pairs={{0,4},{4,8},{8,12},{12,14},{14,10},{10,6},{6,2},{2,0},{1,5},{5,9},... | collective-permute-start | bytes 786440 | tf_op jit(solution)/shard_map/ppermute | solution.py:278
  125.3 7.4 %collective-permute-start.51 = (bf16[256,512]{1,0:T(8,128)(2,1)S(1)}, bf16[256,512]{1,0:T(8,128)(2,1)S(1)}, u32[]{:S(2)}, u32[]{:S(2)}) collective-permute-start(bf16[256,512]{1,0:T(8,128)(2,1)S(1)} %get-tuple-element.171), channel_id=1, source_target_pairs={{4,0},{8,4},{12,8},{14,12},{10,14},{6,10},{2,6},{0,2},{5,1},{9,5},... | collective-permute-start | bytes 786440 | tf_op jit(solution)/shard_map/ppermute | solution.py:281
  (19 other events, 128.8 us)

commit v4 on v3

--- a/solution.py
+++ b/solution.py
@@ -166,7 +166,7 @@
 def expert_body(columns, info, *refs):
     n = len(columns)
     own, other = refs[:n], refs[n : 2 * n]
-    gates, up, down, stay, give, x, total = refs[2 * n :]
+    gates, up, down, stay, give, x, hid = refs[2 * n :]
     core = info[0]
     half = own[0].shape[1]
     here = pl.ds(pl.multiple_of(core * half, half), half)
@@ -178,31 +178,27 @@
         x[begin : begin + size, there] = b[...]
         begin += size
     hidden = up.shape[0]
-    chunk = max(c for c in range(16, 513, 16) if hidden % c == 0)
+    chunk = hidden if hidden % 128 else max(c for c in range(128, 513, 128) if hidden % c == 0)
     for i in range(hidden // chunk):
         at = slice(i * chunk, (i + 1) * chunk)
         h = lax.dot_general(
             x[...], up[at, :], (((1,), (1,)), ((), ())), preferred_element_type=F32
         )
-        h = jnp.square(jnp.maximum(h, 0.0)).astype(BF16)
-        part = jnp.dot(h, down[at, :], preferred_element_type=F32)
-        if i == 0:
-            total[...] = part
-        else:
-            total[...] += part
-    begin = 0
-    for j, (column, first) in enumerate(columns):
-        size = own[j].shape[0]
-        gate = gates[first : first + size, column : column + 1]
-        rows = slice(begin, begin + size)
-        stay[rows, :] = (total[rows, here] * gate).astype(BF16)
-        give[rows, :] = (total[rows, there] * gate).astype(BF16)
-        begin += size
-
-
-def final_body(depth, info, kept, mine, back, *rest):
-    *blocks, out, mixture, full, done = rest
-    core, side, me = info[0], info[1], info[2]
+        hid[:, at] = jnp.square(jnp.maximum(h, 0.0)).astype(BF16)
+    for columns_at, out in ((here, stay), (there, give)):
+        total = jnp.dot(hid[...], down[:, columns_at], preferred_element_type=F32)
+        begin = 0
+        for j, (column, first) in enumerate(columns):
+            size = own[j].shape[0]
+            gate = gates[first : first + size, column : column + 1]
+            rows = slice(begin, begin + size)
+            out[rows, :] = (total[rows] * gate).astype(BF16)
+            begin += size
+
+
+def assemble_body(depth, info, *rest):
+    *blocks, full, done = rest
+    side, me = info[1], info[2]
     count = (len(blocks) - 1) * 2 // 3
     pairs = [(b, b.shape[0] // 2) for b in blocks[1 + count :]]
     blocks = blocks[: 1 + count] + [
@@ -219,11 +215,14 @@
                 begin = begin + size
             places.append(full.at[pl.ds(pl.multiple_of(begin, size), size), at])
     arrived = fetch(blocks, places, done)
-    half = mine.shape[1]
+    for i in range(len(blocks)):
+        arrived(i)
+
+
+def final_body(info, kept, mine, back, full, out, mixture):
+    core, half = info[0], mine.shape[1]
     mixture[:, pl.ds(pl.multiple_of(core * half, half), half)] = mine[...]
     mixture[:, pl.ds(pl.multiple_of((1 - core) * half, half), half)] = back[...]
-    for i in range(len(blocks)):
-        arrived(i)
     step = 512
     for i in range(full.shape[1] // step):
         at = slice(i * step, (i + 1) * step)
@@ -345,7 +344,6 @@
             tokens,
             w_in,
         )
-        block = after(block, *out_blocks)
 
         def norm(x, *others):
             return kernel_call(
@@ -426,6 +424,7 @@
         lat_other = across(lat_there)
         out_step(lat_there)
         latent, gates = mine(len(blocks), ends, lat_other, *lat_mine[::-1])
+        side_info = info.at[1].set(side.astype(jnp.int32))
         up_weight, down_weight = w_up[0].T, w_down[0]
         hidden = up_weight.shape[0]
 
@@ -439,7 +438,7 @@
                 4 + 2 * len(xs),
                 4 * size * width * hidden,
                 4 * hidden * width + 4 * size * width,
-                [pltpu.VMEM((size, width), BF16), pltpu.VMEM((size, width), F32)],
+                [pltpu.VMEM((size, width), BF16), pltpu.VMEM((size, hidden), BF16)],
             )(after(info, *others), *xs, *ys, gates, up_weight, down_weight)
 
         def total(stay, given, more=None):
@@ -476,7 +475,7 @@
         done[far - 2] = expert(
             pairs[far - 2], [(2 * far - 5, 0), (2 * far - 4, 0)], back
         )
-        beside = [*done[far - 2], *pack(back)]
+        beside = [*done[far - 2]]
         out_step(back)
         to_above, to_below = step(
             back[:half_rows], back[half_rows:], *beside, *out_blocks
@@ -512,36 +511,33 @@
             if len(out_blocks) < 2 * far:
                 out_step(to_above, to_below)
                 beside += out_blocks
-            if len(packs) < far:
+            while len(packs) < len(out_blocks) // 2:
                 beside += pack(to_above)
             beside += handed[2:]
             if len(handed) < far:
                 hand(to_above)
+            if d == 1:
+                full = kernel_call(
+                    functools.partial(assemble_body, out_depth),
+                    shape(width, columns),
+                    1,
+                    width * columns,
+                    4 * width * columns,
+                    [pltpu.SemaphoreType.DMA((1 + 2 * len(out_blocks),))],
+                    1 + len(out_blocks) + len(handed),
+                )(side_info, w_out, *out_blocks, *handed)
+                beside = [*beside[: -len(handed)], full]
             to_above, to_below = step(above, below, *beside)
         mixture = total(done[0][0], given0, to_above)
         mixture = (mixture + to_below.astype(F32)).astype(BF16)
         return kernel_call(
-            functools.partial(final_body, out_depth),
+            final_body,
             shape(rows, columns),
-            4,
+            5,
             2 * rows * width * columns,
             2 * width * columns + 4 * rows * columns,
-            [
-                pltpu.VMEM((rows, width), BF16),
-                pltpu.VMEM((width, columns), BF16),
-                pltpu.SemaphoreType.DMA((1 + 2 * len(out_blocks),)),
-            ],
-            1 + len(out_blocks) + len(handed),
-            BIG,
-        )(
-            info.at[1].set(side.astype(jnp.int32)),
-            kept,
-            mixture,
-            swap(mixture),
-            w_out,
-            *out_blocks,
-            *handed,
-        )
+            [pltpu.VMEM((rows, width), BF16)],
+        )(info, kept, mixture, swap(mixture), full)
 
     return local
 

time: 138 us -> 136 us (0.986)
  local copies, waits for them, and re-layouts: 6.88 us -> 3.25 us
  Pallas kernels: 39 us -> 41.1 us
    unnamed x26 -> x15, local copies, waits for them, and re-layouts: 5 us -> 1.62 us
    ppermute x16, starting transfers between devices: 11.4 us -> 9.31 us  [down(): return lax.ppermute(x, 'wide', down_perm)]
    pallas_call x1 -> x2, Pallas kernels: 3.41 us -> 4.61 us  [the longest x1 2.82 us: local(): kernel_call(final_body, shape(rows, columns), 5, 2 * rows * width * colum...]
  transfers between devices with their start and end apart: 54 -> 54, of which waited for: 30 -> 29; matrix products, arithmetic and copies ran while one was open for 2% -> 2% of each run, Pallas kernels for 25% -> 25%
where the time goes in v4:
time: 136 us; the launch traced here: 135 us
  waiting for transfers between devices  45.9 us (34%)
  starting transfers between devices  43.2 us (32%)
  Pallas kernels  41.1 us (30%)
  local copies, waits for them, and re-layouts  3.25 us (2%)
  other arithmetic  1.52 us (1%)
    ppermute x16, starting transfers between devices, up(): return lax.ppermute(x, 'wide', up_perm)  23.6 us
    ppermute x16, waiting for transfers between devices, up(): return lax.ppermute(x, 'wide', up_perm)  20 us
    pallas_call x5, Pallas kernels, expert(): kernel_call(functools.partial(expert_body, columns), (out, out), 4 + 2 *...  17 us
    ppermute x16, waiting for transfers between devices, down(): return lax.ppermute(x, 'wide', down_perm)  12.6 us
    ppermute x6, waiting for transfers between devices, across(): return lax.ppermute(x, 'groups', [(i, i ^ 1) for i in range(groups)])  11.7 us
    ppermute x16, starting transfers between devices, down(): return lax.ppermute(x, 'wide', down_perm)  9.31 us
    ppermute x6, starting transfers between devices, across(): return lax.ppermute(x, 'groups', [(i, i ^ 1) for i in range(groups)])  7.96 us
    pallas_call x2, Pallas kernels, norm(): kernel_call(norm_body, shape(*x.shape), 3, 8 * x.size, 4 * x.size)  5.32 us
  transfers between devices with their start and end apart: 54, of which 29 were waited for; matrix products, arithmetic and copies ran while one was open for 2% of the time, Pallas kernels for 25%

profile of v4, /device:TPU:0, one launch (start us, length us, event | category | flops | bytes accessed | tf_op | source)
XLA Modules:
  0.0 135.4 jit_solution(9539270815177953482)
XLA Ops:
  0.6 3.1 %shard_map.91 = (bf16[128,4096]{1,0:T(8,128)(2,1)}, bf16[544,256]{1,0:T(8,128)(2,1)}) custom-call(s32[2]{0:T(128)} %pad_add_fusion.1.info, s32[4,256]{1,0:T(4,128)} %bitcast.25, f32[4,256]{1,0:T(4,128)} %bitcast.26, bf16[256,4096]{1,0:T(8,128)(2,1)} %tokens.3, bf16[512,1024]{1,0:T(8,128)(2,1)} %w_in.1), custom_call_target="tpu_custom_call" | custom-call | tf_op jit(solution)/shard_map/pallas_call | solution.py:334
  3.7 3.0 %collective-permute-start.8 = (bf16[128,4096]{1,0:T(8,128)(2,1)}, bf16[128,4096]{1,0:T(8,128)(2,1)}, u32[]{:S(2)}, u32[]{:S(2)}) collective-permute-start(bf16[128,4096]{1,0:T(8,128)(2,1)} %get-tuple-element.110), channel_id=1, source_target_pairs={{0,16},{16,0},{1,17},{17,1},{2,18},{18,2},{3,19},{19,3},{4,20},{20... | collective-permute-start | bytes 3145736 | tf_op jit(solution)/shard_map/ppermute | solution.py:286
  6.7 1.6 %collective-permute-start = (bf16[544,256]{1,0:T(8,128)(2,1)}, bf16[544,256]{1,0:T(8,128)(2,1)S(1)}, u32[]{:S(2)}, u32[]{:S(2)}) collective-permute-start(bf16[544,256]{1,0:T(8,128)(2,1)} %get-tuple-element.93.refs_0_.refs_2_), channel_id=1, source_target_pairs={{0,4},{4,8},{8,12},{12,14},{14,10},{10,6},{6,2},{2,0},{1,5},{5,9},... | collective-permute-start | bytes 835592 | tf_op jit(solution)/shard_map/ppermute | solution.py:277
  9.4 1.6 %collective-permute-start.4 = (bf16[128,1024]{1,0:T(8,128)(2,1)}, bf16[128,1024]{1,0:T(8,128)(2,1)}, u32[]{:S(2)}, u32[]{:S(2)}) collective-permute-start(bf16[128,1024]{1,0:T(8,128)(2,1)} %constant_dynamic-slice_fusion), channel_id=1, source_target_pairs={{0,4},{4,8},{8,12},{12,14},{14,10},{10,6},{6,2},{2,0},{1,5},{5,9},... | collective-permute-start | bytes 786440 | tf_op jit(solution)/shard_map/ppermute | solution.py:277
  12.2 1.6 %copy-done = bf16[256,4096]{1,0:T(8,128)(2,1)S(1)} copy-done((bf16[256,4096]{1,0:T(8,128)(2,1)S(1)}, bf16[256,4096]{1,0:T(8,128)(2,1)}, u32[]{:S(2)}) %copy-start) | copy-done | bytes 2097176
  13.8 2.9 %shard_map.92.normed = bf16[256,4096]{1,0:T(8,128)(2,1)S(1)} custom-call(s32[11]{0:T(128)S(1)} %pad_add_fusion.info, bf16[256,4096]{1,0:T(8,128)(2,1)S(1)} %copy-done, f32[1,4096]{1,0:T(1,128)S(1)} %bitcast.23), custom_call_target="tpu_custom_call" | custom-call | flops 8388608 | bytes 4194304 | tf_op jit(solution)/shard_map/pallas_call | solution.py:349
  16.8 1.3 collective-permute-done.1.refs_2_.refs_4_
  18.1 1.6 %collective-permute-start.2 = (bf16[544,256]{1,0:T(8,128)(2,1)S(1)}, bf16[544,256]{1,0:T(8,128)(2,1)}, u32[]{:S(2)}, u32[]{:S(2)}) collective-permute-start(bf16[544,256]{1,0:T(8,128)(2,1)S(1)} %collective-permute-done.refs_1_.refs_3_), channel_id=1, source_target_pairs={{0,4},{4,8},{8,12},{12,14},{14,10},{10,6},{6,2},{2,0},{1,5},{5,9},... | collective-permute-start | bytes 835592 | tf_op jit(solution)/shard_map/ppermute | solution.py:277
  20.1 2.1 %collective-permute-done.4.first.rest_1_ = bf16[128,1024]{1,0:T(8,128)(2,1)} collective-permute-done((bf16[128,1024]{1,0:T(8,128)(2,1)}, bf16[128,1024]{1,0:T(8,128)(2,1)}, u32[]{:S(2)}, u32[]{:S(2)}) %collective-permute-start.4) | collective-permute-done | bytes 262176 | tf_op jit(solution)/shard_map/ppermute | solution.py:277
  22.2 1.6 %collective-permute-done.5.second.rest_2_ = bf16[128,1024]{1,0:T(8,128)(2,1)} collective-permute-done((bf16[128,1024]{1,0:T(8,128)(2,1)}, bf16[128,1024]{1,0:T(8,128)(2,1)}, u32[]{:S(2)}, u32[]{:S(2)}) %collective-permute-start.5) | collective-permute-done | bytes 262176 | tf_op jit(solution)/shard_map/ppermute | solution.py:280
  23.8 1.6 %shard_map.94 = bf16[256,1024]{1,0:T(8,128)(2,1)S(1)} custom-call(s32[11]{0:T(128)S(1)} %pad_add_fusion.info, bf16[128,1024]{1,0:T(8,128)(2,1)} %collective-permute-done.4.first.rest_1_, bf16[128,1024]{1,0:T(8,128)(2,1)} %collective-permute-done.5.second.rest_2_), custom_call_target="tpu_custom_call" | custom-call | flops 262144 | bytes 1048576 | tf_op jit(solution)/shard_map/pallas_call | solution.py:316
  26.7 1.3 collective-permute-done.3.refs_1_.refs_6_
  28.0 1.6 %collective-permute-start.6 = (bf16[544,256]{1,0:T(8,128)(2,1)}, bf16[544,256]{1,0:T(8,128)(2,1)S(1)}, u32[]{:S(2)}, u32[]{:S(2)}) collective-permute-start(bf16[544,256]{1,0:T(8,128)(2,1)} %collective-permute-done.2.refs_0_.refs_5_), channel_id=1, source_target_pairs={{0,4},{4,8},{8,12},{12,14},{14,10},{10,6},{6,2},{2,0},{1,5},{5,9},... | collective-permute-start | bytes 835592 | tf_op jit(solution)/shard_map/ppermute | solution.py:277
  30.0 1.4 shard_map.95
  31.4 2.4 %shard_map.96.refs_0_ = bf16[128,4096]{1,0:T(8,128)(2,1)S(1)} custom-call(s32[11]{0:T(128)S(1)} %pad_add_fusion.info, bf16[128,4096]{1,0:T(8,128)(2,1)} %collective-permute-done.8.tokens, f32[1,4096]{1,0:T(1,128)S(1)} %bitcast.24), custom_call_target="tpu_custom_call" | custom-call | flops 4194304 | bytes 2097152 | tf_op jit(solution)/shard_map/pallas_call | solution.py:349
  33.8 1.3 collective-permute-done.6.refs_7_.refs_0_
  37.0 1.6 %collective-permute-start.9 = (bf16[256,256]{1,0:T(8,128)(2,1)S(1)}, bf16[256,256]{1,0:T(8,128)(2,1)S(1)}, u32[]{:S(2)}, u32[]{:S(2)}) collective-permute-start(bf16[256,256]{1,0:T(8,128)(2,1)S(1)} %slice.84), channel_id=1, source_target_pairs={{0,4},{4,8},{8,12},{12,14},{14,10},{10,6},{6,2},{2,0},{1,5},{5,9},... | collective-permute-start | bytes 393224 | tf_op jit(solution)/shard_map/ppermute | solution.py:277
  39.5 2.7 %shard_map.97 = (f32[256,256]{1,0:T(8,128)S(1)}, bf16[256,512]{1,0:T(8,128)(2,1)S(1)}) custom-call(s32[11]{0:T(128)S(1)} %pad_add_fusion.info, bf16[128,4096]{1,0:T(8,128)(2,1)S(1)} %shard_map.96.refs_0_, bf16[128,4096]{1,0:T(8,128)(2,1)S(1)} %collective-permute-done.11.refs_1_, bf16[544,256]{1,0:T(8,128)(2,1)S(1)} %copy-done.5, ...), custom_call_target="tpu_custom_call" | custom-call | flops 536870912 | bytes 4194304 | tf_op jit(solution)/shard_map/pallas_call | solution.py:365
  44.1 1.6 %collective-permute-start.15 = (bf16[128,1024]{1,0:T(8,128)(2,1)}, bf16[128,1024]{1,0:T(8,128)(2,1)S(1)}, u32[]{:S(2)}, u32[]{:S(2)}) collective-permute-start(bf16[128,1024]{1,0:T(8,128)(2,1)} %collective-permute-done.4.first.rest_1_), channel_id=1, source_target_pairs={{0,4},{4,8},{8,12},{12,14},{14,10},{10,6},{6,2},{2,0},{1,5},{5,9},... | collective-permute-start | bytes 786440 | tf_op jit(solution)/shard_map/ppermute | solution.py:277
  46.1 2.6 %collective-permute-done.12.refs_2_ = bf16[256,256]{1,0:T(8,128)(2,1)S(1)} collective-permute-done((bf16[256,256]{1,0:T(8,128)(2,1)S(1)}, bf16[256,256]{1,0:T(8,128)(2,1)S(1)}, u32[]{:S(2)}, u32[]{:S(2)}) %collective-permute-start.12) | collective-permute-done | bytes 131104 | tf_op jit(solution)/shard_map/ppermute | solution.py:286
  49.5 1.6 %collective-permute-start.13 = (bf16[256,512]{1,0:T(8,128)(2,1)S(1)}, bf16[256,512]{1,0:T(8,128)(2,1)S(1)}, u32[]{:S(2)}, u32[]{:S(2)}) collective-permute-start(bf16[256,512]{1,0:T(8,128)(2,1)S(1)} %get-tuple-element.120.refs_0_), channel_id=1, source_target_pairs={{0,4},{4,8},{8,12},{12,14},{14,10},{10,6},{6,2},{2,0},{1,5},{5,9},... | collective-permute-start | bytes 786440 | tf_op jit(solution)/shard_map/ppermute | solution.py:277
  51.6 1.4 %collective-permute-done.15.first.rest_3_ = bf16[128,1024]{1,0:T(8,128)(2,1)S(1)} collective-permute-done((bf16[128,1024]{1,0:T(8,128)(2,1)}, bf16[128,1024]{1,0:T(8,128)(2,1)S(1)}, u32[]{:S(2)}, u32[]{:S(2)}) %collective-permute-start.15) | collective-permute-done | bytes 262176 | tf_op jit(solution)/shard_map/ppermute | solution.py:277
  52.9 2.1 %collective-permute-start.20 = (bf16[256,1024]{1,0:T(8,128)(2,1)S(1)}, bf16[256,1024]{1,0:T(8,128)(2,1)S(1)}, u32[]{:S(2)}, u32[]{:S(2)}) collective-permute-start(bf16[256,1024]{1,0:T(8,128)(2,1)S(1)} %shard_map.94), channel_id=1, source_target_pairs={{0,16},{16,0},{1,17},{17,1},{2,18},{18,2},{3,19},{19,3},{4,20},{20... | collective-permute-start | bytes 1572872 | tf_op jit(solution)/shard_map/ppermute | solution.py:286
  55.1 2.5 %collective-permute-done.13.refs_0_ = bf16[256,512]{1,0:T(8,128)(2,1)S(1)} collective-permute-done((bf16[256,512]{1,0:T(8,128)(2,1)S(1)}, bf16[256,512]{1,0:T(8,128)(2,1)S(1)}, u32[]{:S(2)}, u32[]{:S(2)}) %collective-permute-start.13) | collective-permute-done | bytes 262176 | tf_op jit(solution)/shard_map/ppermute | solution.py:277
  57.6 1.3 collective-permute-done.14.refs_1_
  58.9 1.5 %collective-permute-start.18 = (bf16[256,512]{1,0:T(8,128)(2,1)S(1)}, bf16[256,512]{1,0:T(8,128)(2,1)S(1)}, u32[]{:S(2)}, u32[]{:S(2)}) collective-permute-start(bf16[256,512]{1,0:T(8,128)(2,1)S(1)} %collective-permute-done.13.refs_0_), channel_id=1, source_target_pairs={{0,4},{4,8},{8,12},{12,14},{14,10},{10,6},{6,2},{2,0},{1,5},{5,9},... | collective-permute-start | bytes 786440 | tf_op jit(solution)/shard_map/ppermute | solution.py:277
  62.1 3.7 %collective-permute-done.18.refs_0_ = bf16[256,512]{1,0:T(8,128)(2,1)S(1)} collective-permute-done((bf16[256,512]{1,0:T(8,128)(2,1)S(1)}, bf16[256,512]{1,0:T(8,128)(2,1)S(1)}, u32[]{:S(2)}, u32[]{:S(2)}) %collective-permute-start.18) | collective-permute-done | bytes 262176 | tf_op jit(solution)/shard_map/ppermute | solution.py:277
  67.0 1.4 %collective-permute-start.21 = (bf16[256,512]{1,0:T(8,128)(2,1)S(1)}, bf16[256,512]{1,0:T(8,128)(2,1)S(1)}, u32[]{:S(2)}, u32[]{:S(2)}) collective-permute-start(bf16[256,512]{1,0:T(8,128)(2,1)S(1)} %collective-permute-done.18.refs_0_), channel_id=1, source_target_pairs={{0,4},{4,8},{8,12},{12,14},{14,10},{10,6},{6,2},{2,0},{1,5},{5,9},... | collective-permute-start | bytes 786440 | tf_op jit(solution)/shard_map/ppermute | solution.py:277
  69.0 4.1 %shard_map.102 = (bf16[512,512]{1,0:T(8,128)(2,1)S(1)}, bf16[512,512]{1,0:T(8,128)(2,1)S(1)}) custom-call(s32[11]{0:T(128)S(1)} %pad_add_fusion.info, bf16[256,512]{1,0:T(8,128)(2,1)S(1)} %collective-permute-done.13.refs_0_, bf16[256,512]{1,0:T(8,128)(2,1)S(1)} %collective-permute-done.14.refs_1_, bf16[256,512]{1,0:T(8,128)(2,1)S(1)} %collective-permute-done.23.refs_2_, ...), custom_call_target="tpu_custom_call" | custom-call | flops 2818572288 | bytes 7602176 | tf_op jit(solution)/shard_map/pallas_call | solution.py:435
  73.4 1.4 %collective-permute-done.22.refs_1_ = bf16[256,512]{1,0:T(8,128)(2,1)S(1)} collective-permute-done((bf16[256,512]{1,0:T(8,128)(2,1)S(1)}, bf16[256,512]{1,0:T(8,128)(2,1)S(1)}, u32[]{:S(2)}, u32[]{:S(2)}) %collective-permute-start.22) | collective-permute-done | bytes 262176 | tf_op jit(solution)/shard_map/ppermute | solution.py:280
  74.8 2.6 %collective-permute-done.25.rest_10_ = bf16[256,1024]{1,0:T(8,128)(2,1)S(1)} collective-permute-done((bf16[256,1024]{1,0:T(8,128)(2,1)S(1)}, bf16[256,1024]{1,0:T(8,128)(2,1)S(1)}, u32[]{:S(2)}, u32[]{:S(2)}) %collective-permute-start.25) | collective-permute-done | bytes 524320 | tf_op jit(solution)/shard_map/ppermute | solution.py:286
  77.9 1.6 %collective-permute-start.29 = (bf16[128,512]{1,0:T(8,128)(2,1)S(1)}, bf16[128,512]{1,0:T(8,128)(2,1)S(1)}, u32[]{:S(2)}, u32[]{:S(2)}) collective-permute-start(bf16[128,512]{1,0:T(8,128)(2,1)S(1)} %slice.89), channel_id=1, source_target_pairs={{0,4},{4,8},{8,12},{12,14},{14,10},{10,6},{6,2},{2,0},{1,5},{5,9},... | collective-permute-start | bytes 393224 | tf_op jit(solution)/shard_map/ppermute | solution.py:277
  79.9 4.1 %shard_map.103 = (bf16[512,512]{1,0:T(8,128)(2,1)S(1)}, bf16[512,512]{1,0:T(8,128)(2,1)S(1)}) custom-call(s32[11]{0:T(128)S(1)} %pad_add_fusion.info, bf16[256,512]{1,0:T(8,128)(2,1)S(1)} %collective-permute-done.21.refs_0_, bf16[256,512]{1,0:T(8,128)(2,1)S(1)} %collective-permute-done.22.refs_1_, bf16[256,512]{1,0:T(8,128)(2,1)S(1)} %collective-permute-done.26.refs_2_, ...), custom_call_target="tpu_custom_call" | custom-call | flops 2818572288 | bytes 7602176 | tf_op jit(solution)/shard_map/pallas_call | solution.py:435
  85.1 1.4 %collective-permute-start.34 = (bf16[128,1024]{1,0:T(8,128)(2,1)S(1)}, bf16[128,1024]{1,0:T(8,128)(2,1)S(1)}, u32[]{:S(2)}, u32[]{:S(2)}) collective-permute-start(bf16[128,1024]{1,0:T(8,128)(2,1)S(1)} %collective-permute-done.15.first.rest_3_), channel_id=1, source_target_pairs={{0,4},{4,8},{8,12},{12,14},{14,10},{10,6},{6,2},{2,0},{1,5},{5,9},... | collective-permute-start | bytes 786440 | tf_op jit(solution)/shard_map/ppermute | solution.py:277
  87.1 2.4 %shard_map.104 = (bf16[256,512]{1,0:T(8,128)(2,1)S(1)}, bf16[256,512]{1,0:T(8,128)(2,1)S(1)}) custom-call(s32[11]{0:T(128)S(1)} %pad_add_fusion.info, bf16[128,512]{1,0:T(8,128)(2,1)S(1)} %collective-permute-done.29.refs_0_, bf16[128,512]{1,0:T(8,128)(2,1)S(1)} %collective-permute-done.30.refs_1_, bf16[128,512]{1,0:T(8,128)(2,1)S(1)} %collective-permute-done.31.refs_2_, ...), custom_call_target="tpu_custom_call" | custom-call | flops 1409286144 | bytes 6553600 | tf_op jit(solution)/shard_map/pallas_call | solution.py:435
  90.2 3.1 %collective-permute-done.34.first.rest_5_ = bf16[128,1024]{1,0:T(8,128)(2,1)S(1)} collective-permute-done((bf16[128,1024]{1,0:T(8,128)(2,1)S(1)}, bf16[128,1024]{1,0:T(8,128)(2,1)S(1)}, u32[]{:S(2)}, u32[]{:S(2)}) %collective-permute-start.34) | collective-permute-done | bytes 262176 | tf_op jit(solution)/shard_map/ppermute | solution.py:277
  94.5 1.4 %collective-permute-start.36 = (bf16[128,512]{1,0:T(8,128)(2,1)S(1)}, bf16[128,512]{1,0:T(8,128)(2,1)S(1)}, u32[]{:S(2)}, u32[]{:S(2)}) collective-permute-start(bf16[128,512]{1,0:T(8,128)(2,1)S(1)} %get-tuple-element.176), channel_id=1, source_target_pairs={{0,4},{4,8},{8,12},{12,14},{14,10},{10,6},{6,2},{2,0},{1,5},{5,9},... | collective-permute-start | bytes 393224 | tf_op jit(solution)/shard_map/ppermute | solution.py:277
  96.6 1.4 %collective-permute-start.40 = (bf16[64,1024]{1,0:T(8,128)(2,1)S(1)}, bf16[64,1024]{1,0:T(8,128)(2,1)S(1)}, u32[]{:S(2)}, u32[]{:S(2)}) collective-permute-start(bf16[64,1024]{1,0:T(8,128)(2,1)S(1)} %slice.93), channel_id=1, source_target_pairs={{0,4},{4,8},{8,12},{12,14},{14,10},{10,6},{6,2},{2,0},{1,5},{5,9},... | collective-permute-start | bytes 393224 | tf_op jit(solution)/shard_map/ppermute | solution.py:277
  98.7 4.1 %shard_map.105 = (bf16[512,512]{1,0:T(8,128)(2,1)S(1)}, bf16[512,512]{1,0:T(8,128)(2,1)S(1)}) custom-call(s32[11]{0:T(128)S(1)} %pad_add_fusion.info, bf16[256,512]{1,0:T(8,128)(2,1)S(1)} %collective-permute-done.18.refs_0_, bf16[256,512]{1,0:T(8,128)(2,1)S(1)} %collective-permute-done.19.refs_1_, bf16[256,512]{1,0:T(8,128)(2,1)S(1)} %collective-permute-done.38.refs_2_, ...), custom_call_target="tpu_custom_call" | custom-call | flops 2818572288 | bytes 7602176 | tf_op jit(solution)/shard_map/pallas_call | solution.py:435
  103.5 1.4 %collective-permute-start.42 = (bf16[256,512]{1,0:T(8,128)(2,1)S(1)}, bf16[256,512]{1,0:T(8,128)(2,1)S(1)}, u32[]{:S(2)}, u32[]{:S(2)}) collective-permute-start(bf16[256,512]{1,0:T(8,128)(2,1)S(1)} %pad_maximum_fusion), channel_id=1, source_target_pairs={{0,4},{4,8},{8,12},{12,14},{14,10},{10,6},{6,2},{2,0},{1,5},{5,9},... | collective-permute-start | bytes 786440 | tf_op jit(solution)/shard_map/ppermute | solution.py:277
  107.8 4.1 %collective-permute-done.42 = bf16[256,512]{1,0:T(8,128)(2,1)S(1)} collective-permute-done((bf16[256,512]{1,0:T(8,128)(2,1)S(1)}, bf16[256,512]{1,0:T(8,128)(2,1)S(1)}, u32[]{:S(2)}, u32[]{:S(2)}) %collective-permute-start.42) | collective-permute-done | bytes 262176 | tf_op jit(solution)/shard_map/ppermute | solution.py:277
  115.9 2.4 %shard_map.108 = (bf16[256,512]{1,0:T(8,128)(2,1)S(1)}, bf16[256,512]{1,0:T(8,128)(2,1)S(1)}) custom-call(s32[11]{0:T(128)S(1)} %pad_add_fusion.info, bf16[256,512]{1,0:T(8,128)(2,1)S(1)} %get-tuple-element.120.refs_0_, bf16[256,512]{1,0:T(8,128)(2,1)S(1)} %collective-permute-done.17.refs_1_, f32[256,8]{1,0:T(8,128)S(1)} %get-tuple-element.132.refs_4_.refs_2_, ...), custom_call_target="tpu_custom_call" | custom-call | flops 1409286144 | bytes 6553600 | tf_op jit(solution)/shard_map/pallas_call | solution.py:435
  118.3 3.7 %collective-permute-done.49.rest_11_ = bf16[256,1024]{1,0:T(8,128)(2,1)S(1)} collective-permute-done((bf16[256,1024]{1,0:T(8,128)(2,1)S(1)}, bf16[256,1024]{1,0:T(8,128)(2,1)S(1)}, u32[]{:S(2)}, u32[]{:S(2)}) %collective-permute-start.49) | collective-permute-done | bytes 524320 | tf_op jit(solution)/shard_map/ppermute | solution.py:286
  122.2 1.4 %collective-permute-start.50 = (bf16[256,512]{1,0:T(8,128)(2,1)S(1)}, bf16[256,512]{1,0:T(8,128)(2,1)S(1)}, u32[]{:S(2)}, u32[]{:S(2)}) collective-permute-start(bf16[256,512]{1,0:T(8,128)(2,1)S(1)} %get-tuple-element.170), channel_id=1, source_target_pairs={{0,4},{4,8},{8,12},{12,14},{14,10},{10,6},{6,2},{2,0},{1,5},{5,9},... | collective-permute-start | bytes 786440 | tf_op jit(solution)/shard_map/ppermute | solution.py:277
  124.3 2.9 %collective-permute-done.52.rest_12_ = bf16[128,1024]{1,0:T(8,128)(2,1)S(1)} collective-permute-done((bf16[128,1024]{1,0:T(8,128)(2,1)S(1)}, bf16[128,1024]{1,0:T(8,128)(2,1)S(1)}, u32[]{:S(2)}, u32[]{:S(2)}) %collective-permute-start.52) | collective-permute-done | bytes 262176 | tf_op jit(solution)/shard_map/ppermute | solution.py:286
  127.2 1.8 %shard_map.109.full = bf16[1024,2048]{1,0:T(8,128)(2,1)S(1)} custom-call(s32[11]{0:T(128)S(1)} %constant_dynamic-update-slice_fusion.info, bf16[128,2048]{1,0:T(8,128)(2,1)S(1)} %copy-done.4, bf16[128,1024]{1,0:T(8,128)(2,1)} %collective-permute-done.4.first.rest_1_, bf16[128,1024]{1,0:T(8,128)(2,1)} %collective-permute-done.5.second.rest_2_, ...), custom_call_target="tpu_custom_call" | custom-call | flops 2097152 | bytes 8388608 | tf_op jit(solution)/shard_map/pallas_call | solution.py:520
  131.1 1.5 %collective-permute-done.53.back = bf16[256,512]{1,0:T(8,128)(2,1)S(1)} collective-permute-done((bf16[256,512]{1,0:T(8,128)(2,1)S(1)}, bf16[256,512]{1,0:T(8,128)(2,1)S(1)}, u32[]{:S(2)}, u32[]{:S(2)}) %collective-permute-start.53) | collective-permute-done | bytes 262176 | tf_op jit(solution)/shard_map/ppermute | solution.py:283
  132.6 2.8 %shard_map.110 = bf16[256,2048]{1,0:T(8,128)(2,1)} custom-call(s32[11]{0:T(128)S(1)} %pad_add_fusion.info, bf16[256,2048]{1,0:T(8,128)(2,1)S(1)} %constant_dynamic-slice_fusion.1.kept, bf16[256,512]{1,0:T(8,128)(2,1)S(1)} %add_convert_fusion.mine, bf16[256,512]{1,0:T(8,128)(2,1)S(1)} %collective-permute-done.53.back, bf16[1024,2048]{1,0:T(8,128)(2,1)S(1)} %shard_map.109.full), custom_call_target="tpu_custom_call" | custom-call | flops 1073741824 | bytes 6291456 | tf_op jit(solution)/shard_map/pallas_call | solution.py:533
  (119 shorter events, 31.8 us)
Async XLA Ops:
  3.7 27.7 %collective-permute-start.8 = (bf16[128,4096]{1,0:T(8,128)(2,1)}, bf16[128,4096]{1,0:T(8,128)(2,1)}, u32[]{:S(2)}, u32[]{:S(2)}) collective-permute-start(bf16[128,4096]{1,0:T(8,128)(2,1)} %get-tuple-element.110), channel_id=1, source_target_pairs={{0,16},{16,0},{1,17},{17,1},{2,18},{18,2},{3,19},{19,3},{4,20},{20... | collective-permute-start | bytes 3145736 | tf_op jit(solution)/shard_map/ppermute | solution.py:286
  6.7 10.1 %collective-permute-start = (bf16[544,256]{1,0:T(8,128)(2,1)}, bf16[544,256]{1,0:T(8,128)(2,1)S(1)}, u32[]{:S(2)}, u32[]{:S(2)}) collective-permute-start(bf16[544,256]{1,0:T(8,128)(2,1)} %get-tuple-element.93.refs_0_.refs_2_), channel_id=1, source_target_pairs={{0,4},{4,8},{8,12},{12,14},{14,10},{10,6},{6,2},{2,0},{1,5},{5,9},... | collective-permute-start | bytes 835592 | tf_op jit(solution)/shard_map/ppermute | solution.py:277
  8.3 9.8 %collective-permute-start.1 = (bf16[544,256]{1,0:T(8,128)(2,1)}, bf16[544,256]{1,0:T(8,128)(2,1)S(1)}, u32[]{:S(2)}, u32[]{:S(2)}) collective-permute-start(bf16[544,256]{1,0:T(8,128)(2,1)} %get-tuple-element.93.refs_0_.refs_2_), channel_id=1, source_target_pairs={{4,0},{8,4},{12,8},{14,12},{10,14},{6,10},{2,6},{0,2},{5,1},{9,5},... | collective-permute-start | bytes 835592 | tf_op jit(solution)/shard_map/ppermute | solution.py:280
  9.4 12.8 %collective-permute-start.4 = (bf16[128,1024]{1,0:T(8,128)(2,1)}, bf16[128,1024]{1,0:T(8,128)(2,1)}, u32[]{:S(2)}, u32[]{:S(2)}) collective-permute-start(bf16[128,1024]{1,0:T(8,128)(2,1)} %constant_dynamic-slice_fusion), channel_id=1, source_target_pairs={{0,4},{4,8},{8,12},{12,14},{14,10},{10,6},{6,2},{2,0},{1,5},{5,9},... | collective-permute-start | bytes 786440 | tf_op jit(solution)/shard_map/ppermute | solution.py:277
  11.0 12.8 %collective-permute-start.5 = (bf16[128,1024]{1,0:T(8,128)(2,1)}, bf16[128,1024]{1,0:T(8,128)(2,1)}, u32[]{:S(2)}, u32[]{:S(2)}) collective-permute-start(bf16[128,1024]{1,0:T(8,128)(2,1)} %constant_dynamic-slice_fusion), channel_id=1, source_target_pairs={{4,0},{8,4},{12,8},{14,12},{10,14},{6,10},{2,6},{0,2},{5,1},{9,5},... | collective-permute-start | bytes 786440 | tf_op jit(solution)/shard_map/ppermute | solution.py:280
  18.1 8.6 %collective-permute-start.2 = (bf16[544,256]{1,0:T(8,128)(2,1)S(1)}, bf16[544,256]{1,0:T(8,128)(2,1)}, u32[]{:S(2)}, u32[]{:S(2)}) collective-permute-start(bf16[544,256]{1,0:T(8,128)(2,1)S(1)} %collective-permute-done.refs_1_.refs_3_), channel_id=1, source_target_pairs={{0,4},{4,8},{8,12},{12,14},{14,10},{10,6},{6,2},{2,0},{1,5},{5,9},... | collective-permute-start | bytes 835592 | tf_op jit(solution)/shard_map/ppermute | solution.py:277
  19.6 8.4 %collective-permute-start.3 = (bf16[544,256]{1,0:T(8,128)(2,1)S(1)}, bf16[544,256]{1,0:T(8,128)(2,1)}, u32[]{:S(2)}, u32[]{:S(2)}) collective-permute-start(bf16[544,256]{1,0:T(8,128)(2,1)S(1)} %collective-permute-done.1.refs_2_.refs_4_), channel_id=1, source_target_pairs={{4,0},{8,4},{12,8},{14,12},{10,14},{6,10},{2,6},{0,2},{5,1},{9,5},... | collective-permute-start | bytes 835592 | tf_op jit(solution)/shard_map/ppermute | solution.py:280
  28.0 7.1 %collective-permute-start.6 = (bf16[544,256]{1,0:T(8,128)(2,1)}, bf16[544,256]{1,0:T(8,128)(2,1)S(1)}, u32[]{:S(2)}, u32[]{:S(2)}) collective-permute-start(bf16[544,256]{1,0:T(8,128)(2,1)} %collective-permute-done.2.refs_0_.refs_5_), channel_id=1, source_target_pairs={{0,4},{4,8},{8,12},{12,14},{14,10},{10,6},{6,2},{2,0},{1,5},{5,9},... | collective-permute-start | bytes 835592 | tf_op jit(solution)/shard_map/ppermute | solution.py:277
  29.6 6.8 %collective-permute-start.7 = (bf16[544,256]{1,0:T(8,128)(2,1)}, bf16[544,256]{1,0:T(8,128)(2,1)S(1)}, u32[]{:S(2)}, u32[]{:S(2)}) collective-permute-start(bf16[544,256]{1,0:T(8,128)(2,1)} %collective-permute-done.3.refs_1_.refs_6_), channel_id=1, source_target_pairs={{4,0},{8,4},{12,8},{14,12},{10,14},{6,10},{2,6},{0,2},{5,1},{9,5},... | collective-permute-start | bytes 835592 | tf_op jit(solution)/shard_map/ppermute | solution.py:280
  36.4 6.3 %collective-permute-start.10 = (bf16[288,256]{1,0:T(8,128)(2,1)S(1)}, bf16[288,256]{1,0:T(8,128)(2,1)S(1)}, u32[]{:S(2)}, u32[]{:S(2)}) collective-permute-start(bf16[288,256]{1,0:T(8,128)(2,1)S(1)} %slice.85), channel_id=1, source_target_pairs={{4,0},{8,4},{12,8},{14,12},{10,14},{6,10},{2,6},{0,2},{5,1},{9,5},... | collective-permute-start | bytes 442376 | tf_op jit(solution)/shard_map/ppermute | solution.py:280
  37.0 5.7 %collective-permute-start.9 = (bf16[256,256]{1,0:T(8,128)(2,1)S(1)}, bf16[256,256]{1,0:T(8,128)(2,1)S(1)}, u32[]{:S(2)}, u32[]{:S(2)}) collective-permute-start(bf16[256,256]{1,0:T(8,128)(2,1)S(1)} %slice.84), channel_id=1, source_target_pairs={{0,4},{4,8},{8,12},{12,14},{14,10},{10,6},{6,2},{2,0},{1,5},{5,9},... | collective-permute-start | bytes 393224 | tf_op jit(solution)/shard_map/ppermute | solution.py:277
  43.5 5.2 %collective-permute-start.12 = (bf16[256,256]{1,0:T(8,128)(2,1)S(1)}, bf16[256,256]{1,0:T(8,128)(2,1)S(1)}, u32[]{:S(2)}, u32[]{:S(2)}) collective-permute-start(bf16[256,256]{1,0:T(8,128)(2,1)S(1)} %shard_map.99), channel_id=1, source_target_pairs={{0,16},{16,0},{1,17},{17,1},{2,18},{18,2},{3,19},{19,3},{4,20},{20... | collective-permute-start | bytes 393224 | tf_op jit(solution)/shard_map/ppermute | solution.py:286
  44.1 8.8 %collective-permute-start.15 = (bf16[128,1024]{1,0:T(8,128)(2,1)}, bf16[128,1024]{1,0:T(8,128)(2,1)S(1)}, u32[]{:S(2)}, u32[]{:S(2)}) collective-permute-start(bf16[128,1024]{1,0:T(8,128)(2,1)} %collective-permute-done.4.first.rest_1_), channel_id=1, source_target_pairs={{0,4},{4,8},{8,12},{12,14},{14,10},{10,6},{6,2},{2,0},{1,5},{5,9},... | collective-permute-start | bytes 786440 | tf_op jit(solution)/shard_map/ppermute | solution.py:277
  45.7 9.4 %collective-permute-start.16 = (bf16[128,1024]{1,0:T(8,128)(2,1)}, bf16[128,1024]{1,0:T(8,128)(2,1)S(1)}, u32[]{:S(2)}, u32[]{:S(2)}) collective-permute-start(bf16[128,1024]{1,0:T(8,128)(2,1)} %collective-permute-done.5.second.rest_2_), channel_id=1, source_target_pairs={{4,0},{8,4},{12,8},{14,12},{10,14},{6,10},{2,6},{0,2},{5,1},{9,5},... | collective-permute-start | bytes 786440 | tf_op jit(solution)/shard_map/ppermute | solution.py:280
  49.5 8.1 %collective-permute-start.13 = (bf16[256,512]{1,0:T(8,128)(2,1)S(1)}, bf16[256,512]{1,0:T(8,128)(2,1)S(1)}, u32[]{:S(2)}, u32[]{:S(2)}) collective-permute-start(bf16[256,512]{1,0:T(8,128)(2,1)S(1)} %get-tuple-element.120.refs_0_), channel_id=1, source_target_pairs={{0,4},{4,8},{8,12},{12,14},{14,10},{10,6},{6,2},{2,0},{1,5},{5,9},... | collective-permute-start | bytes 786440 | tf_op jit(solution)/shard_map/ppermute | solution.py:277
  51.1 7.8 %collective-permute-start.14 = (bf16[256,512]{1,0:T(8,128)(2,1)S(1)}, bf16[256,512]{1,0:T(8,128)(2,1)S(1)}, u32[]{:S(2)}, u32[]{:S(2)}) collective-permute-start(bf16[256,512]{1,0:T(8,128)(2,1)S(1)} %get-tuple-element.120.refs_0_), channel_id=1, source_target_pairs={{4,0},{8,4},{12,8},{14,12},{10,14},{6,10},{2,6},{0,2},{5,1},{9,5},... | collective-permute-start | bytes 786440 | tf_op jit(solution)/shard_map/ppermute | solution.py:280
  51.6 7.3 %collective-permute-start.17 = (bf16[256,512]{1,0:T(8,128)(2,1)S(1)}, bf16[256,512]{1,0:T(8,128)(2,1)S(1)}, u32[]{:S(2)}, u32[]{:S(2)}) collective-permute-start(bf16[256,512]{1,0:T(8,128)(2,1)S(1)} %get-tuple-element.120.refs_0_), channel_id=1, source_target_pairs={{0,1},{1,0},{2,3},{3,2},{4,5},{5,4},{6,7},{7,6},{8,9},{9,8},{10,11... | collective-permute-start | bytes 786440 | tf_op jit(solution)/shard_map/ppermute | solution.py:283
  52.9 14.1 %collective-permute-start.20 = (bf16[256,1024]{1,0:T(8,128)(2,1)S(1)}, bf16[256,1024]{1,0:T(8,128)(2,1)S(1)}, u32[]{:S(2)}, u32[]{:S(2)}) collective-permute-start(bf16[256,1024]{1,0:T(8,128)(2,1)S(1)} %shard_map.94), channel_id=1, source_target_pairs={{0,16},{16,0},{1,17},{17,1},{2,18},{18,2},{3,19},{19,3},{4,20},{20... | collective-permute-start | bytes 1572872 | tf_op jit(solution)/shard_map/ppermute | solution.py:286
  58.9 6.9 %collective-permute-start.18 = (bf16[256,512]{1,0:T(8,128)(2,1)S(1)}, bf16[256,512]{1,0:T(8,128)(2,1)S(1)}, u32[]{:S(2)}, u32[]{:S(2)}) collective-permute-start(bf16[256,512]{1,0:T(8,128)(2,1)S(1)} %collective-permute-done.13.refs_0_), channel_id=1, source_target_pairs={{0,4},{4,8},{8,12},{12,14},{14,10},{10,6},{6,2},{2,0},{1,5},{5,9},... | collective-permute-start | bytes 786440 | tf_op jit(solution)/shard_map/ppermute | solution.py:277
  60.4 6.6 %collective-permute-start.19 = (bf16[256,512]{1,0:T(8,128)(2,1)S(1)}, bf16[256,512]{1,0:T(8,128)(2,1)S(1)}, u32[]{:S(2)}, u32[]{:S(2)}) collective-permute-start(bf16[256,512]{1,0:T(8,128)(2,1)S(1)} %collective-permute-done.14.refs_1_), channel_id=1, source_target_pairs={{4,0},{8,4},{12,8},{14,12},{10,14},{6,10},{2,6},{0,2},{5,1},{9,5},... | collective-permute-start | bytes 786440 | tf_op jit(solution)/shard_map/ppermute | solution.py:280
  60.9 8.1 %collective-permute-start.23 = (bf16[256,512]{1,0:T(8,128)(2,1)S(1)}, bf16[256,512]{1,0:T(8,128)(2,1)S(1)}, u32[]{:S(2)}, u32[]{:S(2)}) collective-permute-start(bf16[256,512]{1,0:T(8,128)(2,1)S(1)} %collective-permute-done.13.refs_0_), channel_id=1, source_target_pairs={{0,1},{1,0},{2,3},{3,2},{4,5},{5,4},{6,7},{7,6},{8,9},{9,8},{10,11... | collective-permute-start | bytes 786440 | tf_op jit(solution)/shard_map/ppermute | solution.py:283
  60.9 8.1 %collective-permute-start.24 = (bf16[256,512]{1,0:T(8,128)(2,1)S(1)}, bf16[256,512]{1,0:T(8,128)(2,1)S(1)}, u32[]{:S(2)}, u32[]{:S(2)}) collective-permute-start(bf16[256,512]{1,0:T(8,128)(2,1)S(1)} %collective-permute-done.14.refs_1_), channel_id=1, source_target_pairs={{0,1},{1,0},{2,3},{3,2},{4,5},{5,4},{6,7},{7,6},{8,9},{9,8},{10,11... | collective-permute-start | bytes 786440 | tf_op jit(solution)/shard_map/ppermute | solution.py:283
  65.8 11.6 %collective-permute-start.25 = (bf16[256,1024]{1,0:T(8,128)(2,1)S(1)}, bf16[256,1024]{1,0:T(8,128)(2,1)S(1)}, u32[]{:S(2)}, u32[]{:S(2)}) collective-permute-start(bf16[256,1024]{1,0:T(8,128)(2,1)S(1)} %shard_map.101), channel_id=1, source_target_pairs={{0,16},{16,0},{1,17},{17,1},{2,18},{18,2},{3,19},{19,3},{4,20},{20... | collective-permute-start | bytes 1572872 | tf_op jit(solution)/shard_map/ppermute | solution.py:286
  67.0 6.4 %collective-permute-start.21 = (bf16[256,512]{1,0:T(8,128)(2,1)S(1)}, bf16[256,512]{1,0:T(8,128)(2,1)S(1)}, u32[]{:S(2)}, u32[]{:S(2)}) collective-permute-start(bf16[256,512]{1,0:T(8,128)(2,1)S(1)} %collective-permute-done.18.refs_0_), channel_id=1, source_target_pairs={{0,4},{4,8},{8,12},{12,14},{14,10},{10,6},{6,2},{2,0},{1,5},{5,9},... | collective-permute-start | bytes 786440 | tf_op jit(solution)/shard_map/ppermute | solution.py:277
  68.4 6.4 %collective-permute-start.22 = (bf16[256,512]{1,0:T(8,128)(2,1)S(1)}, bf16[256,512]{1,0:T(8,128)(2,1)S(1)}, u32[]{:S(2)}, u32[]{:S(2)}) collective-permute-start(bf16[256,512]{1,0:T(8,128)(2,1)S(1)} %collective-permute-done.19.refs_1_), channel_id=1, source_target_pairs={{4,0},{8,4},{12,8},{14,12},{10,14},{6,10},{2,6},{0,2},{5,1},{9,5},... | collective-permute-start | bytes 786440 | tf_op jit(solution)/shard_map/ppermute | solution.py:280
  77.9 6.2 %collective-permute-start.29 = (bf16[128,512]{1,0:T(8,128)(2,1)S(1)}, bf16[128,512]{1,0:T(8,128)(2,1)S(1)}, u32[]{:S(2)}, u32[]{:S(2)}) collective-permute-start(bf16[128,512]{1,0:T(8,128)(2,1)S(1)} %slice.89), channel_id=1, source_target_pairs={{0,4},{4,8},{8,12},{12,14},{14,10},{10,6},{6,2},{2,0},{1,5},{5,9},... | collective-permute-start | bytes 393224 | tf_op jit(solution)/shard_map/ppermute | solution.py:277
  79.4 5.1 %collective-permute-start.30 = (bf16[128,512]{1,0:T(8,128)(2,1)S(1)}, bf16[128,512]{1,0:T(8,128)(2,1)S(1)}, u32[]{:S(2)}, u32[]{:S(2)}) collective-permute-start(bf16[128,512]{1,0:T(8,128)(2,1)S(1)} %slice.90), channel_id=1, source_target_pairs={{4,0},{8,4},{12,8},{14,12},{10,14},{6,10},{2,6},{0,2},{5,1},{9,5},... | collective-permute-start | bytes 393224 | tf_op jit(solution)/shard_map/ppermute | solution.py:280
  85.1 8.2 %collective-permute-start.34 = (bf16[128,1024]{1,0:T(8,128)(2,1)S(1)}, bf16[128,1024]{1,0:T(8,128)(2,1)S(1)}, u32[]{:S(2)}, u32[]{:S(2)}) collective-permute-start(bf16[128,1024]{1,0:T(8,128)(2,1)S(1)} %collective-permute-done.15.first.rest_3_), channel_id=1, source_target_pairs={{0,4},{4,8},{8,12},{12,14},{14,10},{10,6},{6,2},{2,0},{1,5},{5,9},... | collective-permute-start | bytes 786440 | tf_op jit(solution)/shard_map/ppermute | solution.py:277
  86.5 7.9 %collective-permute-start.35 = (bf16[128,1024]{1,0:T(8,128)(2,1)S(1)}, bf16[128,1024]{1,0:T(8,128)(2,1)S(1)}, u32[]{:S(2)}, u32[]{:S(2)}) collective-permute-start(bf16[128,1024]{1,0:T(8,128)(2,1)S(1)} %collective-permute-done.16.second.rest_4_), channel_id=1, source_target_pairs={{4,0},{8,4},{12,8},{14,12},{10,14},{6,10},{2,6},{0,2},{5,1},{9,5},... | collective-permute-start | bytes 786440 | tf_op jit(solution)/shard_map/ppermute | solution.py:280
  89.5 4.9 %collective-permute-start.33 = (bf16[256,512]{1,0:T(8,128)(2,1)S(1)}, bf16[256,512]{1,0:T(8,128)(2,1)S(1)}, u32[]{:S(2)}, u32[]{:S(2)}) collective-permute-start(bf16[256,512]{1,0:T(8,128)(2,1)S(1)} %get-tuple-element.142), channel_id=1, source_target_pairs={{0,1},{1,0},{2,3},{3,2},{4,5},{5,4},{6,7},{7,6},{8,9},{9,8},{10,11... | collective-permute-start | bytes 786440 | tf_op jit(solution)/shard_map/ppermute | solution.py:283
  89.6 7.1 %collective-permute-start.38 = (bf16[256,512]{1,0:T(8,128)(2,1)S(1)}, bf16[256,512]{1,0:T(8,128)(2,1)S(1)}, u32[]{:S(2)}, u32[]{:S(2)}) collective-permute-start(bf16[256,512]{1,0:T(8,128)(2,1)S(1)} %collective-permute-done.18.refs_0_), channel_id=1, source_target_pairs={{0,1},{1,0},{2,3},{3,2},{4,5},{5,4},{6,7},{7,6},{8,9},{9,8},{10,11... | collective-permute-start | bytes 786440 | tf_op jit(solution)/shard_map/ppermute | solution.py:283
  90.1 7.9 %collective-permute-start.39 = (bf16[256,512]{1,0:T(8,128)(2,1)S(1)}, bf16[256,512]{1,0:T(8,128)(2,1)S(1)}, u32[]{:S(2)}, u32[]{:S(2)}) collective-permute-start(bf16[256,512]{1,0:T(8,128)(2,1)S(1)} %collective-permute-done.19.refs_1_), channel_id=1, source_target_pairs={{0,1},{1,0},{2,3},{3,2},{4,5},{5,4},{6,7},{7,6},{8,9},{9,8},{10,11... | collective-permute-start | bytes 786440 | tf_op jit(solution)/shard_map/ppermute | solution.py:283
  93.3 9.5 %collective-permute-start.28 = (bf16[512,512]{1,0:T(8,128)(2,1)S(1)}, bf16[512,512]{1,0:T(8,128)(2,1)S(1)}, u32[]{:S(2)}, u32[]{:S(2)}) collective-permute-start(bf16[512,512]{1,0:T(8,128)(2,1)S(1)} %get-tuple-element.138), channel_id=1, source_target_pairs={{0,1},{1,0},{2,3},{3,2},{4,5},{5,4},{6,7},{7,6},{8,9},{9,8},{10,11... | collective-permute-start | bytes 1572872 | tf_op jit(solution)/shard_map/ppermute | solution.py:283
  94.5 8.9 %collective-permute-start.36 = (bf16[128,512]{1,0:T(8,128)(2,1)S(1)}, bf16[128,512]{1,0:T(8,128)(2,1)S(1)}, u32[]{:S(2)}, u32[]{:S(2)}) collective-permute-start(bf16[128,512]{1,0:T(8,128)(2,1)S(1)} %get-tuple-element.176), channel_id=1, source_target_pairs={{0,4},{4,8},{8,12},{12,14},{14,10},{10,6},{6,2},{2,0},{1,5},{5,9},... | collective-permute-start | bytes 393224 | tf_op jit(solution)/shard_map/ppermute | solution.py:277
  95.9 7.6 %collective-permute-start.37 = (bf16[128,512]{1,0:T(8,128)(2,1)S(1)}, bf16[128,512]{1,0:T(8,128)(2,1)S(1)}, u32[]{:S(2)}, u32[]{:S(2)}) collective-permute-start(bf16[128,512]{1,0:T(8,128)(2,1)S(1)} %get-tuple-element.175), channel_id=1, source_target_pairs={{4,0},{8,4},{12,8},{14,12},{10,14},{6,10},{2,6},{0,2},{5,1},{9,5},... | collective-permute-start | bytes 393224 | tf_op jit(solution)/shard_map/ppermute | solution.py:280
  96.6 6.5 %collective-permute-start.40 = (bf16[64,1024]{1,0:T(8,128)(2,1)S(1)}, bf16[64,1024]{1,0:T(8,128)(2,1)S(1)}, u32[]{:S(2)}, u32[]{:S(2)}) collective-permute-start(bf16[64,1024]{1,0:T(8,128)(2,1)S(1)} %slice.93), channel_id=1, source_target_pairs={{0,4},{4,8},{8,12},{12,14},{14,10},{10,6},{6,2},{2,0},{1,5},{5,9},... | collective-permute-start | bytes 393224 | tf_op jit(solution)/shard_map/ppermute | solution.py:277
  98.0 5.5 %collective-permute-start.41 = (bf16[64,1024]{1,0:T(8,128)(2,1)S(1)}, bf16[64,1024]{1,0:T(8,128)(2,1)S(1)}, u32[]{:S(2)}, u32[]{:S(2)}) collective-permute-start(bf16[64,1024]{1,0:T(8,128)(2,1)S(1)} %slice.94), channel_id=1, source_target_pairs={{4,0},{8,4},{12,8},{14,12},{10,14},{6,10},{2,6},{0,2},{5,1},{9,5},... | collective-permute-start | bytes 393224 | tf_op jit(solution)/shard_map/ppermute | solution.py:280
  102.8 10.3 %collective-permute-start.46 = (bf16[512,512]{1,0:T(8,128)(2,1)S(1)}, bf16[512,512]{1,0:T(8,128)(2,1)S(1)}, u32[]{:S(2)}, u32[]{:S(2)}) collective-permute-start(bf16[512,512]{1,0:T(8,128)(2,1)S(1)} %get-tuple-element.150), channel_id=1, source_target_pairs={{0,1},{1,0},{2,3},{3,2},{4,5},{5,4},{6,7},{7,6},{8,9},{9,8},{10,11... | collective-permute-start | bytes 1572872 | tf_op jit(solution)/shard_map/ppermute | solution.py:283
  103.5 8.4 %collective-permute-start.42 = (bf16[256,512]{1,0:T(8,128)(2,1)S(1)}, bf16[256,512]{1,0:T(8,128)(2,1)S(1)}, u32[]{:S(2)}, u32[]{:S(2)}) collective-permute-start(bf16[256,512]{1,0:T(8,128)(2,1)S(1)} %pad_maximum_fusion), channel_id=1, source_target_pairs={{0,4},{4,8},{8,12},{12,14},{14,10},{10,6},{6,2},{2,0},{1,5},{5,9},... | collective-permute-start | bytes 786440 | tf_op jit(solution)/shard_map/ppermute | solution.py:277
  104.9 8.1 %collective-permute-start.43 = (bf16[256,512]{1,0:T(8,128)(2,1)S(1)}, bf16[256,512]{1,0:T(8,128)(2,1)S(1)}, u32[]{:S(2)}, u32[]{:S(2)}) collective-permute-start(bf16[256,512]{1,0:T(8,128)(2,1)S(1)} %pad_maximum_fusion.1), channel_id=1, source_target_pairs={{4,0},{8,4},{12,8},{14,12},{10,14},{6,10},{2,6},{0,2},{5,1},{9,5},... | collective-permute-start | bytes 786440 | tf_op jit(solution)/shard_map/ppermute | solution.py:280
  105.7 16.3 %collective-permute-start.45 = (bf16[512,512]{1,0:T(8,128)(2,1)S(1)}, bf16[512,512]{1,0:T(8,128)(2,1)S(1)}, u32[]{:S(2)}, u32[]{:S(2)}) collective-permute-start(bf16[512,512]{1,0:T(8,128)(2,1)S(1)} %get-tuple-element.134), channel_id=1, source_target_pairs={{0,1},{1,0},{2,3},{3,2},{4,5},{5,4},{6,7},{7,6},{8,9},{9,8},{10,11... | collective-permute-start | bytes 1572872 | tf_op jit(solution)/shard_map/ppermute | solution.py:283
  107.2 14.8 %collective-permute-start.49 = (bf16[256,1024]{1,0:T(8,128)(2,1)S(1)}, bf16[256,1024]{1,0:T(8,128)(2,1)S(1)}, u32[]{:S(2)}, u32[]{:S(2)}) collective-permute-start(bf16[256,1024]{1,0:T(8,128)(2,1)S(1)} %shard_map.106), channel_id=1, source_target_pairs={{0,16},{16,0},{1,17},{17,1},{2,18},{18,2},{3,19},{19,3},{4,20},{20... | collective-permute-start | bytes 1572872 | tf_op jit(solution)/shard_map/ppermute | solution.py:286
  113.3 8.7 %collective-permute-start.47 = (bf16[256,512]{1,0:T(8,128)(2,1)S(1)}, bf16[256,512]{1,0:T(8,128)(2,1)S(1)}, u32[]{:S(2)}, u32[]{:S(2)}) collective-permute-start(bf16[256,512]{1,0:T(8,128)(2,1)S(1)} %get-tuple-element.172), channel_id=1, source_target_pairs={{0,4},{4,8},{8,12},{12,14},{14,10},{10,6},{6,2},{2,0},{1,5},{5,9},... | collective-permute-start | bytes 786440 | tf_op jit(solution)/shard_map/ppermute | solution.py:277
  114.5 7.5 %collective-permute-start.48 = (bf16[256,512]{1,0:T(8,128)(2,1)S(1)}, bf16[256,512]{1,0:T(8,128)(2,1)S(1)}, u32[]{:S(2)}, u32[]{:S(2)}) collective-permute-start(bf16[256,512]{1,0:T(8,128)(2,1)S(1)} %get-tuple-element.171), channel_id=1, source_target_pairs={{4,0},{8,4},{12,8},{14,12},{10,14},{6,10},{2,6},{0,2},{5,1},{9,5},... | collective-permute-start | bytes 786440 | tf_op jit(solution)/shard_map/ppermute | solution.py:280
  115.4 11.9 %collective-permute-start.52 = (bf16[128,1024]{1,0:T(8,128)(2,1)S(1)}, bf16[128,1024]{1,0:T(8,128)(2,1)S(1)}, u32[]{:S(2)}, u32[]{:S(2)}) collective-permute-start(bf16[128,1024]{1,0:T(8,128)(2,1)S(1)} %shard_map.107), channel_id=1, source_target_pairs={{0,16},{16,0},{1,17},{17,1},{2,18},{18,2},{3,19},{19,3},{4,20},{20... | collective-permute-start | bytes 786440 | tf_op jit(solution)/shard_map/ppermute | solution.py:286
  122.2 7.6 %collective-permute-start.50 = (bf16[256,512]{1,0:T(8,128)(2,1)S(1)}, bf16[256,512]{1,0:T(8,128)(2,1)S(1)}, u32[]{:S(2)}, u32[]{:S(2)}) collective-permute-start(bf16[256,512]{1,0:T(8,128)(2,1)S(1)} %get-tuple-element.170), channel_id=1, source_target_pairs={{0,4},{4,8},{8,12},{12,14},{14,10},{10,6},{6,2},{2,0},{1,5},{5,9},... | collective-permute-start | bytes 786440 | tf_op jit(solution)/shard_map/ppermute | solution.py:277
  123.6 7.3 %collective-permute-start.51 = (bf16[256,512]{1,0:T(8,128)(2,1)S(1)}, bf16[256,512]{1,0:T(8,128)(2,1)S(1)}, u32[]{:S(2)}, u32[]{:S(2)}) collective-permute-start(bf16[256,512]{1,0:T(8,128)(2,1)S(1)} %get-tuple-element.169), channel_id=1, source_target_pairs={{4,0},{8,4},{12,8},{14,12},{10,14},{6,10},{2,6},{0,2},{5,1},{9,5},... | collective-permute-start | bytes 786440 | tf_op jit(solution)/shard_map/ppermute | solution.py:280
  124.3 6.6 %collective-permute-start.44 = (bf16[256,512]{1,0:T(8,128)(2,1)S(1)}, bf16[256,512]{1,0:T(8,128)(2,1)S(1)}, u32[]{:S(2)}, u32[]{:S(2)}) collective-permute-start(bf16[256,512]{1,0:T(8,128)(2,1)S(1)} %get-tuple-element.162), channel_id=1, source_target_pairs={{0,1},{1,0},{2,3},{3,2},{4,5},{5,4},{6,7},{7,6},{8,9},{9,8},{10,11... | collective-permute-start | bytes 786440 | tf_op jit(solution)/shard_map/ppermute | solution.py:283
  (13 other events, 116.8 us)

commit v5 on v4

--- a/solution.py
+++ b/solution.py
@@ -219,15 +219,26 @@
         arrived(i)
 
 
-def final_body(info, kept, mine, back, full, out, mixture):
-    core, half = info[0], mine.shape[1]
-    mixture[:, pl.ds(pl.multiple_of(core * half, half), half)] = mine[...]
-    mixture[:, pl.ds(pl.multiple_of((1 - core) * half, half), half)] = back[...]
-    step = 512
+def half_body(info, kept, mine, full, out):
+    half, step = mine.shape[1], 512
+    rows = pl.ds(pl.multiple_of(info[0] * half, half), half)
     for i in range(full.shape[1] // step):
         at = slice(i * step, (i + 1) * step)
-        branch = jnp.dot(mixture[...], full[:, at], preferred_element_type=F32)
-        out[:, at] = (kept[:, at].astype(F32) + branch).astype(BF16)
+        branch = jnp.dot(mine[...], full[rows, at], preferred_element_type=F32)
+        out[:, at] = kept[:, at].astype(F32) + branch
+
+
+def final_body(info, partial, back, full, out, ready, done):
+    half, step, copies = back.shape[1], 512, []
+    rows = pl.ds(pl.multiple_of((1 - info[0]) * half, half), half)
+    for i in range(full.shape[1] // step):
+        at = slice(i * step, (i + 1) * step)
+        branch = jnp.dot(back[...], full[rows, at], preferred_element_type=F32)
+        ready[:, at] = (partial[:, at] + branch).astype(BF16)
+        copies.append(pltpu.make_async_copy(ready.at[:, at], out.at[:, at], done.at[i]))
+        copies[-1].start()
+    for copy in copies:
+        copy.wait()
 
 
 def after(x, *others):
@@ -530,14 +541,25 @@
             to_above, to_below = step(above, below, *beside)
         mixture = total(done[0][0], given0, to_above)
         mixture = (mixture + to_below.astype(F32)).astype(BF16)
-        return kernel_call(
+        partial = kernel_call(
+            half_body,
+            shape(rows, columns, kind=F32),
+            4,
+            rows * width * columns,
+            width * columns + 6 * rows * columns,
+        )(info, kept, mixture, full)
+        back, partial = both(swap(mixture), partial)
+        return pl.pallas_call(
             final_body,
-            shape(rows, columns),
-            5,
-            2 * rows * width * columns,
-            2 * width * columns + 4 * rows * columns,
-            [pltpu.VMEM((rows, width), BF16)],
-        )(info, kept, mixture, swap(mixture), full)
+            out_shape=shape(rows, columns),
+            in_specs=[SMEM] + [VMEM] * 3,
+            out_specs=ANY,
+            scratch_shapes=[
+                pltpu.VMEM((rows, columns), BF16),
+                pltpu.SemaphoreType.DMA((columns // 512,)),
+            ],
+            compiler_params=pltpu.CompilerParams(vmem_limit_bytes=LIMIT),
+        )(info, partial, back, full)
 
     return local
 

time: 136 us -> 135 us (level)
    pallas_call x1 -> x2, Pallas kernels: 2.82 us -> 3.25 us  [the longest x1 2 us: local(): pl.pallas_call(final_body, out_shape=shape(rows, columns), in_specs=[SMEM...]
  transfers between devices with their start and end apart: 54 -> 54, of which waited for: 29 -> 29; matrix products, arithmetic and copies ran while one was open for 2% -> 2% of each run, Pallas kernels for 25% -> 26%
where the time goes in v5:
time: 135 us
  waiting for transfers between devices  44.7 us (33%)
  starting transfers between devices  43.2 us (32%)
  Pallas kernels  41.5 us (31%)
  local copies, waits for them, and re-layouts  3.25 us (2%)
  other arithmetic  1.52 us (1%)
    ppermute x16, starting transfers between devices, up(): return lax.ppermute(x, 'wide', up_perm)  23.6 us
    ppermute x16, waiting for transfers between devices, up(): return lax.ppermute(x, 'wide', up_perm)  20 us
    pallas_call x5, Pallas kernels, expert(): kernel_call(functools.partial(expert_body, columns), (out, out), 4 + 2 *...  17 us
    ppermute x16, waiting for transfers between devices, down(): return lax.ppermute(x, 'wide', down_perm)  12.6 us
    ppermute x6, waiting for transfers between devices, across(): return lax.ppermute(x, 'groups', [(i, i ^ 1) for i in range(groups)])  11.7 us
    ppermute x16, starting transfers between devices, down(): return lax.ppermute(x, 'wide', down_perm)  9.31 us
    ppermute x6, starting transfers between devices, across(): return lax.ppermute(x, 'groups', [(i, i ^ 1) for i in range(groups)])  7.95 us
    pallas_call x2, Pallas kernels, norm(): kernel_call(norm_body, shape(*x.shape), 3, 8 * x.size, 4 * x.size)  5.32 us
  transfers between devices with their start and end apart: 54, of which 29 were waited for; matrix products, arithmetic and copies ran while one was open for 2% of the time, Pallas kernels for 26%

profile of v5, /device:TPU:0, one launch (start us, length us, event | category | flops | bytes accessed | tf_op | source)
XLA Modules:
  0.0 134.8 jit_solution(6977103198154375425)
XLA Ops:
  0.6 3.1 %shard_map.91 = (bf16[128,4096]{1,0:T(8,128)(2,1)}, bf16[544,256]{1,0:T(8,128)(2,1)}) custom-call(s32[2]{0:T(128)} %pad_add_fusion.1.info, s32[4,256]{1,0:T(4,128)} %bitcast.25, f32[4,256]{1,0:T(4,128)} %bitcast.26, bf16[256,4096]{1,0:T(8,128)(2,1)} %tokens.3, bf16[512,1024]{1,0:T(8,128)(2,1)} %w_in.1), custom_call_target="tpu_custom_call" | custom-call | tf_op jit(solution)/shard_map/pallas_call | solution.py:345
  3.7 3.0 %collective-permute-start.8 = (bf16[128,4096]{1,0:T(8,128)(2,1)}, bf16[128,4096]{1,0:T(8,128)(2,1)}, u32[]{:S(2)}, u32[]{:S(2)}) collective-permute-start(bf16[128,4096]{1,0:T(8,128)(2,1)} %get-tuple-element.112), channel_id=1, source_target_pairs={{0,16},{16,0},{1,17},{17,1},{2,18},{18,2},{3,19},{19,3},{4,20},{20... | collective-permute-start | bytes 3145736 | tf_op jit(solution)/shard_map/ppermute | solution.py:297
  6.7 1.6 %collective-permute-start = (bf16[544,256]{1,0:T(8,128)(2,1)}, bf16[544,256]{1,0:T(8,128)(2,1)S(1)}, u32[]{:S(2)}, u32[]{:S(2)}) collective-permute-start(bf16[544,256]{1,0:T(8,128)(2,1)} %get-tuple-element.95.refs_0_.refs_2_), channel_id=1, source_target_pairs={{0,4},{4,8},{8,12},{12,14},{14,10},{10,6},{6,2},{2,0},{1,5},{5,9},... | collective-permute-start | bytes 835592 | tf_op jit(solution)/shard_map/ppermute | solution.py:288
  9.4 1.6 %collective-permute-start.4 = (bf16[128,1024]{1,0:T(8,128)(2,1)}, bf16[128,1024]{1,0:T(8,128)(2,1)}, u32[]{:S(2)}, u32[]{:S(2)}) collective-permute-start(bf16[128,1024]{1,0:T(8,128)(2,1)} %constant_dynamic-slice_fusion), channel_id=1, source_target_pairs={{0,4},{4,8},{8,12},{12,14},{14,10},{10,6},{6,2},{2,0},{1,5},{5,9},... | collective-permute-start | bytes 786440 | tf_op jit(solution)/shard_map/ppermute | solution.py:288
  12.2 1.6 %copy-done = bf16[256,4096]{1,0:T(8,128)(2,1)S(1)} copy-done((bf16[256,4096]{1,0:T(8,128)(2,1)S(1)}, bf16[256,4096]{1,0:T(8,128)(2,1)}, u32[]{:S(2)}) %copy-start) | copy-done | bytes 2097176
  13.8 2.9 %shard_map.92.normed = bf16[256,4096]{1,0:T(8,128)(2,1)S(1)} custom-call(s32[11]{0:T(128)S(1)} %pad_add_fusion.info, bf16[256,4096]{1,0:T(8,128)(2,1)S(1)} %copy-done, f32[1,4096]{1,0:T(1,128)S(1)} %bitcast.23), custom_call_target="tpu_custom_call" | custom-call | flops 8388608 | bytes 4194304 | tf_op jit(solution)/shard_map/pallas_call | solution.py:360
  16.8 1.3 collective-permute-done.1.refs_2_.refs_4_
  18.1 1.6 %collective-permute-start.2 = (bf16[544,256]{1,0:T(8,128)(2,1)S(1)}, bf16[544,256]{1,0:T(8,128)(2,1)}, u32[]{:S(2)}, u32[]{:S(2)}) collective-permute-start(bf16[544,256]{1,0:T(8,128)(2,1)S(1)} %collective-permute-done.refs_1_.refs_3_), channel_id=1, source_target_pairs={{0,4},{4,8},{8,12},{12,14},{14,10},{10,6},{6,2},{2,0},{1,5},{5,9},... | collective-permute-start | bytes 835592 | tf_op jit(solution)/shard_map/ppermute | solution.py:288
  20.1 2.1 %collective-permute-done.4.first.rest_1_ = bf16[128,1024]{1,0:T(8,128)(2,1)} collective-permute-done((bf16[128,1024]{1,0:T(8,128)(2,1)}, bf16[128,1024]{1,0:T(8,128)(2,1)}, u32[]{:S(2)}, u32[]{:S(2)}) %collective-permute-start.4) | collective-permute-done | bytes 262176 | tf_op jit(solution)/shard_map/ppermute | solution.py:288
  22.2 1.6 %collective-permute-done.5.second.rest_2_ = bf16[128,1024]{1,0:T(8,128)(2,1)} collective-permute-done((bf16[128,1024]{1,0:T(8,128)(2,1)}, bf16[128,1024]{1,0:T(8,128)(2,1)}, u32[]{:S(2)}, u32[]{:S(2)}) %collective-permute-start.5) | collective-permute-done | bytes 262176 | tf_op jit(solution)/shard_map/ppermute | solution.py:291
  23.8 1.6 %shard_map.94 = bf16[256,1024]{1,0:T(8,128)(2,1)S(1)} custom-call(s32[11]{0:T(128)S(1)} %pad_add_fusion.info, bf16[128,1024]{1,0:T(8,128)(2,1)} %collective-permute-done.4.first.rest_1_, bf16[128,1024]{1,0:T(8,128)(2,1)} %collective-permute-done.5.second.rest_2_), custom_call_target="tpu_custom_call" | custom-call | flops 262144 | bytes 1048576 | tf_op jit(solution)/shard_map/pallas_call | solution.py:327
  26.7 1.3 collective-permute-done.3.refs_1_.refs_6_
  28.0 1.6 %collective-permute-start.6 = (bf16[544,256]{1,0:T(8,128)(2,1)}, bf16[544,256]{1,0:T(8,128)(2,1)S(1)}, u32[]{:S(2)}, u32[]{:S(2)}) collective-permute-start(bf16[544,256]{1,0:T(8,128)(2,1)} %collective-permute-done.2.refs_0_.refs_5_), channel_id=1, source_target_pairs={{0,4},{4,8},{8,12},{12,14},{14,10},{10,6},{6,2},{2,0},{1,5},{5,9},... | collective-permute-start | bytes 835592 | tf_op jit(solution)/shard_map/ppermute | solution.py:288
  30.0 1.4 %shard_map.95 = (f32[256,256]{1,0:T(8,128)S(1)}, f32[5,256]{1,0:T(8,128)S(1)}) custom-call(s32[11]{0:T(128)S(1)} %pad_add_fusion.info, bf16[256,4096]{1,0:T(8,128)(2,1)S(1)} %shard_map.92.normed, bf16[544,256]{1,0:T(8,128)(2,1)} %collective-permute-done.2.refs_0_.refs_5_, bf16[544,256]{1,0:T(8,128)(2,1)} %collective-permute-done.3.refs_1_.refs_6_, ...), custom_call_target="tpu_custom_call" | custom-call | flops 134217728 | bytes 1048576 | tf_op jit(solution)/shard_map/pallas_call | solution.py:392
  31.4 2.4 %shard_map.96.refs_0_ = bf16[128,4096]{1,0:T(8,128)(2,1)S(1)} custom-call(s32[11]{0:T(128)S(1)} %pad_add_fusion.info, bf16[128,4096]{1,0:T(8,128)(2,1)} %collective-permute-done.8.tokens, f32[1,4096]{1,0:T(1,128)S(1)} %bitcast.24), custom_call_target="tpu_custom_call" | custom-call | flops 4194304 | bytes 2097152 | tf_op jit(solution)/shard_map/pallas_call | solution.py:360
  33.8 1.3 collective-permute-done.6.refs_7_.refs_0_
  35.1 1.3 collective-permute-done.7.refs_8_.refs_1_
  37.0 1.6 %collective-permute-start.9 = (bf16[256,256]{1,0:T(8,128)(2,1)S(1)}, bf16[256,256]{1,0:T(8,128)(2,1)S(1)}, u32[]{:S(2)}, u32[]{:S(2)}) collective-permute-start(bf16[256,256]{1,0:T(8,128)(2,1)S(1)} %slice.84), channel_id=1, source_target_pairs={{0,4},{4,8},{8,12},{12,14},{14,10},{10,6},{6,2},{2,0},{1,5},{5,9},... | collective-permute-start | bytes 393224 | tf_op jit(solution)/shard_map/ppermute | solution.py:288
  39.5 2.7 %shard_map.97 = (f32[256,256]{1,0:T(8,128)S(1)}, bf16[256,512]{1,0:T(8,128)(2,1)S(1)}) custom-call(s32[11]{0:T(128)S(1)} %pad_add_fusion.info, bf16[128,4096]{1,0:T(8,128)(2,1)S(1)} %shard_map.96.refs_0_, bf16[128,4096]{1,0:T(8,128)(2,1)S(1)} %collective-permute-done.11.refs_1_, bf16[544,256]{1,0:T(8,128)(2,1)S(1)} %copy-done.5, ...), custom_call_target="tpu_custom_call" | custom-call | flops 536870912 | bytes 4194304 | tf_op jit(solution)/shard_map/pallas_call | solution.py:376
  44.1 1.6 %collective-permute-start.15 = (bf16[128,1024]{1,0:T(8,128)(2,1)}, bf16[128,1024]{1,0:T(8,128)(2,1)S(1)}, u32[]{:S(2)}, u32[]{:S(2)}) collective-permute-start(bf16[128,1024]{1,0:T(8,128)(2,1)} %collective-permute-done.4.first.rest_1_), channel_id=1, source_target_pairs={{0,4},{4,8},{8,12},{12,14},{14,10},{10,6},{6,2},{2,0},{1,5},{5,9},... | collective-permute-start | bytes 786440 | tf_op jit(solution)/shard_map/ppermute | solution.py:288
  46.2 2.6 %collective-permute-done.12.refs_2_ = bf16[256,256]{1,0:T(8,128)(2,1)S(1)} collective-permute-done((bf16[256,256]{1,0:T(8,128)(2,1)S(1)}, bf16[256,256]{1,0:T(8,128)(2,1)S(1)}, u32[]{:S(2)}, u32[]{:S(2)}) %collective-permute-start.12) | collective-permute-done | bytes 131104 | tf_op jit(solution)/shard_map/ppermute | solution.py:297
  49.5 1.6 %collective-permute-start.13 = (bf16[256,512]{1,0:T(8,128)(2,1)S(1)}, bf16[256,512]{1,0:T(8,128)(2,1)S(1)}, u32[]{:S(2)}, u32[]{:S(2)}) collective-permute-start(bf16[256,512]{1,0:T(8,128)(2,1)S(1)} %get-tuple-element.122.refs_0_), channel_id=1, source_target_pairs={{0,4},{4,8},{8,12},{12,14},{14,10},{10,6},{6,2},{2,0},{1,5},{5,9},... | collective-permute-start | bytes 786440 | tf_op jit(solution)/shard_map/ppermute | solution.py:288
  51.6 1.4 %collective-permute-done.15.first.rest_3_ = bf16[128,1024]{1,0:T(8,128)(2,1)S(1)} collective-permute-done((bf16[128,1024]{1,0:T(8,128)(2,1)}, bf16[128,1024]{1,0:T(8,128)(2,1)S(1)}, u32[]{:S(2)}, u32[]{:S(2)}) %collective-permute-start.15) | collective-permute-done | bytes 262176 | tf_op jit(solution)/shard_map/ppermute | solution.py:288
  53.0 2.1 %collective-permute-start.20 = (bf16[256,1024]{1,0:T(8,128)(2,1)S(1)}, bf16[256,1024]{1,0:T(8,128)(2,1)S(1)}, u32[]{:S(2)}, u32[]{:S(2)}) collective-permute-start(bf16[256,1024]{1,0:T(8,128)(2,1)S(1)} %shard_map.94), channel_id=1, source_target_pairs={{0,16},{16,0},{1,17},{17,1},{2,18},{18,2},{3,19},{19,3},{4,20},{20... | collective-permute-start | bytes 1572872 | tf_op jit(solution)/shard_map/ppermute | solution.py:297
  55.1 2.5 %collective-permute-done.13.refs_0_ = bf16[256,512]{1,0:T(8,128)(2,1)S(1)} collective-permute-done((bf16[256,512]{1,0:T(8,128)(2,1)S(1)}, bf16[256,512]{1,0:T(8,128)(2,1)S(1)}, u32[]{:S(2)}, u32[]{:S(2)}) %collective-permute-start.13) | collective-permute-done | bytes 262176 | tf_op jit(solution)/shard_map/ppermute | solution.py:288
  57.6 1.3 collective-permute-done.14.refs_1_
  58.9 1.5 %collective-permute-start.18 = (bf16[256,512]{1,0:T(8,128)(2,1)S(1)}, bf16[256,512]{1,0:T(8,128)(2,1)S(1)}, u32[]{:S(2)}, u32[]{:S(2)}) collective-permute-start(bf16[256,512]{1,0:T(8,128)(2,1)S(1)} %collective-permute-done.13.refs_0_), channel_id=1, source_target_pairs={{0,4},{4,8},{8,12},{12,14},{14,10},{10,6},{6,2},{2,0},{1,5},{5,9},... | collective-permute-start | bytes 786440 | tf_op jit(solution)/shard_map/ppermute | solution.py:288
  62.1 3.7 %collective-permute-done.18.refs_0_ = bf16[256,512]{1,0:T(8,128)(2,1)S(1)} collective-permute-done((bf16[256,512]{1,0:T(8,128)(2,1)S(1)}, bf16[256,512]{1,0:T(8,128)(2,1)S(1)}, u32[]{:S(2)}, u32[]{:S(2)}) %collective-permute-start.18) | collective-permute-done | bytes 262176 | tf_op jit(solution)/shard_map/ppermute | solution.py:288
  67.0 1.4 %collective-permute-start.21 = (bf16[256,512]{1,0:T(8,128)(2,1)S(1)}, bf16[256,512]{1,0:T(8,128)(2,1)S(1)}, u32[]{:S(2)}, u32[]{:S(2)}) collective-permute-start(bf16[256,512]{1,0:T(8,128)(2,1)S(1)} %collective-permute-done.18.refs_0_), channel_id=1, source_target_pairs={{0,4},{4,8},{8,12},{12,14},{14,10},{10,6},{6,2},{2,0},{1,5},{5,9},... | collective-permute-start | bytes 786440 | tf_op jit(solution)/shard_map/ppermute | solution.py:288
  69.1 4.1 %shard_map.102 = (bf16[512,512]{1,0:T(8,128)(2,1)S(1)}, bf16[512,512]{1,0:T(8,128)(2,1)S(1)}) custom-call(s32[11]{0:T(128)S(1)} %pad_add_fusion.info, bf16[256,512]{1,0:T(8,128)(2,1)S(1)} %collective-permute-done.13.refs_0_, bf16[256,512]{1,0:T(8,128)(2,1)S(1)} %collective-permute-done.14.refs_1_, bf16[256,512]{1,0:T(8,128)(2,1)S(1)} %collective-permute-done.23.refs_2_, ...), custom_call_target="tpu_custom_call" | custom-call | flops 2818572288 | bytes 7602176 | tf_op jit(solution)/shard_map/pallas_call | solution.py:446
  73.4 1.4 %collective-permute-done.22.refs_1_ = bf16[256,512]{1,0:T(8,128)(2,1)S(1)} collective-permute-done((bf16[256,512]{1,0:T(8,128)(2,1)S(1)}, bf16[256,512]{1,0:T(8,128)(2,1)S(1)}, u32[]{:S(2)}, u32[]{:S(2)}) %collective-permute-start.22) | collective-permute-done | bytes 262176 | tf_op jit(solution)/shard_map/ppermute | solution.py:291
  74.8 2.6 %collective-permute-done.25.rest_10_ = bf16[256,1024]{1,0:T(8,128)(2,1)S(1)} collective-permute-done((bf16[256,1024]{1,0:T(8,128)(2,1)S(1)}, bf16[256,1024]{1,0:T(8,128)(2,1)S(1)}, u32[]{:S(2)}, u32[]{:S(2)}) %collective-permute-start.25) | collective-permute-done | bytes 524320 | tf_op jit(solution)/shard_map/ppermute | solution.py:297
  77.9 1.5 %collective-permute-start.29 = (bf16[128,512]{1,0:T(8,128)(2,1)S(1)}, bf16[128,512]{1,0:T(8,128)(2,1)S(1)}, u32[]{:S(2)}, u32[]{:S(2)}) collective-permute-start(bf16[128,512]{1,0:T(8,128)(2,1)S(1)} %slice.89), channel_id=1, source_target_pairs={{0,4},{4,8},{8,12},{12,14},{14,10},{10,6},{6,2},{2,0},{1,5},{5,9},... | collective-permute-start | bytes 393224 | tf_op jit(solution)/shard_map/ppermute | solution.py:288
  80.0 4.1 %shard_map.103 = (bf16[512,512]{1,0:T(8,128)(2,1)S(1)}, bf16[512,512]{1,0:T(8,128)(2,1)S(1)}) custom-call(s32[11]{0:T(128)S(1)} %pad_add_fusion.info, bf16[256,512]{1,0:T(8,128)(2,1)S(1)} %collective-permute-done.21.refs_0_, bf16[256,512]{1,0:T(8,128)(2,1)S(1)} %collective-permute-done.22.refs_1_, bf16[256,512]{1,0:T(8,128)(2,1)S(1)} %collective-permute-done.26.refs_2_, ...), custom_call_target="tpu_custom_call" | custom-call | flops 2818572288 | bytes 7602176 | tf_op jit(solution)/shard_map/pallas_call | solution.py:446
  85.1 1.4 %collective-permute-start.34 = (bf16[128,1024]{1,0:T(8,128)(2,1)S(1)}, bf16[128,1024]{1,0:T(8,128)(2,1)S(1)}, u32[]{:S(2)}, u32[]{:S(2)}) collective-permute-start(bf16[128,1024]{1,0:T(8,128)(2,1)S(1)} %collective-permute-done.15.first.rest_3_), channel_id=1, source_target_pairs={{0,4},{4,8},{8,12},{12,14},{14,10},{10,6},{6,2},{2,0},{1,5},{5,9},... | collective-permute-start | bytes 786440 | tf_op jit(solution)/shard_map/ppermute | solution.py:288
  87.1 2.4 %shard_map.104 = (bf16[256,512]{1,0:T(8,128)(2,1)S(1)}, bf16[256,512]{1,0:T(8,128)(2,1)S(1)}) custom-call(s32[11]{0:T(128)S(1)} %pad_add_fusion.info, bf16[128,512]{1,0:T(8,128)(2,1)S(1)} %collective-permute-done.29.refs_0_, bf16[128,512]{1,0:T(8,128)(2,1)S(1)} %collective-permute-done.30.refs_1_, bf16[128,512]{1,0:T(8,128)(2,1)S(1)} %collective-permute-done.31.refs_2_, ...), custom_call_target="tpu_custom_call" | custom-call | flops 1409286144 | bytes 6553600 | tf_op jit(solution)/shard_map/pallas_call | solution.py:446
  90.2 3.1 %collective-permute-done.34.first.rest_5_ = bf16[128,1024]{1,0:T(8,128)(2,1)S(1)} collective-permute-done((bf16[128,1024]{1,0:T(8,128)(2,1)S(1)}, bf16[128,1024]{1,0:T(8,128)(2,1)S(1)}, u32[]{:S(2)}, u32[]{:S(2)}) %collective-permute-start.34) | collective-permute-done | bytes 262176 | tf_op jit(solution)/shard_map/ppermute | solution.py:288
  94.5 1.4 %collective-permute-start.36 = (bf16[128,512]{1,0:T(8,128)(2,1)S(1)}, bf16[128,512]{1,0:T(8,128)(2,1)S(1)}, u32[]{:S(2)}, u32[]{:S(2)}) collective-permute-start(bf16[128,512]{1,0:T(8,128)(2,1)S(1)} %get-tuple-element.180), channel_id=1, source_target_pairs={{0,4},{4,8},{8,12},{12,14},{14,10},{10,6},{6,2},{2,0},{1,5},{5,9},... | collective-permute-start | bytes 393224 | tf_op jit(solution)/shard_map/ppermute | solution.py:288
  96.7 1.4 %collective-permute-start.40 = (bf16[64,1024]{1,0:T(8,128)(2,1)S(1)}, bf16[64,1024]{1,0:T(8,128)(2,1)S(1)}, u32[]{:S(2)}, u32[]{:S(2)}) collective-permute-start(bf16[64,1024]{1,0:T(8,128)(2,1)S(1)} %slice.93), channel_id=1, source_target_pairs={{0,4},{4,8},{8,12},{12,14},{14,10},{10,6},{6,2},{2,0},{1,5},{5,9},... | collective-permute-start | bytes 393224 | tf_op jit(solution)/shard_map/ppermute | solution.py:288
  98.7 4.1 %shard_map.105 = (bf16[512,512]{1,0:T(8,128)(2,1)S(1)}, bf16[512,512]{1,0:T(8,128)(2,1)S(1)}) custom-call(s32[11]{0:T(128)S(1)} %pad_add_fusion.info, bf16[256,512]{1,0:T(8,128)(2,1)S(1)} %collective-permute-done.18.refs_0_, bf16[256,512]{1,0:T(8,128)(2,1)S(1)} %collective-permute-done.19.refs_1_, bf16[256,512]{1,0:T(8,128)(2,1)S(1)} %collective-permute-done.38.refs_2_, ...), custom_call_target="tpu_custom_call" | custom-call | flops 2818572288 | bytes 7602176 | tf_op jit(solution)/shard_map/pallas_call | solution.py:446
  103.5 1.4 %collective-permute-start.42 = (bf16[256,512]{1,0:T(8,128)(2,1)S(1)}, bf16[256,512]{1,0:T(8,128)(2,1)S(1)}, u32[]{:S(2)}, u32[]{:S(2)}) collective-permute-start(bf16[256,512]{1,0:T(8,128)(2,1)S(1)} %pad_maximum_fusion), channel_id=1, source_target_pairs={{0,4},{4,8},{8,12},{12,14},{14,10},{10,6},{6,2},{2,0},{1,5},{5,9},... | collective-permute-start | bytes 786440 | tf_op jit(solution)/shard_map/ppermute | solution.py:288
  107.8 4.1 %collective-permute-done.42 = bf16[256,512]{1,0:T(8,128)(2,1)S(1)} collective-permute-done((bf16[256,512]{1,0:T(8,128)(2,1)S(1)}, bf16[256,512]{1,0:T(8,128)(2,1)S(1)}, u32[]{:S(2)}, u32[]{:S(2)}) %collective-permute-start.42) | collective-permute-done | bytes 262176 | tf_op jit(solution)/shard_map/ppermute | solution.py:288
  115.9 2.4 %shard_map.108 = (bf16[256,512]{1,0:T(8,128)(2,1)S(1)}, bf16[256,512]{1,0:T(8,128)(2,1)S(1)}) custom-call(s32[11]{0:T(128)S(1)} %pad_add_fusion.info, bf16[256,512]{1,0:T(8,128)(2,1)S(1)} %get-tuple-element.122.refs_0_, bf16[256,512]{1,0:T(8,128)(2,1)S(1)} %collective-permute-done.17.refs_1_, f32[256,8]{1,0:T(8,128)S(1)} %get-tuple-element.134.refs_4_.refs_2_, ...), custom_call_target="tpu_custom_call" | custom-call | flops 1409286144 | bytes 6553600 | tf_op jit(solution)/shard_map/pallas_call | solution.py:446
  118.3 3.7 %collective-permute-done.49.rest_11_ = bf16[256,1024]{1,0:T(8,128)(2,1)S(1)} collective-permute-done((bf16[256,1024]{1,0:T(8,128)(2,1)S(1)}, bf16[256,1024]{1,0:T(8,128)(2,1)S(1)}, u32[]{:S(2)}, u32[]{:S(2)}) %collective-permute-start.49) | collective-permute-done | bytes 524320 | tf_op jit(solution)/shard_map/ppermute | solution.py:297
  122.3 1.4 %collective-permute-start.50 = (bf16[256,512]{1,0:T(8,128)(2,1)S(1)}, bf16[256,512]{1,0:T(8,128)(2,1)S(1)}, u32[]{:S(2)}, u32[]{:S(2)}) collective-permute-start(bf16[256,512]{1,0:T(8,128)(2,1)S(1)} %get-tuple-element.174), channel_id=1, source_target_pairs={{0,4},{4,8},{8,12},{12,14},{14,10},{10,6},{6,2},{2,0},{1,5},{5,9},... | collective-permute-start | bytes 786440 | tf_op jit(solution)/shard_map/ppermute | solution.py:288
  124.4 2.9 %collective-permute-done.52.rest_12_ = bf16[128,1024]{1,0:T(8,128)(2,1)S(1)} collective-permute-done((bf16[128,1024]{1,0:T(8,128)(2,1)S(1)}, bf16[128,1024]{1,0:T(8,128)(2,1)S(1)}, u32[]{:S(2)}, u32[]{:S(2)}) %collective-permute-start.52) | collective-permute-done | bytes 262176 | tf_op jit(solution)/shard_map/ppermute | solution.py:297
  127.3 1.8 %shard_map.109.full = bf16[1024,2048]{1,0:T(8,128)(2,1)S(1)} custom-call(s32[11]{0:T(128)S(1)} %constant_dynamic-update-slice_fusion.info, bf16[128,2048]{1,0:T(8,128)(2,1)S(1)} %copy-done.4, bf16[128,1024]{1,0:T(8,128)(2,1)} %collective-permute-done.4.first.rest_1_, bf16[128,1024]{1,0:T(8,128)(2,1)} %collective-permute-done.5.second.rest_2_, ...), custom_call_target="tpu_custom_call" | custom-call | flops 2097152 | bytes 8388608 | tf_op jit(solution)/shard_map/pallas_call | solution.py:531
  132.6 2.0 %shard_map.111 = bf16[256,2048]{1,0:T(8,128)(2,1)} custom-call(s32[11]{0:T(128)S(1)} %pad_add_fusion.info, f32[256,2048]{1,0:T(8,128)S(1)} %shard_map.110.partial, bf16[256,512]{1,0:T(8,128)(2,1)S(1)} %collective-permute-done.53.back, bf16[1024,2048]{1,0:T(8,128)(2,1)S(1)} %shard_map.109.full), custom_call_target="tpu_custom_call" | custom-call | tf_op jit(solution)/shard_map/pallas_call | solution.py:552
  (120 shorter events, 32.0 us)
Async XLA Ops:
  3.7 27.7 %collective-permute-start.8 = (bf16[128,4096]{1,0:T(8,128)(2,1)}, bf16[128,4096]{1,0:T(8,128)(2,1)}, u32[]{:S(2)}, u32[]{:S(2)}) collective-permute-start(bf16[128,4096]{1,0:T(8,128)(2,1)} %get-tuple-element.112), channel_id=1, source_target_pairs={{0,16},{16,0},{1,17},{17,1},{2,18},{18,2},{3,19},{19,3},{4,20},{20... | collective-permute-start | bytes 3145736 | tf_op jit(solution)/shard_map/ppermute | solution.py:297
  6.7 10.1 %collective-permute-start = (bf16[544,256]{1,0:T(8,128)(2,1)}, bf16[544,256]{1,0:T(8,128)(2,1)S(1)}, u32[]{:S(2)}, u32[]{:S(2)}) collective-permute-start(bf16[544,256]{1,0:T(8,128)(2,1)} %get-tuple-element.95.refs_0_.refs_2_), channel_id=1, source_target_pairs={{0,4},{4,8},{8,12},{12,14},{14,10},{10,6},{6,2},{2,0},{1,5},{5,9},... | collective-permute-start | bytes 835592 | tf_op jit(solution)/shard_map/ppermute | solution.py:288
  8.3 9.8 %collective-permute-start.1 = (bf16[544,256]{1,0:T(8,128)(2,1)}, bf16[544,256]{1,0:T(8,128)(2,1)S(1)}, u32[]{:S(2)}, u32[]{:S(2)}) collective-permute-start(bf16[544,256]{1,0:T(8,128)(2,1)} %get-tuple-element.95.refs_0_.refs_2_), channel_id=1, source_target_pairs={{4,0},{8,4},{12,8},{14,12},{10,14},{6,10},{2,6},{0,2},{5,1},{9,5},... | collective-permute-start | bytes 835592 | tf_op jit(solution)/shard_map/ppermute | solution.py:291
  9.4 12.8 %collective-permute-start.4 = (bf16[128,1024]{1,0:T(8,128)(2,1)}, bf16[128,1024]{1,0:T(8,128)(2,1)}, u32[]{:S(2)}, u32[]{:S(2)}) collective-permute-start(bf16[128,1024]{1,0:T(8,128)(2,1)} %constant_dynamic-slice_fusion), channel_id=1, source_target_pairs={{0,4},{4,8},{8,12},{12,14},{14,10},{10,6},{6,2},{2,0},{1,5},{5,9},... | collective-permute-start | bytes 786440 | tf_op jit(solution)/shard_map/ppermute | solution.py:288
  11.0 12.8 %collective-permute-start.5 = (bf16[128,1024]{1,0:T(8,128)(2,1)}, bf16[128,1024]{1,0:T(8,128)(2,1)}, u32[]{:S(2)}, u32[]{:S(2)}) collective-permute-start(bf16[128,1024]{1,0:T(8,128)(2,1)} %constant_dynamic-slice_fusion), channel_id=1, source_target_pairs={{4,0},{8,4},{12,8},{14,12},{10,14},{6,10},{2,6},{0,2},{5,1},{9,5},... | collective-permute-start | bytes 786440 | tf_op jit(solution)/shard_map/ppermute | solution.py:291
  18.1 8.6 %collective-permute-start.2 = (bf16[544,256]{1,0:T(8,128)(2,1)S(1)}, bf16[544,256]{1,0:T(8,128)(2,1)}, u32[]{:S(2)}, u32[]{:S(2)}) collective-permute-start(bf16[544,256]{1,0:T(8,128)(2,1)S(1)} %collective-permute-done.refs_1_.refs_3_), channel_id=1, source_target_pairs={{0,4},{4,8},{8,12},{12,14},{14,10},{10,6},{6,2},{2,0},{1,5},{5,9},... | collective-permute-start | bytes 835592 | tf_op jit(solution)/shard_map/ppermute | solution.py:288
  19.6 8.4 %collective-permute-start.3 = (bf16[544,256]{1,0:T(8,128)(2,1)S(1)}, bf16[544,256]{1,0:T(8,128)(2,1)}, u32[]{:S(2)}, u32[]{:S(2)}) collective-permute-start(bf16[544,256]{1,0:T(8,128)(2,1)S(1)} %collective-permute-done.1.refs_2_.refs_4_), channel_id=1, source_target_pairs={{4,0},{8,4},{12,8},{14,12},{10,14},{6,10},{2,6},{0,2},{5,1},{9,5},... | collective-permute-start | bytes 835592 | tf_op jit(solution)/shard_map/ppermute | solution.py:291
  28.0 7.1 %collective-permute-start.6 = (bf16[544,256]{1,0:T(8,128)(2,1)}, bf16[544,256]{1,0:T(8,128)(2,1)S(1)}, u32[]{:S(2)}, u32[]{:S(2)}) collective-permute-start(bf16[544,256]{1,0:T(8,128)(2,1)} %collective-permute-done.2.refs_0_.refs_5_), channel_id=1, source_target_pairs={{0,4},{4,8},{8,12},{12,14},{14,10},{10,6},{6,2},{2,0},{1,5},{5,9},... | collective-permute-start | bytes 835592 | tf_op jit(solution)/shard_map/ppermute | solution.py:288
  29.6 6.8 %collective-permute-start.7 = (bf16[544,256]{1,0:T(8,128)(2,1)}, bf16[544,256]{1,0:T(8,128)(2,1)S(1)}, u32[]{:S(2)}, u32[]{:S(2)}) collective-permute-start(bf16[544,256]{1,0:T(8,128)(2,1)} %collective-permute-done.3.refs_1_.refs_6_), channel_id=1, source_target_pairs={{4,0},{8,4},{12,8},{14,12},{10,14},{6,10},{2,6},{0,2},{5,1},{9,5},... | collective-permute-start | bytes 835592 | tf_op jit(solution)/shard_map/ppermute | solution.py:291
  36.4 6.3 %collective-permute-start.10 = (bf16[288,256]{1,0:T(8,128)(2,1)S(1)}, bf16[288,256]{1,0:T(8,128)(2,1)S(1)}, u32[]{:S(2)}, u32[]{:S(2)}) collective-permute-start(bf16[288,256]{1,0:T(8,128)(2,1)S(1)} %slice.85), channel_id=1, source_target_pairs={{4,0},{8,4},{12,8},{14,12},{10,14},{6,10},{2,6},{0,2},{5,1},{9,5},... | collective-permute-start | bytes 442376 | tf_op jit(solution)/shard_map/ppermute | solution.py:291
  37.0 5.7 %collective-permute-start.9 = (bf16[256,256]{1,0:T(8,128)(2,1)S(1)}, bf16[256,256]{1,0:T(8,128)(2,1)S(1)}, u32[]{:S(2)}, u32[]{:S(2)}) collective-permute-start(bf16[256,256]{1,0:T(8,128)(2,1)S(1)} %slice.84), channel_id=1, source_target_pairs={{0,4},{4,8},{8,12},{12,14},{14,10},{10,6},{6,2},{2,0},{1,5},{5,9},... | collective-permute-start | bytes 393224 | tf_op jit(solution)/shard_map/ppermute | solution.py:288
  43.5 5.2 %collective-permute-start.12 = (bf16[256,256]{1,0:T(8,128)(2,1)S(1)}, bf16[256,256]{1,0:T(8,128)(2,1)S(1)}, u32[]{:S(2)}, u32[]{:S(2)}) collective-permute-start(bf16[256,256]{1,0:T(8,128)(2,1)S(1)} %shard_map.99), channel_id=1, source_target_pairs={{0,16},{16,0},{1,17},{17,1},{2,18},{18,2},{3,19},{19,3},{4,20},{20... | collective-permute-start | bytes 393224 | tf_op jit(solution)/shard_map/ppermute | solution.py:297
  44.1 8.8 %collective-permute-start.15 = (bf16[128,1024]{1,0:T(8,128)(2,1)}, bf16[128,1024]{1,0:T(8,128)(2,1)S(1)}, u32[]{:S(2)}, u32[]{:S(2)}) collective-permute-start(bf16[128,1024]{1,0:T(8,128)(2,1)} %collective-permute-done.4.first.rest_1_), channel_id=1, source_target_pairs={{0,4},{4,8},{8,12},{12,14},{14,10},{10,6},{6,2},{2,0},{1,5},{5,9},... | collective-permute-start | bytes 786440 | tf_op jit(solution)/shard_map/ppermute | solution.py:288
  45.7 9.4 %collective-permute-start.16 = (bf16[128,1024]{1,0:T(8,128)(2,1)}, bf16[128,1024]{1,0:T(8,128)(2,1)S(1)}, u32[]{:S(2)}, u32[]{:S(2)}) collective-permute-start(bf16[128,1024]{1,0:T(8,128)(2,1)} %collective-permute-done.5.second.rest_2_), channel_id=1, source_target_pairs={{4,0},{8,4},{12,8},{14,12},{10,14},{6,10},{2,6},{0,2},{5,1},{9,5},... | collective-permute-start | bytes 786440 | tf_op jit(solution)/shard_map/ppermute | solution.py:291
  49.5 8.1 %collective-permute-start.13 = (bf16[256,512]{1,0:T(8,128)(2,1)S(1)}, bf16[256,512]{1,0:T(8,128)(2,1)S(1)}, u32[]{:S(2)}, u32[]{:S(2)}) collective-permute-start(bf16[256,512]{1,0:T(8,128)(2,1)S(1)} %get-tuple-element.122.refs_0_), channel_id=1, source_target_pairs={{0,4},{4,8},{8,12},{12,14},{14,10},{10,6},{6,2},{2,0},{1,5},{5,9},... | collective-permute-start | bytes 786440 | tf_op jit(solution)/shard_map/ppermute | solution.py:288
  51.1 7.8 %collective-permute-start.14 = (bf16[256,512]{1,0:T(8,128)(2,1)S(1)}, bf16[256,512]{1,0:T(8,128)(2,1)S(1)}, u32[]{:S(2)}, u32[]{:S(2)}) collective-permute-start(bf16[256,512]{1,0:T(8,128)(2,1)S(1)} %get-tuple-element.122.refs_0_), channel_id=1, source_target_pairs={{4,0},{8,4},{12,8},{14,12},{10,14},{6,10},{2,6},{0,2},{5,1},{9,5},... | collective-permute-start | bytes 786440 | tf_op jit(solution)/shard_map/ppermute | solution.py:291
  51.6 7.3 %collective-permute-start.17 = (bf16[256,512]{1,0:T(8,128)(2,1)S(1)}, bf16[256,512]{1,0:T(8,128)(2,1)S(1)}, u32[]{:S(2)}, u32[]{:S(2)}) collective-permute-start(bf16[256,512]{1,0:T(8,128)(2,1)S(1)} %get-tuple-element.122.refs_0_), channel_id=1, source_target_pairs={{0,1},{1,0},{2,3},{3,2},{4,5},{5,4},{6,7},{7,6},{8,9},{9,8},{10,11... | collective-permute-start | bytes 786440 | tf_op jit(solution)/shard_map/ppermute | solution.py:294
  53.0 14.1 %collective-permute-start.20 = (bf16[256,1024]{1,0:T(8,128)(2,1)S(1)}, bf16[256,1024]{1,0:T(8,128)(2,1)S(1)}, u32[]{:S(2)}, u32[]{:S(2)}) collective-permute-start(bf16[256,1024]{1,0:T(8,128)(2,1)S(1)} %shard_map.94), channel_id=1, source_target_pairs={{0,16},{16,0},{1,17},{17,1},{2,18},{18,2},{3,19},{19,3},{4,20},{20... | collective-permute-start | bytes 1572872 | tf_op jit(solution)/shard_map/ppermute | solution.py:297
  58.9 6.9 %collective-permute-start.18 = (bf16[256,512]{1,0:T(8,128)(2,1)S(1)}, bf16[256,512]{1,0:T(8,128)(2,1)S(1)}, u32[]{:S(2)}, u32[]{:S(2)}) collective-permute-start(bf16[256,512]{1,0:T(8,128)(2,1)S(1)} %collective-permute-done.13.refs_0_), channel_id=1, source_target_pairs={{0,4},{4,8},{8,12},{12,14},{14,10},{10,6},{6,2},{2,0},{1,5},{5,9},... | collective-permute-start | bytes 786440 | tf_op jit(solution)/shard_map/ppermute | solution.py:288
  60.4 6.6 %collective-permute-start.19 = (bf16[256,512]{1,0:T(8,128)(2,1)S(1)}, bf16[256,512]{1,0:T(8,128)(2,1)S(1)}, u32[]{:S(2)}, u32[]{:S(2)}) collective-permute-start(bf16[256,512]{1,0:T(8,128)(2,1)S(1)} %collective-permute-done.14.refs_1_), channel_id=1, source_target_pairs={{4,0},{8,4},{12,8},{14,12},{10,14},{6,10},{2,6},{0,2},{5,1},{9,5},... | collective-permute-start | bytes 786440 | tf_op jit(solution)/shard_map/ppermute | solution.py:291
  60.9 8.1 %collective-permute-start.23 = (bf16[256,512]{1,0:T(8,128)(2,1)S(1)}, bf16[256,512]{1,0:T(8,128)(2,1)S(1)}, u32[]{:S(2)}, u32[]{:S(2)}) collective-permute-start(bf16[256,512]{1,0:T(8,128)(2,1)S(1)} %collective-permute-done.13.refs_0_), channel_id=1, source_target_pairs={{0,1},{1,0},{2,3},{3,2},{4,5},{5,4},{6,7},{7,6},{8,9},{9,8},{10,11... | collective-permute-start | bytes 786440 | tf_op jit(solution)/shard_map/ppermute | solution.py:294
  61.0 8.1 %collective-permute-start.24 = (bf16[256,512]{1,0:T(8,128)(2,1)S(1)}, bf16[256,512]{1,0:T(8,128)(2,1)S(1)}, u32[]{:S(2)}, u32[]{:S(2)}) collective-permute-start(bf16[256,512]{1,0:T(8,128)(2,1)S(1)} %collective-permute-done.14.refs_1_), channel_id=1, source_target_pairs={{0,1},{1,0},{2,3},{3,2},{4,5},{5,4},{6,7},{7,6},{8,9},{9,8},{10,11... | collective-permute-start | bytes 786440 | tf_op jit(solution)/shard_map/ppermute | solution.py:294
  65.8 11.6 %collective-permute-start.25 = (bf16[256,1024]{1,0:T(8,128)(2,1)S(1)}, bf16[256,1024]{1,0:T(8,128)(2,1)S(1)}, u32[]{:S(2)}, u32[]{:S(2)}) collective-permute-start(bf16[256,1024]{1,0:T(8,128)(2,1)S(1)} %shard_map.101), channel_id=1, source_target_pairs={{0,16},{16,0},{1,17},{17,1},{2,18},{18,2},{3,19},{19,3},{4,20},{20... | collective-permute-start | bytes 1572872 | tf_op jit(solution)/shard_map/ppermute | solution.py:297
  67.0 6.4 %collective-permute-start.21 = (bf16[256,512]{1,0:T(8,128)(2,1)S(1)}, bf16[256,512]{1,0:T(8,128)(2,1)S(1)}, u32[]{:S(2)}, u32[]{:S(2)}) collective-permute-start(bf16[256,512]{1,0:T(8,128)(2,1)S(1)} %collective-permute-done.18.refs_0_), channel_id=1, source_target_pairs={{0,4},{4,8},{8,12},{12,14},{14,10},{10,6},{6,2},{2,0},{1,5},{5,9},... | collective-permute-start | bytes 786440 | tf_op jit(solution)/shard_map/ppermute | solution.py:288
  68.4 6.4 %collective-permute-start.22 = (bf16[256,512]{1,0:T(8,128)(2,1)S(1)}, bf16[256,512]{1,0:T(8,128)(2,1)S(1)}, u32[]{:S(2)}, u32[]{:S(2)}) collective-permute-start(bf16[256,512]{1,0:T(8,128)(2,1)S(1)} %collective-permute-done.19.refs_1_), channel_id=1, source_target_pairs={{4,0},{8,4},{12,8},{14,12},{10,14},{6,10},{2,6},{0,2},{5,1},{9,5},... | collective-permute-start | bytes 786440 | tf_op jit(solution)/shard_map/ppermute | solution.py:291
  77.9 6.1 %collective-permute-start.29 = (bf16[128,512]{1,0:T(8,128)(2,1)S(1)}, bf16[128,512]{1,0:T(8,128)(2,1)S(1)}, u32[]{:S(2)}, u32[]{:S(2)}) collective-permute-start(bf16[128,512]{1,0:T(8,128)(2,1)S(1)} %slice.89), channel_id=1, source_target_pairs={{0,4},{4,8},{8,12},{12,14},{14,10},{10,6},{6,2},{2,0},{1,5},{5,9},... | collective-permute-start | bytes 393224 | tf_op jit(solution)/shard_map/ppermute | solution.py:288
  79.4 5.1 %collective-permute-start.30 = (bf16[128,512]{1,0:T(8,128)(2,1)S(1)}, bf16[128,512]{1,0:T(8,128)(2,1)S(1)}, u32[]{:S(2)}, u32[]{:S(2)}) collective-permute-start(bf16[128,512]{1,0:T(8,128)(2,1)S(1)} %slice.90), channel_id=1, source_target_pairs={{4,0},{8,4},{12,8},{14,12},{10,14},{6,10},{2,6},{0,2},{5,1},{9,5},... | collective-permute-start | bytes 393224 | tf_op jit(solution)/shard_map/ppermute | solution.py:291
  85.1 8.2 %collective-permute-start.34 = (bf16[128,1024]{1,0:T(8,128)(2,1)S(1)}, bf16[128,1024]{1,0:T(8,128)(2,1)S(1)}, u32[]{:S(2)}, u32[]{:S(2)}) collective-permute-start(bf16[128,1024]{1,0:T(8,128)(2,1)S(1)} %collective-permute-done.15.first.rest_3_), channel_id=1, source_target_pairs={{0,4},{4,8},{8,12},{12,14},{14,10},{10,6},{6,2},{2,0},{1,5},{5,9},... | collective-permute-start | bytes 786440 | tf_op jit(solution)/shard_map/ppermute | solution.py:288
  86.5 7.9 %collective-permute-start.35 = (bf16[128,1024]{1,0:T(8,128)(2,1)S(1)}, bf16[128,1024]{1,0:T(8,128)(2,1)S(1)}, u32[]{:S(2)}, u32[]{:S(2)}) collective-permute-start(bf16[128,1024]{1,0:T(8,128)(2,1)S(1)} %collective-permute-done.16.second.rest_4_), channel_id=1, source_target_pairs={{4,0},{8,4},{12,8},{14,12},{10,14},{6,10},{2,6},{0,2},{5,1},{9,5},... | collective-permute-start | bytes 786440 | tf_op jit(solution)/shard_map/ppermute | solution.py:291
  89.5 4.9 %collective-permute-start.33 = (bf16[256,512]{1,0:T(8,128)(2,1)S(1)}, bf16[256,512]{1,0:T(8,128)(2,1)S(1)}, u32[]{:S(2)}, u32[]{:S(2)}) collective-permute-start(bf16[256,512]{1,0:T(8,128)(2,1)S(1)} %get-tuple-element.144), channel_id=1, source_target_pairs={{0,1},{1,0},{2,3},{3,2},{4,5},{5,4},{6,7},{7,6},{8,9},{9,8},{10,11... | collective-permute-start | bytes 786440 | tf_op jit(solution)/shard_map/ppermute | solution.py:294
  89.6 7.1 %collective-permute-start.38 = (bf16[256,512]{1,0:T(8,128)(2,1)S(1)}, bf16[256,512]{1,0:T(8,128)(2,1)S(1)}, u32[]{:S(2)}, u32[]{:S(2)}) collective-permute-start(bf16[256,512]{1,0:T(8,128)(2,1)S(1)} %collective-permute-done.18.refs_0_), channel_id=1, source_target_pairs={{0,1},{1,0},{2,3},{3,2},{4,5},{5,4},{6,7},{7,6},{8,9},{9,8},{10,11... | collective-permute-start | bytes 786440 | tf_op jit(solution)/shard_map/ppermute | solution.py:294
  90.1 7.9 %collective-permute-start.39 = (bf16[256,512]{1,0:T(8,128)(2,1)S(1)}, bf16[256,512]{1,0:T(8,128)(2,1)S(1)}, u32[]{:S(2)}, u32[]{:S(2)}) collective-permute-start(bf16[256,512]{1,0:T(8,128)(2,1)S(1)} %collective-permute-done.19.refs_1_), channel_id=1, source_target_pairs={{0,1},{1,0},{2,3},{3,2},{4,5},{5,4},{6,7},{7,6},{8,9},{9,8},{10,11... | collective-permute-start | bytes 786440 | tf_op jit(solution)/shard_map/ppermute | solution.py:294
  93.3 9.5 %collective-permute-start.28 = (bf16[512,512]{1,0:T(8,128)(2,1)S(1)}, bf16[512,512]{1,0:T(8,128)(2,1)S(1)}, u32[]{:S(2)}, u32[]{:S(2)}) collective-permute-start(bf16[512,512]{1,0:T(8,128)(2,1)S(1)} %get-tuple-element.140), channel_id=1, source_target_pairs={{0,1},{1,0},{2,3},{3,2},{4,5},{5,4},{6,7},{7,6},{8,9},{9,8},{10,11... | collective-permute-start | bytes 1572872 | tf_op jit(solution)/shard_map/ppermute | solution.py:294
  94.5 8.9 %collective-permute-start.36 = (bf16[128,512]{1,0:T(8,128)(2,1)S(1)}, bf16[128,512]{1,0:T(8,128)(2,1)S(1)}, u32[]{:S(2)}, u32[]{:S(2)}) collective-permute-start(bf16[128,512]{1,0:T(8,128)(2,1)S(1)} %get-tuple-element.180), channel_id=1, source_target_pairs={{0,4},{4,8},{8,12},{12,14},{14,10},{10,6},{6,2},{2,0},{1,5},{5,9},... | collective-permute-start | bytes 393224 | tf_op jit(solution)/shard_map/ppermute | solution.py:288
  95.9 7.6 %collective-permute-start.37 = (bf16[128,512]{1,0:T(8,128)(2,1)S(1)}, bf16[128,512]{1,0:T(8,128)(2,1)S(1)}, u32[]{:S(2)}, u32[]{:S(2)}) collective-permute-start(bf16[128,512]{1,0:T(8,128)(2,1)S(1)} %get-tuple-element.179), channel_id=1, source_target_pairs={{4,0},{8,4},{12,8},{14,12},{10,14},{6,10},{2,6},{0,2},{5,1},{9,5},... | collective-permute-start | bytes 393224 | tf_op jit(solution)/shard_map/ppermute | solution.py:291
  96.7 6.5 %collective-permute-start.40 = (bf16[64,1024]{1,0:T(8,128)(2,1)S(1)}, bf16[64,1024]{1,0:T(8,128)(2,1)S(1)}, u32[]{:S(2)}, u32[]{:S(2)}) collective-permute-start(bf16[64,1024]{1,0:T(8,128)(2,1)S(1)} %slice.93), channel_id=1, source_target_pairs={{0,4},{4,8},{8,12},{12,14},{14,10},{10,6},{6,2},{2,0},{1,5},{5,9},... | collective-permute-start | bytes 393224 | tf_op jit(solution)/shard_map/ppermute | solution.py:288
  98.0 5.5 %collective-permute-start.41 = (bf16[64,1024]{1,0:T(8,128)(2,1)S(1)}, bf16[64,1024]{1,0:T(8,128)(2,1)S(1)}, u32[]{:S(2)}, u32[]{:S(2)}) collective-permute-start(bf16[64,1024]{1,0:T(8,128)(2,1)S(1)} %slice.94), channel_id=1, source_target_pairs={{4,0},{8,4},{12,8},{14,12},{10,14},{6,10},{2,6},{0,2},{5,1},{9,5},... | collective-permute-start | bytes 393224 | tf_op jit(solution)/shard_map/ppermute | solution.py:291
  102.8 10.3 %collective-permute-start.46 = (bf16[512,512]{1,0:T(8,128)(2,1)S(1)}, bf16[512,512]{1,0:T(8,128)(2,1)S(1)}, u32[]{:S(2)}, u32[]{:S(2)}) collective-permute-start(bf16[512,512]{1,0:T(8,128)(2,1)S(1)} %get-tuple-element.152), channel_id=1, source_target_pairs={{0,1},{1,0},{2,3},{3,2},{4,5},{5,4},{6,7},{7,6},{8,9},{9,8},{10,11... | collective-permute-start | bytes 1572872 | tf_op jit(solution)/shard_map/ppermute | solution.py:294
  103.5 8.4 %collective-permute-start.42 = (bf16[256,512]{1,0:T(8,128)(2,1)S(1)}, bf16[256,512]{1,0:T(8,128)(2,1)S(1)}, u32[]{:S(2)}, u32[]{:S(2)}) collective-permute-start(bf16[256,512]{1,0:T(8,128)(2,1)S(1)} %pad_maximum_fusion), channel_id=1, source_target_pairs={{0,4},{4,8},{8,12},{12,14},{14,10},{10,6},{6,2},{2,0},{1,5},{5,9},... | collective-permute-start | bytes 786440 | tf_op jit(solution)/shard_map/ppermute | solution.py:288
  105.0 8.1 %collective-permute-start.43 = (bf16[256,512]{1,0:T(8,128)(2,1)S(1)}, bf16[256,512]{1,0:T(8,128)(2,1)S(1)}, u32[]{:S(2)}, u32[]{:S(2)}) collective-permute-start(bf16[256,512]{1,0:T(8,128)(2,1)S(1)} %pad_maximum_fusion.1), channel_id=1, source_target_pairs={{4,0},{8,4},{12,8},{14,12},{10,14},{6,10},{2,6},{0,2},{5,1},{9,5},... | collective-permute-start | bytes 786440 | tf_op jit(solution)/shard_map/ppermute | solution.py:291
  105.7 16.3 %collective-permute-start.45 = (bf16[512,512]{1,0:T(8,128)(2,1)S(1)}, bf16[512,512]{1,0:T(8,128)(2,1)S(1)}, u32[]{:S(2)}, u32[]{:S(2)}) collective-permute-start(bf16[512,512]{1,0:T(8,128)(2,1)S(1)} %get-tuple-element.136), channel_id=1, source_target_pairs={{0,1},{1,0},{2,3},{3,2},{4,5},{5,4},{6,7},{7,6},{8,9},{9,8},{10,11... | collective-permute-start | bytes 1572872 | tf_op jit(solution)/shard_map/ppermute | solution.py:294
  107.2 14.8 %collective-permute-start.49 = (bf16[256,1024]{1,0:T(8,128)(2,1)S(1)}, bf16[256,1024]{1,0:T(8,128)(2,1)S(1)}, u32[]{:S(2)}, u32[]{:S(2)}) collective-permute-start(bf16[256,1024]{1,0:T(8,128)(2,1)S(1)} %shard_map.106), channel_id=1, source_target_pairs={{0,16},{16,0},{1,17},{17,1},{2,18},{18,2},{3,19},{19,3},{4,20},{20... | collective-permute-start | bytes 1572872 | tf_op jit(solution)/shard_map/ppermute | solution.py:297
  113.3 8.7 %collective-permute-start.47 = (bf16[256,512]{1,0:T(8,128)(2,1)S(1)}, bf16[256,512]{1,0:T(8,128)(2,1)S(1)}, u32[]{:S(2)}, u32[]{:S(2)}) collective-permute-start(bf16[256,512]{1,0:T(8,128)(2,1)S(1)} %get-tuple-element.176), channel_id=1, source_target_pairs={{0,4},{4,8},{8,12},{12,14},{14,10},{10,6},{6,2},{2,0},{1,5},{5,9},... | collective-permute-start | bytes 786440 | tf_op jit(solution)/shard_map/ppermute | solution.py:288
  114.5 7.5 %collective-permute-start.48 = (bf16[256,512]{1,0:T(8,128)(2,1)S(1)}, bf16[256,512]{1,0:T(8,128)(2,1)S(1)}, u32[]{:S(2)}, u32[]{:S(2)}) collective-permute-start(bf16[256,512]{1,0:T(8,128)(2,1)S(1)} %get-tuple-element.175), channel_id=1, source_target_pairs={{4,0},{8,4},{12,8},{14,12},{10,14},{6,10},{2,6},{0,2},{5,1},{9,5},... | collective-permute-start | bytes 786440 | tf_op jit(solution)/shard_map/ppermute | solution.py:291
  115.4 11.9 %collective-permute-start.52 = (bf16[128,1024]{1,0:T(8,128)(2,1)S(1)}, bf16[128,1024]{1,0:T(8,128)(2,1)S(1)}, u32[]{:S(2)}, u32[]{:S(2)}) collective-permute-start(bf16[128,1024]{1,0:T(8,128)(2,1)S(1)} %shard_map.107), channel_id=1, source_target_pairs={{0,16},{16,0},{1,17},{17,1},{2,18},{18,2},{3,19},{19,3},{4,20},{20... | collective-permute-start | bytes 786440 | tf_op jit(solution)/shard_map/ppermute | solution.py:297
  122.3 7.6 %collective-permute-start.50 = (bf16[256,512]{1,0:T(8,128)(2,1)S(1)}, bf16[256,512]{1,0:T(8,128)(2,1)S(1)}, u32[]{:S(2)}, u32[]{:S(2)}) collective-permute-start(bf16[256,512]{1,0:T(8,128)(2,1)S(1)} %get-tuple-element.174), channel_id=1, source_target_pairs={{0,4},{4,8},{8,12},{12,14},{14,10},{10,6},{6,2},{2,0},{1,5},{5,9},... | collective-permute-start | bytes 786440 | tf_op jit(solution)/shard_map/ppermute | solution.py:288
  123.6 7.3 %collective-permute-start.51 = (bf16[256,512]{1,0:T(8,128)(2,1)S(1)}, bf16[256,512]{1,0:T(8,128)(2,1)S(1)}, u32[]{:S(2)}, u32[]{:S(2)}) collective-permute-start(bf16[256,512]{1,0:T(8,128)(2,1)S(1)} %get-tuple-element.173), channel_id=1, source_target_pairs={{4,0},{8,4},{12,8},{14,12},{10,14},{6,10},{2,6},{0,2},{5,1},{9,5},... | collective-permute-start | bytes 786440 | tf_op jit(solution)/shard_map/ppermute | solution.py:291
  124.3 6.6 %collective-permute-start.44 = (bf16[256,512]{1,0:T(8,128)(2,1)S(1)}, bf16[256,512]{1,0:T(8,128)(2,1)S(1)}, u32[]{:S(2)}, u32[]{:S(2)}) collective-permute-start(bf16[256,512]{1,0:T(8,128)(2,1)S(1)} %get-tuple-element.164), channel_id=1, source_target_pairs={{0,1},{1,0},{2,3},{3,2},{4,5},{5,4},{6,7},{7,6},{8,9},{9,8},{10,11... | collective-permute-start | bytes 786440 | tf_op jit(solution)/shard_map/ppermute | solution.py:294
  (13 other events, 110.4 us)

commit v6 on v5

--- a/solution.py
+++ b/solution.py
@@ -30,7 +30,7 @@
 
 def norm_body(info, tokens, gain, out):
     rows, model = tokens.shape
-    step = 16
+    step = 32
 
     @pl.loop(0, rows // step)
     def _(i):

time: 135 us -> 135 us (level)
  Pallas kernels: 41.5 us -> 40 us
  waiting for transfers between devices: 44.7 us -> 46.2 us
    pallas_call x2, Pallas kernels: 5.32 us -> 3.84 us  [norm(): kernel_call(norm_body, shape(*x.shape), 3, 8 * x.size, 4 * x.size)]
  transfers between devices with their start and end apart: 54 -> 54, of which waited for: 29 -> 30; matrix products, arithmetic and copies ran while one was open for 2% -> 2% of each run, Pallas kernels for 26% -> 25%
where the time goes in v6:
time: 135 us
  waiting for transfers between devices  46.2 us (34%)
  starting transfers between devices  43.2 us (32%)
  Pallas kernels  40 us (30%)
  local copies, waits for them, and re-layouts  3.25 us (2%)
  other arithmetic  1.52 us (1%)
    ppermute x16, starting transfers between devices, up(): return lax.ppermute(x, 'wide', up_perm)  23.6 us
    ppermute x16, waiting for transfers between devices, up(): return lax.ppermute(x, 'wide', up_perm)  21.2 us
    pallas_call x5, Pallas kernels, expert(): kernel_call(functools.partial(expert_body, columns), (out, out), 4 + 2 *...  17 us
    ppermute x16, waiting for transfers between devices, down(): return lax.ppermute(x, 'wide', down_perm)  12.9 us
    ppermute x6, waiting for transfers between devices, across(): return lax.ppermute(x, 'groups', [(i, i ^ 1) for i in range(groups)])  11.7 us
    ppermute x16, starting transfers between devices, down(): return lax.ppermute(x, 'wide', down_perm)  9.31 us
    ppermute x6, starting transfers between devices, across(): return lax.ppermute(x, 'groups', [(i, i ^ 1) for i in range(groups)])  7.95 us
    pallas_call x4, Pallas kernels, mine(): kernel_call(functools.partial(mine_body, depth, wide, first), (outs, line...  3.89 us
  transfers between devices with their start and end apart: 54, of which 30 were waited for; matrix products, arithmetic and copies ran while one was open for 2% of the time, Pallas kernels for 25%

profile of v6, /device:TPU:0, one launch (start us, length us, event | category | flops | bytes accessed | tf_op | source)
XLA Modules:
  0.0 134.8 jit_solution(17655403963519995514)
XLA Ops:
  0.6 3.1 %shard_map.91 = (bf16[128,4096]{1,0:T(8,128)(2,1)}, bf16[544,256]{1,0:T(8,128)(2,1)}) custom-call(s32[2]{0:T(128)} %pad_add_fusion.1.info, s32[4,256]{1,0:T(4,128)} %bitcast.25, f32[4,256]{1,0:T(4,128)} %bitcast.26, bf16[256,4096]{1,0:T(8,128)(2,1)} %tokens.3, bf16[512,1024]{1,0:T(8,128)(2,1)} %w_in.1), custom_call_target="tpu_custom_call" | custom-call | tf_op jit(solution)/shard_map/pallas_call | solution.py:345
  3.7 3.0 %collective-permute-start.8 = (bf16[128,4096]{1,0:T(8,128)(2,1)}, bf16[128,4096]{1,0:T(8,128)(2,1)}, u32[]{:S(2)}, u32[]{:S(2)}) collective-permute-start(bf16[128,4096]{1,0:T(8,128)(2,1)} %get-tuple-element.112), channel_id=1, source_target_pairs={{0,16},{16,0},{1,17},{17,1},{2,18},{18,2},{3,19},{19,3},{4,20},{20... | collective-permute-start | bytes 3145736 | tf_op jit(solution)/shard_map/ppermute | solution.py:297
  6.7 1.6 %collective-permute-start = (bf16[544,256]{1,0:T(8,128)(2,1)}, bf16[544,256]{1,0:T(8,128)(2,1)S(1)}, u32[]{:S(2)}, u32[]{:S(2)}) collective-permute-start(bf16[544,256]{1,0:T(8,128)(2,1)} %get-tuple-element.95.refs_0_.refs_2_), channel_id=1, source_target_pairs={{0,4},{4,8},{8,12},{12,14},{14,10},{10,6},{6,2},{2,0},{1,5},{5,9},... | collective-permute-start | bytes 835592 | tf_op jit(solution)/shard_map/ppermute | solution.py:288
  9.4 1.6 %collective-permute-start.4 = (bf16[128,1024]{1,0:T(8,128)(2,1)}, bf16[128,1024]{1,0:T(8,128)(2,1)}, u32[]{:S(2)}, u32[]{:S(2)}) collective-permute-start(bf16[128,1024]{1,0:T(8,128)(2,1)} %constant_dynamic-slice_fusion), channel_id=1, source_target_pairs={{0,4},{4,8},{8,12},{12,14},{14,10},{10,6},{6,2},{2,0},{1,5},{5,9},... | collective-permute-start | bytes 786440 | tf_op jit(solution)/shard_map/ppermute | solution.py:288
  12.2 1.6 %copy-done = bf16[256,4096]{1,0:T(8,128)(2,1)S(1)} copy-done((bf16[256,4096]{1,0:T(8,128)(2,1)S(1)}, bf16[256,4096]{1,0:T(8,128)(2,1)}, u32[]{:S(2)}) %copy-start) | copy-done | bytes 2097176
  13.8 1.9 %shard_map.92.normed = bf16[256,4096]{1,0:T(8,128)(2,1)S(1)} custom-call(s32[11]{0:T(128)S(1)} %pad_add_fusion.info, bf16[256,4096]{1,0:T(8,128)(2,1)S(1)} %copy-done, f32[1,4096]{1,0:T(1,128)S(1)} %bitcast.23), custom_call_target="tpu_custom_call" | custom-call | flops 8388608 | bytes 4194304 | tf_op jit(solution)/shard_map/pallas_call | solution.py:360
  16.5 1.6 %collective-permute-done.1.refs_2_.refs_4_ = bf16[544,256]{1,0:T(8,128)(2,1)S(1)} collective-permute-done((bf16[544,256]{1,0:T(8,128)(2,1)}, bf16[544,256]{1,0:T(8,128)(2,1)S(1)}, u32[]{:S(2)}, u32[]{:S(2)}) %collective-permute-start.1) | collective-permute-done | bytes 278560 | tf_op jit(solution)/shard_map/ppermute | solution.py:291
  18.1 1.6 %collective-permute-start.2 = (bf16[544,256]{1,0:T(8,128)(2,1)S(1)}, bf16[544,256]{1,0:T(8,128)(2,1)}, u32[]{:S(2)}, u32[]{:S(2)}) collective-permute-start(bf16[544,256]{1,0:T(8,128)(2,1)S(1)} %collective-permute-done.refs_1_.refs_3_), channel_id=1, source_target_pairs={{0,4},{4,8},{8,12},{12,14},{14,10},{10,6},{6,2},{2,0},{1,5},{5,9},... | collective-permute-start | bytes 835592 | tf_op jit(solution)/shard_map/ppermute | solution.py:288
  20.1 2.1 %collective-permute-done.4.first.rest_1_ = bf16[128,1024]{1,0:T(8,128)(2,1)} collective-permute-done((bf16[128,1024]{1,0:T(8,128)(2,1)}, bf16[128,1024]{1,0:T(8,128)(2,1)}, u32[]{:S(2)}, u32[]{:S(2)}) %collective-permute-start.4) | collective-permute-done | bytes 262176 | tf_op jit(solution)/shard_map/ppermute | solution.py:288
  22.2 1.6 %collective-permute-done.5.second.rest_2_ = bf16[128,1024]{1,0:T(8,128)(2,1)} collective-permute-done((bf16[128,1024]{1,0:T(8,128)(2,1)}, bf16[128,1024]{1,0:T(8,128)(2,1)}, u32[]{:S(2)}, u32[]{:S(2)}) %collective-permute-start.5) | collective-permute-done | bytes 262176 | tf_op jit(solution)/shard_map/ppermute | solution.py:291
  23.8 1.6 %shard_map.94 = bf16[256,1024]{1,0:T(8,128)(2,1)S(1)} custom-call(s32[11]{0:T(128)S(1)} %pad_add_fusion.info, bf16[128,1024]{1,0:T(8,128)(2,1)} %collective-permute-done.4.first.rest_1_, bf16[128,1024]{1,0:T(8,128)(2,1)} %collective-permute-done.5.second.rest_2_), custom_call_target="tpu_custom_call" | custom-call | flops 262144 | bytes 1048576 | tf_op jit(solution)/shard_map/pallas_call | solution.py:327
  26.7 1.3 collective-permute-done.3.refs_1_.refs_6_
  28.0 1.6 %collective-permute-start.6 = (bf16[544,256]{1,0:T(8,128)(2,1)}, bf16[544,256]{1,0:T(8,128)(2,1)S(1)}, u32[]{:S(2)}, u32[]{:S(2)}) collective-permute-start(bf16[544,256]{1,0:T(8,128)(2,1)} %collective-permute-done.2.refs_0_.refs_5_), channel_id=1, source_target_pairs={{0,4},{4,8},{8,12},{12,14},{14,10},{10,6},{6,2},{2,0},{1,5},{5,9},... | collective-permute-start | bytes 835592 | tf_op jit(solution)/shard_map/ppermute | solution.py:288
  30.0 1.4 %shard_map.95 = (f32[256,256]{1,0:T(8,128)S(1)}, f32[5,256]{1,0:T(8,128)S(1)}) custom-call(s32[11]{0:T(128)S(1)} %pad_add_fusion.info, bf16[256,4096]{1,0:T(8,128)(2,1)S(1)} %shard_map.92.normed, bf16[544,256]{1,0:T(8,128)(2,1)} %collective-permute-done.2.refs_0_.refs_5_, bf16[544,256]{1,0:T(8,128)(2,1)} %collective-permute-done.3.refs_1_.refs_6_, ...), custom_call_target="tpu_custom_call" | custom-call | flops 134217728 | bytes 1048576 | tf_op jit(solution)/shard_map/pallas_call | solution.py:392
  31.4 1.9 %shard_map.96.refs_0_ = bf16[128,4096]{1,0:T(8,128)(2,1)S(1)} custom-call(s32[11]{0:T(128)S(1)} %pad_add_fusion.info, bf16[128,4096]{1,0:T(8,128)(2,1)} %collective-permute-done.8.tokens, f32[1,4096]{1,0:T(1,128)S(1)} %bitcast.24), custom_call_target="tpu_custom_call" | custom-call | flops 4194304 | bytes 2097152 | tf_op jit(solution)/shard_map/pallas_call | solution.py:360
  33.3 1.8 %collective-permute-done.6.refs_7_.refs_0_ = bf16[544,256]{1,0:T(8,128)(2,1)S(1)} collective-permute-done((bf16[544,256]{1,0:T(8,128)(2,1)}, bf16[544,256]{1,0:T(8,128)(2,1)S(1)}, u32[]{:S(2)}, u32[]{:S(2)}) %collective-permute-start.6) | collective-permute-done | bytes 278560 | tf_op jit(solution)/shard_map/ppermute | solution.py:288
  35.1 1.3 collective-permute-done.7.refs_8_.refs_1_
  37.0 1.6 %collective-permute-start.9 = (bf16[256,256]{1,0:T(8,128)(2,1)S(1)}, bf16[256,256]{1,0:T(8,128)(2,1)S(1)}, u32[]{:S(2)}, u32[]{:S(2)}) collective-permute-start(bf16[256,256]{1,0:T(8,128)(2,1)S(1)} %slice.84), channel_id=1, source_target_pairs={{0,4},{4,8},{8,12},{12,14},{14,10},{10,6},{6,2},{2,0},{1,5},{5,9},... | collective-permute-start | bytes 393224 | tf_op jit(solution)/shard_map/ppermute | solution.py:288
  39.5 2.7 %shard_map.97 = (f32[256,256]{1,0:T(8,128)S(1)}, bf16[256,512]{1,0:T(8,128)(2,1)S(1)}) custom-call(s32[11]{0:T(128)S(1)} %pad_add_fusion.info, bf16[128,4096]{1,0:T(8,128)(2,1)S(1)} %shard_map.96.refs_0_, bf16[128,4096]{1,0:T(8,128)(2,1)S(1)} %collective-permute-done.11.refs_1_, bf16[544,256]{1,0:T(8,128)(2,1)S(1)} %copy-done.5, ...), custom_call_target="tpu_custom_call" | custom-call | flops 536870912 | bytes 4194304 | tf_op jit(solution)/shard_map/pallas_call | solution.py:376
  44.1 1.6 %collective-permute-start.15 = (bf16[128,1024]{1,0:T(8,128)(2,1)}, bf16[128,1024]{1,0:T(8,128)(2,1)S(1)}, u32[]{:S(2)}, u32[]{:S(2)}) collective-permute-start(bf16[128,1024]{1,0:T(8,128)(2,1)} %collective-permute-done.4.first.rest_1_), channel_id=1, source_target_pairs={{0,4},{4,8},{8,12},{12,14},{14,10},{10,6},{6,2},{2,0},{1,5},{5,9},... | collective-permute-start | bytes 786440 | tf_op jit(solution)/shard_map/ppermute | solution.py:288
  46.2 2.6 %collective-permute-done.12.refs_2_ = bf16[256,256]{1,0:T(8,128)(2,1)S(1)} collective-permute-done((bf16[256,256]{1,0:T(8,128)(2,1)S(1)}, bf16[256,256]{1,0:T(8,128)(2,1)S(1)}, u32[]{:S(2)}, u32[]{:S(2)}) %collective-permute-start.12) | collective-permute-done | bytes 131104 | tf_op jit(solution)/shard_map/ppermute | solution.py:297
  49.5 1.6 %collective-permute-start.13 = (bf16[256,512]{1,0:T(8,128)(2,1)S(1)}, bf16[256,512]{1,0:T(8,128)(2,1)S(1)}, u32[]{:S(2)}, u32[]{:S(2)}) collective-permute-start(bf16[256,512]{1,0:T(8,128)(2,1)S(1)} %get-tuple-element.122.refs_0_), channel_id=1, source_target_pairs={{0,4},{4,8},{8,12},{12,14},{14,10},{10,6},{6,2},{2,0},{1,5},{5,9},... | collective-permute-start | bytes 786440 | tf_op jit(solution)/shard_map/ppermute | solution.py:288
  51.6 1.4 %collective-permute-done.15.first.rest_3_ = bf16[128,1024]{1,0:T(8,128)(2,1)S(1)} collective-permute-done((bf16[128,1024]{1,0:T(8,128)(2,1)}, bf16[128,1024]{1,0:T(8,128)(2,1)S(1)}, u32[]{:S(2)}, u32[]{:S(2)}) %collective-permute-start.15) | collective-permute-done | bytes 262176 | tf_op jit(solution)/shard_map/ppermute | solution.py:288
  53.0 2.1 %collective-permute-start.20 = (bf16[256,1024]{1,0:T(8,128)(2,1)S(1)}, bf16[256,1024]{1,0:T(8,128)(2,1)S(1)}, u32[]{:S(2)}, u32[]{:S(2)}) collective-permute-start(bf16[256,1024]{1,0:T(8,128)(2,1)S(1)} %shard_map.94), channel_id=1, source_target_pairs={{0,16},{16,0},{1,17},{17,1},{2,18},{18,2},{3,19},{19,3},{4,20},{20... | collective-permute-start | bytes 1572872 | tf_op jit(solution)/shard_map/ppermute | solution.py:297
  55.1 2.5 %collective-permute-done.13.refs_0_ = bf16[256,512]{1,0:T(8,128)(2,1)S(1)} collective-permute-done((bf16[256,512]{1,0:T(8,128)(2,1)S(1)}, bf16[256,512]{1,0:T(8,128)(2,1)S(1)}, u32[]{:S(2)}, u32[]{:S(2)}) %collective-permute-start.13) | collective-permute-done | bytes 262176 | tf_op jit(solution)/shard_map/ppermute | solution.py:288
  57.6 1.3 collective-permute-done.14.refs_1_
  58.9 1.5 %collective-permute-start.18 = (bf16[256,512]{1,0:T(8,128)(2,1)S(1)}, bf16[256,512]{1,0:T(8,128)(2,1)S(1)}, u32[]{:S(2)}, u32[]{:S(2)}) collective-permute-start(bf16[256,512]{1,0:T(8,128)(2,1)S(1)} %collective-permute-done.13.refs_0_), channel_id=1, source_target_pairs={{0,4},{4,8},{8,12},{12,14},{14,10},{10,6},{6,2},{2,0},{1,5},{5,9},... | collective-permute-start | bytes 786440 | tf_op jit(solution)/shard_map/ppermute | solution.py:288
  62.1 3.7 %collective-permute-done.18.refs_0_ = bf16[256,512]{1,0:T(8,128)(2,1)S(1)} collective-permute-done((bf16[256,512]{1,0:T(8,128)(2,1)S(1)}, bf16[256,512]{1,0:T(8,128)(2,1)S(1)}, u32[]{:S(2)}, u32[]{:S(2)}) %collective-permute-start.18) | collective-permute-done | bytes 262176 | tf_op jit(solution)/shard_map/ppermute | solution.py:288
  67.0 1.4 %collective-permute-start.21 = (bf16[256,512]{1,0:T(8,128)(2,1)S(1)}, bf16[256,512]{1,0:T(8,128)(2,1)S(1)}, u32[]{:S(2)}, u32[]{:S(2)}) collective-permute-start(bf16[256,512]{1,0:T(8,128)(2,1)S(1)} %collective-permute-done.18.refs_0_), channel_id=1, source_target_pairs={{0,4},{4,8},{8,12},{12,14},{14,10},{10,6},{6,2},{2,0},{1,5},{5,9},... | collective-permute-start | bytes 786440 | tf_op jit(solution)/shard_map/ppermute | solution.py:288
  69.1 4.1 %shard_map.102 = (bf16[512,512]{1,0:T(8,128)(2,1)S(1)}, bf16[512,512]{1,0:T(8,128)(2,1)S(1)}) custom-call(s32[11]{0:T(128)S(1)} %pad_add_fusion.info, bf16[256,512]{1,0:T(8,128)(2,1)S(1)} %collective-permute-done.13.refs_0_, bf16[256,512]{1,0:T(8,128)(2,1)S(1)} %collective-permute-done.14.refs_1_, bf16[256,512]{1,0:T(8,128)(2,1)S(1)} %collective-permute-done.23.refs_2_, ...), custom_call_target="tpu_custom_call" | custom-call | flops 2818572288 | bytes 7602176 | tf_op jit(solution)/shard_map/pallas_call | solution.py:446
  73.4 1.4 %collective-permute-done.22.refs_1_ = bf16[256,512]{1,0:T(8,128)(2,1)S(1)} collective-permute-done((bf16[256,512]{1,0:T(8,128)(2,1)S(1)}, bf16[256,512]{1,0:T(8,128)(2,1)S(1)}, u32[]{:S(2)}, u32[]{:S(2)}) %collective-permute-start.22) | collective-permute-done | bytes 262176 | tf_op jit(solution)/shard_map/ppermute | solution.py:291
  74.8 2.6 %collective-permute-done.25.rest_10_ = bf16[256,1024]{1,0:T(8,128)(2,1)S(1)} collective-permute-done((bf16[256,1024]{1,0:T(8,128)(2,1)S(1)}, bf16[256,1024]{1,0:T(8,128)(2,1)S(1)}, u32[]{:S(2)}, u32[]{:S(2)}) %collective-permute-start.25) | collective-permute-done | bytes 524320 | tf_op jit(solution)/shard_map/ppermute | solution.py:297
  77.9 1.5 %collective-permute-start.29 = (bf16[128,512]{1,0:T(8,128)(2,1)S(1)}, bf16[128,512]{1,0:T(8,128)(2,1)S(1)}, u32[]{:S(2)}, u32[]{:S(2)}) collective-permute-start(bf16[128,512]{1,0:T(8,128)(2,1)S(1)} %slice.89), channel_id=1, source_target_pairs={{0,4},{4,8},{8,12},{12,14},{14,10},{10,6},{6,2},{2,0},{1,5},{5,9},... | collective-permute-start | bytes 393224 | tf_op jit(solution)/shard_map/ppermute | solution.py:288
  80.0 4.1 %shard_map.103 = (bf16[512,512]{1,0:T(8,128)(2,1)S(1)}, bf16[512,512]{1,0:T(8,128)(2,1)S(1)}) custom-call(s32[11]{0:T(128)S(1)} %pad_add_fusion.info, bf16[256,512]{1,0:T(8,128)(2,1)S(1)} %collective-permute-done.21.refs_0_, bf16[256,512]{1,0:T(8,128)(2,1)S(1)} %collective-permute-done.22.refs_1_, bf16[256,512]{1,0:T(8,128)(2,1)S(1)} %collective-permute-done.26.refs_2_, ...), custom_call_target="tpu_custom_call" | custom-call | flops 2818572288 | bytes 7602176 | tf_op jit(solution)/shard_map/pallas_call | solution.py:446
  85.1 1.4 %collective-permute-start.34 = (bf16[128,1024]{1,0:T(8,128)(2,1)S(1)}, bf16[128,1024]{1,0:T(8,128)(2,1)S(1)}, u32[]{:S(2)}, u32[]{:S(2)}) collective-permute-start(bf16[128,1024]{1,0:T(8,128)(2,1)S(1)} %collective-permute-done.15.first.rest_3_), channel_id=1, source_target_pairs={{0,4},{4,8},{8,12},{12,14},{14,10},{10,6},{6,2},{2,0},{1,5},{5,9},... | collective-permute-start | bytes 786440 | tf_op jit(solution)/shard_map/ppermute | solution.py:288
  87.1 2.4 %shard_map.104 = (bf16[256,512]{1,0:T(8,128)(2,1)S(1)}, bf16[256,512]{1,0:T(8,128)(2,1)S(1)}) custom-call(s32[11]{0:T(128)S(1)} %pad_add_fusion.info, bf16[128,512]{1,0:T(8,128)(2,1)S(1)} %collective-permute-done.29.refs_0_, bf16[128,512]{1,0:T(8,128)(2,1)S(1)} %collective-permute-done.30.refs_1_, bf16[128,512]{1,0:T(8,128)(2,1)S(1)} %collective-permute-done.31.refs_2_, ...), custom_call_target="tpu_custom_call" | custom-call | flops 1409286144 | bytes 6553600 | tf_op jit(solution)/shard_map/pallas_call | solution.py:446
  90.2 3.1 %collective-permute-done.34.first.rest_5_ = bf16[128,1024]{1,0:T(8,128)(2,1)S(1)} collective-permute-done((bf16[128,1024]{1,0:T(8,128)(2,1)S(1)}, bf16[128,1024]{1,0:T(8,128)(2,1)S(1)}, u32[]{:S(2)}, u32[]{:S(2)}) %collective-permute-start.34) | collective-permute-done | bytes 262176 | tf_op jit(solution)/shard_map/ppermute | solution.py:288
  94.5 1.4 %collective-permute-start.36 = (bf16[128,512]{1,0:T(8,128)(2,1)S(1)}, bf16[128,512]{1,0:T(8,128)(2,1)S(1)}, u32[]{:S(2)}, u32[]{:S(2)}) collective-permute-start(bf16[128,512]{1,0:T(8,128)(2,1)S(1)} %get-tuple-element.180), channel_id=1, source_target_pairs={{0,4},{4,8},{8,12},{12,14},{14,10},{10,6},{6,2},{2,0},{1,5},{5,9},... | collective-permute-start | bytes 393224 | tf_op jit(solution)/shard_map/ppermute | solution.py:288
  96.7 1.4 %collective-permute-start.40 = (bf16[64,1024]{1,0:T(8,128)(2,1)S(1)}, bf16[64,1024]{1,0:T(8,128)(2,1)S(1)}, u32[]{:S(2)}, u32[]{:S(2)}) collective-permute-start(bf16[64,1024]{1,0:T(8,128)(2,1)S(1)} %slice.93), channel_id=1, source_target_pairs={{0,4},{4,8},{8,12},{12,14},{14,10},{10,6},{6,2},{2,0},{1,5},{5,9},... | collective-permute-start | bytes 393224 | tf_op jit(solution)/shard_map/ppermute | solution.py:288
  98.7 4.1 %shard_map.105 = (bf16[512,512]{1,0:T(8,128)(2,1)S(1)}, bf16[512,512]{1,0:T(8,128)(2,1)S(1)}) custom-call(s32[11]{0:T(128)S(1)} %pad_add_fusion.info, bf16[256,512]{1,0:T(8,128)(2,1)S(1)} %collective-permute-done.18.refs_0_, bf16[256,512]{1,0:T(8,128)(2,1)S(1)} %collective-permute-done.19.refs_1_, bf16[256,512]{1,0:T(8,128)(2,1)S(1)} %collective-permute-done.38.refs_2_, ...), custom_call_target="tpu_custom_call" | custom-call | flops 2818572288 | bytes 7602176 | tf_op jit(solution)/shard_map/pallas_call | solution.py:446
  103.5 1.4 %collective-permute-start.42 = (bf16[256,512]{1,0:T(8,128)(2,1)S(1)}, bf16[256,512]{1,0:T(8,128)(2,1)S(1)}, u32[]{:S(2)}, u32[]{:S(2)}) collective-permute-start(bf16[256,512]{1,0:T(8,128)(2,1)S(1)} %pad_maximum_fusion), channel_id=1, source_target_pairs={{0,4},{4,8},{8,12},{12,14},{14,10},{10,6},{6,2},{2,0},{1,5},{5,9},... | collective-permute-start | bytes 786440 | tf_op jit(solution)/shard_map/ppermute | solution.py:288
  107.8 4.1 %collective-permute-done.42 = bf16[256,512]{1,0:T(8,128)(2,1)S(1)} collective-permute-done((bf16[256,512]{1,0:T(8,128)(2,1)S(1)}, bf16[256,512]{1,0:T(8,128)(2,1)S(1)}, u32[]{:S(2)}, u32[]{:S(2)}) %collective-permute-start.42) | collective-permute-done | bytes 262176 | tf_op jit(solution)/shard_map/ppermute | solution.py:288
  115.9 2.4 %shard_map.108 = (bf16[256,512]{1,0:T(8,128)(2,1)S(1)}, bf16[256,512]{1,0:T(8,128)(2,1)S(1)}) custom-call(s32[11]{0:T(128)S(1)} %pad_add_fusion.info, bf16[256,512]{1,0:T(8,128)(2,1)S(1)} %get-tuple-element.122.refs_0_, bf16[256,512]{1,0:T(8,128)(2,1)S(1)} %collective-permute-done.17.refs_1_, f32[256,8]{1,0:T(8,128)S(1)} %get-tuple-element.134.refs_4_.refs_2_, ...), custom_call_target="tpu_custom_call" | custom-call | flops 1409286144 | bytes 6553600 | tf_op jit(solution)/shard_map/pallas_call | solution.py:446
  118.3 3.7 %collective-permute-done.49.rest_11_ = bf16[256,1024]{1,0:T(8,128)(2,1)S(1)} collective-permute-done((bf16[256,1024]{1,0:T(8,128)(2,1)S(1)}, bf16[256,1024]{1,0:T(8,128)(2,1)S(1)}, u32[]{:S(2)}, u32[]{:S(2)}) %collective-permute-start.49) | collective-permute-done | bytes 524320 | tf_op jit(solution)/shard_map/ppermute | solution.py:297
  122.3 1.4 %collective-permute-start.50 = (bf16[256,512]{1,0:T(8,128)(2,1)S(1)}, bf16[256,512]{1,0:T(8,128)(2,1)S(1)}, u32[]{:S(2)}, u32[]{:S(2)}) collective-permute-start(bf16[256,512]{1,0:T(8,128)(2,1)S(1)} %get-tuple-element.174), channel_id=1, source_target_pairs={{0,4},{4,8},{8,12},{12,14},{14,10},{10,6},{6,2},{2,0},{1,5},{5,9},... | collective-permute-start | bytes 786440 | tf_op jit(solution)/shard_map/ppermute | solution.py:288
  124.4 2.9 %collective-permute-done.52.rest_12_ = bf16[128,1024]{1,0:T(8,128)(2,1)S(1)} collective-permute-done((bf16[128,1024]{1,0:T(8,128)(2,1)S(1)}, bf16[128,1024]{1,0:T(8,128)(2,1)S(1)}, u32[]{:S(2)}, u32[]{:S(2)}) %collective-permute-start.52) | collective-permute-done | bytes 262176 | tf_op jit(solution)/shard_map/ppermute | solution.py:297
  127.3 1.8 %shard_map.109.full = bf16[1024,2048]{1,0:T(8,128)(2,1)S(1)} custom-call(s32[11]{0:T(128)S(1)} %constant_dynamic-update-slice_fusion.info, bf16[128,2048]{1,0:T(8,128)(2,1)S(1)} %copy-done.4, bf16[128,1024]{1,0:T(8,128)(2,1)} %collective-permute-done.4.first.rest_1_, bf16[128,1024]{1,0:T(8,128)(2,1)} %collective-permute-done.5.second.rest_2_, ...), custom_call_target="tpu_custom_call" | custom-call | flops 2097152 | bytes 8388608 | tf_op jit(solution)/shard_map/pallas_call | solution.py:531
  132.6 2.0 %shard_map.111 = bf16[256,2048]{1,0:T(8,128)(2,1)} custom-call(s32[11]{0:T(128)S(1)} %pad_add_fusion.info, f32[256,2048]{1,0:T(8,128)S(1)} %shard_map.110.partial, bf16[256,512]{1,0:T(8,128)(2,1)S(1)} %collective-permute-done.53.back, bf16[1024,2048]{1,0:T(8,128)(2,1)S(1)} %shard_map.109.full), custom_call_target="tpu_custom_call" | custom-call | tf_op jit(solution)/shard_map/pallas_call | solution.py:552
  (120 shorter events, 32.7 us)
Async XLA Ops:
  3.7 27.7 %collective-permute-start.8 = (bf16[128,4096]{1,0:T(8,128)(2,1)}, bf16[128,4096]{1,0:T(8,128)(2,1)}, u32[]{:S(2)}, u32[]{:S(2)}) collective-permute-start(bf16[128,4096]{1,0:T(8,128)(2,1)} %get-tuple-element.112), channel_id=1, source_target_pairs={{0,16},{16,0},{1,17},{17,1},{2,18},{18,2},{3,19},{19,3},{4,20},{20... | collective-permute-start | bytes 3145736 | tf_op jit(solution)/shard_map/ppermute | solution.py:297
  6.7 9.8 %collective-permute-start = (bf16[544,256]{1,0:T(8,128)(2,1)}, bf16[544,256]{1,0:T(8,128)(2,1)S(1)}, u32[]{:S(2)}, u32[]{:S(2)}) collective-permute-start(bf16[544,256]{1,0:T(8,128)(2,1)} %get-tuple-element.95.refs_0_.refs_2_), channel_id=1, source_target_pairs={{0,4},{4,8},{8,12},{12,14},{14,10},{10,6},{6,2},{2,0},{1,5},{5,9},... | collective-permute-start | bytes 835592 | tf_op jit(solution)/shard_map/ppermute | solution.py:288
  8.3 9.8 %collective-permute-start.1 = (bf16[544,256]{1,0:T(8,128)(2,1)}, bf16[544,256]{1,0:T(8,128)(2,1)S(1)}, u32[]{:S(2)}, u32[]{:S(2)}) collective-permute-start(bf16[544,256]{1,0:T(8,128)(2,1)} %get-tuple-element.95.refs_0_.refs_2_), channel_id=1, source_target_pairs={{4,0},{8,4},{12,8},{14,12},{10,14},{6,10},{2,6},{0,2},{5,1},{9,5},... | collective-permute-start | bytes 835592 | tf_op jit(solution)/shard_map/ppermute | solution.py:291
  9.4 12.8 %collective-permute-start.4 = (bf16[128,1024]{1,0:T(8,128)(2,1)}, bf16[128,1024]{1,0:T(8,128)(2,1)}, u32[]{:S(2)}, u32[]{:S(2)}) collective-permute-start(bf16[128,1024]{1,0:T(8,128)(2,1)} %constant_dynamic-slice_fusion), channel_id=1, source_target_pairs={{0,4},{4,8},{8,12},{12,14},{14,10},{10,6},{6,2},{2,0},{1,5},{5,9},... | collective-permute-start | bytes 786440 | tf_op jit(solution)/shard_map/ppermute | solution.py:288
  11.0 12.8 %collective-permute-start.5 = (bf16[128,1024]{1,0:T(8,128)(2,1)}, bf16[128,1024]{1,0:T(8,128)(2,1)}, u32[]{:S(2)}, u32[]{:S(2)}) collective-permute-start(bf16[128,1024]{1,0:T(8,128)(2,1)} %constant_dynamic-slice_fusion), channel_id=1, source_target_pairs={{4,0},{8,4},{12,8},{14,12},{10,14},{6,10},{2,6},{0,2},{5,1},{9,5},... | collective-permute-start | bytes 786440 | tf_op jit(solution)/shard_map/ppermute | solution.py:291
  18.1 8.6 %collective-permute-start.2 = (bf16[544,256]{1,0:T(8,128)(2,1)S(1)}, bf16[544,256]{1,0:T(8,128)(2,1)}, u32[]{:S(2)}, u32[]{:S(2)}) collective-permute-start(bf16[544,256]{1,0:T(8,128)(2,1)S(1)} %collective-permute-done.refs_1_.refs_3_), channel_id=1, source_target_pairs={{0,4},{4,8},{8,12},{12,14},{14,10},{10,6},{6,2},{2,0},{1,5},{5,9},... | collective-permute-start | bytes 835592 | tf_op jit(solution)/shard_map/ppermute | solution.py:288
  19.6 8.4 %collective-permute-start.3 = (bf16[544,256]{1,0:T(8,128)(2,1)S(1)}, bf16[544,256]{1,0:T(8,128)(2,1)}, u32[]{:S(2)}, u32[]{:S(2)}) collective-permute-start(bf16[544,256]{1,0:T(8,128)(2,1)S(1)} %collective-permute-done.1.refs_2_.refs_4_), channel_id=1, source_target_pairs={{4,0},{8,4},{12,8},{14,12},{10,14},{6,10},{2,6},{0,2},{5,1},{9,5},... | collective-permute-start | bytes 835592 | tf_op jit(solution)/shard_map/ppermute | solution.py:291
  28.0 7.1 %collective-permute-start.6 = (bf16[544,256]{1,0:T(8,128)(2,1)}, bf16[544,256]{1,0:T(8,128)(2,1)S(1)}, u32[]{:S(2)}, u32[]{:S(2)}) collective-permute-start(bf16[544,256]{1,0:T(8,128)(2,1)} %collective-permute-done.2.refs_0_.refs_5_), channel_id=1, source_target_pairs={{0,4},{4,8},{8,12},{12,14},{14,10},{10,6},{6,2},{2,0},{1,5},{5,9},... | collective-permute-start | bytes 835592 | tf_op jit(solution)/shard_map/ppermute | solution.py:288
  29.6 6.8 %collective-permute-start.7 = (bf16[544,256]{1,0:T(8,128)(2,1)}, bf16[544,256]{1,0:T(8,128)(2,1)S(1)}, u32[]{:S(2)}, u32[]{:S(2)}) collective-permute-start(bf16[544,256]{1,0:T(8,128)(2,1)} %collective-permute-done.3.refs_1_.refs_6_), channel_id=1, source_target_pairs={{4,0},{8,4},{12,8},{14,12},{10,14},{6,10},{2,6},{0,2},{5,1},{9,5},... | collective-permute-start | bytes 835592 | tf_op jit(solution)/shard_map/ppermute | solution.py:291
  36.4 6.3 %collective-permute-start.10 = (bf16[288,256]{1,0:T(8,128)(2,1)S(1)}, bf16[288,256]{1,0:T(8,128)(2,1)S(1)}, u32[]{:S(2)}, u32[]{:S(2)}) collective-permute-start(bf16[288,256]{1,0:T(8,128)(2,1)S(1)} %slice.85), channel_id=1, source_target_pairs={{4,0},{8,4},{12,8},{14,12},{10,14},{6,10},{2,6},{0,2},{5,1},{9,5},... | collective-permute-start | bytes 442376 | tf_op jit(solution)/shard_map/ppermute | solution.py:291
  37.0 5.7 %collective-permute-start.9 = (bf16[256,256]{1,0:T(8,128)(2,1)S(1)}, bf16[256,256]{1,0:T(8,128)(2,1)S(1)}, u32[]{:S(2)}, u32[]{:S(2)}) collective-permute-start(bf16[256,256]{1,0:T(8,128)(2,1)S(1)} %slice.84), channel_id=1, source_target_pairs={{0,4},{4,8},{8,12},{12,14},{14,10},{10,6},{6,2},{2,0},{1,5},{5,9},... | collective-permute-start | bytes 393224 | tf_op jit(solution)/shard_map/ppermute | solution.py:288
  43.5 5.2 %collective-permute-start.12 = (bf16[256,256]{1,0:T(8,128)(2,1)S(1)}, bf16[256,256]{1,0:T(8,128)(2,1)S(1)}, u32[]{:S(2)}, u32[]{:S(2)}) collective-permute-start(bf16[256,256]{1,0:T(8,128)(2,1)S(1)} %shard_map.99), channel_id=1, source_target_pairs={{0,16},{16,0},{1,17},{17,1},{2,18},{18,2},{3,19},{19,3},{4,20},{20... | collective-permute-start | bytes 393224 | tf_op jit(solution)/shard_map/ppermute | solution.py:297
  44.1 8.8 %collective-permute-start.15 = (bf16[128,1024]{1,0:T(8,128)(2,1)}, bf16[128,1024]{1,0:T(8,128)(2,1)S(1)}, u32[]{:S(2)}, u32[]{:S(2)}) collective-permute-start(bf16[128,1024]{1,0:T(8,128)(2,1)} %collective-permute-done.4.first.rest_1_), channel_id=1, source_target_pairs={{0,4},{4,8},{8,12},{12,14},{14,10},{10,6},{6,2},{2,0},{1,5},{5,9},... | collective-permute-start | bytes 786440 | tf_op jit(solution)/shard_map/ppermute | solution.py:288
  45.7 9.4 %collective-permute-start.16 = (bf16[128,1024]{1,0:T(8,128)(2,1)}, bf16[128,1024]{1,0:T(8,128)(2,1)S(1)}, u32[]{:S(2)}, u32[]{:S(2)}) collective-permute-start(bf16[128,1024]{1,0:T(8,128)(2,1)} %collective-permute-done.5.second.rest_2_), channel_id=1, source_target_pairs={{4,0},{8,4},{12,8},{14,12},{10,14},{6,10},{2,6},{0,2},{5,1},{9,5},... | collective-permute-start | bytes 786440 | tf_op jit(solution)/shard_map/ppermute | solution.py:291
  49.5 8.1 %collective-permute-start.13 = (bf16[256,512]{1,0:T(8,128)(2,1)S(1)}, bf16[256,512]{1,0:T(8,128)(2,1)S(1)}, u32[]{:S(2)}, u32[]{:S(2)}) collective-permute-start(bf16[256,512]{1,0:T(8,128)(2,1)S(1)} %get-tuple-element.122.refs_0_), channel_id=1, source_target_pairs={{0,4},{4,8},{8,12},{12,14},{14,10},{10,6},{6,2},{2,0},{1,5},{5,9},... | collective-permute-start | bytes 786440 | tf_op jit(solution)/shard_map/ppermute | solution.py:288
  51.1 7.8 %collective-permute-start.14 = (bf16[256,512]{1,0:T(8,128)(2,1)S(1)}, bf16[256,512]{1,0:T(8,128)(2,1)S(1)}, u32[]{:S(2)}, u32[]{:S(2)}) collective-permute-start(bf16[256,512]{1,0:T(8,128)(2,1)S(1)} %get-tuple-element.122.refs_0_), channel_id=1, source_target_pairs={{4,0},{8,4},{12,8},{14,12},{10,14},{6,10},{2,6},{0,2},{5,1},{9,5},... | collective-permute-start | bytes 786440 | tf_op jit(solution)/shard_map/ppermute | solution.py:291
  51.6 7.3 %collective-permute-start.17 = (bf16[256,512]{1,0:T(8,128)(2,1)S(1)}, bf16[256,512]{1,0:T(8,128)(2,1)S(1)}, u32[]{:S(2)}, u32[]{:S(2)}) collective-permute-start(bf16[256,512]{1,0:T(8,128)(2,1)S(1)} %get-tuple-element.122.refs_0_), channel_id=1, source_target_pairs={{0,1},{1,0},{2,3},{3,2},{4,5},{5,4},{6,7},{7,6},{8,9},{9,8},{10,11... | collective-permute-start | bytes 786440 | tf_op jit(solution)/shard_map/ppermute | solution.py:294
  53.0 14.1 %collective-permute-start.20 = (bf16[256,1024]{1,0:T(8,128)(2,1)S(1)}, bf16[256,1024]{1,0:T(8,128)(2,1)S(1)}, u32[]{:S(2)}, u32[]{:S(2)}) collective-permute-start(bf16[256,1024]{1,0:T(8,128)(2,1)S(1)} %shard_map.94), channel_id=1, source_target_pairs={{0,16},{16,0},{1,17},{17,1},{2,18},{18,2},{3,19},{19,3},{4,20},{20... | collective-permute-start | bytes 1572872 | tf_op jit(solution)/shard_map/ppermute | solution.py:297
  58.9 6.9 %collective-permute-start.18 = (bf16[256,512]{1,0:T(8,128)(2,1)S(1)}, bf16[256,512]{1,0:T(8,128)(2,1)S(1)}, u32[]{:S(2)}, u32[]{:S(2)}) collective-permute-start(bf16[256,512]{1,0:T(8,128)(2,1)S(1)} %collective-permute-done.13.refs_0_), channel_id=1, source_target_pairs={{0,4},{4,8},{8,12},{12,14},{14,10},{10,6},{6,2},{2,0},{1,5},{5,9},... | collective-permute-start | bytes 786440 | tf_op jit(solution)/shard_map/ppermute | solution.py:288
  60.4 6.6 %collective-permute-start.19 = (bf16[256,512]{1,0:T(8,128)(2,1)S(1)}, bf16[256,512]{1,0:T(8,128)(2,1)S(1)}, u32[]{:S(2)}, u32[]{:S(2)}) collective-permute-start(bf16[256,512]{1,0:T(8,128)(2,1)S(1)} %collective-permute-done.14.refs_1_), channel_id=1, source_target_pairs={{4,0},{8,4},{12,8},{14,12},{10,14},{6,10},{2,6},{0,2},{5,1},{9,5},... | collective-permute-start | bytes 786440 | tf_op jit(solution)/shard_map/ppermute | solution.py:291
  60.9 8.1 %collective-permute-start.23 = (bf16[256,512]{1,0:T(8,128)(2,1)S(1)}, bf16[256,512]{1,0:T(8,128)(2,1)S(1)}, u32[]{:S(2)}, u32[]{:S(2)}) collective-permute-start(bf16[256,512]{1,0:T(8,128)(2,1)S(1)} %collective-permute-done.13.refs_0_), channel_id=1, source_target_pairs={{0,1},{1,0},{2,3},{3,2},{4,5},{5,4},{6,7},{7,6},{8,9},{9,8},{10,11... | collective-permute-start | bytes 786440 | tf_op jit(solution)/shard_map/ppermute | solution.py:294
  61.0 8.1 %collective-permute-start.24 = (bf16[256,512]{1,0:T(8,128)(2,1)S(1)}, bf16[256,512]{1,0:T(8,128)(2,1)S(1)}, u32[]{:S(2)}, u32[]{:S(2)}) collective-permute-start(bf16[256,512]{1,0:T(8,128)(2,1)S(1)} %collective-permute-done.14.refs_1_), channel_id=1, source_target_pairs={{0,1},{1,0},{2,3},{3,2},{4,5},{5,4},{6,7},{7,6},{8,9},{9,8},{10,11... | collective-permute-start | bytes 786440 | tf_op jit(solution)/shard_map/ppermute | solution.py:294
  65.8 11.6 %collective-permute-start.25 = (bf16[256,1024]{1,0:T(8,128)(2,1)S(1)}, bf16[256,1024]{1,0:T(8,128)(2,1)S(1)}, u32[]{:S(2)}, u32[]{:S(2)}) collective-permute-start(bf16[256,1024]{1,0:T(8,128)(2,1)S(1)} %shard_map.101), channel_id=1, source_target_pairs={{0,16},{16,0},{1,17},{17,1},{2,18},{18,2},{3,19},{19,3},{4,20},{20... | collective-permute-start | bytes 1572872 | tf_op jit(solution)/shard_map/ppermute | solution.py:297
  67.0 6.4 %collective-permute-start.21 = (bf16[256,512]{1,0:T(8,128)(2,1)S(1)}, bf16[256,512]{1,0:T(8,128)(2,1)S(1)}, u32[]{:S(2)}, u32[]{:S(2)}) collective-permute-start(bf16[256,512]{1,0:T(8,128)(2,1)S(1)} %collective-permute-done.18.refs_0_), channel_id=1, source_target_pairs={{0,4},{4,8},{8,12},{12,14},{14,10},{10,6},{6,2},{2,0},{1,5},{5,9},... | collective-permute-start | bytes 786440 | tf_op jit(solution)/shard_map/ppermute | solution.py:288
  68.4 6.4 %collective-permute-start.22 = (bf16[256,512]{1,0:T(8,128)(2,1)S(1)}, bf16[256,512]{1,0:T(8,128)(2,1)S(1)}, u32[]{:S(2)}, u32[]{:S(2)}) collective-permute-start(bf16[256,512]{1,0:T(8,128)(2,1)S(1)} %collective-permute-done.19.refs_1_), channel_id=1, source_target_pairs={{4,0},{8,4},{12,8},{14,12},{10,14},{6,10},{2,6},{0,2},{5,1},{9,5},... | collective-permute-start | bytes 786440 | tf_op jit(solution)/shard_map/ppermute | solution.py:291
  77.9 6.1 %collective-permute-start.29 = (bf16[128,512]{1,0:T(8,128)(2,1)S(1)}, bf16[128,512]{1,0:T(8,128)(2,1)S(1)}, u32[]{:S(2)}, u32[]{:S(2)}) collective-permute-start(bf16[128,512]{1,0:T(8,128)(2,1)S(1)} %slice.89), channel_id=1, source_target_pairs={{0,4},{4,8},{8,12},{12,14},{14,10},{10,6},{6,2},{2,0},{1,5},{5,9},... | collective-permute-start | bytes 393224 | tf_op jit(solution)/shard_map/ppermute | solution.py:288
  79.4 5.1 %collective-permute-start.30 = (bf16[128,512]{1,0:T(8,128)(2,1)S(1)}, bf16[128,512]{1,0:T(8,128)(2,1)S(1)}, u32[]{:S(2)}, u32[]{:S(2)}) collective-permute-start(bf16[128,512]{1,0:T(8,128)(2,1)S(1)} %slice.90), channel_id=1, source_target_pairs={{4,0},{8,4},{12,8},{14,12},{10,14},{6,10},{2,6},{0,2},{5,1},{9,5},... | collective-permute-start | bytes 393224 | tf_op jit(solution)/shard_map/ppermute | solution.py:291
  85.1 8.2 %collective-permute-start.34 = (bf16[128,1024]{1,0:T(8,128)(2,1)S(1)}, bf16[128,1024]{1,0:T(8,128)(2,1)S(1)}, u32[]{:S(2)}, u32[]{:S(2)}) collective-permute-start(bf16[128,1024]{1,0:T(8,128)(2,1)S(1)} %collective-permute-done.15.first.rest_3_), channel_id=1, source_target_pairs={{0,4},{4,8},{8,12},{12,14},{14,10},{10,6},{6,2},{2,0},{1,5},{5,9},... | collective-permute-start | bytes 786440 | tf_op jit(solution)/shard_map/ppermute | solution.py:288
  86.5 7.9 %collective-permute-start.35 = (bf16[128,1024]{1,0:T(8,128)(2,1)S(1)}, bf16[128,1024]{1,0:T(8,128)(2,1)S(1)}, u32[]{:S(2)}, u32[]{:S(2)}) collective-permute-start(bf16[128,1024]{1,0:T(8,128)(2,1)S(1)} %collective-permute-done.16.second.rest_4_), channel_id=1, source_target_pairs={{4,0},{8,4},{12,8},{14,12},{10,14},{6,10},{2,6},{0,2},{5,1},{9,5},... | collective-permute-start | bytes 786440 | tf_op jit(solution)/shard_map/ppermute | solution.py:291
  89.5 4.9 %collective-permute-start.33 = (bf16[256,512]{1,0:T(8,128)(2,1)S(1)}, bf16[256,512]{1,0:T(8,128)(2,1)S(1)}, u32[]{:S(2)}, u32[]{:S(2)}) collective-permute-start(bf16[256,512]{1,0:T(8,128)(2,1)S(1)} %get-tuple-element.144), channel_id=1, source_target_pairs={{0,1},{1,0},{2,3},{3,2},{4,5},{5,4},{6,7},{7,6},{8,9},{9,8},{10,11... | collective-permute-start | bytes 786440 | tf_op jit(solution)/shard_map/ppermute | solution.py:294
  89.6 7.1 %collective-permute-start.38 = (bf16[256,512]{1,0:T(8,128)(2,1)S(1)}, bf16[256,512]{1,0:T(8,128)(2,1)S(1)}, u32[]{:S(2)}, u32[]{:S(2)}) collective-permute-start(bf16[256,512]{1,0:T(8,128)(2,1)S(1)} %collective-permute-done.18.refs_0_), channel_id=1, source_target_pairs={{0,1},{1,0},{2,3},{3,2},{4,5},{5,4},{6,7},{7,6},{8,9},{9,8},{10,11... | collective-permute-start | bytes 786440 | tf_op jit(solution)/shard_map/ppermute | solution.py:294
  90.1 7.9 %collective-permute-start.39 = (bf16[256,512]{1,0:T(8,128)(2,1)S(1)}, bf16[256,512]{1,0:T(8,128)(2,1)S(1)}, u32[]{:S(2)}, u32[]{:S(2)}) collective-permute-start(bf16[256,512]{1,0:T(8,128)(2,1)S(1)} %collective-permute-done.19.refs_1_), channel_id=1, source_target_pairs={{0,1},{1,0},{2,3},{3,2},{4,5},{5,4},{6,7},{7,6},{8,9},{9,8},{10,11... | collective-permute-start | bytes 786440 | tf_op jit(solution)/shard_map/ppermute | solution.py:294
  93.3 9.5 %collective-permute-start.28 = (bf16[512,512]{1,0:T(8,128)(2,1)S(1)}, bf16[512,512]{1,0:T(8,128)(2,1)S(1)}, u32[]{:S(2)}, u32[]{:S(2)}) collective-permute-start(bf16[512,512]{1,0:T(8,128)(2,1)S(1)} %get-tuple-element.140), channel_id=1, source_target_pairs={{0,1},{1,0},{2,3},{3,2},{4,5},{5,4},{6,7},{7,6},{8,9},{9,8},{10,11... | collective-permute-start | bytes 1572872 | tf_op jit(solution)/shard_map/ppermute | solution.py:294
  94.5 8.9 %collective-permute-start.36 = (bf16[128,512]{1,0:T(8,128)(2,1)S(1)}, bf16[128,512]{1,0:T(8,128)(2,1)S(1)}, u32[]{:S(2)}, u32[]{:S(2)}) collective-permute-start(bf16[128,512]{1,0:T(8,128)(2,1)S(1)} %get-tuple-element.180), channel_id=1, source_target_pairs={{0,4},{4,8},{8,12},{12,14},{14,10},{10,6},{6,2},{2,0},{1,5},{5,9},... | collective-permute-start | bytes 393224 | tf_op jit(solution)/shard_map/ppermute | solution.py:288
  95.9 7.6 %collective-permute-start.37 = (bf16[128,512]{1,0:T(8,128)(2,1)S(1)}, bf16[128,512]{1,0:T(8,128)(2,1)S(1)}, u32[]{:S(2)}, u32[]{:S(2)}) collective-permute-start(bf16[128,512]{1,0:T(8,128)(2,1)S(1)} %get-tuple-element.179), channel_id=1, source_target_pairs={{4,0},{8,4},{12,8},{14,12},{10,14},{6,10},{2,6},{0,2},{5,1},{9,5},... | collective-permute-start | bytes 393224 | tf_op jit(solution)/shard_map/ppermute | solution.py:291
  96.7 6.5 %collective-permute-start.40 = (bf16[64,1024]{1,0:T(8,128)(2,1)S(1)}, bf16[64,1024]{1,0:T(8,128)(2,1)S(1)}, u32[]{:S(2)}, u32[]{:S(2)}) collective-permute-start(bf16[64,1024]{1,0:T(8,128)(2,1)S(1)} %slice.93), channel_id=1, source_target_pairs={{0,4},{4,8},{8,12},{12,14},{14,10},{10,6},{6,2},{2,0},{1,5},{5,9},... | collective-permute-start | bytes 393224 | tf_op jit(solution)/shard_map/ppermute | solution.py:288
  98.0 5.5 %collective-permute-start.41 = (bf16[64,1024]{1,0:T(8,128)(2,1)S(1)}, bf16[64,1024]{1,0:T(8,128)(2,1)S(1)}, u32[]{:S(2)}, u32[]{:S(2)}) collective-permute-start(bf16[64,1024]{1,0:T(8,128)(2,1)S(1)} %slice.94), channel_id=1, source_target_pairs={{4,0},{8,4},{12,8},{14,12},{10,14},{6,10},{2,6},{0,2},{5,1},{9,5},... | collective-permute-start | bytes 393224 | tf_op jit(solution)/shard_map/ppermute | solution.py:291
  102.8 10.3 %collective-permute-start.46 = (bf16[512,512]{1,0:T(8,128)(2,1)S(1)}, bf16[512,512]{1,0:T(8,128)(2,1)S(1)}, u32[]{:S(2)}, u32[]{:S(2)}) collective-permute-start(bf16[512,512]{1,0:T(8,128)(2,1)S(1)} %get-tuple-element.152), channel_id=1, source_target_pairs={{0,1},{1,0},{2,3},{3,2},{4,5},{5,4},{6,7},{7,6},{8,9},{9,8},{10,11... | collective-permute-start | bytes 1572872 | tf_op jit(solution)/shard_map/ppermute | solution.py:294
  103.5 8.4 %collective-permute-start.42 = (bf16[256,512]{1,0:T(8,128)(2,1)S(1)}, bf16[256,512]{1,0:T(8,128)(2,1)S(1)}, u32[]{:S(2)}, u32[]{:S(2)}) collective-permute-start(bf16[256,512]{1,0:T(8,128)(2,1)S(1)} %pad_maximum_fusion), channel_id=1, source_target_pairs={{0,4},{4,8},{8,12},{12,14},{14,10},{10,6},{6,2},{2,0},{1,5},{5,9},... | collective-permute-start | bytes 786440 | tf_op jit(solution)/shard_map/ppermute | solution.py:288
  105.0 8.1 %collective-permute-start.43 = (bf16[256,512]{1,0:T(8,128)(2,1)S(1)}, bf16[256,512]{1,0:T(8,128)(2,1)S(1)}, u32[]{:S(2)}, u32[]{:S(2)}) collective-permute-start(bf16[256,512]{1,0:T(8,128)(2,1)S(1)} %pad_maximum_fusion.1), channel_id=1, source_target_pairs={{4,0},{8,4},{12,8},{14,12},{10,14},{6,10},{2,6},{0,2},{5,1},{9,5},... | collective-permute-start | bytes 786440 | tf_op jit(solution)/shard_map/ppermute | solution.py:291
  105.7 16.3 %collective-permute-start.45 = (bf16[512,512]{1,0:T(8,128)(2,1)S(1)}, bf16[512,512]{1,0:T(8,128)(2,1)S(1)}, u32[]{:S(2)}, u32[]{:S(2)}) collective-permute-start(bf16[512,512]{1,0:T(8,128)(2,1)S(1)} %get-tuple-element.136), channel_id=1, source_target_pairs={{0,1},{1,0},{2,3},{3,2},{4,5},{5,4},{6,7},{7,6},{8,9},{9,8},{10,11... | collective-permute-start | bytes 1572872 | tf_op jit(solution)/shard_map/ppermute | solution.py:294
  107.2 14.8 %collective-permute-start.49 = (bf16[256,1024]{1,0:T(8,128)(2,1)S(1)}, bf16[256,1024]{1,0:T(8,128)(2,1)S(1)}, u32[]{:S(2)}, u32[]{:S(2)}) collective-permute-start(bf16[256,1024]{1,0:T(8,128)(2,1)S(1)} %shard_map.106), channel_id=1, source_target_pairs={{0,16},{16,0},{1,17},{17,1},{2,18},{18,2},{3,19},{19,3},{4,20},{20... | collective-permute-start | bytes 1572872 | tf_op jit(solution)/shard_map/ppermute | solution.py:297
  113.3 8.7 %collective-permute-start.47 = (bf16[256,512]{1,0:T(8,128)(2,1)S(1)}, bf16[256,512]{1,0:T(8,128)(2,1)S(1)}, u32[]{:S(2)}, u32[]{:S(2)}) collective-permute-start(bf16[256,512]{1,0:T(8,128)(2,1)S(1)} %get-tuple-element.176), channel_id=1, source_target_pairs={{0,4},{4,8},{8,12},{12,14},{14,10},{10,6},{6,2},{2,0},{1,5},{5,9},... | collective-permute-start | bytes 786440 | tf_op jit(solution)/shard_map/ppermute | solution.py:288
  114.5 7.5 %collective-permute-start.48 = (bf16[256,512]{1,0:T(8,128)(2,1)S(1)}, bf16[256,512]{1,0:T(8,128)(2,1)S(1)}, u32[]{:S(2)}, u32[]{:S(2)}) collective-permute-start(bf16[256,512]{1,0:T(8,128)(2,1)S(1)} %get-tuple-element.175), channel_id=1, source_target_pairs={{4,0},{8,4},{12,8},{14,12},{10,14},{6,10},{2,6},{0,2},{5,1},{9,5},... | collective-permute-start | bytes 786440 | tf_op jit(solution)/shard_map/ppermute | solution.py:291
  115.4 11.9 %collective-permute-start.52 = (bf16[128,1024]{1,0:T(8,128)(2,1)S(1)}, bf16[128,1024]{1,0:T(8,128)(2,1)S(1)}, u32[]{:S(2)}, u32[]{:S(2)}) collective-permute-start(bf16[128,1024]{1,0:T(8,128)(2,1)S(1)} %shard_map.107), channel_id=1, source_target_pairs={{0,16},{16,0},{1,17},{17,1},{2,18},{18,2},{3,19},{19,3},{4,20},{20... | collective-permute-start | bytes 786440 | tf_op jit(solution)/shard_map/ppermute | solution.py:297
  122.3 7.6 %collective-permute-start.50 = (bf16[256,512]{1,0:T(8,128)(2,1)S(1)}, bf16[256,512]{1,0:T(8,128)(2,1)S(1)}, u32[]{:S(2)}, u32[]{:S(2)}) collective-permute-start(bf16[256,512]{1,0:T(8,128)(2,1)S(1)} %get-tuple-element.174), channel_id=1, source_target_pairs={{0,4},{4,8},{8,12},{12,14},{14,10},{10,6},{6,2},{2,0},{1,5},{5,9},... | collective-permute-start | bytes 786440 | tf_op jit(solution)/shard_map/ppermute | solution.py:288
  123.6 7.3 %collective-permute-start.51 = (bf16[256,512]{1,0:T(8,128)(2,1)S(1)}, bf16[256,512]{1,0:T(8,128)(2,1)S(1)}, u32[]{:S(2)}, u32[]{:S(2)}) collective-permute-start(bf16[256,512]{1,0:T(8,128)(2,1)S(1)} %get-tuple-element.173), channel_id=1, source_target_pairs={{4,0},{8,4},{12,8},{14,12},{10,14},{6,10},{2,6},{0,2},{5,1},{9,5},... | collective-permute-start | bytes 786440 | tf_op jit(solution)/shard_map/ppermute | solution.py:291
  124.3 6.6 %collective-permute-start.44 = (bf16[256,512]{1,0:T(8,128)(2,1)S(1)}, bf16[256,512]{1,0:T(8,128)(2,1)S(1)}, u32[]{:S(2)}, u32[]{:S(2)}) collective-permute-start(bf16[256,512]{1,0:T(8,128)(2,1)S(1)} %get-tuple-element.164), channel_id=1, source_target_pairs={{0,1},{1,0},{2,3},{3,2},{4,5},{5,4},{6,7},{7,6},{8,9},{9,8},{10,11... | collective-permute-start | bytes 786440 | tf_op jit(solution)/shard_map/ppermute | solution.py:294
  (13 other events, 110.4 us)
